TPU v7x, 32 devices: a whole 2x2x4 slice. The times are simulated.
32 devices in a mesh: ra: 16 (over z, x, core), band: 2 (over y).
Axes of the slice: x: 2, y: 2, z: 4, core: 2. Of those that a mesh axis runs over, the one named last changes fastest.
Arguments:
- tiles: bfloat16 [1024, 64, 128], P(('ra', 'band')), may hold values from -6 to 6
- tile_patch: int32 [1024], P(('ra', 'band')), may hold values from 0 to 15, as said below
- tile_offset: int32 [1024], P(('ra', 'band')), may hold values from 0 to 128
- tile_weight: bfloat16 [1024], P(('ra', 'band')), may hold values from 0.25 to 4
- visit_band: int32 [128], P(('ra', 'band')), may hold values from 0 to 5
- coeff_index: int32 [1024], P(('ra', 'band')), may hold values from 0 to 63
- coeff_table: float32 [64, 21], replicated, may hold values from -1.3 to 1.3
- row_kernels: bfloat16 [21, 21], replicated, may hold values from -1.25 to 1.25
- column_kernels: bfloat16 [21, 21], replicated, may hold values from -1.25 to 1.25
- band_weight: float32 [6], replicated, may hold values from 0.3 to 1.5
Outputs:
- band_coadds: float32 [6, 64, 4096], P(None, 'band', 'ra')
- detection: float32 [64, 4096], P('band', 'ra')
Inputs may be any that keep to these rules, and one draw needn't show every extreme that they name: `tile_patch`: tile j is owned by RA index o = j // 64 and by group g = (j // 32) % 2 of visit owners; its patch lies within 2 patches of o around the cycle of 16 patches. Among the tiles of one device at most 16 fall on one patch, and in every draw, for each group g, one patch receives exactly 16 tiles from each of the 5 devices of group g within reach.
All inputs are finite; a program needn't handle non-finite values.
Results may differ from a plain program's by a relative error of at most 0.005.
Values may be sent and summed in bfloat16 or wider, within the bound.
No kernel may reach another device: no remote copies, remote signals or barrier semaphores. Data moves between devices by JAX's collectives and lax.ppermute only.
A program may use at most 64 MiB of HBM per device.

v0:
```python
import jax
import jax.numpy as jnp
from jax import lax
from jax.sharding import PartitionSpec as P

PW = 256
BANDS = 6
REACH = 2


HIGHEST_PRECISION = lax.Precision.HIGHEST


def shifted(block, axis, distance):
    devices = range(lax.axis_size(axis))
    route = [((i - distance) % len(devices), i) for i in devices]
    return lax.ppermute(block, axis, route)


def band_matrices(kernels, extent):
    tap_count = kernels.shape[1]
    tap_of = jnp.arange(extent)[None, :] - jnp.arange(extent)[:, None] + tap_count // 2
    tap_hits = (tap_of[None, :, :] == jnp.arange(tap_count)[:, None, None]).astype(jnp.float32)
    return jnp.einsum(
        "kl,lab->kab", kernels.astype(jnp.float32), tap_hits, precision=HIGHEST_PRECISION
    )


def lookup(table_index, coeff_rows):
    one_hot = (table_index[:, None] == jnp.arange(coeff_rows.shape[0])[None, :]).astype(jnp.float32)
    return jnp.dot(one_hot, coeff_rows, precision=HIGHEST_PRECISION)


def match_block(tiles_in, coeffs, colmats, rowmats):
    column_pass = jnp.einsum(
        "jic,kdc->jkid", tiles_in, colmats, preferred_element_type=jnp.float32
    ).astype(jnp.bfloat16)
    scaled = (coeffs[:, :, None, None] * rowmats[None]).astype(jnp.bfloat16)
    return jnp.einsum(
        "jkab,jkbd->jad", scaled, column_pass, preferred_element_type=jnp.float32
    ).astype(jnp.bfloat16)


def place_block(matched, tile_meta):
    weights = tile_meta[:, 0].astype(jnp.float32)
    offsets = tile_meta[:, 1].astype(jnp.int32)
    bands = tile_meta[:, 2].astype(jnp.int32)
    tile_width = matched.shape[2]
    columns = jnp.arange(PW)
    lands = columns[None, None, :] == offsets[:, None, None] + jnp.arange(tile_width)[None, :, None]
    shifter = jnp.where(lands, weights[:, None, None], 0.0).astype(jnp.bfloat16)
    placed = jnp.einsum("jid,jdq->jiq", matched, shifter, preferred_element_type=jnp.float32)
    one_hot = (bands[:, None] == jnp.arange(BANDS)[None, :]).astype(jnp.float32)
    numerator = jnp.einsum("jb,jiq->biq", one_hot, placed, precision=HIGHEST_PRECISION)
    covered = (columns[None, :] >= offsets[:, None]) & (
        columns[None, :] < offsets[:, None] + tile_width
    )
    weight_sum = jnp.einsum(
        "jb,jq->bq", one_hot, jnp.where(covered, weights[:, None], 0.0), precision=HIGHEST_PRECISION
    )
    return (numerator, weight_sum)


def local(
    tiles,
    tile_patch,
    tile_offset,
    tile_weight,
    visit_band,
    coeff_index,
    coeff_table,
    row_kernels,
    column_kernels,
    band_weight,
):
    tile_count = tiles.shape[0]
    tile_rows = tiles.shape[1]
    tile_width = tiles.shape[2]
    capacity = tile_count // 2
    spread = 2 * REACH + 1
    rowmats = band_matrices(row_kernels, tile_rows)
    colmats = band_matrices(column_kernels, tile_width).astype(jnp.bfloat16)
    tile_band = jnp.repeat(visit_band, tile_count // visit_band.shape[0])
    tile_meta = jnp.stack(
        [
            tile_weight.astype(jnp.float32),
            tile_offset.astype(jnp.float32),
            tile_band.astype(jnp.float32),
            coeff_index.astype(jnp.float32),
        ],
        axis=1,
    ).astype(jnp.bfloat16)
    owner_index = lax.axis_index("ra")
    patch_total = lax.axis_size("ra")
    bucket = (tile_patch - owner_index + REACH) % patch_total
    in_bucket = (bucket[:, None] == jnp.arange(spread)[None, :]).astype(jnp.int32)
    earlier = jnp.cumsum(in_bucket, axis=0) - in_bucket
    slot_rank = jnp.sum(earlier * in_bucket, axis=1)
    selector = (
        (bucket[None, None, :] == jnp.arange(spread)[:, None, None])
        & (slot_rank[None, None, :] == jnp.arange(capacity)[None, :, None])
    ).astype(jnp.bfloat16)
    packed = jnp.einsum(
        "bsj,jhd->bshd", selector, tiles, preferred_element_type=jnp.float32
    ).astype(jnp.bfloat16)
    packed_meta = jnp.einsum(
        "bsj,jm->bsm", selector, tile_meta, preferred_element_type=jnp.float32
    ).astype(jnp.bfloat16)
    arrived = [(packed[REACH], packed_meta[REACH])]
    for distance in list(range(-REACH, 0)) + list(range(1, REACH + 1)):
        arrived.append(
            shifted((packed[distance + REACH], packed_meta[distance + REACH]), "ra", distance)
        )
    slots = jnp.concatenate([piece[0] for piece in arrived], axis=0)
    slot_meta = jnp.concatenate([piece[1] for piece in arrived], axis=0)

    def accumulate(carry, block_in):
        tiles_in, meta_in = block_in
        matched = match_block(
            tiles_in, lookup(meta_in[:, 3].astype(jnp.int32), coeff_table), colmats, rowmats
        )
        add_numerator, add_weight = place_block(matched, meta_in)
        return ((carry[0] + add_numerator, carry[1] + add_weight), None)

    start_state = (
        jnp.zeros((BANDS, tile_rows, PW), jnp.float32),
        jnp.zeros((BANDS, PW), jnp.float32),
    )
    (numerator, weight_sum), unused = lax.scan(
        accumulate,
        start_state,
        (slots.reshape(-1, 8, tile_rows, tile_width), slot_meta.reshape(-1, 8, slot_meta.shape[1])),
    )
    row_share = tile_rows // lax.axis_size("band")
    totals, weight_total = lax.psum((numerator, weight_sum), "band")
    own_rows = lax.dynamic_slice_in_dim(totals, lax.axis_index("band") * row_share, row_share, 1)
    band_coadds = own_rows / jnp.maximum(weight_total, 1.0)[:, None, :]
    detection = jnp.einsum("b,biq->iq", band_weight, band_coadds, precision=HIGHEST_PRECISION)
    return (band_coadds, detection)


def solution(mesh):
    return jax.shard_map(
        local,
        mesh=mesh,
        in_specs=(
            P(("ra", "band"), None, None),
            P(("ra", "band")),
            P(("ra", "band")),
            P(("ra", "band")),
            P(("ra", "band")),
            P(("ra", "band")),
            P(),
            P(),
            P(),
            P(),
        ),
        out_specs=(P(None, "band", "ra"), P("band", "ra")),
        check_vma=False,
    )
```

profile of v0, /device:TPU:0, one launch (start us, length us, event | category | flops | bytes accessed | tf_op | source)
XLA Modules:
  0.0 179.0 jit_solution(10462603016168617349)
XLA Ops:
  10.6 6.0 %collective-permute-start = (bf16[16,4]{0,1:T(4,128)(2,1)S(1)}, bf16[16,4]{0,1:T(4,128)(2,1)S(1)}, u32[]{:S(2)}, u32[]{:S(2)}) collective-permute-start(bf16[16,4]{0,1:T(4,128)(2,1)S(1)} %get-tuple-element.117), channel_id=1, source_target_pairs={{4,0},{6,2},{8,4},{10,6},{12,8},{14,10},{16,12},{18,14},{20,16},{2... | collective-permute-start | bytes 392 | tf_op jit(solution)/shard_map/ppermute | solution.py:17
  26.8 2.9 %collective-permute-done.2 = bf16[16,4]{0,1:T(4,128)(2,1)S(1)} collective-permute-done((bf16[16,4]{0,1:T(4,128)(2,1)S(1)}, bf16[16,4]{0,1:T(4,128)(2,1)S(1)}, u32[]{:S(2)}, u32[]{:S(2)}) %collective-permute-start.2) | collective-permute-done | bytes 160 | tf_op jit(solution)/shard_map/ppermute | solution.py:17
  29.7 3.5 %collective-permute-start.7 = (bf16[16,64,128]{2,0,1:T(8,128)(2,1)S(1)}, bf16[16,64,128]{2,0,1:T(8,128)(2,1)S(1)}, u32[]{:S(2)}, u32[]{:S(2)}) collective-permute-start(bf16[16,64,128]{2,0,1:T(8,128)(2,1)S(1)} %get-tuple-element.110), channel_id=1, source_target_pairs={{28,0},{30,2},{0,4},{2,6},{4,8},{6,10},{8,12},{10,14},{12,16},{14,... | collective-permute-start | bytes 786440 | tf_op jit(solution)/shard_map/ppermute | solution.py:17
  35.8 6.0 %collective-permute-done.7 = bf16[16,64,128]{2,0,1:T(8,128)(2,1)S(1)} collective-permute-done((bf16[16,64,128]{2,0,1:T(8,128)(2,1)S(1)}, bf16[16,64,128]{2,0,1:T(8,128)(2,1)S(1)}, u32[]{:S(2)}, u32[]{:S(2)}) %collective-permute-start.7) | collective-permute-done | bytes 262176 | tf_op jit(solution)/shard_map/ppermute | solution.py:17
  42.6 102.3 %while.13 = (s32[]{:T(128)}, f32[6,64,256]{2,0,1:T(8,128)}, f32[6,256]{1,0:T(8,128)S(1)}, bf16[10,8,4]{1,2,0:T(4,128)(2,1)S(1)}, f32[64,21]{0,1:T(8,128)S(1)}, /...) while((s32[]{:T(128)}, f32[6,64,256]{2,0,1:T(8,128)}, ...), condition=%wide.region_3.4_spmd.clone, body=%wide.region_2.3_spmd.clone.sunk | while | flops 573926016 | bytes 19803496 | solution.py:129
  46.7 3.2 %fusion.82 = f32[8,64,256]{2,1,0:T(8,128)} fusion(bf16[8,21,64,128]{3,1,2,0:T(8,128)(2,1)S(1)} %bitcast.113, f32[21,64,64]{2,1,0:T(8,128)} %get-tuple-element.203, f32[8,21]{1,0:T(8,128)S(1)} %fusion.81, f32[8]{0:T(128)S(1)} %get-tuple-element.175, s32[8,128]{1,0:T(8,128)S(1)} %iota_add_fusion.2), kind=kOutput, calls=%fused_computation.10.clone.1 | convolution fusion | flops 211681280 | bytes 3625664 | tf_op jit(solution)/shard_map/while/body/eval_jaxpr/jid,jdq->jiq/dot_general | solution.py:52
  56.8 3.2 %fusion.82 = f32[8,64,256]{2,1,0:T(8,128)} fusion(bf16[8,21,64,128]{3,1,2,0:T(8,128)(2,1)S(1)} %bitcast.113, f32[21,64,64]{2,1,0:T(8,128)} %get-tuple-element.203, f32[8,21]{1,0:T(8,128)S(1)} %fusion.81, f32[8]{0:T(128)S(1)} %get-tuple-element.175, s32[8,128]{1,0:T(8,128)S(1)} %iota_add_fusion.2), kind=kOutput, calls=%fused_computation.10.clone.1 | convolution fusion | flops 211681280 | bytes 3625664 | tf_op jit(solution)/shard_map/while/body/eval_jaxpr/jid,jdq->jiq/dot_general | solution.py:52
  60.0 2.7 %convolution_add_fusion.4 = f32[6,64,256]{2,0,1:T(8,128)} fusion(f32[8,64,256]{2,1,0:T(8,128)} %fusion.82, f32[6,64,256]{2,0,1:T(8,128)} %get-tuple-element.189, pred[]{:T(512)S(6)} %compare.4, s32[8]{0:T(128)S(1)} %get-tuple-element.177), kind=kOutput, calls=%fused_computation.7.clone.1 | convolution fusion | flops 9633840 | bytes 1310753 | tf_op jit(solution)/shard_map/while/body/eval_jaxpr/jb,jiq->biq/dot_general | solution.py:54
  67.0 3.2 %fusion.82 = f32[8,64,256]{2,1,0:T(8,128)} fusion(bf16[8,21,64,128]{3,1,2,0:T(8,128)(2,1)S(1)} %bitcast.113, f32[21,64,64]{2,1,0:T(8,128)} %get-tuple-element.203, f32[8,21]{1,0:T(8,128)S(1)} %fusion.81, f32[8]{0:T(128)S(1)} %get-tuple-element.175, s32[8,128]{1,0:T(8,128)S(1)} %iota_add_fusion.2), kind=kOutput, calls=%fused_computation.10.clone.1 | convolution fusion | flops 211681280 | bytes 3625664 | tf_op jit(solution)/shard_map/while/body/eval_jaxpr/jid,jdq->jiq/dot_general | solution.py:52
  70.2 2.7 %convolution_add_fusion.4 = f32[6,64,256]{2,0,1:T(8,128)} fusion(f32[8,64,256]{2,1,0:T(8,128)} %fusion.82, f32[6,64,256]{2,0,1:T(8,128)} %get-tuple-element.189, pred[]{:T(512)S(6)} %compare.4, s32[8]{0:T(128)S(1)} %get-tuple-element.177), kind=kOutput, calls=%fused_computation.7.clone.1 | convolution fusion | flops 9633840 | bytes 1310753 | tf_op jit(solution)/shard_map/while/body/eval_jaxpr/jb,jiq->biq/dot_general | solution.py:54
  77.3 3.2 %fusion.82 = f32[8,64,256]{2,1,0:T(8,128)} fusion(bf16[8,21,64,128]{3,1,2,0:T(8,128)(2,1)S(1)} %bitcast.113, f32[21,64,64]{2,1,0:T(8,128)} %get-tuple-element.203, f32[8,21]{1,0:T(8,128)S(1)} %fusion.81, f32[8]{0:T(128)S(1)} %get-tuple-element.175, s32[8,128]{1,0:T(8,128)S(1)} %iota_add_fusion.2), kind=kOutput, calls=%fused_computation.10.clone.1 | convolution fusion | flops 211681280 | bytes 3625664 | tf_op jit(solution)/shard_map/while/body/eval_jaxpr/jid,jdq->jiq/dot_general | solution.py:52
  80.5 2.7 %convolution_add_fusion.4 = f32[6,64,256]{2,0,1:T(8,128)} fusion(f32[8,64,256]{2,1,0:T(8,128)} %fusion.82, f32[6,64,256]{2,0,1:T(8,128)} %get-tuple-element.189, pred[]{:T(512)S(6)} %compare.4, s32[8]{0:T(128)S(1)} %get-tuple-element.177), kind=kOutput, calls=%fused_computation.7.clone.1 | convolution fusion | flops 9633840 | bytes 1310753 | tf_op jit(solution)/shard_map/while/body/eval_jaxpr/jb,jiq->biq/dot_general | solution.py:54
  87.5 3.2 %fusion.82 = f32[8,64,256]{2,1,0:T(8,128)} fusion(bf16[8,21,64,128]{3,1,2,0:T(8,128)(2,1)S(1)} %bitcast.113, f32[21,64,64]{2,1,0:T(8,128)} %get-tuple-element.203, f32[8,21]{1,0:T(8,128)S(1)} %fusion.81, f32[8]{0:T(128)S(1)} %get-tuple-element.175, s32[8,128]{1,0:T(8,128)S(1)} %iota_add_fusion.2), kind=kOutput, calls=%fused_computation.10.clone.1 | convolution fusion | flops 211681280 | bytes 3625664 | tf_op jit(solution)/shard_map/while/body/eval_jaxpr/jid,jdq->jiq/dot_general | solution.py:52
  90.7 2.7 %convolution_add_fusion.4 = f32[6,64,256]{2,0,1:T(8,128)} fusion(f32[8,64,256]{2,1,0:T(8,128)} %fusion.82, f32[6,64,256]{2,0,1:T(8,128)} %get-tuple-element.189, pred[]{:T(512)S(6)} %compare.4, s32[8]{0:T(128)S(1)} %get-tuple-element.177), kind=kOutput, calls=%fused_computation.7.clone.1 | convolution fusion | flops 9633840 | bytes 1310753 | tf_op jit(solution)/shard_map/while/body/eval_jaxpr/jb,jiq->biq/dot_general | solution.py:54
  97.8 3.2 %fusion.82 = f32[8,64,256]{2,1,0:T(8,128)} fusion(bf16[8,21,64,128]{3,1,2,0:T(8,128)(2,1)S(1)} %bitcast.113, f32[21,64,64]{2,1,0:T(8,128)} %get-tuple-element.203, f32[8,21]{1,0:T(8,128)S(1)} %fusion.81, f32[8]{0:T(128)S(1)} %get-tuple-element.175, s32[8,128]{1,0:T(8,128)S(1)} %iota_add_fusion.2), kind=kOutput, calls=%fused_computation.10.clone.1 | convolution fusion | flops 211681280 | bytes 3625664 | tf_op jit(solution)/shard_map/while/body/eval_jaxpr/jid,jdq->jiq/dot_general | solution.py:52
  101.0 2.7 %convolution_add_fusion.4 = f32[6,64,256]{2,0,1:T(8,128)} fusion(f32[8,64,256]{2,1,0:T(8,128)} %fusion.82, f32[6,64,256]{2,0,1:T(8,128)} %get-tuple-element.189, pred[]{:T(512)S(6)} %compare.4, s32[8]{0:T(128)S(1)} %get-tuple-element.177), kind=kOutput, calls=%fused_computation.7.clone.1 | convolution fusion | flops 9633840 | bytes 1310753 | tf_op jit(solution)/shard_map/while/body/eval_jaxpr/jb,jiq->biq/dot_general | solution.py:54
  108.0 3.2 %fusion.82 = f32[8,64,256]{2,1,0:T(8,128)} fusion(bf16[8,21,64,128]{3,1,2,0:T(8,128)(2,1)S(1)} %bitcast.113, f32[21,64,64]{2,1,0:T(8,128)} %get-tuple-element.203, f32[8,21]{1,0:T(8,128)S(1)} %fusion.81, f32[8]{0:T(128)S(1)} %get-tuple-element.175, s32[8,128]{1,0:T(8,128)S(1)} %iota_add_fusion.2), kind=kOutput, calls=%fused_computation.10.clone.1 | convolution fusion | flops 211681280 | bytes 3625664 | tf_op jit(solution)/shard_map/while/body/eval_jaxpr/jid,jdq->jiq/dot_general | solution.py:52
  118.3 3.2 %fusion.82 = f32[8,64,256]{2,1,0:T(8,128)} fusion(bf16[8,21,64,128]{3,1,2,0:T(8,128)(2,1)S(1)} %bitcast.113, f32[21,64,64]{2,1,0:T(8,128)} %get-tuple-element.203, f32[8,21]{1,0:T(8,128)S(1)} %fusion.81, f32[8]{0:T(128)S(1)} %get-tuple-element.175, s32[8,128]{1,0:T(8,128)S(1)} %iota_add_fusion.2), kind=kOutput, calls=%fused_computation.10.clone.1 | convolution fusion | flops 211681280 | bytes 3625664 | tf_op jit(solution)/shard_map/while/body/eval_jaxpr/jid,jdq->jiq/dot_general | solution.py:52
  121.5 2.7 %convolution_add_fusion.4 = f32[6,64,256]{2,0,1:T(8,128)} fusion(f32[8,64,256]{2,1,0:T(8,128)} %fusion.82, f32[6,64,256]{2,0,1:T(8,128)} %get-tuple-element.189, pred[]{:T(512)S(6)} %compare.4, s32[8]{0:T(128)S(1)} %get-tuple-element.177), kind=kOutput, calls=%fused_computation.7.clone.1 | convolution fusion | flops 9633840 | bytes 1310753 | tf_op jit(solution)/shard_map/while/body/eval_jaxpr/jb,jiq->biq/dot_general | solution.py:54
  128.5 3.2 %fusion.82 = f32[8,64,256]{2,1,0:T(8,128)} fusion(bf16[8,21,64,128]{3,1,2,0:T(8,128)(2,1)S(1)} %bitcast.113, f32[21,64,64]{2,1,0:T(8,128)} %get-tuple-element.203, f32[8,21]{1,0:T(8,128)S(1)} %fusion.81, f32[8]{0:T(128)S(1)} %get-tuple-element.175, s32[8,128]{1,0:T(8,128)S(1)} %iota_add_fusion.2), kind=kOutput, calls=%fused_computation.10.clone.1 | convolution fusion | flops 211681280 | bytes 3625664 | tf_op jit(solution)/shard_map/while/body/eval_jaxpr/jid,jdq->jiq/dot_general | solution.py:52
  138.7 3.2 %fusion.82 = f32[8,64,256]{2,1,0:T(8,128)} fusion(bf16[8,21,64,128]{3,1,2,0:T(8,128)(2,1)S(1)} %bitcast.113, f32[21,64,64]{2,1,0:T(8,128)} %get-tuple-element.203, f32[8,21]{1,0:T(8,128)S(1)} %fusion.81, f32[8]{0:T(128)S(1)} %get-tuple-element.175, s32[8,128]{1,0:T(8,128)S(1)} %iota_add_fusion.2), kind=kOutput, calls=%fused_computation.10.clone.1 | convolution fusion | flops 211681280 | bytes 3625664 | tf_op jit(solution)/shard_map/while/body/eval_jaxpr/jid,jdq->jiq/dot_general | solution.py:52
  142.0 2.7 %convolution_add_fusion.4 = f32[6,64,256]{2,0,1:T(8,128)} fusion(f32[8,64,256]{2,1,0:T(8,128)} %fusion.82, f32[6,64,256]{2,0,1:T(8,128)} %get-tuple-element.189, pred[]{:T(512)S(6)} %compare.4, s32[8]{0:T(128)S(1)} %get-tuple-element.177), kind=kOutput, calls=%fused_computation.7.clone.1 | convolution fusion | flops 9633840 | bytes 1310753 | tf_op jit(solution)/shard_map/while/body/eval_jaxpr/jb,jiq->biq/dot_general | solution.py:54
  146.9 5.0 %psum.15 = f32[6,256]{1,0:T(8,128)S(1)} all-reduce(f32[6,256]{1,0:T(8,128)S(1)} %get-tuple-element.46), channel_id=1, replica_groups=mesh['ra'=16,'band'=2] {'band'}, use_global_device_ids=true, to_apply=%region_5.6 | all-reduce | flops 1536 | bytes 12288 | tf_op jit(solution)/shard_map/psum | solution.py:135
  151.9 18.2 %all-reduce.2.cloned.1.call-done = f32[6,64,256]{2,1,0:T(8,128)} async-done(((f32[6,64,256]{2,1,0:T(8,128)}), f32[6,64,256]{2,1,0:T(8,128)}) %all-reduce.2.cloned.1.call-update) | async-done | bytes 393232 | tf_op jit(solution)/shard_map/psum | solution.py:135
  (192 shorter events, 71.4 us)
Async XLA Ops:
  7.2 13.8 %copy-start = (bf16[21,21]{1,0:T(8,128)(2,1)S(1)}, bf16[21,21]{1,0:T(8,128)(2,1)}, u32[]{:S(2)}) copy-start(bf16[21,21]{1,0:T(8,128)(2,1)} %param.20) | copy-start | bytes 2650
  7.2 162.9 %all-reduce.2.cloned.1.call-start = ((), (), s32[]{:S(2)}) async-start(), calls=%async_computation | async-start | bytes 786432 | tf_op jit(solution)/shard_map/psum | solution.py:135
  10.6 13.1 %collective-permute-start = (bf16[16,4]{0,1:T(4,128)(2,1)S(1)}, bf16[16,4]{0,1:T(4,128)(2,1)S(1)}, u32[]{:S(2)}, u32[]{:S(2)}) collective-permute-start(bf16[16,4]{0,1:T(4,128)(2,1)S(1)} %get-tuple-element.117), channel_id=1, source_target_pairs={{4,0},{6,2},{8,4},{10,6},{12,8},{14,10},{16,12},{18,14},{20,16},{2... | collective-permute-start | bytes 392 | tf_op jit(solution)/shard_map/ppermute | solution.py:17
  16.6 7.8 %collective-permute-start.1 = (bf16[16,4]{0,1:T(4,128)(2,1)S(1)}, bf16[16,4]{0,1:T(4,128)(2,1)S(1)}, u32[]{:S(2)}, u32[]{:S(2)}) collective-permute-start(bf16[16,4]{0,1:T(4,128)(2,1)S(1)} %get-tuple-element.116), channel_id=1, source_target_pairs={{2,0},{4,2},{6,4},{8,6},{10,8},{12,10},{14,12},{16,14},{18,16},{20... | collective-permute-start | bytes 392 | tf_op jit(solution)/shard_map/ppermute | solution.py:17
  18.2 3.2 %copy-start.4 = (bf16[21,21]{1,0:T(8,128)(2,1)S(1)}, bf16[21,21]{1,0:T(8,128)(2,1)}, u32[]{:S(2)}) copy-start(bf16[21,21]{1,0:T(8,128)(2,1)} %param.19) | copy-start | bytes 2650
  19.1 14.3 %collective-permute-start.4 = (bf16[16,64,128]{2,0,1:T(8,128)(2,1)}, bf16[16,64,128]{2,0,1:T(8,128)(2,1)S(1)}, u32[]{:S(2)}, u32[]{:S(2)}) collective-permute-start(bf16[16,64,128]{2,0,1:T(8,128)(2,1)} %get-tuple-element.113), channel_id=1, source_target_pairs={{4,0},{6,2},{8,4},{10,6},{12,8},{14,10},{16,12},{18,14},{20,16},{2... | collective-permute-start | bytes 786440 | tf_op jit(solution)/shard_map/ppermute | solution.py:17
  20.2 14.0 %collective-permute-start.5 = (bf16[16,64,128]{2,0,1:T(8,128)(2,1)}, bf16[16,64,128]{2,0,1:T(8,128)(2,1)S(1)}, u32[]{:S(2)}, u32[]{:S(2)}) collective-permute-start(bf16[16,64,128]{2,0,1:T(8,128)(2,1)} %get-tuple-element.112), channel_id=1, source_target_pairs={{2,0},{4,2},{6,4},{8,6},{10,8},{12,10},{14,12},{16,14},{18,16},{20... | collective-permute-start | bytes 786440 | tf_op jit(solution)/shard_map/ppermute | solution.py:17
  20.9 14.1 %collective-permute-start.6 = (bf16[16,64,128]{2,0,1:T(8,128)(2,1)}, bf16[16,64,128]{2,0,1:T(8,128)(2,1)S(1)}, u32[]{:S(2)}, u32[]{:S(2)}) collective-permute-start(bf16[16,64,128]{2,0,1:T(8,128)(2,1)} %get-tuple-element.111), channel_id=1, source_target_pairs={{30,0},{0,2},{2,4},{4,6},{6,8},{8,10},{10,12},{12,14},{14,16},{16,... | collective-permute-start | bytes 786440 | tf_op jit(solution)/shard_map/ppermute | solution.py:17
  23.6 19.0 %copy-start.6 = (f32[64,21]{0,1:T(8,128)S(1)}, f32[64,21]{0,1:T(8,128)}, u32[]{:S(2)}) copy-start(f32[64,21]{0,1:T(8,128)} %param.18) | copy-start | bytes 16132
  23.6 6.1 %collective-permute-start.2 = (bf16[16,4]{0,1:T(4,128)(2,1)S(1)}, bf16[16,4]{0,1:T(4,128)(2,1)S(1)}, u32[]{:S(2)}, u32[]{:S(2)}) collective-permute-start(bf16[16,4]{0,1:T(4,128)(2,1)S(1)} %get-tuple-element.115), channel_id=1, source_target_pairs={{30,0},{0,2},{2,4},{4,6},{6,8},{8,10},{10,12},{12,14},{14,16},{16,... | collective-permute-start | bytes 392 | tf_op jit(solution)/shard_map/ppermute | solution.py:17
  24.4 8.8 %collective-permute-start.3 = (bf16[16,4]{0,1:T(4,128)(2,1)S(1)}, bf16[16,4]{0,1:T(4,128)(2,1)S(1)}, u32[]{:S(2)}, u32[]{:S(2)}) collective-permute-start(bf16[16,4]{0,1:T(4,128)(2,1)S(1)} %get-tuple-element.114), channel_id=1, source_target_pairs={{28,0},{30,2},{0,4},{2,6},{4,8},{6,10},{8,12},{10,14},{12,16},{14,... | collective-permute-start | bytes 392 | tf_op jit(solution)/shard_map/ppermute | solution.py:17
  29.7 12.1 %collective-permute-start.7 = (bf16[16,64,128]{2,0,1:T(8,128)(2,1)S(1)}, bf16[16,64,128]{2,0,1:T(8,128)(2,1)S(1)}, u32[]{:S(2)}, u32[]{:S(2)}) collective-permute-start(bf16[16,64,128]{2,0,1:T(8,128)(2,1)S(1)} %get-tuple-element.110), channel_id=1, source_target_pairs={{28,0},{30,2},{0,4},{2,6},{4,8},{6,10},{8,12},{10,14},{12,16},{14,... | collective-permute-start | bytes 786440 | tf_op jit(solution)/shard_map/ppermute | solution.py:17
  49.9 2.8 %copy-start.2 = (bf16[21,128,128]{2,1,0:T(8,128)(2,1)S(1)}, bf16[21,128,128]{2,1,0:T(8,128)(2,1)}, u32[]{:S(2)}) copy-start(bf16[21,128,128]{2,1,0:T(8,128)(2,1)} %copy-done.1) | copy-start | bytes 2064388 | tf_op jit(solution)/shard_map/while
  60.0 2.9 %copy-start.2 = (bf16[21,128,128]{2,1,0:T(8,128)(2,1)S(1)}, bf16[21,128,128]{2,1,0:T(8,128)(2,1)}, u32[]{:S(2)}) copy-start(bf16[21,128,128]{2,1,0:T(8,128)(2,1)} %copy-done.1) | copy-start | bytes 2064388 | tf_op jit(solution)/shard_map/while
  70.2 2.9 %copy-start.2 = (bf16[21,128,128]{2,1,0:T(8,128)(2,1)S(1)}, bf16[21,128,128]{2,1,0:T(8,128)(2,1)}, u32[]{:S(2)}) copy-start(bf16[21,128,128]{2,1,0:T(8,128)(2,1)} %copy-done.1) | copy-start | bytes 2064388 | tf_op jit(solution)/shard_map/while
  80.5 2.9 %copy-start.2 = (bf16[21,128,128]{2,1,0:T(8,128)(2,1)S(1)}, bf16[21,128,128]{2,1,0:T(8,128)(2,1)}, u32[]{:S(2)}) copy-start(bf16[21,128,128]{2,1,0:T(8,128)(2,1)} %copy-done.1) | copy-start | bytes 2064388 | tf_op jit(solution)/shard_map/while
  90.7 2.9 %copy-start.2 = (bf16[21,128,128]{2,1,0:T(8,128)(2,1)S(1)}, bf16[21,128,128]{2,1,0:T(8,128)(2,1)}, u32[]{:S(2)}) copy-start(bf16[21,128,128]{2,1,0:T(8,128)(2,1)} %copy-done.1) | copy-start | bytes 2064388 | tf_op jit(solution)/shard_map/while
  101.0 2.9 %copy-start.2 = (bf16[21,128,128]{2,1,0:T(8,128)(2,1)S(1)}, bf16[21,128,128]{2,1,0:T(8,128)(2,1)}, u32[]{:S(2)}) copy-start(bf16[21,128,128]{2,1,0:T(8,128)(2,1)} %copy-done.1) | copy-start | bytes 2064388 | tf_op jit(solution)/shard_map/while
  111.2 2.9 %copy-start.2 = (bf16[21,128,128]{2,1,0:T(8,128)(2,1)S(1)}, bf16[21,128,128]{2,1,0:T(8,128)(2,1)}, u32[]{:S(2)}) copy-start(bf16[21,128,128]{2,1,0:T(8,128)(2,1)} %copy-done.1) | copy-start | bytes 2064388 | tf_op jit(solution)/shard_map/while
  121.5 2.9 %copy-start.2 = (bf16[21,128,128]{2,1,0:T(8,128)(2,1)S(1)}, bf16[21,128,128]{2,1,0:T(8,128)(2,1)}, u32[]{:S(2)}) copy-start(bf16[21,128,128]{2,1,0:T(8,128)(2,1)} %copy-done.1) | copy-start | bytes 2064388 | tf_op jit(solution)/shard_map/while
  131.7 2.9 %copy-start.2 = (bf16[21,128,128]{2,1,0:T(8,128)(2,1)S(1)}, bf16[21,128,128]{2,1,0:T(8,128)(2,1)}, u32[]{:S(2)}) copy-start(bf16[21,128,128]{2,1,0:T(8,128)(2,1)} %copy-done.1) | copy-start | bytes 2064388 | tf_op jit(solution)/shard_map/while
  142.0 2.9 %copy-start.2 = (bf16[21,128,128]{2,1,0:T(8,128)(2,1)S(1)}, bf16[21,128,128]{2,1,0:T(8,128)(2,1)}, u32[]{:S(2)}) copy-start(bf16[21,128,128]{2,1,0:T(8,128)(2,1)} %copy-done.1) | copy-start | bytes 2064388 | tf_op jit(solution)/shard_map/while
  144.9 26.1 %copy-start.5 = (f32[6]{0:T(128)S(1)}, f32[6]{0:T(128)}, u32[]{:S(2)}) copy-start(f32[6]{0:T(128)} %param.21) | copy-start | bytes 76
  171.0 1.1 copy-start.3
  (10 other events, 10.7 us)
Sparse Core Ops, SparseCore 0:
  147.0 23.0 all-reduce.1
where the time goes:
time: 180 us; the launch traced here: 179 us
  matrix products  75.4 us (42%)
  local copies, waits for them, and re-layouts  38.1 us (21%)
  waiting for transfers between devices  27.1 us (15%)
  starting transfers between devices  14.5 us (8%)
  between operations  14.2 us (8%)
  blocking collectives  5.01 us (3%)
  other arithmetic  4.18 us (2%)
    dot_general x10, matrix products, place_block(): jnp.einsum('jid,jdq->jiq', matched, shifter, preferred_element_type=jnp.f...  32.1 us
    dot_general x10, matrix products, place_block(): jnp.einsum('jb,jiq->biq', one_hot, placed, precision=HIGHEST_PRECISION)  27.2 us
    dot_general x10, local copies, waits for them, and re-layouts, match_block(): jnp.einsum('jic,kdc->jkid', tiles_in, colmats, preferred_element_type=jnp...  18.3 us
    psum x1, waiting for transfers between devices, local(): totals, weight_total = lax.psum((numerator, weight_sum), 'band')  18.2 us
    ppermute x8, starting transfers between devices, shifted(): return lax.ppermute(block, axis, route)  14.4 us
    dynamic_slice x10, local copies, waits for them, and re-layouts, local(): lax.scan(accumulate, start_state, (slots.reshape(-1, 8, tile_rows, tile_w...  10.6 us
    ppermute x8, waiting for transfers between devices, shifted(): return lax.ppermute(block, axis, route)  8.95 us
    dot_general x10, matrix products, match_block(): jnp.einsum('jic,kdc->jkid', tiles_in, colmats, preferred_element_type=jnp...  8.78 us
  transfers between devices with their start and end apart: 9, of which 3 were waited for; matrix products, arithmetic and copies ran while one was open for 4% of the time, Pallas kernels for 0%

commit v1 on v0

v1 whole, which is shorter than its diff:
```python
import functools

import jax
import jax.numpy as jnp
from jax import lax
from jax.experimental import pallas as pl
from jax.experimental.pallas import tpu as pltpu
from jax.sharding import PartitionSpec as P

PW = 256
BANDS = 6
REACH = 2
SPREAD = 2 * REACH + 1
EXTRA = 16


def slot_rows(row_share):
    return max(row_share, 16)


def match_kernel(
    patches,
    groups,
    patch_ref,
    offset_ref,
    index_ref,
    band_ref,
    table_ref,
    weight_ref,
    rowk_ref,
    colk_ref,
    tiles_ref,
    *rest,
):
    messages = rest[: SPREAD * groups]
    rowmat, colmat, scaled, sums, extra = rest[SPREAD * groups :]
    visit = pl.program_id(0)
    visits = pl.num_programs(0)
    per_visit, rows, width = tiles_ref.shape
    basis, taps = rowk_ref.shape
    half = taps // 2
    row_share = rows // groups
    slot = slot_rows(row_share)
    owner = lax.axis_index("ra")
    group = lax.axis_index("band")

    @pl.when(visit == 0)
    def build():
        tap = lax.broadcasted_iota(jnp.int32, (taps, width), 0)
        lane = lax.broadcasted_iota(jnp.int32, (taps, width), 1)
        back = half // 8 * 8
        shifted = lax.rem(lane + half - back, width)
        forward = (shifted == tap).astype(jnp.bfloat16)
        backward = (shifted == taps - 1 - tap).astype(jnp.bfloat16)
        row_taps = jnp.dot(rowk_ref[...], forward, preferred_element_type=jnp.float32)
        col_taps = jnp.dot(colk_ref[...], backward, preferred_element_type=jnp.float32)
        apart = lax.broadcasted_iota(jnp.int32, (width, width), 0) - lax.broadcasted_iota(
            jnp.int32, (width, width), 1
        )
        near = jnp.abs(apart) <= half
        for k in range(basis):
            spread = jnp.broadcast_to(row_taps[k : k + 1], (rows, width))
            turned = pltpu.roll(spread, width - back, 1, stride=1, stride_axis=0)
            rowmat[k * rows : (k + 1) * rows, :] = turned[:, :rows].astype(jnp.bfloat16)
            spread = jnp.broadcast_to(col_taps[k : k + 1], (width, width))
            turned = pltpu.roll(spread, width - back, 1, stride=1, stride_axis=0)
            colmat[k * width : (k + 1) * width, :] = jnp.where(near, turned, 0.0).astype(
                jnp.bfloat16
            )
        extra[...] = jnp.zeros_like(extra)

    sums[...] = jnp.zeros_like(sums)
    first = visit * per_visit
    for pair in range(per_visit // 2):
        both = jnp.concatenate([tiles_ref[2 * pair], tiles_ref[2 * pair + 1]], axis=1)
        passed = jnp.dot(rowmat[...], both, preferred_element_type=jnp.float32)
        for side in range(2):
            place = 2 * pair + side
            table_row = index_ref[first + place]
            for k in range(basis):
                block = passed[k * rows : (k + 1) * rows, side * width : (side + 1) * width]
                scaled[place * rows : (place + 1) * rows, k * width : (k + 1) * width] = (
                    block * table_ref[table_row, k]
                ).astype(jnp.bfloat16)
    matched = jnp.dot(scaled[...], colmat[...], preferred_element_type=jnp.float32)

    lane = lax.broadcasted_iota(jnp.int32, (rows, width), 1)
    column = lax.broadcasted_iota(jnp.int32, (1, PW), 1)
    tile_lane = lax.broadcasted_iota(jnp.int32, weight_ref.shape, 1)
    weights = weight_ref[...].astype(jnp.float32)
    for place in range(per_visit):
        tile = first + place
        offset = offset_ref[tile]
        bucket = lax.rem(patch_ref[tile] - owner + REACH + patches, patches)
        weight = jnp.sum(jnp.where(tile_lane == tile, weights, 0.0), axis=1, keepdims=True)
        turned = pltpu.roll(
            matched[place * rows : (place + 1) * rows] * weight, lax.rem(offset, width), 1
        )
        sums[bucket, :, :width] += jnp.where(lane >= offset, turned, 0.0)
        sums[bucket, :, width:] += jnp.where(lane < offset, turned, 0.0)
        covered = (column >= offset) & (column < offset + width)
        extra[bucket, pl.ds(visit, 1), :] += jnp.where(covered, weight, 0.0)

    for bucket in range(SPREAD):
        extra[bucket, pl.ds(2 * visits + visit, 1), :] = jnp.full(
            (1, PW), band_ref[visit], jnp.int32
        ).astype(jnp.float32)
        for turn in range(groups):
            part = lax.rem(group + turn, groups)
            own = sums[bucket, pl.ds(pl.multiple_of(part * row_share, row_share), row_share), :]
            if slot > row_share:
                own = jnp.concatenate(
                    [own, jnp.zeros((slot - row_share, PW), jnp.float32)], axis=0
                )
            messages[bucket * groups + turn][
                pl.ds(pl.multiple_of(visit * slot, slot), slot), :
            ] = own.astype(jnp.bfloat16)

    @pl.when(visit == visits - 1)
    def finish():
        row = lax.broadcasted_iota(jnp.int32, (EXTRA, PW), 0)
        count = extra.shape[1] // 4
        for bucket in range(SPREAD):
            held = extra[bucket]
            high = held.astype(jnp.bfloat16).astype(jnp.float32)
            low = jnp.concatenate([held[-count:], (held - high)[:-count]], axis=0)
            mixed = jnp.where((row >= count) & (row < 2 * count), low, high).astype(jnp.bfloat16)
            for turn in range(groups):
                messages[bucket * groups + turn][slot * count :, :] = mixed


def combine_kernel(count, weight_ref, *refs):
    messages = refs[:-2]
    coadd_ref, detection_ref = refs[-2:]
    row_share = coadd_ref.shape[1]
    slot = slot_rows(row_share)
    totals = [jnp.zeros((row_share, PW), jnp.float32) for _ in range(BANDS)]
    weight_totals = [jnp.zeros((1, PW), jnp.float32) for _ in range(BANDS)]
    for message in messages:
        extra = message[slot * count :, :].astype(jnp.float32)
        for visit in range(count):
            band = extra[2 * count + visit : 2 * count + visit + 1]
            weight = extra[visit : visit + 1] + extra[count + visit : count + visit + 1]
            part = message[slot * visit : slot * (visit + 1), :].astype(jnp.float32)[:row_share]
            for b in range(BANDS):
                here = band == float(b)
                totals[b] += jnp.where(here, part, 0.0)
                weight_totals[b] += jnp.where(here, weight, 0.0)
    detection = jnp.zeros((row_share, PW), jnp.float32)
    for b in range(BANDS):
        coadd = totals[b] / jnp.maximum(weight_totals[b], 1.0)
        coadd_ref[b] = coadd
        detection += weight_ref[b] * coadd
    detection_ref[...] = detection


def local(
    tiles,
    tile_patch,
    tile_offset,
    tile_weight,
    visit_band,
    coeff_index,
    coeff_table,
    row_kernels,
    column_kernels,
    band_weight,
):
    tile_count, rows, width = tiles.shape
    visits = visit_band.shape[0]
    per_visit = tile_count // visits
    basis, taps = row_kernels.shape
    patches = lax.axis_size("ra")
    groups = lax.axis_size("band")
    row_share = rows // groups
    slot = slot_rows(row_share)
    length = visits * slot + EXTRA
    smem = pl.BlockSpec(memory_space=pltpu.SMEM)

    def whole(shape):
        return pl.BlockSpec(shape, lambda v: (0,) * len(shape))

    messages = pl.pallas_call(
        functools.partial(match_kernel, patches, groups),
        grid=(visits,),
        in_specs=[smem] * 5
        + [
            whole((1, tile_count)),
            whole((basis, taps)),
            whole((basis, taps)),
            pl.BlockSpec((per_visit, rows, width), lambda v: (v, 0, 0)),
        ],
        out_specs=[whole((length, PW))] * (SPREAD * groups),
        out_shape=[jax.ShapeDtypeStruct((length, PW), jnp.bfloat16)] * (SPREAD * groups),
        scratch_shapes=[
            pltpu.VMEM((basis * rows, rows), jnp.bfloat16),
            pltpu.VMEM((basis * width, width), jnp.bfloat16),
            pltpu.VMEM((per_visit * rows, basis * width), jnp.bfloat16),
            pltpu.VMEM((SPREAD, rows, PW), jnp.float32),
            pltpu.VMEM((SPREAD, EXTRA, PW), jnp.float32),
        ],
        compiler_params=pltpu.CompilerParams(vmem_limit_bytes=40 * 1024 * 1024),
        name="match_and_sum",
    )(
        tile_patch,
        tile_offset,
        coeff_index,
        visit_band,
        coeff_table,
        tile_weight.reshape(1, tile_count),
        row_kernels,
        column_kernels,
        tiles,
    )

    arrived = []
    for bucket in range(SPREAD):
        for turn in range(groups):
            message = messages[bucket * groups + turn]
            distance = bucket - REACH
            if distance != 0 or turn != 0:
                route = [
                    (o * groups + g, (o + distance) % patches * groups + (g + turn) % groups)
                    for o in range(patches)
                    for g in range(groups)
                ]
                message = lax.ppermute(message, ("ra", "band"), route)
            arrived.append(message)

    vmem = pl.BlockSpec(memory_space=pltpu.VMEM)
    return pl.pallas_call(
        functools.partial(combine_kernel, visits),
        in_specs=[smem] + [vmem] * len(arrived),
        out_specs=(vmem, vmem),
        out_shape=(
            jax.ShapeDtypeStruct((BANDS, row_share, PW), jnp.float32),
            jax.ShapeDtypeStruct((row_share, PW), jnp.float32),
        ),
        compiler_params=pltpu.CompilerParams(vmem_limit_bytes=40 * 1024 * 1024),
        name="combine",
    )(band_weight, *arrived)


def solution(mesh):
    return jax.shard_map(
        local,
        mesh=mesh,
        in_specs=(
            P(("ra", "band"), None, None),
            P(("ra", "band")),
            P(("ra", "band")),
            P(("ra", "band")),
            P(("ra", "band")),
            P(("ra", "band")),
            P(),
            P(),
            P(),
            P(),
        ),
        out_specs=(P(None, "band", "ra"), P("band", "ra")),
        check_vma=False,
    )
```

time: 180 us -> 40.2 us (0.22)
  matrix products: 75.4 us -> 0 us
  local copies, waits for them, and re-layouts: 38.1 us -> 2.51 us
  waiting for transfers between devices: 27.1 us -> 7.93 us
  Pallas kernels: 0 us -> 14.8 us
  between operations: 14.2 us -> 0.73 us
  blocking collectives: 5.01 us -> 0 us
  other arithmetic: 4.18 us -> 0 us
    dot_general x55 -> x0, matrix products: 75.4 us -> none  [the longest x10 32.1 us: place_block(): jnp.einsum('jid,jdq->jiq', matched, shifter, preferred_element_type=jnp.f...]
    dot_general x11 -> x0, local copies, waits for them, and re-layouts: 19 us -> none  [the longest x10 18.3 us: match_block(): jnp.einsum('jic,kdc->jkid', tiles_in, colmats, preferred_element_type=jnp...]
    psum x1 -> x0, waiting for transfers between devices: 18.2 us -> none  [local(): totals, weight_total = lax.psum((numerator, weight_sum), 'band')]
    pallas_call x0 -> x2, Pallas kernels: none -> 14.8 us  [the longest x1 12.4 us: local(): pl.pallas_call(functools.partial(match_kernel, patches, groups), grid=(vi...]
    dynamic_slice x10 -> x0, local copies, waits for them, and re-layouts: 10.6 us -> none  [local(): lax.scan(accumulate, start_state, (slots.reshape(-1, 8, tile_rows, tile_w...]
    psum x1 -> x0, blocking collectives: 5.01 us -> none  [local(): totals, weight_total = lax.psum((numerator, weight_sum), 'band')]
    while x41 -> x0, local copies, waits for them, and re-layouts: 2.01 us -> none  [the longest x1 1.92 us: local(): lax.scan(accumulate, start_state, (slots.reshape(-1, 8, tile_rows, tile_w...]
    unnamed x17 -> x19, local copies, waits for them, and re-layouts: 4.32 us -> 2.51 us
  transfers between devices with their start and end apart: 9 -> 9, of which waited for: 3 -> 4; matrix products, arithmetic and copies ran while one was open for 4% -> 0% of each run, Pallas kernels for 0% -> 0%
where the time goes in v1:
time: 40.2 us; the launch traced here: 39.9 us
  Pallas kernels  14.8 us (37%)
  starting transfers between devices  13.9 us (35%)
  waiting for transfers between devices  7.93 us (20%)
  local copies, waits for them, and re-layouts  2.51 us (6%)
  between operations  0.73 us (2%)
    ppermute x9, starting transfers between devices, local(): message = lax.ppermute(message, ('ra', 'band'), route)  13.9 us
    pallas_call x1, Pallas kernels, local(): pl.pallas_call(functools.partial(match_kernel, patches, groups), grid=(vi...  12.4 us
    ppermute x9, waiting for transfers between devices, local(): message = lax.ppermute(message, ('ra', 'band'), route)  7.93 us
    unnamed x19, local copies, waits for them, and re-layouts  2.51 us
    pallas_call x1, Pallas kernels, local(): pl.pallas_call(functools.partial(combine_kernel, visits), in_specs=[smem]...  2.43 us
  transfers between devices with their start and end apart: 9, of which 4 were waited for; matrix products, arithmetic and copies ran while one was open for 0% of the time, Pallas kernels for 0%

profile of v1, /device:TPU:0, one launch (start us, length us, event | category | flops | bytes accessed | tf_op | source)
XLA Modules:
  0.0 39.9 jit_solution(10755383458563994850)
XLA Ops:
  0.7 0.8 %copy.12.table_ref = f32[64,21]{1,0:T(8,128)S(1)} copy(f32[64,21]{0,1:T(8,128)} %param.16) | data formatting | bytes 10752 | tf_op args[6]
  1.5 0.0 copy-start.6
  1.6 0.6 %copy-done.4 = s32[32]{0:T(128)S(1)} copy-done((s32[32]{0:T(128)S(1)}, s32[32]{0:T(128)}, u32[]{:S(2)}) %copy-start.4) | copy-done | bytes 152
  2.1 0.0 copy-done.5
  2.2 0.0 copy-done.6
  2.2 1.0 %copy-done = bf16[32,64,128]{2,1,0:T(8,128)(2,1)S(1)} copy-done((bf16[32,64,128]{2,1,0:T(8,128)(2,1)S(1)}, bf16[32,64,128]{2,1,0:T(8,128)(2,1)}, u32[]{:S(2)}) %copy-start) | copy-done | bytes 524312
  3.2 12.4 %match_and_sum.1 = (bf16[144,256]{1,0:T(8,128)(2,1)S(1)}, bf16[144,256]{1,0:T(8,128)(2,1)S(1)}, bf16[144,256]{1,0:T(8,128)(2,1)S(1)}, bf16[144,256]{1,0:T(8,128)...) custom-call(s32[32]{0:T(128)S(1)} %copy-done.4, ...), custom_call_target="tpu_custom_call" | custom-call | tf_op jit(solution)/shard_map/match_and_sum/pallas_call | solution.py:183
  15.6 6.0 %collective-permute-start = (bf16[144,256]{1,0:T(8,128)(2,1)S(1)}, bf16[144,256]{1,0:T(8,128)(2,1)S(1)}, u32[]{:S(2)}, u32[]{:S(2)}) collective-permute-start(bf16[144,256]{1,0:T(8,128)(2,1)S(1)} %get-tuple-element.12), channel_id=1, source_target_pairs={{0,28},{1,29},{2,30},{3,31},{4,0},{5,1},{6,2},{7,3},{8,4},{9,5},{1... | collective-permute-start | bytes 221192 | tf_op jit(solution)/shard_map/ppermute | solution.py:227
  21.7 1.5 %collective-permute-start.1 = (bf16[144,256]{1,0:T(8,128)(2,1)S(1)}, bf16[144,256]{1,0:T(8,128)(2,1)S(1)}, u32[]{:S(2)}, u32[]{:S(2)}) collective-permute-start(bf16[144,256]{1,0:T(8,128)(2,1)S(1)} %get-tuple-element.13), channel_id=1, source_target_pairs={{0,29},{1,28},{2,31},{3,30},{4,1},{5,0},{6,3},{7,2},{8,5},{9,4},{1... | collective-permute-start | bytes 221192 | tf_op jit(solution)/shard_map/ppermute | solution.py:227
  23.2 0.3 collective-permute-start.2
  23.4 1.2 %collective-permute-start.3 = (bf16[144,256]{1,0:T(8,128)(2,1)S(1)}, bf16[144,256]{1,0:T(8,128)(2,1)S(1)}, u32[]{:S(2)}, u32[]{:S(2)}) collective-permute-start(bf16[144,256]{1,0:T(8,128)(2,1)S(1)} %get-tuple-element.15), channel_id=1, source_target_pairs={{0,31},{1,30},{2,1},{3,0},{4,3},{5,2},{6,5},{7,4},{8,7},{9,6},{10,... | collective-permute-start | bytes 221192 | tf_op jit(solution)/shard_map/ppermute | solution.py:227
  24.6 1.5 %collective-permute-start.4 = (bf16[144,256]{1,0:T(8,128)(2,1)S(1)}, bf16[144,256]{1,0:T(8,128)(2,1)S(1)}, u32[]{:S(2)}, u32[]{:S(2)}) collective-permute-start(bf16[144,256]{1,0:T(8,128)(2,1)S(1)} %get-tuple-element.17), channel_id=1, source_target_pairs={{0,1},{1,0},{2,3},{3,2},{4,5},{5,4},{6,7},{7,6},{8,9},{9,8},{10,11... | collective-permute-start | bytes 221192 | tf_op jit(solution)/shard_map/ppermute | solution.py:227
  26.1 0.0 collective-permute-done.refs_0_
  26.1 0.9 %collective-permute-done.1.refs_1_ = bf16[144,256]{1,0:T(8,128)(2,1)S(1)} collective-permute-done((bf16[144,256]{1,0:T(8,128)(2,1)S(1)}, bf16[144,256]{1,0:T(8,128)(2,1)S(1)}, u32[]{:S(2)}, u32[]{:S(2)}) %collective-permute-start.1) | collective-permute-done | bytes 73760 | tf_op jit(solution)/shard_map/ppermute | solution.py:227
  27.0 0.0 collective-permute-start.6
  27.0 2.4 %collective-permute-start.7 = (bf16[144,256]{1,0:T(8,128)(2,1)S(1)}, bf16[144,256]{1,0:T(8,128)(2,1)S(1)}, u32[]{:S(2)}, u32[]{:S(2)}) collective-permute-start(bf16[144,256]{1,0:T(8,128)(2,1)S(1)} %get-tuple-element.20), channel_id=1, source_target_pairs={{0,4},{1,5},{2,6},{3,7},{4,8},{5,9},{6,10},{7,11},{8,12},{9,13},{1... | collective-permute-start | bytes 221192 | tf_op jit(solution)/shard_map/ppermute | solution.py:227
  29.4 0.0 collective-permute-done.3.refs_3_
  29.4 1.0 %collective-permute-start.8 = (bf16[144,256]{1,0:T(8,128)(2,1)S(1)}, bf16[144,256]{1,0:T(8,128)(2,1)S(1)}, u32[]{:S(2)}, u32[]{:S(2)}) collective-permute-start(bf16[144,256]{1,0:T(8,128)(2,1)S(1)} %get-tuple-element.21), channel_id=1, source_target_pairs={{0,5},{1,4},{2,7},{3,6},{4,9},{5,8},{6,11},{7,10},{8,13},{9,12},{1... | collective-permute-start | bytes 221192 | tf_op jit(solution)/shard_map/ppermute | solution.py:227
  30.4 0.0 collective-permute-done.4.refs_5_
  30.4 2.1 %collective-permute-done.5.refs_6_ = bf16[144,256]{1,0:T(8,128)(2,1)S(1)} collective-permute-done((bf16[144,256]{1,0:T(8,128)(2,1)S(1)}, bf16[144,256]{1,0:T(8,128)(2,1)S(1)}, u32[]{:S(2)}, u32[]{:S(2)}) %collective-permute-start.5) | collective-permute-done | bytes 73760 | tf_op jit(solution)/shard_map/ppermute | solution.py:227
  32.6 1.9 %collective-permute-done.6.refs_7_ = bf16[144,256]{1,0:T(8,128)(2,1)S(1)} collective-permute-done((bf16[144,256]{1,0:T(8,128)(2,1)S(1)}, bf16[144,256]{1,0:T(8,128)(2,1)S(1)}, u32[]{:S(2)}, u32[]{:S(2)}) %collective-permute-start.6) | collective-permute-done | bytes 73760 | tf_op jit(solution)/shard_map/ppermute | solution.py:227
  34.5 0.0 collective-permute-done.7.refs_8_
  34.5 3.0 %collective-permute-done.8.refs_9_ = bf16[144,256]{1,0:T(8,128)(2,1)S(1)} collective-permute-done((bf16[144,256]{1,0:T(8,128)(2,1)S(1)}, bf16[144,256]{1,0:T(8,128)(2,1)S(1)}, u32[]{:S(2)}, u32[]{:S(2)}) %collective-permute-start.8) | collective-permute-done | bytes 73760 | tf_op jit(solution)/shard_map/ppermute | solution.py:227
  37.5 2.4 %combine.1 = (f32[6,32,256]{2,1,0:T(8,128)}, f32[32,256]{1,0:T(8,128)}) custom-call(f32[6]{0:T(128)S(1)} %copy-done.3, bf16[144,256]{1,0:T(8,128)(2,1)S(1)} %collective-permute-done.refs_0_, bf16[144,256]{1,0:T(8,128)(2,1)S(1)} %collective-permute-done.1.refs_1_, bf16[144,256]{1,0:T(8,128)(2,1)S(1)} %collective-permute-done.2.refs_2_, ...), custom_call_target="tpu_custom_call" | custom-call | tf_op jit(solution)/shard_map/combine/pallas_call | solution.py:231
  (15 shorter events, 0.0 us)
Async XLA Ops:
  0.6 0.9 %copy-start.1 = (bf16[21,21]{1,0:T(8,128)(2,1)S(1)}, bf16[21,21]{1,0:T(8,128)(2,1)}, u32[]{:S(2)}) copy-start(bf16[21,21]{1,0:T(8,128)(2,1)} %rowk_ref.1) | copy-start | bytes 2650
  0.6 0.9 %copy-start.2 = (bf16[21,21]{1,0:T(8,128)(2,1)S(1)}, bf16[21,21]{1,0:T(8,128)(2,1)}, u32[]{:S(2)}) copy-start(bf16[21,21]{1,0:T(8,128)(2,1)} %colk_ref.1) | copy-start | bytes 2650
  0.7 0.9 %copy-start.7 = (s32[4]{0:T(128)S(1)}, s32[4]{0:T(128)}, u32[]{:S(2)}) copy-start(s32[4]{0:T(128)} %band_ref.1) | copy-start | bytes 52
  0.7 0.9 %copy-start.8 = (bf16[32]{0:T(256)(128)(2,1)S(1)}, bf16[32]{0:T(256)(128)(2,1)}, u32[]{:S(2)}) copy-start(bf16[32]{0:T(256)(128)(2,1)} %param.13) | copy-start | bytes 196
  1.5 0.7 %copy-start.4 = (s32[32]{0:T(128)S(1)}, s32[32]{0:T(128)}, u32[]{:S(2)}) copy-start(s32[32]{0:T(128)} %patch_ref.1) | copy-start | bytes 388
  1.5 0.7 %copy-start.5 = (s32[32]{0:T(128)S(1)}, s32[32]{0:T(128)}, u32[]{:S(2)}) copy-start(s32[32]{0:T(128)} %offset_ref.1) | copy-start | bytes 388
  1.5 0.7 %copy-start.6 = (s32[32]{0:T(128)S(1)}, s32[32]{0:T(128)}, u32[]{:S(2)}) copy-start(s32[32]{0:T(128)} %index_ref.1) | copy-start | bytes 388
  2.2 1.0 %copy-start = (bf16[32,64,128]{2,1,0:T(8,128)(2,1)S(1)}, bf16[32,64,128]{2,1,0:T(8,128)(2,1)}, u32[]{:S(2)}) copy-start(bf16[32,64,128]{2,1,0:T(8,128)(2,1)} %tiles_ref.1) | copy-start | bytes 1572868
  15.6 10.5 %collective-permute-start = (bf16[144,256]{1,0:T(8,128)(2,1)S(1)}, bf16[144,256]{1,0:T(8,128)(2,1)S(1)}, u32[]{:S(2)}, u32[]{:S(2)}) collective-permute-start(bf16[144,256]{1,0:T(8,128)(2,1)S(1)} %get-tuple-element.12), channel_id=1, source_target_pairs={{0,28},{1,29},{2,30},{3,31},{4,0},{5,1},{6,2},{7,3},{8,4},{9,5},{1... | collective-permute-start | bytes 221192 | tf_op jit(solution)/shard_map/ppermute | solution.py:227
  21.7 5.3 %collective-permute-start.1 = (bf16[144,256]{1,0:T(8,128)(2,1)S(1)}, bf16[144,256]{1,0:T(8,128)(2,1)S(1)}, u32[]{:S(2)}, u32[]{:S(2)}) collective-permute-start(bf16[144,256]{1,0:T(8,128)(2,1)S(1)} %get-tuple-element.13), channel_id=1, source_target_pairs={{0,29},{1,28},{2,31},{3,30},{4,1},{5,0},{6,3},{7,2},{8,5},{9,4},{1... | collective-permute-start | bytes 221192 | tf_op jit(solution)/shard_map/ppermute | solution.py:227
  23.2 3.8 %collective-permute-start.2 = (bf16[144,256]{1,0:T(8,128)(2,1)S(1)}, bf16[144,256]{1,0:T(8,128)(2,1)S(1)}, u32[]{:S(2)}, u32[]{:S(2)}) collective-permute-start(bf16[144,256]{1,0:T(8,128)(2,1)S(1)} %get-tuple-element.14), channel_id=1, source_target_pairs={{0,30},{1,31},{2,0},{3,1},{4,2},{5,3},{6,4},{7,5},{8,6},{9,7},{10,... | collective-permute-start | bytes 221192 | tf_op jit(solution)/shard_map/ppermute | solution.py:227
  23.4 6.0 %collective-permute-start.3 = (bf16[144,256]{1,0:T(8,128)(2,1)S(1)}, bf16[144,256]{1,0:T(8,128)(2,1)S(1)}, u32[]{:S(2)}, u32[]{:S(2)}) collective-permute-start(bf16[144,256]{1,0:T(8,128)(2,1)S(1)} %get-tuple-element.15), channel_id=1, source_target_pairs={{0,31},{1,30},{2,1},{3,0},{4,3},{5,2},{6,5},{7,4},{8,7},{9,6},{10,... | collective-permute-start | bytes 221192 | tf_op jit(solution)/shard_map/ppermute | solution.py:227
  24.6 5.8 %collective-permute-start.4 = (bf16[144,256]{1,0:T(8,128)(2,1)S(1)}, bf16[144,256]{1,0:T(8,128)(2,1)S(1)}, u32[]{:S(2)}, u32[]{:S(2)}) collective-permute-start(bf16[144,256]{1,0:T(8,128)(2,1)S(1)} %get-tuple-element.17), channel_id=1, source_target_pairs={{0,1},{1,0},{2,3},{3,2},{4,5},{5,4},{6,7},{7,6},{8,9},{9,8},{10,11... | collective-permute-start | bytes 221192 | tf_op jit(solution)/shard_map/ppermute | solution.py:227
  26.1 6.5 %collective-permute-start.5 = (bf16[144,256]{1,0:T(8,128)(2,1)S(1)}, bf16[144,256]{1,0:T(8,128)(2,1)S(1)}, u32[]{:S(2)}, u32[]{:S(2)}) collective-permute-start(bf16[144,256]{1,0:T(8,128)(2,1)S(1)} %get-tuple-element.18), channel_id=1, source_target_pairs={{0,2},{1,3},{2,4},{3,5},{4,6},{5,7},{6,8},{7,9},{8,10},{9,11},{10,... | collective-permute-start | bytes 221192 | tf_op jit(solution)/shard_map/ppermute | solution.py:227
  27.0 7.5 %collective-permute-start.6 = (bf16[144,256]{1,0:T(8,128)(2,1)S(1)}, bf16[144,256]{1,0:T(8,128)(2,1)S(1)}, u32[]{:S(2)}, u32[]{:S(2)}) collective-permute-start(bf16[144,256]{1,0:T(8,128)(2,1)S(1)} %get-tuple-element.19), channel_id=1, source_target_pairs={{0,3},{1,2},{2,5},{3,4},{4,7},{5,6},{6,9},{7,8},{8,11},{9,10},{10,... | collective-permute-start | bytes 221192 | tf_op jit(solution)/shard_map/ppermute | solution.py:227
  27.0 7.5 %collective-permute-start.7 = (bf16[144,256]{1,0:T(8,128)(2,1)S(1)}, bf16[144,256]{1,0:T(8,128)(2,1)S(1)}, u32[]{:S(2)}, u32[]{:S(2)}) collective-permute-start(bf16[144,256]{1,0:T(8,128)(2,1)S(1)} %get-tuple-element.20), channel_id=1, source_target_pairs={{0,4},{1,5},{2,6},{3,7},{4,8},{5,9},{6,10},{7,11},{8,12},{9,13},{1... | collective-permute-start | bytes 221192 | tf_op jit(solution)/shard_map/ppermute | solution.py:227
  29.4 8.1 %copy-start.3 = (f32[6]{0:T(128)S(1)}, f32[6]{0:T(128)}, u32[]{:S(2)}) copy-start(f32[6]{0:T(128)} %weight_ref.1) | copy-start | bytes 76
  29.4 8.1 %collective-permute-start.8 = (bf16[144,256]{1,0:T(8,128)(2,1)S(1)}, bf16[144,256]{1,0:T(8,128)(2,1)S(1)}, u32[]{:S(2)}, u32[]{:S(2)}) collective-permute-start(bf16[144,256]{1,0:T(8,128)(2,1)S(1)} %get-tuple-element.21), channel_id=1, source_target_pairs={{0,5},{1,4},{2,7},{3,6},{4,9},{5,8},{6,11},{7,10},{8,13},{9,12},{1... | collective-permute-start | bytes 221192 | tf_op jit(solution)/shard_map/ppermute | solution.py:227

commit v2 on v1

v2 whole, which is shorter than its diff:
```python
import functools

import jax
import jax.numpy as jnp
from jax import lax
from jax.experimental import pallas as pl
from jax.experimental.pallas import tpu as pltpu
from jax.sharding import PartitionSpec as P

PW = 256
BANDS = 6
REACH = 2
SPREAD = 2 * REACH + 1
EXTRA = 16


def slot_rows(row_share):
    return max(row_share, 16)


def match_kernel(
    patches,
    groups,
    patch_ref,
    offset_ref,
    index_ref,
    band_ref,
    table_ref,
    weight_ref,
    rowk_ref,
    colk_ref,
    tiles_hbm,
    *rest,
):
    messages = rest[: SPREAD * groups]
    tiles_ref, kernels, weights, toeplitz, sums, extra, arrival = rest[SPREAD * groups :]
    visits = band_ref.shape[0]
    tile_count, rows, width = tiles_ref.shape
    per_visit = tile_count // visits
    basis, taps = rowk_ref.shape
    half = taps // 2
    back = half // 8 * 8
    lead = half - back
    deep = kernels.shape[1]
    row_share = rows // groups
    slot = slot_rows(row_share)
    owner = lax.axis_index("ra")
    group = lax.axis_index("band")

    def fetch(visit):
        held = pl.ds(visit * per_visit, per_visit)
        return pltpu.make_async_copy(tiles_hbm.at[held], tiles_ref.at[held], arrival.at[visit])

    for visit in range(visits):
        fetch(visit).start()

    def iota(shape, axis):
        return lax.broadcasted_iota(jnp.int32, shape, axis)

    def across(left, right, **options):
        return lax.dot_general(
            left,
            right,
            (((1,), (1,)), ((), ())),
            preferred_element_type=jnp.float32,
            **options,
        )

    eye = (iota((tile_count, tile_count), 0) == iota((tile_count, tile_count), 1)).astype(
        jnp.bfloat16
    )
    weights[...] = across(eye, jnp.broadcast_to(weight_ref[...], (width, tile_count)))
    entry = iota((1, table_ref.shape[1]), 1)
    chosen = jnp.concatenate(
        [(entry == index_ref[j]).astype(jnp.float32) for j in range(tile_count)], axis=0
    )
    coeffs = across(chosen, table_ref[...], precision=lax.Precision.HIGHEST)
    tap_rows = (iota((deep, taps), 0) == iota((deep, taps), 1)).astype(jnp.bfloat16)
    col_taps = across(tap_rows, colk_ref[...])
    tap = iota((taps, 2 * width), 0)
    lane = iota((taps, 2 * width), 1)
    spot = jnp.where(
        lane < width, lax.rem(lane + lead, width), lane - width - rows + lead
    )
    row_taps = jnp.dot(
        rowk_ref[...], (spot == tap).astype(jnp.bfloat16), preferred_element_type=jnp.float32
    ).astype(jnp.bfloat16)
    for pair in range(tile_count // 2):
        parts = []
        for side in range(2):
            mix = col_taps * coeffs[2 * pair + side : 2 * pair + side + 1]
            high = mix.astype(jnp.bfloat16)
            low = (mix - high.astype(jnp.float32)).astype(jnp.bfloat16)
            place = row_taps[:, side * width : (side + 1) * width]
            parts.append(
                jnp.dot(high, place, preferred_element_type=jnp.float32)
                + jnp.dot(low, place, preferred_element_type=jnp.float32)
            )
        kernels[pair] = parts[0] + parts[1]
    extra[...] = jnp.zeros_like(extra)

    lane = iota((rows, width), 1)
    near = jnp.abs(lax.rem(lane, rows) - iota((rows, width), 0)) <= half
    edge = 2 * half // 8 * 8
    column = iota((1, width), 1)
    empty = jnp.zeros((rows, width), jnp.bfloat16)

    def one_visit(visit, unused):
        fetch(visit).wait()
        sums[...] = jnp.zeros_like(sums)
        first = visit * per_visit
        for pair in range(per_visit // 2):
            for m in range(taps):
                spread = jnp.broadcast_to(
                    kernels[visit * (per_visit // 2) + pair, pl.ds(m, 1), :], (rows, width)
                )
                turned = pltpu.roll(spread, width - back, 1, stride=1, stride_axis=0)
                turned = jnp.concatenate(
                    [
                        jnp.where(near[:edge], turned[:edge], 0.0),
                        turned[edge : rows - edge],
                        jnp.where(near[rows - edge :], turned[rows - edge :], 0.0),
                    ],
                    axis=0,
                )
                toeplitz[pair, m * rows : (m + 1) * rows, :] = turned.astype(jnp.bfloat16)
            both = jnp.concatenate(
                [
                    jnp.concatenate([tiles_ref[first + 2 * pair], empty], axis=1),
                    jnp.concatenate([empty, tiles_ref[first + 2 * pair + 1]], axis=1),
                ],
                axis=0,
            )
            passed = jnp.dot(toeplitz[pair], both, preferred_element_type=jnp.float32)
            for side in range(2):
                matched = jnp.zeros((rows, width), jnp.float32)
                for m in range(taps):
                    block = passed[m * rows : (m + 1) * rows, side * width : (side + 1) * width]
                    if m != half:
                        turned = pltpu.roll(block, (half - m) % width, 1)
                        inside = (lane + (m - half) >= 0) & (lane + (m - half) < width)
                        block = jnp.where(inside, turned, 0.0)
                    matched += block
                tile = first + 2 * pair + side
                offset = offset_ref[tile]
                bucket = lax.rem(patch_ref[tile] - owner + REACH + patches, patches)
                weight = weights[pl.ds(tile, 1), :]
                turned = pltpu.roll(matched * weight, lax.rem(offset, width), 1)
                sums[bucket, :, :width] += jnp.where(lane >= offset, turned, 0.0)
                sums[bucket, :, width:] += jnp.where(lane < offset, turned, 0.0)
                extra[bucket, pl.ds(visit, 1), :] += jnp.concatenate(
                    [
                        jnp.where(column >= offset, weight, 0.0),
                        jnp.where(column < offset, weight, 0.0),
                    ],
                    axis=1,
                )

        for bucket in range(SPREAD):
            extra[bucket, pl.ds(2 * visits + visit, 1), :] = jnp.full(
                (1, PW), band_ref[visit], jnp.int32
            ).astype(jnp.float32)
            for turn in range(groups):
                part = lax.rem(group + turn, groups)
                own = sums[bucket, pl.ds(pl.multiple_of(part * row_share, row_share), row_share), :]
                if slot > row_share:
                    own = jnp.concatenate(
                        [own, jnp.zeros((slot - row_share, PW), jnp.float32)], axis=0
                    )
                messages[bucket * groups + turn][
                    pl.ds(pl.multiple_of(visit * slot, slot), slot), :
                ] = own.astype(jnp.bfloat16)
        return unused

    lax.fori_loop(0, visits, one_visit, 0)

    row = iota((EXTRA, PW), 0)
    for bucket in range(SPREAD):
        held = extra[bucket]
        high = held.astype(jnp.bfloat16).astype(jnp.float32)
        low = jnp.concatenate([held[-visits:], (held - high)[:-visits]], axis=0)
        mixed = jnp.where((row >= visits) & (row < 2 * visits), low, high).astype(jnp.bfloat16)
        for turn in range(groups):
            messages[bucket * groups + turn][slot * visits :, :] = mixed


def combine_kernel(count, weight_ref, *refs):
    messages = refs[:-2]
    coadd_ref, detection_ref = refs[-2:]
    row_share = coadd_ref.shape[1]
    slot = slot_rows(row_share)
    totals = [jnp.zeros((row_share, PW), jnp.float32) for _ in range(BANDS)]
    weight_totals = [jnp.zeros((1, PW), jnp.float32) for _ in range(BANDS)]
    for message in messages:
        extra = message[slot * count :, :].astype(jnp.float32)
        for visit in range(count):
            band = extra[2 * count + visit : 2 * count + visit + 1]
            weight = extra[visit : visit + 1] + extra[count + visit : count + visit + 1]
            part = message[slot * visit : slot * (visit + 1), :].astype(jnp.float32)[:row_share]
            for b in range(BANDS):
                here = band == float(b)
                totals[b] += jnp.where(here, part, 0.0)
                weight_totals[b] += jnp.where(here, weight, 0.0)
    detection = jnp.zeros((row_share, PW), jnp.float32)
    for b in range(BANDS):
        coadd = totals[b] / jnp.maximum(weight_totals[b], 1.0)
        coadd_ref[b] = coadd
        detection += weight_ref[b] * coadd
    detection_ref[...] = detection


def local(
    tiles,
    tile_patch,
    tile_offset,
    tile_weight,
    visit_band,
    coeff_index,
    coeff_table,
    row_kernels,
    column_kernels,
    band_weight,
):
    tile_count, rows, width = tiles.shape
    visits = visit_band.shape[0]
    per_visit = tile_count // visits
    basis, taps = row_kernels.shape
    patches = lax.axis_size("ra")
    groups = lax.axis_size("band")
    row_share = rows // groups
    slot = slot_rows(row_share)
    length = visits * slot + EXTRA
    smem = pl.BlockSpec(memory_space=pltpu.SMEM)

    vmem = pl.BlockSpec(memory_space=pltpu.VMEM)
    deep = (taps + 7) // 8 * 8
    messages = pl.pallas_call(
        functools.partial(match_kernel, patches, groups),
        in_specs=[smem] * 4 + [vmem] * 4 + [pl.BlockSpec(memory_space=pltpu.HBM)],
        out_specs=[vmem] * (SPREAD * groups),
        out_shape=[jax.ShapeDtypeStruct((length, PW), jnp.bfloat16)] * (SPREAD * groups),
        scratch_shapes=[
            pltpu.VMEM((tile_count, rows, width), jnp.bfloat16),
            pltpu.VMEM((tile_count // 2, deep, width), jnp.float32),
            pltpu.VMEM((tile_count, width), jnp.float32),
            pltpu.VMEM((per_visit // 2, taps * rows, width), jnp.bfloat16),
            pltpu.VMEM((SPREAD, rows, PW), jnp.float32),
            pltpu.VMEM((SPREAD, EXTRA, PW), jnp.float32),
            pltpu.SemaphoreType.DMA((visits,)),
        ],
        compiler_params=pltpu.CompilerParams(vmem_limit_bytes=40 * 1024 * 1024),
        name="match_and_sum",
    )(
        tile_patch,
        tile_offset,
        coeff_index,
        visit_band,
        coeff_table.T,
        tile_weight.reshape(1, tile_count),
        row_kernels,
        column_kernels,
        tiles,
    )

    arrived = []
    for bucket in range(SPREAD):
        for turn in range(groups):
            message = messages[bucket * groups + turn]
            distance = bucket - REACH
            if distance != 0 or turn != 0:
                route = [
                    (o * groups + g, (o + distance) % patches * groups + (g + turn) % groups)
                    for o in range(patches)
                    for g in range(groups)
                ]
                message = lax.ppermute(message, ("ra", "band"), route)
            arrived.append(message)

    return pl.pallas_call(
        functools.partial(combine_kernel, visits),
        in_specs=[smem] + [vmem] * len(arrived),
        out_specs=(vmem, vmem),
        out_shape=(
            jax.ShapeDtypeStruct((BANDS, row_share, PW), jnp.float32),
            jax.ShapeDtypeStruct((row_share, PW), jnp.float32),
        ),
        compiler_params=pltpu.CompilerParams(vmem_limit_bytes=40 * 1024 * 1024),
        name="combine",
    )(band_weight, *arrived)


def solution(mesh):
    return jax.shard_map(
        local,
        mesh=mesh,
        in_specs=(
            P(("ra", "band"), None, None),
            P(("ra", "band")),
            P(("ra", "band")),
            P(("ra", "band")),
            P(("ra", "band")),
            P(("ra", "band")),
            P(),
            P(),
            P(),
            P(),
        ),
        out_specs=(P(None, "band", "ra"), P("band", "ra")),
        check_vma=False,
    )
```

time: 40.2 us -> 42.4 us (1.055)
  local copies, waits for them, and re-layouts: 2.51 us -> 3.81 us
  Pallas kernels: 14.8 us -> 15.7 us
    unnamed x19 -> x20, local copies, waits for them, and re-layouts: 2.51 us -> 3.81 us
    pallas_call x1, Pallas kernels: 12.4 us -> 13.3 us  [local(): pl.pallas_call(functools.partial(match_kernel, patches, groups), in_specs...]
  transfers between devices with their start and end apart: 9 -> 9, of which waited for: 4 -> 5; matrix products, arithmetic and copies ran while one was open for 0% -> 0% of each run, Pallas kernels for 0% -> 0%
where the time goes in v2:
time: 42.4 us; the launch traced here: 42.1 us
  Pallas kernels  15.7 us (37%)
  starting transfers between devices  13.9 us (33%)
  waiting for transfers between devices  7.93 us (19%)
  local copies, waits for them, and re-layouts  3.81 us (9%)
  between operations  0.7 us (2%)
    ppermute x9, starting transfers between devices, local(): message = lax.ppermute(message, ('ra', 'band'), route)  13.9 us
    pallas_call x1, Pallas kernels, local(): pl.pallas_call(functools.partial(match_kernel, patches, groups), in_specs...  13.3 us
    ppermute x9, waiting for transfers between devices, local(): message = lax.ppermute(message, ('ra', 'band'), route)  7.93 us
    unnamed x20, local copies, waits for them, and re-layouts  3.81 us
    pallas_call x1, Pallas kernels, local(): pl.pallas_call(functools.partial(combine_kernel, visits), in_specs=[smem]...  2.43 us
  transfers between devices with their start and end apart: 9, of which 5 were waited for; matrix products, arithmetic and copies ran while one was open for 0% of the time, Pallas kernels for 0%

profile of v2, /device:TPU:0, one launch (start us, length us, event | category | flops | bytes accessed | tf_op | source)
XLA Modules:
  0.0 42.1 jit_solution(4791010544179907223)
XLA Ops:
  0.7 0.6 %copy-done.7 = s32[4]{0:T(128)S(1)} copy-done((s32[4]{0:T(128)S(1)}, s32[4]{0:T(128)}, u32[]{:S(2)}) %copy-start.7) | copy-done | bytes 40
  1.3 0.0 copy-done.8
  1.3 0.0 copy-done.4
  1.3 0.0 copy-done.5
  1.3 0.0 copy-done.6
  1.4 1.0 %copy-done = bf16[32,64,128]{2,1,0:T(8,128)(2,1)S(1)} copy-done((bf16[32,64,128]{2,1,0:T(8,128)(2,1)S(1)}, bf16[32,64,128]{2,1,0:T(8,128)(2,1)}, u32[]{:S(2)}) %copy-start) | copy-done | bytes 524312
  2.4 0.7 %copy-done.1 = f32[64,21]{0,1:T(8,128)S(1)} copy-done((f32[64,21]{0,1:T(8,128)S(1)}, f32[64,21]{0,1:T(8,128)}, u32[]{:S(2)}) %copy-start.1) | copy-done | bytes 5400
  3.1 0.7 %copy-done.2 = bf16[21,21]{1,0:T(8,128)(2,1)S(1)} copy-done((bf16[21,21]{1,0:T(8,128)(2,1)S(1)}, bf16[21,21]{1,0:T(8,128)(2,1)}, u32[]{:S(2)}) %copy-start.2) | copy-done | bytes 906
  3.8 0.7 %copy-done.3 = bf16[21,21]{1,0:T(8,128)(2,1)S(1)} copy-done((bf16[21,21]{1,0:T(8,128)(2,1)S(1)}, bf16[21,21]{1,0:T(8,128)(2,1)}, u32[]{:S(2)}) %copy-start.3) | copy-done | bytes 906
  4.5 13.3 %match_and_sum.1 = (bf16[144,256]{1,0:T(8,128)(2,1)S(1)}, bf16[144,256]{1,0:T(8,128)(2,1)S(1)}, bf16[144,256]{1,0:T(8,128)(2,1)S(1)}, bf16[144,256]{1,0:T(8,128)...) custom-call(s32[32]{0:T(128)S(1)} %copy-done.4, ...), custom_call_target="tpu_custom_call" | custom-call | tf_op jit(solution)/shard_map/match_and_sum/pallas_call | solution.py:237
  17.8 6.0 %collective-permute-start = (bf16[144,256]{1,0:T(8,128)(2,1)S(1)}, bf16[144,256]{1,0:T(8,128)(2,1)S(1)}, u32[]{:S(2)}, u32[]{:S(2)}) collective-permute-start(bf16[144,256]{1,0:T(8,128)(2,1)S(1)} %get-tuple-element.12), channel_id=1, source_target_pairs={{0,28},{1,29},{2,30},{3,31},{4,0},{5,1},{6,2},{7,3},{8,4},{9,5},{1... | collective-permute-start | bytes 221192 | tf_op jit(solution)/shard_map/ppermute | solution.py:276
  23.8 1.5 %collective-permute-start.1 = (bf16[144,256]{1,0:T(8,128)(2,1)S(1)}, bf16[144,256]{1,0:T(8,128)(2,1)S(1)}, u32[]{:S(2)}, u32[]{:S(2)}) collective-permute-start(bf16[144,256]{1,0:T(8,128)(2,1)S(1)} %get-tuple-element.13), channel_id=1, source_target_pairs={{0,29},{1,28},{2,31},{3,30},{4,1},{5,0},{6,3},{7,2},{8,5},{9,4},{1... | collective-permute-start | bytes 221192 | tf_op jit(solution)/shard_map/ppermute | solution.py:276
  25.3 0.3 collective-permute-start.2
  25.5 1.2 %collective-permute-start.3 = (bf16[144,256]{1,0:T(8,128)(2,1)S(1)}, bf16[144,256]{1,0:T(8,128)(2,1)S(1)}, u32[]{:S(2)}, u32[]{:S(2)}) collective-permute-start(bf16[144,256]{1,0:T(8,128)(2,1)S(1)} %get-tuple-element.15), channel_id=1, source_target_pairs={{0,31},{1,30},{2,1},{3,0},{4,3},{5,2},{6,5},{7,4},{8,7},{9,6},{10,... | collective-permute-start | bytes 221192 | tf_op jit(solution)/shard_map/ppermute | solution.py:276
  26.7 1.5 %collective-permute-start.4 = (bf16[144,256]{1,0:T(8,128)(2,1)S(1)}, bf16[144,256]{1,0:T(8,128)(2,1)S(1)}, u32[]{:S(2)}, u32[]{:S(2)}) collective-permute-start(bf16[144,256]{1,0:T(8,128)(2,1)S(1)} %get-tuple-element.17), channel_id=1, source_target_pairs={{0,1},{1,0},{2,3},{3,2},{4,5},{5,4},{6,7},{7,6},{8,9},{9,8},{10,11... | collective-permute-start | bytes 221192 | tf_op jit(solution)/shard_map/ppermute | solution.py:276
  28.2 0.8 %collective-permute-done.1.refs_1_ = bf16[144,256]{1,0:T(8,128)(2,1)S(1)} collective-permute-done((bf16[144,256]{1,0:T(8,128)(2,1)S(1)}, bf16[144,256]{1,0:T(8,128)(2,1)S(1)}, u32[]{:S(2)}, u32[]{:S(2)}) %collective-permute-start.1) | collective-permute-done | bytes 73760 | tf_op jit(solution)/shard_map/ppermute | solution.py:276
  29.1 0.0 collective-permute-start.6
  29.1 2.4 %collective-permute-start.7 = (bf16[144,256]{1,0:T(8,128)(2,1)S(1)}, bf16[144,256]{1,0:T(8,128)(2,1)S(1)}, u32[]{:S(2)}, u32[]{:S(2)}) collective-permute-start(bf16[144,256]{1,0:T(8,128)(2,1)S(1)} %get-tuple-element.20), channel_id=1, source_target_pairs={{0,4},{1,5},{2,6},{3,7},{4,8},{5,9},{6,10},{7,11},{8,12},{9,13},{1... | collective-permute-start | bytes 221192 | tf_op jit(solution)/shard_map/ppermute | solution.py:276
  31.5 1.0 %collective-permute-start.8 = (bf16[144,256]{1,0:T(8,128)(2,1)S(1)}, bf16[144,256]{1,0:T(8,128)(2,1)S(1)}, u32[]{:S(2)}, u32[]{:S(2)}) collective-permute-start(bf16[144,256]{1,0:T(8,128)(2,1)S(1)} %get-tuple-element.21), channel_id=1, source_target_pairs={{0,5},{1,4},{2,7},{3,6},{4,9},{5,8},{6,11},{7,10},{8,13},{9,12},{1... | collective-permute-start | bytes 221192 | tf_op jit(solution)/shard_map/ppermute | solution.py:276
  32.6 2.2 %collective-permute-done.5.refs_6_ = bf16[144,256]{1,0:T(8,128)(2,1)S(1)} collective-permute-done((bf16[144,256]{1,0:T(8,128)(2,1)S(1)}, bf16[144,256]{1,0:T(8,128)(2,1)S(1)}, u32[]{:S(2)}, u32[]{:S(2)}) %collective-permute-start.5) | collective-permute-done | bytes 73760 | tf_op jit(solution)/shard_map/ppermute | solution.py:276
  34.7 1.9 %collective-permute-done.6.refs_7_ = bf16[144,256]{1,0:T(8,128)(2,1)S(1)} collective-permute-done((bf16[144,256]{1,0:T(8,128)(2,1)S(1)}, bf16[144,256]{1,0:T(8,128)(2,1)S(1)}, u32[]{:S(2)}, u32[]{:S(2)}) %collective-permute-start.6) | collective-permute-done | bytes 73760 | tf_op jit(solution)/shard_map/ppermute | solution.py:276
  36.6 0.1 collective-permute-done.7.refs_8_
  36.7 3.0 %collective-permute-done.8.refs_9_ = bf16[144,256]{1,0:T(8,128)(2,1)S(1)} collective-permute-done((bf16[144,256]{1,0:T(8,128)(2,1)S(1)}, bf16[144,256]{1,0:T(8,128)(2,1)S(1)}, u32[]{:S(2)}, u32[]{:S(2)}) %collective-permute-start.8) | collective-permute-done | bytes 73760 | tf_op jit(solution)/shard_map/ppermute | solution.py:276
  39.6 2.4 %combine.1 = (f32[6,32,256]{2,1,0:T(8,128)}, f32[32,256]{1,0:T(8,128)}) custom-call(f32[6]{0:T(128)S(1)} %copy-done.9, bf16[144,256]{1,0:T(8,128)(2,1)S(1)} %collective-permute-done.refs_0_, bf16[144,256]{1,0:T(8,128)(2,1)S(1)} %collective-permute-done.1.refs_1_, bf16[144,256]{1,0:T(8,128)(2,1)S(1)} %collective-permute-done.2.refs_2_, ...), custom_call_target="tpu_custom_call" | custom-call | tf_op jit(solution)/shard_map/combine/pallas_call | solution.py:279
  (16 shorter events, 0.0 us)
Async XLA Ops:
  0.6 0.7 %copy-start.7 = (s32[4]{0:T(128)S(1)}, s32[4]{0:T(128)}, u32[]{:S(2)}) copy-start(s32[4]{0:T(128)} %band_ref.1) | copy-start | bytes 52
  0.6 0.7 %copy-start.8 = (bf16[32]{0:T(256)(128)(2,1)S(1)}, bf16[32]{0:T(256)(128)(2,1)}, u32[]{:S(2)}) copy-start(bf16[32]{0:T(256)(128)(2,1)} %param.13) | copy-start | bytes 196
  0.7 0.7 %copy-start.4 = (s32[32]{0:T(128)S(1)}, s32[32]{0:T(128)}, u32[]{:S(2)}) copy-start(s32[32]{0:T(128)} %patch_ref.1) | copy-start | bytes 388
  0.7 0.7 %copy-start.5 = (s32[32]{0:T(128)S(1)}, s32[32]{0:T(128)}, u32[]{:S(2)}) copy-start(s32[32]{0:T(128)} %offset_ref.1) | copy-start | bytes 388
  0.7 0.7 %copy-start.6 = (s32[32]{0:T(128)S(1)}, s32[32]{0:T(128)}, u32[]{:S(2)}) copy-start(s32[32]{0:T(128)} %index_ref.1) | copy-start | bytes 388
  1.4 1.0 %copy-start = (bf16[32,64,128]{2,1,0:T(8,128)(2,1)S(1)}, bf16[32,64,128]{2,1,0:T(8,128)(2,1)}, u32[]{:S(2)}) copy-start(bf16[32,64,128]{2,1,0:T(8,128)(2,1)} %tiles_hbm.1) | copy-start | bytes 1572868
  2.4 0.7 %copy-start.1 = (f32[64,21]{0,1:T(8,128)S(1)}, f32[64,21]{0,1:T(8,128)}, u32[]{:S(2)}) copy-start(f32[64,21]{0,1:T(8,128)} %param.16) | copy-start | bytes 16132
  3.1 0.7 %copy-start.2 = (bf16[21,21]{1,0:T(8,128)(2,1)S(1)}, bf16[21,21]{1,0:T(8,128)(2,1)}, u32[]{:S(2)}) copy-start(bf16[21,21]{1,0:T(8,128)(2,1)} %rowk_ref.1) | copy-start | bytes 2650
  3.8 0.7 %copy-start.3 = (bf16[21,21]{1,0:T(8,128)(2,1)S(1)}, bf16[21,21]{1,0:T(8,128)(2,1)}, u32[]{:S(2)}) copy-start(bf16[21,21]{1,0:T(8,128)(2,1)} %colk_ref.1) | copy-start | bytes 2650
  17.8 10.5 %collective-permute-start = (bf16[144,256]{1,0:T(8,128)(2,1)S(1)}, bf16[144,256]{1,0:T(8,128)(2,1)S(1)}, u32[]{:S(2)}, u32[]{:S(2)}) collective-permute-start(bf16[144,256]{1,0:T(8,128)(2,1)S(1)} %get-tuple-element.12), channel_id=1, source_target_pairs={{0,28},{1,29},{2,30},{3,31},{4,0},{5,1},{6,2},{7,3},{8,4},{9,5},{1... | collective-permute-start | bytes 221192 | tf_op jit(solution)/shard_map/ppermute | solution.py:276
  23.8 5.3 %collective-permute-start.1 = (bf16[144,256]{1,0:T(8,128)(2,1)S(1)}, bf16[144,256]{1,0:T(8,128)(2,1)S(1)}, u32[]{:S(2)}, u32[]{:S(2)}) collective-permute-start(bf16[144,256]{1,0:T(8,128)(2,1)S(1)} %get-tuple-element.13), channel_id=1, source_target_pairs={{0,29},{1,28},{2,31},{3,30},{4,1},{5,0},{6,3},{7,2},{8,5},{9,4},{1... | collective-permute-start | bytes 221192 | tf_op jit(solution)/shard_map/ppermute | solution.py:276
  25.3 3.9 %collective-permute-start.2 = (bf16[144,256]{1,0:T(8,128)(2,1)S(1)}, bf16[144,256]{1,0:T(8,128)(2,1)S(1)}, u32[]{:S(2)}, u32[]{:S(2)}) collective-permute-start(bf16[144,256]{1,0:T(8,128)(2,1)S(1)} %get-tuple-element.14), channel_id=1, source_target_pairs={{0,30},{1,31},{2,0},{3,1},{4,2},{5,3},{6,4},{7,5},{8,6},{9,7},{10,... | collective-permute-start | bytes 221192 | tf_op jit(solution)/shard_map/ppermute | solution.py:276
  25.5 6.0 %collective-permute-start.3 = (bf16[144,256]{1,0:T(8,128)(2,1)S(1)}, bf16[144,256]{1,0:T(8,128)(2,1)S(1)}, u32[]{:S(2)}, u32[]{:S(2)}) collective-permute-start(bf16[144,256]{1,0:T(8,128)(2,1)S(1)} %get-tuple-element.15), channel_id=1, source_target_pairs={{0,31},{1,30},{2,1},{3,0},{4,3},{5,2},{6,5},{7,4},{8,7},{9,6},{10,... | collective-permute-start | bytes 221192 | tf_op jit(solution)/shard_map/ppermute | solution.py:276
  26.7 5.8 %collective-permute-start.4 = (bf16[144,256]{1,0:T(8,128)(2,1)S(1)}, bf16[144,256]{1,0:T(8,128)(2,1)S(1)}, u32[]{:S(2)}, u32[]{:S(2)}) collective-permute-start(bf16[144,256]{1,0:T(8,128)(2,1)S(1)} %get-tuple-element.17), channel_id=1, source_target_pairs={{0,1},{1,0},{2,3},{3,2},{4,5},{5,4},{6,7},{7,6},{8,9},{9,8},{10,11... | collective-permute-start | bytes 221192 | tf_op jit(solution)/shard_map/ppermute | solution.py:276
  28.2 6.5 %collective-permute-start.5 = (bf16[144,256]{1,0:T(8,128)(2,1)S(1)}, bf16[144,256]{1,0:T(8,128)(2,1)S(1)}, u32[]{:S(2)}, u32[]{:S(2)}) collective-permute-start(bf16[144,256]{1,0:T(8,128)(2,1)S(1)} %get-tuple-element.18), channel_id=1, source_target_pairs={{0,2},{1,3},{2,4},{3,5},{4,6},{5,7},{6,8},{7,9},{8,10},{9,11},{10,... | collective-permute-start | bytes 221192 | tf_op jit(solution)/shard_map/ppermute | solution.py:276
  29.1 7.5 %collective-permute-start.6 = (bf16[144,256]{1,0:T(8,128)(2,1)S(1)}, bf16[144,256]{1,0:T(8,128)(2,1)S(1)}, u32[]{:S(2)}, u32[]{:S(2)}) collective-permute-start(bf16[144,256]{1,0:T(8,128)(2,1)S(1)} %get-tuple-element.19), channel_id=1, source_target_pairs={{0,3},{1,2},{2,5},{3,4},{4,7},{5,6},{6,9},{7,8},{8,11},{9,10},{10,... | collective-permute-start | bytes 221192 | tf_op jit(solution)/shard_map/ppermute | solution.py:276
  29.1 7.5 %collective-permute-start.7 = (bf16[144,256]{1,0:T(8,128)(2,1)S(1)}, bf16[144,256]{1,0:T(8,128)(2,1)S(1)}, u32[]{:S(2)}, u32[]{:S(2)}) collective-permute-start(bf16[144,256]{1,0:T(8,128)(2,1)S(1)} %get-tuple-element.20), channel_id=1, source_target_pairs={{0,4},{1,5},{2,6},{3,7},{4,8},{5,9},{6,10},{7,11},{8,12},{9,13},{1... | collective-permute-start | bytes 221192 | tf_op jit(solution)/shard_map/ppermute | solution.py:276
  31.5 8.1 %copy-start.9 = (f32[6]{0:T(128)S(1)}, f32[6]{0:T(128)}, u32[]{:S(2)}) copy-start(f32[6]{0:T(128)} %weight_ref.1) | copy-start | bytes 76
  31.5 8.1 %collective-permute-start.8 = (bf16[144,256]{1,0:T(8,128)(2,1)S(1)}, bf16[144,256]{1,0:T(8,128)(2,1)S(1)}, u32[]{:S(2)}, u32[]{:S(2)}) collective-permute-start(bf16[144,256]{1,0:T(8,128)(2,1)S(1)} %get-tuple-element.21), channel_id=1, source_target_pairs={{0,5},{1,4},{2,7},{3,6},{4,9},{5,8},{6,11},{7,10},{8,13},{9,12},{1... | collective-permute-start | bytes 221192 | tf_op jit(solution)/shard_map/ppermute | solution.py:276

commit v3 on v2

--- a/solution.py
+++ b/solution.py
@@ -12,6 +12,11 @@
 REACH = 2
 SPREAD = 2 * REACH + 1
 EXTRA = 16
+BLOCK = 32
+COARSE = 3
+VECTORS = 16
+FINE_ROWS = 64
+LEAD = 6
 
 
 def slot_rows(row_share):
@@ -25,27 +30,52 @@
     offset_ref,
     index_ref,
     band_ref,
-    table_ref,
-    weight_ref,
-    rowk_ref,
-    colk_ref,
+    table_hbm,
+    weight_hbm,
+    rowk_hbm,
+    colk_hbm,
     tiles_hbm,
     *rest,
 ):
     messages = rest[: SPREAD * groups]
-    tiles_ref, kernels, weights, toeplitz, sums, extra, arrival = rest[SPREAD * groups :]
+    (
+        table_ref,
+        weight_ref,
+        rowk_ref,
+        colk_ref,
+        tiles_ref,
+        kernels,
+        weights,
+        shifted,
+        toeplitz,
+        sums,
+        extra,
+        arrival,
+        ready,
+    ) = rest[SPREAD * groups :]
     visits = band_ref.shape[0]
     tile_count, rows, width = tiles_ref.shape
     per_visit = tile_count // visits
     basis, taps = rowk_ref.shape
     half = taps // 2
-    back = half // 8 * 8
-    lead = half - back
-    deep = kernels.shape[1]
     row_share = rows // groups
     slot = slot_rows(row_share)
     owner = lax.axis_index("ra")
     group = lax.axis_index("band")
+
+    small = [
+        pltpu.make_async_copy(source, target, ready.at[place])
+        for place, (source, target) in enumerate(
+            (
+                (table_hbm, table_ref),
+                (weight_hbm, weight_ref),
+                (rowk_hbm, rowk_ref),
+                (colk_hbm, colk_ref),
+            )
+        )
+    ]
+    for copy in small:
+        copy.start()
 
     def fetch(visit):
         held = pl.ds(visit * per_visit, per_visit)
@@ -66,95 +96,112 @@
             **options,
         )
 
+    extra[...] = jnp.zeros_like(extra)
+    shifted[...] = jnp.zeros_like(shifted)
     eye = (iota((tile_count, tile_count), 0) == iota((tile_count, tile_count), 1)).astype(
         jnp.bfloat16
     )
-    weights[...] = across(eye, jnp.broadcast_to(weight_ref[...], (width, tile_count)))
     entry = iota((1, table_ref.shape[1]), 1)
     chosen = jnp.concatenate(
         [(entry == index_ref[j]).astype(jnp.float32) for j in range(tile_count)], axis=0
     )
+    for copy in small:
+        copy.wait()
+    weights[...] = across(eye, jnp.broadcast_to(weight_ref[...], (width, tile_count)))
     coeffs = across(chosen, table_ref[...], precision=lax.Precision.HIGHEST)
-    tap_rows = (iota((deep, taps), 0) == iota((deep, taps), 1)).astype(jnp.bfloat16)
-    col_taps = across(tap_rows, colk_ref[...])
-    tap = iota((taps, 2 * width), 0)
-    lane = iota((taps, 2 * width), 1)
-    spot = jnp.where(
-        lane < width, lax.rem(lane + lead, width), lane - width - rows + lead
-    )
-    row_taps = jnp.dot(
-        rowk_ref[...], (spot == tap).astype(jnp.bfloat16), preferred_element_type=jnp.float32
-    ).astype(jnp.bfloat16)
-    for pair in range(tile_count // 2):
-        parts = []
-        for side in range(2):
-            mix = col_taps * coeffs[2 * pair + side : 2 * pair + side + 1]
-            high = mix.astype(jnp.bfloat16)
-            low = (mix - high.astype(jnp.float32)).astype(jnp.bfloat16)
-            place = row_taps[:, side * width : (side + 1) * width]
-            parts.append(
-                jnp.dot(high, place, preferred_element_type=jnp.float32)
-                + jnp.dot(low, place, preferred_element_type=jnp.float32)
-            )
-        kernels[pair] = parts[0] + parts[1]
-    extra[...] = jnp.zeros_like(extra)
+
+    line = iota((2 * VECTORS, taps), 0)
+    column = iota((2 * VECTORS, taps), 1)
+    block = lax.rem(line, VECTORS) // 2
+    step = 4 * lax.rem(block, COARSE) + 2 * lax.rem(line, 2) + line // VECTORS
+    wanted = jnp.where(block < COARSE, half + step, half - 1 - step)
+    wanted = jnp.where(lax.rem(line, VECTORS) < 4 * COARSE, wanted, -1)
+    col_taps = across((wanted == column).astype(jnp.bfloat16), colk_ref[...])
+    tap = iota((taps, width), 0)
+    lane = iota((taps, width), 1)
+    total = None
+    for side in range(2):
+        place = (lane == tap + LEAD + side * FINE_ROWS).astype(jnp.bfloat16)
+        row_taps = jnp.dot(
+            rowk_ref[...], place, preferred_element_type=jnp.float32
+        ).astype(jnp.bfloat16)
+        part = col_taps[side * VECTORS : (side + 1) * VECTORS]
+        mix = jnp.concatenate([part * coeffs[j : j + 1] for j in range(tile_count)], axis=0)
+        high = mix.astype(jnp.bfloat16)
+        low = (mix - high.astype(jnp.float32)).astype(jnp.bfloat16)
+        term = jnp.dot(high, row_taps, preferred_element_type=jnp.float32) + jnp.dot(
+            low, row_taps, preferred_element_type=jnp.float32
+        )
+        total = term if total is None else total + term
+    kernels[...] = total
 
     lane = iota((rows, width), 1)
-    near = jnp.abs(lax.rem(lane, rows) - iota((rows, width), 0)) <= half
-    edge = 2 * half // 8 * 8
     column = iota((1, width), 1)
-    empty = jnp.zeros((rows, width), jnp.bfloat16)
+
+    def moved(value, distance):
+        if distance == 0:
+            return value
+        turned = pltpu.roll(value, -distance % width, 1)
+        here = lane[: value.shape[0]] + distance
+        return jnp.where((here >= 0) & (here < width), turned, jnp.zeros_like(turned))
 
     def one_visit(visit, unused):
         fetch(visit).wait()
         sums[...] = jnp.zeros_like(sums)
         first = visit * per_visit
-        for pair in range(per_visit // 2):
-            for m in range(taps):
-                spread = jnp.broadcast_to(
-                    kernels[visit * (per_visit // 2) + pair, pl.ds(m, 1), :], (rows, width)
+        for place in range(per_visit):
+            tile = first + place
+            pixels = tiles_ref[tile].astype(jnp.float32)
+            for side in range(2):
+                for fine in range(4):
+                    part = moved(pixels, -1 - fine if side else fine).astype(jnp.bfloat16)
+                    top = fine * FINE_ROWS
+                    shifted[place, side, top + 16 : top + 64, :width] = part[:48]
+                    shifted[place, side, top : top + 48, width:] = part[16:]
+                for coarse in range(COARSE):
+                    for pair in range(2):
+                        vector = pl.ds(
+                            tile * VECTORS + (side * COARSE + coarse) * 2 + pair, 1
+                        )
+                        spread = jnp.broadcast_to(kernels[vector, :], (BLOCK, width))
+                        turned = pltpu.roll(spread, 0, 1, stride=1, stride_axis=0)
+                        toeplitz[
+                            place,
+                            side,
+                            coarse * BLOCK : (coarse + 1) * BLOCK,
+                            pair * width : (pair + 1) * width,
+                        ] = turned.astype(jnp.bfloat16)
+            matched = [jnp.zeros((BLOCK, width), jnp.float32) for _ in range(2)]
+            for side in range(2):
+                passed = jnp.dot(
+                    toeplitz[place, side],
+                    shifted[place, side],
+                    preferred_element_type=jnp.float32,
                 )
-                turned = pltpu.roll(spread, width - back, 1, stride=1, stride_axis=0)
-                turned = jnp.concatenate(
-                    [
-                        jnp.where(near[:edge], turned[:edge], 0.0),
-                        turned[edge : rows - edge],
-                        jnp.where(near[rows - edge :], turned[rows - edge :], 0.0),
-                    ],
-                    axis=0,
-                )
-                toeplitz[pair, m * rows : (m + 1) * rows, :] = turned.astype(jnp.bfloat16)
-            both = jnp.concatenate(
+                for part in range(2):
+                    for coarse in range(COARSE):
+                        matched[part] += moved(
+                            passed[
+                                coarse * BLOCK : (coarse + 1) * BLOCK,
+                                part * width : (part + 1) * width,
+                            ],
+                            -4 * coarse if side else 4 * coarse,
+                        )
+            offset = offset_ref[tile]
+            bucket = lax.rem(patch_ref[tile] - owner + REACH + patches, patches)
+            weight = weights[pl.ds(tile, 1), :]
+            turned = pltpu.roll(
+                jnp.concatenate(matched, axis=0) * weight, lax.rem(offset, width), 1
+            )
+            sums[bucket, :, :width] += jnp.where(lane >= offset, turned, 0.0)
+            sums[bucket, :, width:] += jnp.where(lane < offset, turned, 0.0)
+            extra[bucket, pl.ds(visit, 1), :] += jnp.concatenate(
                 [
-                    jnp.concatenate([tiles_ref[first + 2 * pair], empty], axis=1),
-                    jnp.concatenate([empty, tiles_ref[first + 2 * pair + 1]], axis=1),
+                    jnp.where(column >= offset, weight, 0.0),
+                    jnp.where(column < offset, weight, 0.0),
                 ],
-                axis=0,
+                axis=1,
             )
-            passed = jnp.dot(toeplitz[pair], both, preferred_element_type=jnp.float32)
-            for side in range(2):
-                matched = jnp.zeros((rows, width), jnp.float32)
-                for m in range(taps):
-                    block = passed[m * rows : (m + 1) * rows, side * width : (side + 1) * width]
-                    if m != half:
-                        turned = pltpu.roll(block, (half - m) % width, 1)
-                        inside = (lane + (m - half) >= 0) & (lane + (m - half) < width)
-                        block = jnp.where(inside, turned, 0.0)
-                    matched += block
-                tile = first + 2 * pair + side
-                offset = offset_ref[tile]
-                bucket = lax.rem(patch_ref[tile] - owner + REACH + patches, patches)
-                weight = weights[pl.ds(tile, 1), :]
-                turned = pltpu.roll(matched * weight, lax.rem(offset, width), 1)
-                sums[bucket, :, :width] += jnp.where(lane >= offset, turned, 0.0)
-                sums[bucket, :, width:] += jnp.where(lane < offset, turned, 0.0)
-                extra[bucket, pl.ds(visit, 1), :] += jnp.concatenate(
-                    [
-                        jnp.where(column >= offset, weight, 0.0),
-                        jnp.where(column < offset, weight, 0.0),
-                    ],
-                    axis=1,
-                )
 
         for bucket in range(SPREAD):
             extra[bucket, pl.ds(2 * visits + visit, 1), :] = jnp.full(
@@ -233,22 +280,28 @@
     smem = pl.BlockSpec(memory_space=pltpu.SMEM)
 
     vmem = pl.BlockSpec(memory_space=pltpu.VMEM)
-    deep = (taps + 7) // 8 * 8
+    anywhere = pl.BlockSpec(memory_space=pl.ANY)
     messages = pl.pallas_call(
         functools.partial(match_kernel, patches, groups),
-        in_specs=[smem] * 4 + [vmem] * 4 + [pl.BlockSpec(memory_space=pltpu.HBM)],
+        in_specs=[smem] * 4 + [anywhere] * 5,
         out_specs=[vmem] * (SPREAD * groups),
         out_shape=[jax.ShapeDtypeStruct((length, PW), jnp.bfloat16)] * (SPREAD * groups),
         scratch_shapes=[
+            pltpu.VMEM(coeff_table.shape[::-1], jnp.float32),
+            pltpu.VMEM((1, tile_count), jnp.bfloat16),
+            pltpu.VMEM((basis, taps), jnp.bfloat16),
+            pltpu.VMEM((basis, taps), jnp.bfloat16),
             pltpu.VMEM((tile_count, rows, width), jnp.bfloat16),
-            pltpu.VMEM((tile_count // 2, deep, width), jnp.float32),
+            pltpu.VMEM((tile_count * VECTORS, width), jnp.float32),
             pltpu.VMEM((tile_count, width), jnp.float32),
-            pltpu.VMEM((per_visit // 2, taps * rows, width), jnp.bfloat16),
+            pltpu.VMEM((per_visit, 2, 4 * FINE_ROWS, 2 * width), jnp.bfloat16),
+            pltpu.VMEM((per_visit, 2, COARSE * BLOCK, 2 * width), jnp.bfloat16),
             pltpu.VMEM((SPREAD, rows, PW), jnp.float32),
             pltpu.VMEM((SPREAD, EXTRA, PW), jnp.float32),
             pltpu.SemaphoreType.DMA((visits,)),
+            pltpu.SemaphoreType.DMA((4,)),
         ],
-        compiler_params=pltpu.CompilerParams(vmem_limit_bytes=40 * 1024 * 1024),
+        compiler_params=pltpu.CompilerParams(vmem_limit_bytes=62 * 1024 * 1024),
         name="match_and_sum",
     )(
         tile_patch,

time: 42.4 us -> 37.2 us (0.88)
  local copies, waits for them, and re-layouts: 3.81 us -> 0.89 us
  Pallas kernels: 15.7 us -> 13.1 us
  waiting for transfers between devices: 7.93 us -> 8.58 us
    unnamed x20 -> x4, local copies, waits for them, and re-layouts: 3.81 us -> 0.89 us
    pallas_call x1, Pallas kernels: 13.3 us -> 10.7 us  [local(): pl.pallas_call(functools.partial(match_kernel, patches, groups), in_specs...]
    ppermute x9, waiting for transfers between devices: 7.93 us -> 8.58 us  [local(): message = lax.ppermute(message, ('ra', 'band'), route)]
  transfers between devices with their start and end apart: 9 -> 9, of which waited for: 5 -> 4; matrix products, arithmetic and copies ran while one was open for 0% -> 0% of each run, Pallas kernels for 0% -> 0%
where the time goes in v3:
time: 37.2 us; the launch traced here: 36.9 us
  starting transfers between devices  13.7 us (37%)
  Pallas kernels  13.1 us (35%)
  waiting for transfers between devices  8.58 us (23%)
  local copies, waits for them, and re-layouts  0.89 us (2%)
  between operations  0.65 us (2%)
    ppermute x9, starting transfers between devices, local(): message = lax.ppermute(message, ('ra', 'band'), route)  13.7 us
    pallas_call x1, Pallas kernels, local(): pl.pallas_call(functools.partial(match_kernel, patches, groups), in_specs...  10.7 us
    ppermute x9, waiting for transfers between devices, local(): message = lax.ppermute(message, ('ra', 'band'), route)  8.58 us
    pallas_call x1, Pallas kernels, local(): pl.pallas_call(functools.partial(combine_kernel, visits), in_specs=[smem]...  2.43 us
    unnamed x4, local copies, waits for them, and re-layouts  0.89 us
  transfers between devices with their start and end apart: 9, of which 4 were waited for; matrix products, arithmetic and copies ran while one was open for 0% of the time, Pallas kernels for 0%

profile of v3, /device:TPU:0, one launch (start us, length us, event | category | flops | bytes accessed | tf_op | source)
XLA Modules:
  0.0 36.9 jit_solution(7653055553583556289)
XLA Ops:
  0.6 10.7 %match_and_sum.1 = (bf16[144,256]{1,0:T(8,128)(2,1)}, bf16[144,256]{1,0:T(8,128)(2,1)}, bf16[144,256]{1,0:T(8,128)(2,1)}, bf16[144,256]{1,0:T(8,128)(2,1)}, bf16...) custom-call(s32[32]{0:T(128)} %patch_ref.1, ...), custom_call_target="tpu_custom_call" | custom-call | tf_op jit(solution)/shard_map/match_and_sum/pallas_call | solution.py:284
  11.3 6.0 %collective-permute-start = (bf16[144,256]{1,0:T(8,128)(2,1)}, bf16[144,256]{1,0:T(8,128)(2,1)S(1)}, u32[]{:S(2)}, u32[]{:S(2)}) collective-permute-start(bf16[144,256]{1,0:T(8,128)(2,1)} %get-tuple-element.12), channel_id=1, source_target_pairs={{0,28},{1,29},{2,30},{3,31},{4,0},{5,1},{6,2},{7,3},{8,4},{9,5},{1... | collective-permute-start | bytes 221192 | tf_op jit(solution)/shard_map/ppermute | solution.py:329
  17.3 1.5 %collective-permute-start.1 = (bf16[144,256]{1,0:T(8,128)(2,1)}, bf16[144,256]{1,0:T(8,128)(2,1)S(1)}, u32[]{:S(2)}, u32[]{:S(2)}) collective-permute-start(bf16[144,256]{1,0:T(8,128)(2,1)} %get-tuple-element.13), channel_id=1, source_target_pairs={{0,29},{1,28},{2,31},{3,30},{4,1},{5,0},{6,3},{7,2},{8,5},{9,4},{1... | collective-permute-start | bytes 221192 | tf_op jit(solution)/shard_map/ppermute | solution.py:329
  18.8 0.3 collective-permute-start.2
  19.1 1.2 %collective-permute-start.3 = (bf16[144,256]{1,0:T(8,128)(2,1)}, bf16[144,256]{1,0:T(8,128)(2,1)S(1)}, u32[]{:S(2)}, u32[]{:S(2)}) collective-permute-start(bf16[144,256]{1,0:T(8,128)(2,1)} %get-tuple-element.15), channel_id=1, source_target_pairs={{0,31},{1,30},{2,1},{3,0},{4,3},{5,2},{6,5},{7,4},{8,7},{9,6},{10,... | collective-permute-start | bytes 221192 | tf_op jit(solution)/shard_map/ppermute | solution.py:329
  20.3 1.5 %collective-permute-start.4 = (bf16[144,256]{1,0:T(8,128)(2,1)}, bf16[144,256]{1,0:T(8,128)(2,1)S(1)}, u32[]{:S(2)}, u32[]{:S(2)}) collective-permute-start(bf16[144,256]{1,0:T(8,128)(2,1)} %get-tuple-element.17), channel_id=1, source_target_pairs={{0,1},{1,0},{2,3},{3,2},{4,5},{5,4},{6,7},{7,6},{8,9},{9,8},{10,11... | collective-permute-start | bytes 221192 | tf_op jit(solution)/shard_map/ppermute | solution.py:329
  21.8 0.0 collective-permute-done.refs_0_
  21.8 0.0 collective-permute-start.5
  21.8 1.1 %collective-permute-done.1.refs_1_ = bf16[144,256]{1,0:T(8,128)(2,1)S(1)} collective-permute-done((bf16[144,256]{1,0:T(8,128)(2,1)}, bf16[144,256]{1,0:T(8,128)(2,1)S(1)}, u32[]{:S(2)}, u32[]{:S(2)}) %collective-permute-start.1) | collective-permute-done | bytes 73760 | tf_op jit(solution)/shard_map/ppermute | solution.py:329
  22.9 0.0 collective-permute-start.6
  22.9 0.0 collective-permute-done.2.refs_2_
  22.9 2.2 %collective-permute-start.7 = (bf16[144,256]{1,0:T(8,128)(2,1)}, bf16[144,256]{1,0:T(8,128)(2,1)S(1)}, u32[]{:S(2)}, u32[]{:S(2)}) collective-permute-start(bf16[144,256]{1,0:T(8,128)(2,1)} %get-tuple-element.20), channel_id=1, source_target_pairs={{0,4},{1,5},{2,6},{3,7},{4,8},{5,9},{6,10},{7,11},{8,12},{9,13},{1... | collective-permute-start | bytes 221192 | tf_op jit(solution)/shard_map/ppermute | solution.py:329
  25.1 0.0 collective-permute-done.3.refs_3_
  25.1 0.0 copy-start.1
  25.1 1.0 %collective-permute-start.8 = (bf16[144,256]{1,0:T(8,128)(2,1)}, bf16[144,256]{1,0:T(8,128)(2,1)S(1)}, u32[]{:S(2)}, u32[]{:S(2)}) collective-permute-start(bf16[144,256]{1,0:T(8,128)(2,1)} %get-tuple-element.21), channel_id=1, source_target_pairs={{0,5},{1,4},{2,7},{3,6},{4,9},{5,8},{6,11},{7,10},{8,13},{9,12},{1... | collective-permute-start | bytes 221192 | tf_op jit(solution)/shard_map/ppermute | solution.py:329
  26.1 0.0 collective-permute-done.4.refs_5_
  26.1 2.4 %collective-permute-done.5.refs_6_ = bf16[144,256]{1,0:T(8,128)(2,1)S(1)} collective-permute-done((bf16[144,256]{1,0:T(8,128)(2,1)}, bf16[144,256]{1,0:T(8,128)(2,1)S(1)}, u32[]{:S(2)}, u32[]{:S(2)}) %collective-permute-start.5) | collective-permute-done | bytes 73760 | tf_op jit(solution)/shard_map/ppermute | solution.py:329
  28.5 2.1 %collective-permute-done.6.refs_7_ = bf16[144,256]{1,0:T(8,128)(2,1)S(1)} collective-permute-done((bf16[144,256]{1,0:T(8,128)(2,1)}, bf16[144,256]{1,0:T(8,128)(2,1)S(1)}, u32[]{:S(2)}, u32[]{:S(2)}) %collective-permute-start.6) | collective-permute-done | bytes 73760 | tf_op jit(solution)/shard_map/ppermute | solution.py:329
  30.6 0.0 collective-permute-done.7.refs_8_
  30.6 3.0 %collective-permute-done.8.refs_9_ = bf16[144,256]{1,0:T(8,128)(2,1)S(1)} collective-permute-done((bf16[144,256]{1,0:T(8,128)(2,1)}, bf16[144,256]{1,0:T(8,128)(2,1)S(1)}, u32[]{:S(2)}, u32[]{:S(2)}) %collective-permute-start.8) | collective-permute-done | bytes 73760 | tf_op jit(solution)/shard_map/ppermute | solution.py:329
  33.6 0.0 copy-done.1
  33.6 0.0 copy-start
  33.6 0.9 %copy-done = bf16[144,256]{1,0:T(8,128)(2,1)S(1)} copy-done((bf16[144,256]{1,0:T(8,128)(2,1)S(1)}, bf16[144,256]{1,0:T(8,128)(2,1)}, u32[]{:S(2)}) %copy-start) | copy-done | bytes 73752
  34.5 2.4 %combine.1 = (f32[6,32,256]{2,1,0:T(8,128)}, f32[32,256]{1,0:T(8,128)}) custom-call(f32[6]{0:T(128)S(1)} %copy-done.1, bf16[144,256]{1,0:T(8,128)(2,1)S(1)} %collective-permute-done.refs_0_, bf16[144,256]{1,0:T(8,128)(2,1)S(1)} %collective-permute-done.1.refs_1_, bf16[144,256]{1,0:T(8,128)(2,1)S(1)} %collective-permute-done.2.refs_2_, ...), custom_call_target="tpu_custom_call" | custom-call | tf_op jit(solution)/shard_map/combine/pallas_call | solution.py:332
Async XLA Ops:
  11.3 10.5 %collective-permute-start = (bf16[144,256]{1,0:T(8,128)(2,1)}, bf16[144,256]{1,0:T(8,128)(2,1)S(1)}, u32[]{:S(2)}, u32[]{:S(2)}) collective-permute-start(bf16[144,256]{1,0:T(8,128)(2,1)} %get-tuple-element.12), channel_id=1, source_target_pairs={{0,28},{1,29},{2,30},{3,31},{4,0},{5,1},{6,2},{7,3},{8,4},{9,5},{1... | collective-permute-start | bytes 221192 | tf_op jit(solution)/shard_map/ppermute | solution.py:329
  17.3 5.5 %collective-permute-start.1 = (bf16[144,256]{1,0:T(8,128)(2,1)}, bf16[144,256]{1,0:T(8,128)(2,1)S(1)}, u32[]{:S(2)}, u32[]{:S(2)}) collective-permute-start(bf16[144,256]{1,0:T(8,128)(2,1)} %get-tuple-element.13), channel_id=1, source_target_pairs={{0,29},{1,28},{2,31},{3,30},{4,1},{5,0},{6,3},{7,2},{8,5},{9,4},{1... | collective-permute-start | bytes 221192 | tf_op jit(solution)/shard_map/ppermute | solution.py:329
  18.8 4.0 %collective-permute-start.2 = (bf16[144,256]{1,0:T(8,128)(2,1)}, bf16[144,256]{1,0:T(8,128)(2,1)S(1)}, u32[]{:S(2)}, u32[]{:S(2)}) collective-permute-start(bf16[144,256]{1,0:T(8,128)(2,1)} %get-tuple-element.14), channel_id=1, source_target_pairs={{0,30},{1,31},{2,0},{3,1},{4,2},{5,3},{6,4},{7,5},{8,6},{9,7},{10,... | collective-permute-start | bytes 221192 | tf_op jit(solution)/shard_map/ppermute | solution.py:329
  19.1 6.0 %collective-permute-start.3 = (bf16[144,256]{1,0:T(8,128)(2,1)}, bf16[144,256]{1,0:T(8,128)(2,1)S(1)}, u32[]{:S(2)}, u32[]{:S(2)}) collective-permute-start(bf16[144,256]{1,0:T(8,128)(2,1)} %get-tuple-element.15), channel_id=1, source_target_pairs={{0,31},{1,30},{2,1},{3,0},{4,3},{5,2},{6,5},{7,4},{8,7},{9,6},{10,... | collective-permute-start | bytes 221192 | tf_op jit(solution)/shard_map/ppermute | solution.py:329
  20.3 5.8 %collective-permute-start.4 = (bf16[144,256]{1,0:T(8,128)(2,1)}, bf16[144,256]{1,0:T(8,128)(2,1)S(1)}, u32[]{:S(2)}, u32[]{:S(2)}) collective-permute-start(bf16[144,256]{1,0:T(8,128)(2,1)} %get-tuple-element.17), channel_id=1, source_target_pairs={{0,1},{1,0},{2,3},{3,2},{4,5},{5,4},{6,7},{7,6},{8,9},{9,8},{10,11... | collective-permute-start | bytes 221192 | tf_op jit(solution)/shard_map/ppermute | solution.py:329
  21.8 6.7 %collective-permute-start.5 = (bf16[144,256]{1,0:T(8,128)(2,1)}, bf16[144,256]{1,0:T(8,128)(2,1)S(1)}, u32[]{:S(2)}, u32[]{:S(2)}) collective-permute-start(bf16[144,256]{1,0:T(8,128)(2,1)} %get-tuple-element.18), channel_id=1, source_target_pairs={{0,2},{1,3},{2,4},{3,5},{4,6},{5,7},{6,8},{7,9},{8,10},{9,11},{10,... | collective-permute-start | bytes 221192 | tf_op jit(solution)/shard_map/ppermute | solution.py:329
  22.9 7.7 %collective-permute-start.6 = (bf16[144,256]{1,0:T(8,128)(2,1)}, bf16[144,256]{1,0:T(8,128)(2,1)S(1)}, u32[]{:S(2)}, u32[]{:S(2)}) collective-permute-start(bf16[144,256]{1,0:T(8,128)(2,1)} %get-tuple-element.19), channel_id=1, source_target_pairs={{0,3},{1,2},{2,5},{3,4},{4,7},{5,6},{6,9},{7,8},{8,11},{9,10},{10,... | collective-permute-start | bytes 221192 | tf_op jit(solution)/shard_map/ppermute | solution.py:329
  22.9 7.7 %collective-permute-start.7 = (bf16[144,256]{1,0:T(8,128)(2,1)}, bf16[144,256]{1,0:T(8,128)(2,1)S(1)}, u32[]{:S(2)}, u32[]{:S(2)}) collective-permute-start(bf16[144,256]{1,0:T(8,128)(2,1)} %get-tuple-element.20), channel_id=1, source_target_pairs={{0,4},{1,5},{2,6},{3,7},{4,8},{5,9},{6,10},{7,11},{8,12},{9,13},{1... | collective-permute-start | bytes 221192 | tf_op jit(solution)/shard_map/ppermute | solution.py:329
  25.1 8.5 %copy-start.1 = (f32[6]{0:T(128)S(1)}, f32[6]{0:T(128)}, u32[]{:S(2)}) copy-start(f32[6]{0:T(128)} %weight_ref.1) | copy-start | bytes 76
  25.1 8.5 %collective-permute-start.8 = (bf16[144,256]{1,0:T(8,128)(2,1)}, bf16[144,256]{1,0:T(8,128)(2,1)S(1)}, u32[]{:S(2)}, u32[]{:S(2)}) collective-permute-start(bf16[144,256]{1,0:T(8,128)(2,1)} %get-tuple-element.21), channel_id=1, source_target_pairs={{0,5},{1,4},{2,7},{3,6},{4,9},{5,8},{6,11},{7,10},{8,13},{9,12},{1... | collective-permute-start | bytes 221192 | tf_op jit(solution)/shard_map/ppermute | solution.py:329
  33.6 0.9 %copy-start = (bf16[144,256]{1,0:T(8,128)(2,1)S(1)}, bf16[144,256]{1,0:T(8,128)(2,1)}, u32[]{:S(2)}) copy-start(bf16[144,256]{1,0:T(8,128)(2,1)} %get-tuple-element.16.refs_4_) | copy-start | bytes 221188

commit v4 on v3

--- a/solution.py
+++ b/solution.py
@@ -48,6 +48,7 @@
         weights,
         shifted,
         toeplitz,
+        matches,
         sums,
         extra,
         arrival,
@@ -151,10 +152,10 @@
         first = visit * per_visit
         for place in range(per_visit):
             tile = first + place
-            pixels = tiles_ref[tile].astype(jnp.float32)
+            pixels = tiles_ref[tile]
             for side in range(2):
                 for fine in range(4):
-                    part = moved(pixels, -1 - fine if side else fine).astype(jnp.bfloat16)
+                    part = moved(pixels, -1 - fine if side else fine)
                     top = fine * FINE_ROWS
                     shifted[place, side, top + 16 : top + 64, :width] = part[:48]
                     shifted[place, side, top : top + 48, width:] = part[16:]
@@ -171,6 +172,7 @@
                             coarse * BLOCK : (coarse + 1) * BLOCK,
                             pair * width : (pair + 1) * width,
                         ] = turned.astype(jnp.bfloat16)
+        for place in range(per_visit):
             matched = [jnp.zeros((BLOCK, width), jnp.float32) for _ in range(2)]
             for side in range(2):
                 passed = jnp.dot(
@@ -187,11 +189,14 @@
                             ],
                             -4 * coarse if side else 4 * coarse,
                         )
+            matches[place] = jnp.concatenate(matched, axis=0)
+        for place in range(per_visit):
+            tile = first + place
             offset = offset_ref[tile]
             bucket = lax.rem(patch_ref[tile] - owner + REACH + patches, patches)
             weight = weights[pl.ds(tile, 1), :]
             turned = pltpu.roll(
-                jnp.concatenate(matched, axis=0) * weight, lax.rem(offset, width), 1
+                matches[place] * weight, lax.rem(offset, width), 1
             )
             sums[bucket, :, :width] += jnp.where(lane >= offset, turned, 0.0)
             sums[bucket, :, width:] += jnp.where(lane < offset, turned, 0.0)
@@ -296,6 +301,7 @@
             pltpu.VMEM((tile_count, width), jnp.float32),
             pltpu.VMEM((per_visit, 2, 4 * FINE_ROWS, 2 * width), jnp.bfloat16),
             pltpu.VMEM((per_visit, 2, COARSE * BLOCK, 2 * width), jnp.bfloat16),
+            pltpu.VMEM((per_visit, rows, width), jnp.float32),
             pltpu.VMEM((SPREAD, rows, PW), jnp.float32),
             pltpu.VMEM((SPREAD, EXTRA, PW), jnp.float32),
             pltpu.SemaphoreType.DMA((visits,)),

time: 37.2 us -> 33.5 us (0.901)
  Pallas kernels: 13.1 us -> 9.44 us
    pallas_call x1, Pallas kernels: 10.7 us -> 7 us  [local(): pl.pallas_call(functools.partial(match_kernel, patches, groups), in_specs...]
where the time goes in v4:
time: 33.5 us; the launch traced here: 33.3 us
  starting transfers between devices  13.7 us (41%)
  Pallas kernels  9.44 us (28%)
  waiting for transfers between devices  8.57 us (26%)
  local copies, waits for them, and re-layouts  0.89 us (3%)
  between operations  0.65 us (2%)
    ppermute x9, starting transfers between devices, local(): message = lax.ppermute(message, ('ra', 'band'), route)  13.7 us
    ppermute x9, waiting for transfers between devices, local(): message = lax.ppermute(message, ('ra', 'band'), route)  8.57 us
    pallas_call x1, Pallas kernels, local(): pl.pallas_call(functools.partial(match_kernel, patches, groups), in_specs...  7 us
    pallas_call x1, Pallas kernels, local(): pl.pallas_call(functools.partial(combine_kernel, visits), in_specs=[smem]...  2.43 us
    unnamed x4, local copies, waits for them, and re-layouts  0.89 us
  transfers between devices with their start and end apart: 9, of which 4 were waited for; matrix products, arithmetic and copies ran while one was open for 0% of the time, Pallas kernels for 0%

profile of v4, /device:TPU:0, one launch (start us, length us, event | category | flops | bytes accessed | tf_op | source)
XLA Modules:
  0.0 33.3 jit_solution(16254589982404722328)
XLA Ops:
  0.6 7.0 %match_and_sum.1 = (bf16[144,256]{1,0:T(8,128)(2,1)}, bf16[144,256]{1,0:T(8,128)(2,1)}, bf16[144,256]{1,0:T(8,128)(2,1)}, bf16[144,256]{1,0:T(8,128)(2,1)}, bf16...) custom-call(s32[32]{0:T(128)} %patch_ref.1, ...), custom_call_target="tpu_custom_call" | custom-call | tf_op jit(solution)/shard_map/match_and_sum/pallas_call | solution.py:289
  7.6 6.0 %collective-permute-start = (bf16[144,256]{1,0:T(8,128)(2,1)}, bf16[144,256]{1,0:T(8,128)(2,1)S(1)}, u32[]{:S(2)}, u32[]{:S(2)}) collective-permute-start(bf16[144,256]{1,0:T(8,128)(2,1)} %get-tuple-element.12), channel_id=1, source_target_pairs={{0,28},{1,29},{2,30},{3,31},{4,0},{5,1},{6,2},{7,3},{8,4},{9,5},{1... | collective-permute-start | bytes 221192 | tf_op jit(solution)/shard_map/ppermute | solution.py:335
  13.7 1.5 %collective-permute-start.1 = (bf16[144,256]{1,0:T(8,128)(2,1)}, bf16[144,256]{1,0:T(8,128)(2,1)S(1)}, u32[]{:S(2)}, u32[]{:S(2)}) collective-permute-start(bf16[144,256]{1,0:T(8,128)(2,1)} %get-tuple-element.13), channel_id=1, source_target_pairs={{0,29},{1,28},{2,31},{3,30},{4,1},{5,0},{6,3},{7,2},{8,5},{9,4},{1... | collective-permute-start | bytes 221192 | tf_op jit(solution)/shard_map/ppermute | solution.py:335
  15.2 0.3 collective-permute-start.2
  15.4 1.2 %collective-permute-start.3 = (bf16[144,256]{1,0:T(8,128)(2,1)}, bf16[144,256]{1,0:T(8,128)(2,1)S(1)}, u32[]{:S(2)}, u32[]{:S(2)}) collective-permute-start(bf16[144,256]{1,0:T(8,128)(2,1)} %get-tuple-element.15), channel_id=1, source_target_pairs={{0,31},{1,30},{2,1},{3,0},{4,3},{5,2},{6,5},{7,4},{8,7},{9,6},{10,... | collective-permute-start | bytes 221192 | tf_op jit(solution)/shard_map/ppermute | solution.py:335
  16.6 1.5 %collective-permute-start.4 = (bf16[144,256]{1,0:T(8,128)(2,1)}, bf16[144,256]{1,0:T(8,128)(2,1)S(1)}, u32[]{:S(2)}, u32[]{:S(2)}) collective-permute-start(bf16[144,256]{1,0:T(8,128)(2,1)} %get-tuple-element.17), channel_id=1, source_target_pairs={{0,1},{1,0},{2,3},{3,2},{4,5},{5,4},{6,7},{7,6},{8,9},{9,8},{10,11... | collective-permute-start | bytes 221192 | tf_op jit(solution)/shard_map/ppermute | solution.py:335
  18.1 0.0 collective-permute-done.refs_0_
  18.1 0.0 collective-permute-start.5
  18.1 1.1 %collective-permute-done.1.refs_1_ = bf16[144,256]{1,0:T(8,128)(2,1)S(1)} collective-permute-done((bf16[144,256]{1,0:T(8,128)(2,1)}, bf16[144,256]{1,0:T(8,128)(2,1)S(1)}, u32[]{:S(2)}, u32[]{:S(2)}) %collective-permute-start.1) | collective-permute-done | bytes 73760 | tf_op jit(solution)/shard_map/ppermute | solution.py:335
  19.2 0.0 collective-permute-start.6
  19.2 0.0 collective-permute-done.2.refs_2_
  19.2 2.2 %collective-permute-start.7 = (bf16[144,256]{1,0:T(8,128)(2,1)}, bf16[144,256]{1,0:T(8,128)(2,1)S(1)}, u32[]{:S(2)}, u32[]{:S(2)}) collective-permute-start(bf16[144,256]{1,0:T(8,128)(2,1)} %get-tuple-element.20), channel_id=1, source_target_pairs={{0,4},{1,5},{2,6},{3,7},{4,8},{5,9},{6,10},{7,11},{8,12},{9,13},{1... | collective-permute-start | bytes 221192 | tf_op jit(solution)/shard_map/ppermute | solution.py:335
  21.4 0.0 collective-permute-done.3.refs_3_
  21.4 0.0 copy-start.1
  21.4 1.0 %collective-permute-start.8 = (bf16[144,256]{1,0:T(8,128)(2,1)}, bf16[144,256]{1,0:T(8,128)(2,1)S(1)}, u32[]{:S(2)}, u32[]{:S(2)}) collective-permute-start(bf16[144,256]{1,0:T(8,128)(2,1)} %get-tuple-element.21), channel_id=1, source_target_pairs={{0,5},{1,4},{2,7},{3,6},{4,9},{5,8},{6,11},{7,10},{8,13},{9,12},{1... | collective-permute-start | bytes 221192 | tf_op jit(solution)/shard_map/ppermute | solution.py:335
  22.4 0.0 collective-permute-done.4.refs_5_
  22.4 2.4 %collective-permute-done.5.refs_6_ = bf16[144,256]{1,0:T(8,128)(2,1)S(1)} collective-permute-done((bf16[144,256]{1,0:T(8,128)(2,1)}, bf16[144,256]{1,0:T(8,128)(2,1)S(1)}, u32[]{:S(2)}, u32[]{:S(2)}) %collective-permute-start.5) | collective-permute-done | bytes 73760 | tf_op jit(solution)/shard_map/ppermute | solution.py:335
  24.8 2.1 %collective-permute-done.6.refs_7_ = bf16[144,256]{1,0:T(8,128)(2,1)S(1)} collective-permute-done((bf16[144,256]{1,0:T(8,128)(2,1)}, bf16[144,256]{1,0:T(8,128)(2,1)S(1)}, u32[]{:S(2)}, u32[]{:S(2)}) %collective-permute-start.6) | collective-permute-done | bytes 73760 | tf_op jit(solution)/shard_map/ppermute | solution.py:335
  26.9 0.0 collective-permute-done.7.refs_8_
  26.9 3.0 %collective-permute-done.8.refs_9_ = bf16[144,256]{1,0:T(8,128)(2,1)S(1)} collective-permute-done((bf16[144,256]{1,0:T(8,128)(2,1)}, bf16[144,256]{1,0:T(8,128)(2,1)S(1)}, u32[]{:S(2)}, u32[]{:S(2)}) %collective-permute-start.8) | collective-permute-done | bytes 73760 | tf_op jit(solution)/shard_map/ppermute | solution.py:335
  29.9 0.0 copy-done.1
  29.9 0.0 copy-start
  29.9 0.9 %copy-done = bf16[144,256]{1,0:T(8,128)(2,1)S(1)} copy-done((bf16[144,256]{1,0:T(8,128)(2,1)S(1)}, bf16[144,256]{1,0:T(8,128)(2,1)}, u32[]{:S(2)}) %copy-start) | copy-done | bytes 73752
  30.8 2.4 %combine.1 = (f32[6,32,256]{2,1,0:T(8,128)}, f32[32,256]{1,0:T(8,128)}) custom-call(f32[6]{0:T(128)S(1)} %copy-done.1, bf16[144,256]{1,0:T(8,128)(2,1)S(1)} %collective-permute-done.refs_0_, bf16[144,256]{1,0:T(8,128)(2,1)S(1)} %collective-permute-done.1.refs_1_, bf16[144,256]{1,0:T(8,128)(2,1)S(1)} %collective-permute-done.2.refs_2_, ...), custom_call_target="tpu_custom_call" | custom-call | tf_op jit(solution)/shard_map/combine/pallas_call | solution.py:338
Async XLA Ops:
  7.6 10.5 %collective-permute-start = (bf16[144,256]{1,0:T(8,128)(2,1)}, bf16[144,256]{1,0:T(8,128)(2,1)S(1)}, u32[]{:S(2)}, u32[]{:S(2)}) collective-permute-start(bf16[144,256]{1,0:T(8,128)(2,1)} %get-tuple-element.12), channel_id=1, source_target_pairs={{0,28},{1,29},{2,30},{3,31},{4,0},{5,1},{6,2},{7,3},{8,4},{9,5},{1... | collective-permute-start | bytes 221192 | tf_op jit(solution)/shard_map/ppermute | solution.py:335
  13.7 5.5 %collective-permute-start.1 = (bf16[144,256]{1,0:T(8,128)(2,1)}, bf16[144,256]{1,0:T(8,128)(2,1)S(1)}, u32[]{:S(2)}, u32[]{:S(2)}) collective-permute-start(bf16[144,256]{1,0:T(8,128)(2,1)} %get-tuple-element.13), channel_id=1, source_target_pairs={{0,29},{1,28},{2,31},{3,30},{4,1},{5,0},{6,3},{7,2},{8,5},{9,4},{1... | collective-permute-start | bytes 221192 | tf_op jit(solution)/shard_map/ppermute | solution.py:335
  15.2 4.0 %collective-permute-start.2 = (bf16[144,256]{1,0:T(8,128)(2,1)}, bf16[144,256]{1,0:T(8,128)(2,1)S(1)}, u32[]{:S(2)}, u32[]{:S(2)}) collective-permute-start(bf16[144,256]{1,0:T(8,128)(2,1)} %get-tuple-element.14), channel_id=1, source_target_pairs={{0,30},{1,31},{2,0},{3,1},{4,2},{5,3},{6,4},{7,5},{8,6},{9,7},{10,... | collective-permute-start | bytes 221192 | tf_op jit(solution)/shard_map/ppermute | solution.py:335
  15.4 6.0 %collective-permute-start.3 = (bf16[144,256]{1,0:T(8,128)(2,1)}, bf16[144,256]{1,0:T(8,128)(2,1)S(1)}, u32[]{:S(2)}, u32[]{:S(2)}) collective-permute-start(bf16[144,256]{1,0:T(8,128)(2,1)} %get-tuple-element.15), channel_id=1, source_target_pairs={{0,31},{1,30},{2,1},{3,0},{4,3},{5,2},{6,5},{7,4},{8,7},{9,6},{10,... | collective-permute-start | bytes 221192 | tf_op jit(solution)/shard_map/ppermute | solution.py:335
  16.6 5.8 %collective-permute-start.4 = (bf16[144,256]{1,0:T(8,128)(2,1)}, bf16[144,256]{1,0:T(8,128)(2,1)S(1)}, u32[]{:S(2)}, u32[]{:S(2)}) collective-permute-start(bf16[144,256]{1,0:T(8,128)(2,1)} %get-tuple-element.17), channel_id=1, source_target_pairs={{0,1},{1,0},{2,3},{3,2},{4,5},{5,4},{6,7},{7,6},{8,9},{9,8},{10,11... | collective-permute-start | bytes 221192 | tf_op jit(solution)/shard_map/ppermute | solution.py:335
  18.1 6.7 %collective-permute-start.5 = (bf16[144,256]{1,0:T(8,128)(2,1)}, bf16[144,256]{1,0:T(8,128)(2,1)S(1)}, u32[]{:S(2)}, u32[]{:S(2)}) collective-permute-start(bf16[144,256]{1,0:T(8,128)(2,1)} %get-tuple-element.18), channel_id=1, source_target_pairs={{0,2},{1,3},{2,4},{3,5},{4,6},{5,7},{6,8},{7,9},{8,10},{9,11},{10,... | collective-permute-start | bytes 221192 | tf_op jit(solution)/shard_map/ppermute | solution.py:335
  19.2 7.7 %collective-permute-start.6 = (bf16[144,256]{1,0:T(8,128)(2,1)}, bf16[144,256]{1,0:T(8,128)(2,1)S(1)}, u32[]{:S(2)}, u32[]{:S(2)}) collective-permute-start(bf16[144,256]{1,0:T(8,128)(2,1)} %get-tuple-element.19), channel_id=1, source_target_pairs={{0,3},{1,2},{2,5},{3,4},{4,7},{5,6},{6,9},{7,8},{8,11},{9,10},{10,... | collective-permute-start | bytes 221192 | tf_op jit(solution)/shard_map/ppermute | solution.py:335
  19.2 7.7 %collective-permute-start.7 = (bf16[144,256]{1,0:T(8,128)(2,1)}, bf16[144,256]{1,0:T(8,128)(2,1)S(1)}, u32[]{:S(2)}, u32[]{:S(2)}) collective-permute-start(bf16[144,256]{1,0:T(8,128)(2,1)} %get-tuple-element.20), channel_id=1, source_target_pairs={{0,4},{1,5},{2,6},{3,7},{4,8},{5,9},{6,10},{7,11},{8,12},{9,13},{1... | collective-permute-start | bytes 221192 | tf_op jit(solution)/shard_map/ppermute | solution.py:335
  21.4 8.5 %copy-start.1 = (f32[6]{0:T(128)S(1)}, f32[6]{0:T(128)}, u32[]{:S(2)}) copy-start(f32[6]{0:T(128)} %weight_ref.1) | copy-start | bytes 76
  21.4 8.5 %collective-permute-start.8 = (bf16[144,256]{1,0:T(8,128)(2,1)}, bf16[144,256]{1,0:T(8,128)(2,1)S(1)}, u32[]{:S(2)}, u32[]{:S(2)}) collective-permute-start(bf16[144,256]{1,0:T(8,128)(2,1)} %get-tuple-element.21), channel_id=1, source_target_pairs={{0,5},{1,4},{2,7},{3,6},{4,9},{5,8},{6,11},{7,10},{8,13},{9,12},{1... | collective-permute-start | bytes 221192 | tf_op jit(solution)/shard_map/ppermute | solution.py:335
  29.9 0.9 %copy-start = (bf16[144,256]{1,0:T(8,128)(2,1)S(1)}, bf16[144,256]{1,0:T(8,128)(2,1)}, u32[]{:S(2)}) copy-start(bf16[144,256]{1,0:T(8,128)(2,1)} %get-tuple-element.16.refs_4_) | copy-start | bytes 221188

commit v5 on v4

--- a/solution.py
+++ b/solution.py
@@ -209,9 +209,6 @@
             )
 
         for bucket in range(SPREAD):
-            extra[bucket, pl.ds(2 * visits + visit, 1), :] = jnp.full(
-                (1, PW), band_ref[visit], jnp.int32
-            ).astype(jnp.float32)
             for turn in range(groups):
                 part = lax.rem(group + turn, groups)
                 own = sums[bucket, pl.ds(pl.multiple_of(part * row_share, row_share), row_share), :]
@@ -227,35 +224,55 @@
     lax.fori_loop(0, visits, one_visit, 0)
 
     row = iota((EXTRA, PW), 0)
+    lane = iota((1, PW), 1)
+    by_row = jnp.zeros((1, PW), jnp.float32)
+    by_weight = jnp.full((1, PW), -1.0, jnp.float32)
+    for visit in range(visits):
+        band = band_ref[visit].astype(jnp.float32)
+        by_row = jnp.where(lane // slot == visit, band, by_row)
+        by_weight = jnp.where(
+            (lane < 2 * visits) & (lax.rem(lane, visits) == visit), band, by_weight
+        )
     for bucket in range(SPREAD):
         held = extra[bucket]
         high = held.astype(jnp.bfloat16).astype(jnp.float32)
         low = jnp.concatenate([held[-visits:], (held - high)[:-visits]], axis=0)
-        mixed = jnp.where((row >= visits) & (row < 2 * visits), low, high).astype(jnp.bfloat16)
+        mixed = jnp.where((row >= visits) & (row < 2 * visits), low, high)
+        mixed = jnp.where(row == 2 * visits, by_row, mixed)
+        mixed = jnp.where(row == 2 * visits + 1, by_weight, mixed).astype(jnp.bfloat16)
         for turn in range(groups):
             messages[bucket * groups + turn][slot * visits :, :] = mixed
 
 
-def combine_kernel(count, weight_ref, *refs):
-    messages = refs[:-2]
-    coadd_ref, detection_ref = refs[-2:]
+def combine_kernel(count, weight_ref, own_hbm, *refs):
+    coadd_ref, detection_ref, own_ref, arrival = refs[-4:]
     row_share = coadd_ref.shape[1]
     slot = slot_rows(row_share)
-    totals = [jnp.zeros((row_share, PW), jnp.float32) for _ in range(BANDS)]
-    weight_totals = [jnp.zeros((1, PW), jnp.float32) for _ in range(BANDS)]
-    for message in messages:
-        extra = message[slot * count :, :].astype(jnp.float32)
-        for visit in range(count):
-            band = extra[2 * count + visit : 2 * count + visit + 1]
-            weight = extra[visit : visit + 1] + extra[count + visit : count + visit + 1]
-            part = message[slot * visit : slot * (visit + 1), :].astype(jnp.float32)[:row_share]
-            for b in range(BANDS):
-                here = band == float(b)
-                totals[b] += jnp.where(here, part, 0.0)
-                weight_totals[b] += jnp.where(here, weight, 0.0)
+    depth = slot * count
+    fetch = pltpu.make_async_copy(own_hbm, own_ref, arrival)
+    fetch.start()
+    line = lax.broadcasted_iota(jnp.int32, (row_share, depth), 0)
+    lane = lax.broadcasted_iota(jnp.int32, (row_share, depth), 1)
+    same = (lax.rem(lane, slot) == line).astype(jnp.float32)
+    band_line = lax.broadcasted_iota(jnp.int32, (8, EXTRA), 0).astype(jnp.float32)
+    totals = jnp.zeros((BANDS * row_share, PW), jnp.float32)
+    weight_totals = jnp.zeros((8, PW), jnp.float32)
+    for message in refs[:-4] + (own_ref,):
+        if message is own_ref:
+            fetch.wait()
+        extra = message[depth:, :]
+        bands = extra[2 * count : 2 * count + 2].astype(jnp.float32)
+        pick = jnp.concatenate(
+            [jnp.where(bands[:1, :depth] == float(b), same, 0.0) for b in range(BANDS)], axis=0
+        ).astype(jnp.bfloat16)
+        totals += jnp.dot(pick, message[:depth, :], preferred_element_type=jnp.float32)
+        pick = (bands[1:, :EXTRA] == band_line).astype(jnp.bfloat16)
+        weight_totals += jnp.dot(pick, extra, preferred_element_type=jnp.float32)
     detection = jnp.zeros((row_share, PW), jnp.float32)
     for b in range(BANDS):
-        coadd = totals[b] / jnp.maximum(weight_totals[b], 1.0)
+        coadd = totals[b * row_share : (b + 1) * row_share] / jnp.maximum(
+            weight_totals[b : b + 1], 1.0
+        )
         coadd_ref[b] = coadd
         detection += weight_ref[b] * coadd
     detection_ref[...] = detection
@@ -322,27 +339,29 @@
     )
 
     arrived = []
-    for bucket in range(SPREAD):
-        for turn in range(groups):
-            message = messages[bucket * groups + turn]
-            distance = bucket - REACH
-            if distance != 0 or turn != 0:
-                route = [
-                    (o * groups + g, (o + distance) % patches * groups + (g + turn) % groups)
-                    for o in range(patches)
-                    for g in range(groups)
-                ]
-                message = lax.ppermute(message, ("ra", "band"), route)
-            arrived.append(message)
+    for distance, turn in sorted(
+        ((d, t) for d in range(-REACH, REACH + 1) for t in range(groups)),
+        key=lambda way: (abs(way[0]), way[1], way[0]),
+    ):
+        message = messages[(distance + REACH) * groups + turn]
+        if distance != 0 or turn != 0:
+            route = [
+                (o * groups + g, (o + distance) % patches * groups + (g + turn) % groups)
+                for o in range(patches)
+                for g in range(groups)
+            ]
+            message = lax.ppermute(message, ("ra", "band"), route)
+        arrived.append(message)
 
     return pl.pallas_call(
         functools.partial(combine_kernel, visits),
-        in_specs=[smem] + [vmem] * len(arrived),
+        in_specs=[smem, anywhere] + [vmem] * (len(arrived) - 1),
         out_specs=(vmem, vmem),
         out_shape=(
             jax.ShapeDtypeStruct((BANDS, row_share, PW), jnp.float32),
             jax.ShapeDtypeStruct((row_share, PW), jnp.float32),
         ),
+        scratch_shapes=[pltpu.VMEM((length, PW), jnp.bfloat16), pltpu.SemaphoreType.DMA],
         compiler_params=pltpu.CompilerParams(vmem_limit_bytes=40 * 1024 * 1024),
         name="combine",
     )(band_weight, *arrived)

time: 33.5 us -> 38 us (1.13)
  the two profiles are of different devices: /device:TPU:0 before, /device:TPU:1 now
where the time goes in v5:
time: 38 us; the launch traced here: 37.7 us
  starting transfers between devices  20.3 us (53%)
  Pallas kernels  8.9 us (23%)
  waiting for transfers between devices  7 us (18%)
  local copies, waits for them, and re-layouts  0.89 us (2%)
  between operations  0.67 us (2%)
    ppermute x9, starting transfers between devices, local(): message = lax.ppermute(message, ('ra', 'band'), route)  20.3 us
    ppermute x9, waiting for transfers between devices, local(): message = lax.ppermute(message, ('ra', 'band'), route)  7 us
    pallas_call x1, Pallas kernels, local(): pl.pallas_call(functools.partial(match_kernel, patches, groups), in_specs...  7 us
    pallas_call x1, Pallas kernels, local(): pl.pallas_call(functools.partial(combine_kernel, visits), in_specs=[smem,...  1.91 us
    unnamed x4, local copies, waits for them, and re-layouts  0.89 us
  transfers between devices with their start and end apart: 9, of which 2 were waited for; matrix products, arithmetic and copies ran while one was open for 0% of the time, Pallas kernels for 0%

profile of v5, /device:TPU:1, one launch (start us, length us, event | category | flops | bytes accessed | tf_op | source)
XLA Modules:
  0.0 37.7 jit_solution(3878683176115061299)
XLA Ops:
  0.6 7.0 %match_and_sum.1 = (bf16[144,256]{1,0:T(8,128)(2,1)}, bf16[144,256]{1,0:T(8,128)(2,1)}, bf16[144,256]{1,0:T(8,128)(2,1)}, bf16[144,256]{1,0:T(8,128)(2,1)}, bf16...) custom-call(s32[32]{0:T(128)} %patch_ref.1, ...), custom_call_target="tpu_custom_call" | custom-call | tf_op jit(solution)/shard_map/match_and_sum/pallas_call | solution.py:306
  7.6 2.1 %collective-permute-start = (bf16[144,256]{1,0:T(8,128)(2,1)}, bf16[144,256]{1,0:T(8,128)(2,1)S(1)}, u32[]{:S(2)}, u32[]{:S(2)}) collective-permute-start(bf16[144,256]{1,0:T(8,128)(2,1)} %get-tuple-element.13), channel_id=1, source_target_pairs={{0,1},{1,0},{2,3},{3,2},{4,5},{5,4},{6,7},{7,6},{8,9},{9,8},{10,11... | collective-permute-start | bytes 221192 | tf_op jit(solution)/shard_map/ppermute | solution.py:353
  9.8 1.0 %collective-permute-start.1 = (bf16[144,256]{1,0:T(8,128)(2,1)}, bf16[144,256]{1,0:T(8,128)(2,1)S(1)}, u32[]{:S(2)}, u32[]{:S(2)}) collective-permute-start(bf16[144,256]{1,0:T(8,128)(2,1)} %get-tuple-element.14), channel_id=1, source_target_pairs={{0,30},{1,31},{2,0},{3,1},{4,2},{5,3},{6,4},{7,5},{8,6},{9,7},{10,... | collective-permute-start | bytes 221192 | tf_op jit(solution)/shard_map/ppermute | solution.py:353
  10.7 1.1 %collective-permute-start.2 = (bf16[144,256]{1,0:T(8,128)(2,1)}, bf16[144,256]{1,0:T(8,128)(2,1)S(1)}, u32[]{:S(2)}, u32[]{:S(2)}) collective-permute-start(bf16[144,256]{1,0:T(8,128)(2,1)} %get-tuple-element.15), channel_id=1, source_target_pairs={{0,2},{1,3},{2,4},{3,5},{4,6},{5,7},{6,8},{7,9},{8,10},{9,11},{10,... | collective-permute-start | bytes 221192 | tf_op jit(solution)/shard_map/ppermute | solution.py:353
  11.8 2.7 %collective-permute-start.3 = (bf16[144,256]{1,0:T(8,128)(2,1)}, bf16[144,256]{1,0:T(8,128)(2,1)S(1)}, u32[]{:S(2)}, u32[]{:S(2)}) collective-permute-start(bf16[144,256]{1,0:T(8,128)(2,1)} %get-tuple-element.16), channel_id=1, source_target_pairs={{0,31},{1,30},{2,1},{3,0},{4,3},{5,2},{6,5},{7,4},{8,7},{9,6},{10,... | collective-permute-start | bytes 221192 | tf_op jit(solution)/shard_map/ppermute | solution.py:353
  14.5 0.0 collective-permute-start.4
  14.5 0.0 collective-permute-done.refs_0_
  14.5 9.3 %collective-permute-start.5 = (bf16[144,256]{1,0:T(8,128)(2,1)}, bf16[144,256]{1,0:T(8,128)(2,1)S(1)}, u32[]{:S(2)}, u32[]{:S(2)}) collective-permute-start(bf16[144,256]{1,0:T(8,128)(2,1)} %get-tuple-element.18), channel_id=1, source_target_pairs={{0,28},{1,29},{2,30},{3,31},{4,0},{5,1},{6,2},{7,3},{8,4},{9,5},{1... | collective-permute-start | bytes 221192 | tf_op jit(solution)/shard_map/ppermute | solution.py:353
  23.8 0.0 collective-permute-done.1.refs_1_
  23.8 0.0 collective-permute-start.6
  23.8 0.0 collective-permute-done.2.refs_2_
  23.8 4.1 %collective-permute-start.7 = (bf16[144,256]{1,0:T(8,128)(2,1)}, bf16[144,256]{1,0:T(8,128)(2,1)S(1)}, u32[]{:S(2)}, u32[]{:S(2)}) collective-permute-start(bf16[144,256]{1,0:T(8,128)(2,1)} %get-tuple-element.20), channel_id=1, source_target_pairs={{0,29},{1,28},{2,31},{3,30},{4,1},{5,0},{6,3},{7,2},{8,5},{9,4},{1... | collective-permute-start | bytes 221192 | tf_op jit(solution)/shard_map/ppermute | solution.py:353
  27.9 0.0 collective-permute-done.3.refs_3_
  27.9 0.0 copy-start.1
  27.9 0.0 collective-permute-start.8
  27.9 0.0 collective-permute-done.4.refs_4_
  27.9 0.0 collective-permute-done.5.refs_5_
  28.0 2.0 %collective-permute-done.6.refs_6_ = bf16[144,256]{1,0:T(8,128)(2,1)S(1)} collective-permute-done((bf16[144,256]{1,0:T(8,128)(2,1)}, bf16[144,256]{1,0:T(8,128)(2,1)S(1)}, u32[]{:S(2)}, u32[]{:S(2)}) %collective-permute-start.6) | collective-permute-done | bytes 73760 | tf_op jit(solution)/shard_map/ppermute | solution.py:353
  29.9 0.0 collective-permute-done.7.refs_7_
  29.9 5.0 %collective-permute-done.8.refs_8_ = bf16[144,256]{1,0:T(8,128)(2,1)S(1)} collective-permute-done((bf16[144,256]{1,0:T(8,128)(2,1)}, bf16[144,256]{1,0:T(8,128)(2,1)S(1)}, u32[]{:S(2)}, u32[]{:S(2)}) %collective-permute-start.8) | collective-permute-done | bytes 73760 | tf_op jit(solution)/shard_map/ppermute | solution.py:353
  34.9 0.0 copy-done.1
  34.9 0.0 copy-start
  34.9 0.9 %copy-done = bf16[144,256]{1,0:T(8,128)(2,1)S(1)} copy-done((bf16[144,256]{1,0:T(8,128)(2,1)S(1)}, bf16[144,256]{1,0:T(8,128)(2,1)}, u32[]{:S(2)}) %copy-start) | copy-done | bytes 73752
  35.8 1.9 %combine.1 = (f32[6,32,256]{2,1,0:T(8,128)}, f32[32,256]{1,0:T(8,128)}) custom-call(f32[6]{0:T(128)S(1)} %copy-done.1, bf16[144,256]{1,0:T(8,128)(2,1)S(1)} %copy-done, bf16[144,256]{1,0:T(8,128)(2,1)S(1)} %collective-permute-done.refs_0_, bf16[144,256]{1,0:T(8,128)(2,1)S(1)} %collective-permute-done.1.refs_1_, ...), custom_call_target="tpu_custom_call" | custom-call | tf_op jit(solution)/shard_map/combine/pallas_call | solution.py:356
Async XLA Ops:
  7.6 6.9 %collective-permute-start = (bf16[144,256]{1,0:T(8,128)(2,1)}, bf16[144,256]{1,0:T(8,128)(2,1)S(1)}, u32[]{:S(2)}, u32[]{:S(2)}) collective-permute-start(bf16[144,256]{1,0:T(8,128)(2,1)} %get-tuple-element.13), channel_id=1, source_target_pairs={{0,1},{1,0},{2,3},{3,2},{4,5},{5,4},{6,7},{7,6},{8,9},{9,8},{10,11... | collective-permute-start | bytes 221192 | tf_op jit(solution)/shard_map/ppermute | solution.py:353
  9.8 14.0 %collective-permute-start.1 = (bf16[144,256]{1,0:T(8,128)(2,1)}, bf16[144,256]{1,0:T(8,128)(2,1)S(1)}, u32[]{:S(2)}, u32[]{:S(2)}) collective-permute-start(bf16[144,256]{1,0:T(8,128)(2,1)} %get-tuple-element.14), channel_id=1, source_target_pairs={{0,30},{1,31},{2,0},{3,1},{4,2},{5,3},{6,4},{7,5},{8,6},{9,7},{10,... | collective-permute-start | bytes 221192 | tf_op jit(solution)/shard_map/ppermute | solution.py:353
  10.7 13.1 %collective-permute-start.2 = (bf16[144,256]{1,0:T(8,128)(2,1)}, bf16[144,256]{1,0:T(8,128)(2,1)S(1)}, u32[]{:S(2)}, u32[]{:S(2)}) collective-permute-start(bf16[144,256]{1,0:T(8,128)(2,1)} %get-tuple-element.15), channel_id=1, source_target_pairs={{0,2},{1,3},{2,4},{3,5},{4,6},{5,7},{6,8},{7,9},{8,10},{9,11},{10,... | collective-permute-start | bytes 221192 | tf_op jit(solution)/shard_map/ppermute | solution.py:353
  11.8 16.1 %collective-permute-start.3 = (bf16[144,256]{1,0:T(8,128)(2,1)}, bf16[144,256]{1,0:T(8,128)(2,1)S(1)}, u32[]{:S(2)}, u32[]{:S(2)}) collective-permute-start(bf16[144,256]{1,0:T(8,128)(2,1)} %get-tuple-element.16), channel_id=1, source_target_pairs={{0,31},{1,30},{2,1},{3,0},{4,3},{5,2},{6,5},{7,4},{8,7},{9,6},{10,... | collective-permute-start | bytes 221192 | tf_op jit(solution)/shard_map/ppermute | solution.py:353
  14.5 13.4 %collective-permute-start.4 = (bf16[144,256]{1,0:T(8,128)(2,1)}, bf16[144,256]{1,0:T(8,128)(2,1)S(1)}, u32[]{:S(2)}, u32[]{:S(2)}) collective-permute-start(bf16[144,256]{1,0:T(8,128)(2,1)} %get-tuple-element.17), channel_id=1, source_target_pairs={{0,3},{1,2},{2,5},{3,4},{4,7},{5,6},{6,9},{7,8},{8,11},{9,10},{10,... | collective-permute-start | bytes 221192 | tf_op jit(solution)/shard_map/ppermute | solution.py:353
  14.5 13.4 %collective-permute-start.5 = (bf16[144,256]{1,0:T(8,128)(2,1)}, bf16[144,256]{1,0:T(8,128)(2,1)S(1)}, u32[]{:S(2)}, u32[]{:S(2)}) collective-permute-start(bf16[144,256]{1,0:T(8,128)(2,1)} %get-tuple-element.18), channel_id=1, source_target_pairs={{0,28},{1,29},{2,30},{3,31},{4,0},{5,1},{6,2},{7,3},{8,4},{9,5},{1... | collective-permute-start | bytes 221192 | tf_op jit(solution)/shard_map/ppermute | solution.py:353
  23.8 6.1 %collective-permute-start.6 = (bf16[144,256]{1,0:T(8,128)(2,1)}, bf16[144,256]{1,0:T(8,128)(2,1)S(1)}, u32[]{:S(2)}, u32[]{:S(2)}) collective-permute-start(bf16[144,256]{1,0:T(8,128)(2,1)} %get-tuple-element.19), channel_id=1, source_target_pairs={{0,4},{1,5},{2,6},{3,7},{4,8},{5,9},{6,10},{7,11},{8,12},{9,13},{1... | collective-permute-start | bytes 221192 | tf_op jit(solution)/shard_map/ppermute | solution.py:353
  23.8 6.1 %collective-permute-start.7 = (bf16[144,256]{1,0:T(8,128)(2,1)}, bf16[144,256]{1,0:T(8,128)(2,1)S(1)}, u32[]{:S(2)}, u32[]{:S(2)}) collective-permute-start(bf16[144,256]{1,0:T(8,128)(2,1)} %get-tuple-element.20), channel_id=1, source_target_pairs={{0,29},{1,28},{2,31},{3,30},{4,1},{5,0},{6,3},{7,2},{8,5},{9,4},{1... | collective-permute-start | bytes 221192 | tf_op jit(solution)/shard_map/ppermute | solution.py:353
  27.9 7.0 %copy-start.1 = (f32[6]{0:T(128)S(1)}, f32[6]{0:T(128)}, u32[]{:S(2)}) copy-start(f32[6]{0:T(128)} %weight_ref.1) | copy-start | bytes 76
  27.9 7.0 %collective-permute-start.8 = (bf16[144,256]{1,0:T(8,128)(2,1)}, bf16[144,256]{1,0:T(8,128)(2,1)S(1)}, u32[]{:S(2)}, u32[]{:S(2)}) collective-permute-start(bf16[144,256]{1,0:T(8,128)(2,1)} %get-tuple-element.21), channel_id=1, source_target_pairs={{0,5},{1,4},{2,7},{3,6},{4,9},{5,8},{6,11},{7,10},{8,13},{9,12},{1... | collective-permute-start | bytes 221192 | tf_op jit(solution)/shard_map/ppermute | solution.py:353
  34.9 0.9 %copy-start = (bf16[144,256]{1,0:T(8,128)(2,1)S(1)}, bf16[144,256]{1,0:T(8,128)(2,1)}, u32[]{:S(2)}) copy-start(bf16[144,256]{1,0:T(8,128)(2,1)} %get-tuple-element.12.own_hbm) | copy-start | bytes 221188

commit v6 on v5

--- a/solution.py
+++ b/solution.py
@@ -244,22 +244,16 @@
             messages[bucket * groups + turn][slot * visits :, :] = mixed
 
 
-def combine_kernel(count, weight_ref, own_hbm, *refs):
-    coadd_ref, detection_ref, own_ref, arrival = refs[-4:]
-    row_share = coadd_ref.shape[1]
+def add_messages(count, row_share, messages):
     slot = slot_rows(row_share)
     depth = slot * count
-    fetch = pltpu.make_async_copy(own_hbm, own_ref, arrival)
-    fetch.start()
     line = lax.broadcasted_iota(jnp.int32, (row_share, depth), 0)
     lane = lax.broadcasted_iota(jnp.int32, (row_share, depth), 1)
     same = (lax.rem(lane, slot) == line).astype(jnp.float32)
     band_line = lax.broadcasted_iota(jnp.int32, (8, EXTRA), 0).astype(jnp.float32)
     totals = jnp.zeros((BANDS * row_share, PW), jnp.float32)
     weight_totals = jnp.zeros((8, PW), jnp.float32)
-    for message in refs[:-4] + (own_ref,):
-        if message is own_ref:
-            fetch.wait()
+    for message in messages:
         extra = message[depth:, :]
         bands = extra[2 * count : 2 * count + 2].astype(jnp.float32)
         pick = jnp.concatenate(
@@ -268,10 +262,24 @@
         totals += jnp.dot(pick, message[:depth, :], preferred_element_type=jnp.float32)
         pick = (bands[1:, :EXTRA] == band_line).astype(jnp.bfloat16)
         weight_totals += jnp.dot(pick, extra, preferred_element_type=jnp.float32)
+    return totals, weight_totals
+
+
+def early_kernel(count, row_share, *refs):
+    totals_ref, weight_totals_ref = refs[-2:]
+    totals_ref[...], weight_totals_ref[...] = add_messages(count, row_share, refs[:-2])
+
+
+def combine_kernel(count, weight_ref, totals_ref, weight_totals_ref, *refs):
+    coadd_ref, detection_ref = refs[-2:]
+    row_share = coadd_ref.shape[1]
+    totals, weight_totals = add_messages(count, row_share, refs[:-2])
+    weight_totals = jnp.maximum(weight_totals + weight_totals_ref[...], 1.0)
     detection = jnp.zeros((row_share, PW), jnp.float32)
     for b in range(BANDS):
-        coadd = totals[b * row_share : (b + 1) * row_share] / jnp.maximum(
-            weight_totals[b : b + 1], 1.0
+        held = pl.ds(b * row_share, row_share)
+        coadd = (totals[b * row_share : (b + 1) * row_share] + totals_ref[held, :]) / (
+            weight_totals[b : b + 1]
         )
         coadd_ref[b] = coadd
         detection += weight_ref[b] * coadd
@@ -338,33 +346,45 @@
         tiles,
     )
 
+    order = [(d, t) for d in range(-1, -REACH - 1, -1) for t in range(groups)]
+    order += [(0, t) for t in range(1, groups)]
+    early = len(order)
+    order += [(d, t) for d in range(REACH, 0, -1) for t in range(groups)]
     arrived = []
-    for distance, turn in sorted(
-        ((d, t) for d in range(-REACH, REACH + 1) for t in range(groups)),
-        key=lambda way: (abs(way[0]), way[1], way[0]),
-    ):
-        message = messages[(distance + REACH) * groups + turn]
-        if distance != 0 or turn != 0:
-            route = [
-                (o * groups + g, (o + distance) % patches * groups + (g + turn) % groups)
-                for o in range(patches)
-                for g in range(groups)
-            ]
-            message = lax.ppermute(message, ("ra", "band"), route)
-        arrived.append(message)
-
+    for distance, turn in order:
+        route = [
+            (o * groups + g, (o + distance) % patches * groups + (g + turn) % groups)
+            for o in range(patches)
+            for g in range(groups)
+        ]
+        arrived.append(
+            lax.ppermute(messages[(distance + REACH) * groups + turn], ("ra", "band"), route)
+        )
+
+    params = pltpu.CompilerParams(vmem_limit_bytes=40 * 1024 * 1024)
+    first = [messages[REACH * groups]] + arrived[:early]
+    totals = pl.pallas_call(
+        functools.partial(early_kernel, visits, row_share),
+        in_specs=[vmem] * len(first),
+        out_specs=(vmem, vmem),
+        out_shape=(
+            jax.ShapeDtypeStruct((BANDS * row_share, PW), jnp.float32),
+            jax.ShapeDtypeStruct((8, PW), jnp.float32),
+        ),
+        compiler_params=params,
+        name="combine_early",
+    )(*first)
     return pl.pallas_call(
         functools.partial(combine_kernel, visits),
-        in_specs=[smem, anywhere] + [vmem] * (len(arrived) - 1),
+        in_specs=[smem] + [vmem] * (len(arrived) - early + 2),
         out_specs=(vmem, vmem),
         out_shape=(
             jax.ShapeDtypeStruct((BANDS, row_share, PW), jnp.float32),
             jax.ShapeDtypeStruct((row_share, PW), jnp.float32),
         ),
-        scratch_shapes=[pltpu.VMEM((length, PW), jnp.bfloat16), pltpu.SemaphoreType.DMA],
-        compiler_params=pltpu.CompilerParams(vmem_limit_bytes=40 * 1024 * 1024),
+        compiler_params=params,
         name="combine",
-    )(band_weight, *arrived)
+    )(band_weight, *totals, *arrived[early:])
 
 
 def solution(mesh):

time: 38 us -> 31.9 us (0.84)
  the two profiles are of different devices: /device:TPU:1 before, /device:TPU:0 now
where the time goes in v6:
time: 31.9 us; the launch traced here: 31.7 us
  starting transfers between devices  14.8 us (46%)
  Pallas kernels  8.82 us (28%)
  waiting for transfers between devices  5.92 us (19%)
  local copies, waits for them, and re-layouts  1.54 us (5%)
  between operations  0.66 us (2%)
    ppermute x9, starting transfers between devices, local(): lax.ppermute(messages[(distance + REACH) * groups + turn], ('ra', 'band')...  14.8 us
    pallas_call x1, Pallas kernels, local(): pl.pallas_call(functools.partial(match_kernel, patches, groups), in_specs...  7 us
    ppermute x9, waiting for transfers between devices, local(): lax.ppermute(messages[(distance + REACH) * groups + turn], ('ra', 'band')...  5.92 us
    unnamed x4, local copies, waits for them, and re-layouts  1.54 us
    pallas_call x1, Pallas kernels, local(): pl.pallas_call(functools.partial(combine_kernel, visits), in_specs=[smem]...  1.5 us
  transfers between devices with their start and end apart: 9, of which 4 were waited for; matrix products, arithmetic and copies ran while one was open for 0% of the time, Pallas kernels for 1%

profile of v6, /device:TPU:0, one launch (start us, length us, event | category | flops | bytes accessed | tf_op | source)
XLA Modules:
  0.0 31.7 jit_solution(3362514288616134671)
XLA Ops:
  0.6 7.0 %match_and_sum.1 = (bf16[144,256]{1,0:T(8,128)(2,1)}, bf16[144,256]{1,0:T(8,128)(2,1)}, bf16[144,256]{1,0:T(8,128)(2,1)}, bf16[144,256]{1,0:T(8,128)(2,1)}, bf16...) custom-call(s32[32]{0:T(128)} %patch_ref.1, ...), custom_call_target="tpu_custom_call" | custom-call | tf_op jit(solution)/shard_map/match_and_sum/pallas_call | solution.py:314
  7.6 5.5 %collective-permute-start = (bf16[144,256]{1,0:T(8,128)(2,1)}, bf16[144,256]{1,0:T(8,128)(2,1)S(1)}, u32[]{:S(2)}, u32[]{:S(2)}) collective-permute-start(bf16[144,256]{1,0:T(8,128)(2,1)} %get-tuple-element.15), channel_id=1, source_target_pairs={{0,30},{1,31},{2,0},{3,1},{4,2},{5,3},{6,4},{7,5},{8,6},{9,7},{10,... | collective-permute-start | bytes 221192 | tf_op jit(solution)/shard_map/ppermute | solution.py:361
  13.1 1.6 %collective-permute-start.1 = (bf16[144,256]{1,0:T(8,128)(2,1)}, bf16[144,256]{1,0:T(8,128)(2,1)S(1)}, u32[]{:S(2)}, u32[]{:S(2)}) collective-permute-start(bf16[144,256]{1,0:T(8,128)(2,1)} %get-tuple-element.16), channel_id=1, source_target_pairs={{0,31},{1,30},{2,1},{3,0},{4,3},{5,2},{6,5},{7,4},{8,7},{9,6},{10,... | collective-permute-start | bytes 221192 | tf_op jit(solution)/shard_map/ppermute | solution.py:361
  14.7 0.5 %collective-permute-start.2 = (bf16[144,256]{1,0:T(8,128)(2,1)}, bf16[144,256]{1,0:T(8,128)(2,1)S(1)}, u32[]{:S(2)}, u32[]{:S(2)}) collective-permute-start(bf16[144,256]{1,0:T(8,128)(2,1)} %get-tuple-element.17), channel_id=1, source_target_pairs={{0,28},{1,29},{2,30},{3,31},{4,0},{5,1},{6,2},{7,3},{8,4},{9,5},{1... | collective-permute-start | bytes 221192 | tf_op jit(solution)/shard_map/ppermute | solution.py:361
  15.3 1.3 %collective-permute-start.3 = (bf16[144,256]{1,0:T(8,128)(2,1)}, bf16[144,256]{1,0:T(8,128)(2,1)S(1)}, u32[]{:S(2)}, u32[]{:S(2)}) collective-permute-start(bf16[144,256]{1,0:T(8,128)(2,1)} %get-tuple-element.18), channel_id=1, source_target_pairs={{0,29},{1,28},{2,31},{3,30},{4,1},{5,0},{6,3},{7,2},{8,5},{9,4},{1... | collective-permute-start | bytes 221192 | tf_op jit(solution)/shard_map/ppermute | solution.py:361
  16.6 1.5 %collective-permute-start.4 = (bf16[144,256]{1,0:T(8,128)(2,1)}, bf16[144,256]{1,0:T(8,128)(2,1)S(1)}, u32[]{:S(2)}, u32[]{:S(2)}) collective-permute-start(bf16[144,256]{1,0:T(8,128)(2,1)} %get-tuple-element.19), channel_id=1, source_target_pairs={{0,1},{1,0},{2,3},{3,2},{4,5},{5,4},{6,7},{7,6},{8,9},{9,8},{10,11... | collective-permute-start | bytes 221192 | tf_op jit(solution)/shard_map/ppermute | solution.py:361
  18.1 0.0 collective-permute-done.refs_1_
  18.1 0.7 %collective-permute-start.5 = (bf16[144,256]{1,0:T(8,128)(2,1)}, bf16[144,256]{1,0:T(8,128)(2,1)S(1)}, u32[]{:S(2)}, u32[]{:S(2)}) collective-permute-start(bf16[144,256]{1,0:T(8,128)(2,1)} %get-tuple-element.22), channel_id=1, source_target_pairs={{0,4},{1,5},{2,6},{3,7},{4,8},{5,9},{6,10},{7,11},{8,12},{9,13},{1... | collective-permute-start | bytes 221192 | tf_op jit(solution)/shard_map/ppermute | solution.py:361
  18.8 0.0 collective-permute-done.1.refs_2_
  18.8 2.3 %collective-permute-start.6 = (bf16[144,256]{1,0:T(8,128)(2,1)}, bf16[144,256]{1,0:T(8,128)(2,1)S(1)}, u32[]{:S(2)}, u32[]{:S(2)}) collective-permute-start(bf16[144,256]{1,0:T(8,128)(2,1)} %get-tuple-element.23), channel_id=1, source_target_pairs={{0,5},{1,4},{2,7},{3,6},{4,9},{5,8},{6,11},{7,10},{8,13},{9,12},{1... | collective-permute-start | bytes 221192 | tf_op jit(solution)/shard_map/ppermute | solution.py:361
  21.1 0.0 collective-permute-done.2.refs_3_
  21.1 0.0 collective-permute-start.7
  21.1 0.0 collective-permute-done.3.refs_4_
  21.1 1.3 %collective-permute-start.8 = (bf16[144,256]{1,0:T(8,128)(2,1)}, bf16[144,256]{1,0:T(8,128)(2,1)S(1)}, u32[]{:S(2)}, u32[]{:S(2)}) collective-permute-start(bf16[144,256]{1,0:T(8,128)(2,1)} %get-tuple-element.25), channel_id=1, source_target_pairs={{0,3},{1,2},{2,5},{3,4},{4,7},{5,6},{6,9},{7,8},{8,11},{9,10},{10,... | collective-permute-start | bytes 221192 | tf_op jit(solution)/shard_map/ppermute | solution.py:361
  22.4 0.0 collective-permute-done.4.refs_5_
  22.4 0.9 %copy-done = bf16[144,256]{1,0:T(8,128)(2,1)S(1)} copy-done((bf16[144,256]{1,0:T(8,128)(2,1)S(1)}, bf16[144,256]{1,0:T(8,128)(2,1)}, u32[]{:S(2)}) %copy-start) | copy-done | bytes 73752
  23.3 0.3 %combine_early.1 = (f32[192,256]{1,0:T(8,128)S(1)}, f32[8,256]{1,0:T(8,128)S(1)}) custom-call(bf16[144,256]{1,0:T(8,128)(2,1)S(1)} %copy-done, bf16[144,256]{1,0:T(8,128)(2,1)S(1)} %collective-permute-done.refs_1_, bf16[144,256]{1,0:T(8,128)(2,1)S(1)} %collective-permute-done.1.refs_2_, bf16[144,256]{1,0:T(8,128)(2,1)S(1)} %collective-permute-done.2.refs_3_, ...), custom_call_target="tpu_custom_call" | custom-call | tf_op jit(solution)/shard_map/combine_early/pallas_call | solution.py:366
  23.6 1.8 %collective-permute-done.5.refs_0_ = bf16[144,256]{1,0:T(8,128)(2,1)S(1)} collective-permute-done((bf16[144,256]{1,0:T(8,128)(2,1)}, bf16[144,256]{1,0:T(8,128)(2,1)S(1)}, u32[]{:S(2)}, u32[]{:S(2)}) %collective-permute-start.5) | collective-permute-done | bytes 73760 | tf_op jit(solution)/shard_map/ppermute | solution.py:361
  25.5 1.5 %collective-permute-done.6.refs_1_ = bf16[144,256]{1,0:T(8,128)(2,1)S(1)} collective-permute-done((bf16[144,256]{1,0:T(8,128)(2,1)}, bf16[144,256]{1,0:T(8,128)(2,1)S(1)}, u32[]{:S(2)}, u32[]{:S(2)}) %collective-permute-start.6) | collective-permute-done | bytes 73760 | tf_op jit(solution)/shard_map/ppermute | solution.py:361
  27.0 0.8 %collective-permute-done.7.refs_2_ = bf16[144,256]{1,0:T(8,128)(2,1)S(1)} collective-permute-done((bf16[144,256]{1,0:T(8,128)(2,1)}, bf16[144,256]{1,0:T(8,128)(2,1)S(1)}, u32[]{:S(2)}, u32[]{:S(2)}) %collective-permute-start.7) | collective-permute-done | bytes 73760 | tf_op jit(solution)/shard_map/ppermute | solution.py:361
  27.8 1.8 %collective-permute-done.8.refs_3_ = bf16[144,256]{1,0:T(8,128)(2,1)S(1)} collective-permute-done((bf16[144,256]{1,0:T(8,128)(2,1)}, bf16[144,256]{1,0:T(8,128)(2,1)S(1)}, u32[]{:S(2)}, u32[]{:S(2)}) %collective-permute-start.8) | collective-permute-done | bytes 73760 | tf_op jit(solution)/shard_map/ppermute | solution.py:361
  29.5 0.0 copy-start.1
  29.6 0.7 %copy-done.1 = f32[6]{0:T(128)S(1)} copy-done((f32[6]{0:T(128)S(1)}, f32[6]{0:T(128)}, u32[]{:S(2)}) %copy-start.1) | copy-done | bytes 48
  30.2 1.5 %combine.1 = (f32[6,32,256]{2,1,0:T(8,128)}, f32[32,256]{1,0:T(8,128)}) custom-call(f32[6]{0:T(128)S(1)} %copy-done.1, f32[192,256]{1,0:T(8,128)S(1)} %get-tuple-element.20.totals_ref, f32[8,256]{1,0:T(8,128)S(1)} %get-tuple-element.21.weight_totals_ref, bf16[144,256]{1,0:T(8,128)(2,1)S(1)} %collective-permute-done.5.refs_0_, ...), custom_call_target="tpu_custom_call" | custom-call | tf_op jit(solution)/shard_map/combine/pallas_call | solution.py:377
  (1 shorter events, 0.0 us)
Async XLA Ops:
  7.6 10.5 %collective-permute-start = (bf16[144,256]{1,0:T(8,128)(2,1)}, bf16[144,256]{1,0:T(8,128)(2,1)S(1)}, u32[]{:S(2)}, u32[]{:S(2)}) collective-permute-start(bf16[144,256]{1,0:T(8,128)(2,1)} %get-tuple-element.15), channel_id=1, source_target_pairs={{0,30},{1,31},{2,0},{3,1},{4,2},{5,3},{6,4},{7,5},{8,6},{9,7},{10,... | collective-permute-start | bytes 221192 | tf_op jit(solution)/shard_map/ppermute | solution.py:361
  13.1 5.7 %collective-permute-start.1 = (bf16[144,256]{1,0:T(8,128)(2,1)}, bf16[144,256]{1,0:T(8,128)(2,1)S(1)}, u32[]{:S(2)}, u32[]{:S(2)}) collective-permute-start(bf16[144,256]{1,0:T(8,128)(2,1)} %get-tuple-element.16), channel_id=1, source_target_pairs={{0,31},{1,30},{2,1},{3,0},{4,3},{5,2},{6,5},{7,4},{8,7},{9,6},{10,... | collective-permute-start | bytes 221192 | tf_op jit(solution)/shard_map/ppermute | solution.py:361
  14.7 6.4 %collective-permute-start.2 = (bf16[144,256]{1,0:T(8,128)(2,1)}, bf16[144,256]{1,0:T(8,128)(2,1)S(1)}, u32[]{:S(2)}, u32[]{:S(2)}) collective-permute-start(bf16[144,256]{1,0:T(8,128)(2,1)} %get-tuple-element.17), channel_id=1, source_target_pairs={{0,28},{1,29},{2,30},{3,31},{4,0},{5,1},{6,2},{7,3},{8,4},{9,5},{1... | collective-permute-start | bytes 221192 | tf_op jit(solution)/shard_map/ppermute | solution.py:361
  15.3 5.8 %collective-permute-start.3 = (bf16[144,256]{1,0:T(8,128)(2,1)}, bf16[144,256]{1,0:T(8,128)(2,1)S(1)}, u32[]{:S(2)}, u32[]{:S(2)}) collective-permute-start(bf16[144,256]{1,0:T(8,128)(2,1)} %get-tuple-element.18), channel_id=1, source_target_pairs={{0,29},{1,28},{2,31},{3,30},{4,1},{5,0},{6,3},{7,2},{8,5},{9,4},{1... | collective-permute-start | bytes 221192 | tf_op jit(solution)/shard_map/ppermute | solution.py:361
  16.6 5.8 %collective-permute-start.4 = (bf16[144,256]{1,0:T(8,128)(2,1)}, bf16[144,256]{1,0:T(8,128)(2,1)S(1)}, u32[]{:S(2)}, u32[]{:S(2)}) collective-permute-start(bf16[144,256]{1,0:T(8,128)(2,1)} %get-tuple-element.19), channel_id=1, source_target_pairs={{0,1},{1,0},{2,3},{3,2},{4,5},{5,4},{6,7},{7,6},{8,9},{9,8},{10,11... | collective-permute-start | bytes 221192 | tf_op jit(solution)/shard_map/ppermute | solution.py:361
  18.1 7.4 %collective-permute-start.5 = (bf16[144,256]{1,0:T(8,128)(2,1)}, bf16[144,256]{1,0:T(8,128)(2,1)S(1)}, u32[]{:S(2)}, u32[]{:S(2)}) collective-permute-start(bf16[144,256]{1,0:T(8,128)(2,1)} %get-tuple-element.22), channel_id=1, source_target_pairs={{0,4},{1,5},{2,6},{3,7},{4,8},{5,9},{6,10},{7,11},{8,12},{9,13},{1... | collective-permute-start | bytes 221192 | tf_op jit(solution)/shard_map/ppermute | solution.py:361
  18.8 8.2 %collective-permute-start.6 = (bf16[144,256]{1,0:T(8,128)(2,1)}, bf16[144,256]{1,0:T(8,128)(2,1)S(1)}, u32[]{:S(2)}, u32[]{:S(2)}) collective-permute-start(bf16[144,256]{1,0:T(8,128)(2,1)} %get-tuple-element.23), channel_id=1, source_target_pairs={{0,5},{1,4},{2,7},{3,6},{4,9},{5,8},{6,11},{7,10},{8,13},{9,12},{1... | collective-permute-start | bytes 221192 | tf_op jit(solution)/shard_map/ppermute | solution.py:361
  21.1 6.7 %collective-permute-start.7 = (bf16[144,256]{1,0:T(8,128)(2,1)}, bf16[144,256]{1,0:T(8,128)(2,1)S(1)}, u32[]{:S(2)}, u32[]{:S(2)}) collective-permute-start(bf16[144,256]{1,0:T(8,128)(2,1)} %get-tuple-element.24), channel_id=1, source_target_pairs={{0,2},{1,3},{2,4},{3,5},{4,6},{5,7},{6,8},{7,9},{8,10},{9,11},{10,... | collective-permute-start | bytes 221192 | tf_op jit(solution)/shard_map/ppermute | solution.py:361
  21.1 8.4 %collective-permute-start.8 = (bf16[144,256]{1,0:T(8,128)(2,1)}, bf16[144,256]{1,0:T(8,128)(2,1)S(1)}, u32[]{:S(2)}, u32[]{:S(2)}) collective-permute-start(bf16[144,256]{1,0:T(8,128)(2,1)} %get-tuple-element.25), channel_id=1, source_target_pairs={{0,3},{1,2},{2,5},{3,4},{4,7},{5,6},{6,9},{7,8},{8,11},{9,10},{10,... | collective-permute-start | bytes 221192 | tf_op jit(solution)/shard_map/ppermute | solution.py:361
  22.4 0.9 %copy-start = (bf16[144,256]{1,0:T(8,128)(2,1)S(1)}, bf16[144,256]{1,0:T(8,128)(2,1)}, u32[]{:S(2)}) copy-start(bf16[144,256]{1,0:T(8,128)(2,1)} %get-tuple-element.14.refs_0_) | copy-start | bytes 221188
  29.5 0.7 %copy-start.1 = (f32[6]{0:T(128)S(1)}, f32[6]{0:T(128)}, u32[]{:S(2)}) copy-start(f32[6]{0:T(128)} %weight_ref.1) | copy-start | bytes 76

commit v7 on v6

--- a/solution.py
+++ b/solution.py
@@ -265,16 +265,21 @@
     return totals, weight_totals
 
 
-def early_kernel(count, row_share, *refs):
-    totals_ref, weight_totals_ref = refs[-2:]
-    totals_ref[...], weight_totals_ref[...] = add_messages(count, row_share, refs[:-2])
-
-
-def combine_kernel(count, weight_ref, totals_ref, weight_totals_ref, *refs):
+def early_kernel(count, row_share, weight_ref, *refs):
+    totals_ref, rows_ref = refs[-2:]
+    totals_ref[...], rows_ref[:8] = add_messages(count, row_share, refs[:-2])
+    line = lax.broadcasted_iota(jnp.int32, (8, PW), 0)
+    band_weights = jnp.zeros((8, PW), jnp.float32)
+    for b in range(BANDS):
+        band_weights = jnp.where(line == b, weight_ref[b], band_weights)
+    rows_ref[8:] = band_weights
+
+
+def combine_kernel(count, totals_ref, rows_ref, *refs):
     coadd_ref, detection_ref = refs[-2:]
     row_share = coadd_ref.shape[1]
     totals, weight_totals = add_messages(count, row_share, refs[:-2])
-    weight_totals = jnp.maximum(weight_totals + weight_totals_ref[...], 1.0)
+    weight_totals = jnp.maximum(weight_totals + rows_ref[:8], 1.0)
     detection = jnp.zeros((row_share, PW), jnp.float32)
     for b in range(BANDS):
         held = pl.ds(b * row_share, row_share)
@@ -282,7 +287,7 @@
             weight_totals[b : b + 1]
         )
         coadd_ref[b] = coadd
-        detection += weight_ref[b] * coadd
+        detection += rows_ref[8 + b : 9 + b] * coadd
     detection_ref[...] = detection
 
 
@@ -346,10 +351,10 @@
         tiles,
     )
 
-    order = [(d, t) for d in range(-1, -REACH - 1, -1) for t in range(groups)]
+    order = [(d, t) for d in range(1, REACH + 1) for t in range(groups)]
     order += [(0, t) for t in range(1, groups)]
     early = len(order)
-    order += [(d, t) for d in range(REACH, 0, -1) for t in range(groups)]
+    order += [(d, t) for d in range(-REACH, 0) for t in range(groups)]
     arrived = []
     for distance, turn in order:
         route = [
@@ -365,18 +370,18 @@
     first = [messages[REACH * groups]] + arrived[:early]
     totals = pl.pallas_call(
         functools.partial(early_kernel, visits, row_share),
-        in_specs=[vmem] * len(first),
+        in_specs=[smem] + [vmem] * len(first),
         out_specs=(vmem, vmem),
         out_shape=(
             jax.ShapeDtypeStruct((BANDS * row_share, PW), jnp.float32),
-            jax.ShapeDtypeStruct((8, PW), jnp.float32),
+            jax.ShapeDtypeStruct((16, PW), jnp.float32),
         ),
         compiler_params=params,
         name="combine_early",
-    )(*first)
+    )(band_weight, *first)
     return pl.pallas_call(
         functools.partial(combine_kernel, visits),
-        in_specs=[smem] + [vmem] * (len(arrived) - early + 2),
+        in_specs=[vmem] * (len(arrived) - early + 2),
         out_specs=(vmem, vmem),
         out_shape=(
             jax.ShapeDtypeStruct((BANDS, row_share, PW), jnp.float32),
@@ -384,7 +389,7 @@
         ),
         compiler_params=params,
         name="combine",
-    )(band_weight, *totals, *arrived[early:])
+    )(*totals, *arrived[early:])
 
 
 def solution(mesh):

time: 31.9 us -> 27.2 us (0.85)
  waiting for transfers between devices: 5.92 us -> 2.07 us
  local copies, waits for them, and re-layouts: 1.54 us -> 0.89 us
  starting transfers between devices: 14.8 us -> 14.4 us
    ppermute x9, waiting for transfers between devices: 5.92 us -> 2.07 us  [local(): lax.ppermute(messages[(distance + REACH) * groups + turn], ('ra', 'band')...]
    unnamed x4, local copies, waits for them, and re-layouts: 1.54 us -> 0.89 us
    pallas_call x1, Pallas kernels: 1.5 us -> 0.96 us  [local(): pl.pallas_call(functools.partial(combine_kernel, visits), in_specs=[vmem]...]
    pallas_call x1, Pallas kernels: 0.33 us -> 0.87 us  [local(): pl.pallas_call(functools.partial(early_kernel, visits, row_share), in_spe...]
    ppermute x9, starting transfers between devices: 14.8 us -> 14.4 us  [local(): lax.ppermute(messages[(distance + REACH) * groups + turn], ('ra', 'band')...]
  transfers between devices with their start and end apart: 9 -> 9, of which waited for: 4 -> 3; matrix products, arithmetic and copies ran while one was open for 0% -> 0% of each run, Pallas kernels for 1% -> 3%
where the time goes in v7:
time: 27.2 us; the launch traced here: 26.8 us
  starting transfers between devices  14.4 us (53%)
  Pallas kernels  8.82 us (32%)
  waiting for transfers between devices  2.07 us (8%)
  local copies, waits for them, and re-layouts  0.89 us (3%)
  between operations  0.67 us (2%)
    ppermute x9, starting transfers between devices, local(): lax.ppermute(messages[(distance + REACH) * groups + turn], ('ra', 'band')...  14.4 us
    pallas_call x1, Pallas kernels, local(): pl.pallas_call(functools.partial(match_kernel, patches, groups), in_specs...  7 us
    ppermute x9, waiting for transfers between devices, local(): lax.ppermute(messages[(distance + REACH) * groups + turn], ('ra', 'band')...  2.07 us
    pallas_call x1, Pallas kernels, local(): pl.pallas_call(functools.partial(combine_kernel, visits), in_specs=[vmem]...  0.96 us
    unnamed x4, local copies, waits for them, and re-layouts  0.89 us
    pallas_call x1, Pallas kernels, local(): pl.pallas_call(functools.partial(early_kernel, visits, row_share), in_spe...  0.87 us
  transfers between devices with their start and end apart: 9, of which 3 were waited for; matrix products, arithmetic and copies ran while one was open for 0% of the time, Pallas kernels for 3%

profile of v7, /device:TPU:0, one launch (start us, length us, event | category | flops | bytes accessed | tf_op | source)
XLA Modules:
  0.0 26.8 jit_solution(6063209681375913505)
XLA Ops:
  0.6 7.0 %match_and_sum.1 = (bf16[144,256]{1,0:T(8,128)(2,1)}, bf16[144,256]{1,0:T(8,128)(2,1)}, bf16[144,256]{1,0:T(8,128)(2,1)}, bf16[144,256]{1,0:T(8,128)(2,1)}, bf16...) custom-call(s32[32]{0:T(128)} %patch_ref.1, ...), custom_call_target="tpu_custom_call" | custom-call | tf_op jit(solution)/shard_map/match_and_sum/pallas_call | solution.py:319
  7.6 0.5 %collective-permute-start = (bf16[144,256]{1,0:T(8,128)(2,1)}, bf16[144,256]{1,0:T(8,128)(2,1)S(1)}, u32[]{:S(2)}, u32[]{:S(2)}) collective-permute-start(bf16[144,256]{1,0:T(8,128)(2,1)} %get-tuple-element.15), channel_id=1, source_target_pairs={{0,2},{1,3},{2,4},{3,5},{4,6},{5,7},{6,8},{7,9},{8,10},{9,11},{10,... | collective-permute-start | bytes 221192 | tf_op jit(solution)/shard_map/ppermute | solution.py:366
  8.1 3.7 %collective-permute-start.1 = (bf16[144,256]{1,0:T(8,128)(2,1)}, bf16[144,256]{1,0:T(8,128)(2,1)S(1)}, u32[]{:S(2)}, u32[]{:S(2)}) collective-permute-start(bf16[144,256]{1,0:T(8,128)(2,1)} %get-tuple-element.16), channel_id=1, source_target_pairs={{0,3},{1,2},{2,5},{3,4},{4,7},{5,6},{6,9},{7,8},{8,11},{9,10},{10,... | collective-permute-start | bytes 221192 | tf_op jit(solution)/shard_map/ppermute | solution.py:366
  11.9 1.6 %collective-permute-start.2 = (bf16[144,256]{1,0:T(8,128)(2,1)}, bf16[144,256]{1,0:T(8,128)(2,1)S(1)}, u32[]{:S(2)}, u32[]{:S(2)}) collective-permute-start(bf16[144,256]{1,0:T(8,128)(2,1)} %get-tuple-element.17), channel_id=1, source_target_pairs={{0,4},{1,5},{2,6},{3,7},{4,8},{5,9},{6,10},{7,11},{8,12},{9,13},{1... | collective-permute-start | bytes 221192 | tf_op jit(solution)/shard_map/ppermute | solution.py:366
  13.4 1.4 %collective-permute-start.3 = (bf16[144,256]{1,0:T(8,128)(2,1)}, bf16[144,256]{1,0:T(8,128)(2,1)S(1)}, u32[]{:S(2)}, u32[]{:S(2)}) collective-permute-start(bf16[144,256]{1,0:T(8,128)(2,1)} %get-tuple-element.18), channel_id=1, source_target_pairs={{0,5},{1,4},{2,7},{3,6},{4,9},{5,8},{6,11},{7,10},{8,13},{9,12},{1... | collective-permute-start | bytes 221192 | tf_op jit(solution)/shard_map/ppermute | solution.py:366
  14.8 1.5 %collective-permute-start.4 = (bf16[144,256]{1,0:T(8,128)(2,1)}, bf16[144,256]{1,0:T(8,128)(2,1)S(1)}, u32[]{:S(2)}, u32[]{:S(2)}) collective-permute-start(bf16[144,256]{1,0:T(8,128)(2,1)} %get-tuple-element.19), channel_id=1, source_target_pairs={{0,1},{1,0},{2,3},{3,2},{4,5},{5,4},{6,7},{7,6},{8,9},{9,8},{10,11... | collective-permute-start | bytes 221192 | tf_op jit(solution)/shard_map/ppermute | solution.py:366
  16.4 0.0 collective-permute-done.refs_1_
  16.4 3.2 %collective-permute-start.5 = (bf16[144,256]{1,0:T(8,128)(2,1)}, bf16[144,256]{1,0:T(8,128)(2,1)S(1)}, u32[]{:S(2)}, u32[]{:S(2)}) collective-permute-start(bf16[144,256]{1,0:T(8,128)(2,1)} %get-tuple-element.22), channel_id=1, source_target_pairs={{0,28},{1,29},{2,30},{3,31},{4,0},{5,1},{6,2},{7,3},{8,4},{9,5},{1... | collective-permute-start | bytes 221192 | tf_op jit(solution)/shard_map/ppermute | solution.py:366
  19.6 0.0 collective-permute-done.1.refs_2_
  19.6 0.4 %collective-permute-start.6 = (bf16[144,256]{1,0:T(8,128)(2,1)}, bf16[144,256]{1,0:T(8,128)(2,1)S(1)}, u32[]{:S(2)}, u32[]{:S(2)}) collective-permute-start(bf16[144,256]{1,0:T(8,128)(2,1)} %get-tuple-element.23), channel_id=1, source_target_pairs={{0,29},{1,28},{2,31},{3,30},{4,1},{5,0},{6,3},{7,2},{8,5},{9,4},{1... | collective-permute-start | bytes 221192 | tf_op jit(solution)/shard_map/ppermute | solution.py:366
  20.1 0.0 collective-permute-done.2.refs_3_
  20.1 1.1 %collective-permute-start.7 = (bf16[144,256]{1,0:T(8,128)(2,1)}, bf16[144,256]{1,0:T(8,128)(2,1)S(1)}, u32[]{:S(2)}, u32[]{:S(2)}) collective-permute-start(bf16[144,256]{1,0:T(8,128)(2,1)} %get-tuple-element.24), channel_id=1, source_target_pairs={{0,30},{1,31},{2,0},{3,1},{4,2},{5,3},{6,4},{7,5},{8,6},{9,7},{10,... | collective-permute-start | bytes 221192 | tf_op jit(solution)/shard_map/ppermute | solution.py:366
  21.2 0.5 %collective-permute-done.3.refs_4_ = bf16[144,256]{1,0:T(8,128)(2,1)S(1)} collective-permute-done((bf16[144,256]{1,0:T(8,128)(2,1)}, bf16[144,256]{1,0:T(8,128)(2,1)S(1)}, u32[]{:S(2)}, u32[]{:S(2)}) %collective-permute-start.3) | collective-permute-done | bytes 73760 | tf_op jit(solution)/shard_map/ppermute | solution.py:366
  21.7 0.0 copy-start.1
  21.7 0.9 %collective-permute-start.8 = (bf16[144,256]{1,0:T(8,128)(2,1)}, bf16[144,256]{1,0:T(8,128)(2,1)S(1)}, u32[]{:S(2)}, u32[]{:S(2)}) collective-permute-start(bf16[144,256]{1,0:T(8,128)(2,1)} %get-tuple-element.25), channel_id=1, source_target_pairs={{0,31},{1,30},{2,1},{3,0},{4,3},{5,2},{6,5},{7,4},{8,7},{9,6},{10,... | collective-permute-start | bytes 221192 | tf_op jit(solution)/shard_map/ppermute | solution.py:366
  22.6 0.0 collective-permute-done.4.refs_5_
  22.6 0.0 copy-done.1
  22.6 0.9 %copy-done = bf16[144,256]{1,0:T(8,128)(2,1)S(1)} copy-done((bf16[144,256]{1,0:T(8,128)(2,1)S(1)}, bf16[144,256]{1,0:T(8,128)(2,1)}, u32[]{:S(2)}) %copy-start) | copy-done | bytes 73752
  23.4 0.9 %combine_early.1 = (f32[192,256]{1,0:T(8,128)S(1)}, f32[16,256]{1,0:T(8,128)S(1)}) custom-call(f32[6]{0:T(128)S(1)} %copy-done.1, bf16[144,256]{1,0:T(8,128)(2,1)S(1)} %copy-done, bf16[144,256]{1,0:T(8,128)(2,1)S(1)} %collective-permute-done.refs_1_, bf16[144,256]{1,0:T(8,128)(2,1)S(1)} %collective-permute-done.1.refs_2_, ...), custom_call_target="tpu_custom_call" | custom-call | tf_op jit(solution)/shard_map/combine_early/pallas_call | solution.py:371
  24.3 0.0 collective-permute-done.5.refs_0_
  24.3 0.8 %collective-permute-done.6.refs_1_ = bf16[144,256]{1,0:T(8,128)(2,1)S(1)} collective-permute-done((bf16[144,256]{1,0:T(8,128)(2,1)}, bf16[144,256]{1,0:T(8,128)(2,1)S(1)}, u32[]{:S(2)}, u32[]{:S(2)}) %collective-permute-start.6) | collective-permute-done | bytes 73760 | tf_op jit(solution)/shard_map/ppermute | solution.py:366
  25.1 0.0 collective-permute-done.7.refs_2_
  25.1 0.8 %collective-permute-done.8.refs_3_ = bf16[144,256]{1,0:T(8,128)(2,1)S(1)} collective-permute-done((bf16[144,256]{1,0:T(8,128)(2,1)}, bf16[144,256]{1,0:T(8,128)(2,1)S(1)}, u32[]{:S(2)}, u32[]{:S(2)}) %collective-permute-start.8) | collective-permute-done | bytes 73760 | tf_op jit(solution)/shard_map/ppermute | solution.py:366
  25.9 1.0 %combine.1 = (f32[6,32,256]{2,1,0:T(8,128)}, f32[32,256]{1,0:T(8,128)}) custom-call(f32[192,256]{1,0:T(8,128)S(1)} %get-tuple-element.20.totals_ref, f32[16,256]{1,0:T(8,128)S(1)} %get-tuple-element.21.rows_ref, bf16[144,256]{1,0:T(8,128)(2,1)S(1)} %collective-permute-done.5.refs_0_, bf16[144,256]{1,0:T(8,128)(2,1)S(1)} %collective-permute-done.6.refs_1_, ...), custom_call_target="tpu_custom_call" | custom-call | tf_op jit(solution)/shard_map/combine/pallas_call | solution.py:382
  (1 shorter events, 0.0 us)
Async XLA Ops:
  7.6 8.8 %collective-permute-start = (bf16[144,256]{1,0:T(8,128)(2,1)}, bf16[144,256]{1,0:T(8,128)(2,1)S(1)}, u32[]{:S(2)}, u32[]{:S(2)}) collective-permute-start(bf16[144,256]{1,0:T(8,128)(2,1)} %get-tuple-element.15), channel_id=1, source_target_pairs={{0,2},{1,3},{2,4},{3,5},{4,6},{5,7},{6,8},{7,9},{8,10},{9,11},{10,... | collective-permute-start | bytes 221192 | tf_op jit(solution)/shard_map/ppermute | solution.py:366
  8.1 11.5 %collective-permute-start.1 = (bf16[144,256]{1,0:T(8,128)(2,1)}, bf16[144,256]{1,0:T(8,128)(2,1)S(1)}, u32[]{:S(2)}, u32[]{:S(2)}) collective-permute-start(bf16[144,256]{1,0:T(8,128)(2,1)} %get-tuple-element.16), channel_id=1, source_target_pairs={{0,3},{1,2},{2,5},{3,4},{4,7},{5,6},{6,9},{7,8},{8,11},{9,10},{10,... | collective-permute-start | bytes 221192 | tf_op jit(solution)/shard_map/ppermute | solution.py:366
  11.9 8.2 %collective-permute-start.2 = (bf16[144,256]{1,0:T(8,128)(2,1)}, bf16[144,256]{1,0:T(8,128)(2,1)S(1)}, u32[]{:S(2)}, u32[]{:S(2)}) collective-permute-start(bf16[144,256]{1,0:T(8,128)(2,1)} %get-tuple-element.17), channel_id=1, source_target_pairs={{0,4},{1,5},{2,6},{3,7},{4,8},{5,9},{6,10},{7,11},{8,12},{9,13},{1... | collective-permute-start | bytes 221192 | tf_op jit(solution)/shard_map/ppermute | solution.py:366
  13.4 8.3 %collective-permute-start.3 = (bf16[144,256]{1,0:T(8,128)(2,1)}, bf16[144,256]{1,0:T(8,128)(2,1)S(1)}, u32[]{:S(2)}, u32[]{:S(2)}) collective-permute-start(bf16[144,256]{1,0:T(8,128)(2,1)} %get-tuple-element.18), channel_id=1, source_target_pairs={{0,5},{1,4},{2,7},{3,6},{4,9},{5,8},{6,11},{7,10},{8,13},{9,12},{1... | collective-permute-start | bytes 221192 | tf_op jit(solution)/shard_map/ppermute | solution.py:366
  14.8 7.7 %collective-permute-start.4 = (bf16[144,256]{1,0:T(8,128)(2,1)}, bf16[144,256]{1,0:T(8,128)(2,1)S(1)}, u32[]{:S(2)}, u32[]{:S(2)}) collective-permute-start(bf16[144,256]{1,0:T(8,128)(2,1)} %get-tuple-element.19), channel_id=1, source_target_pairs={{0,1},{1,0},{2,3},{3,2},{4,5},{5,4},{6,7},{7,6},{8,9},{9,8},{10,11... | collective-permute-start | bytes 221192 | tf_op jit(solution)/shard_map/ppermute | solution.py:366
  16.4 7.9 %collective-permute-start.5 = (bf16[144,256]{1,0:T(8,128)(2,1)}, bf16[144,256]{1,0:T(8,128)(2,1)S(1)}, u32[]{:S(2)}, u32[]{:S(2)}) collective-permute-start(bf16[144,256]{1,0:T(8,128)(2,1)} %get-tuple-element.22), channel_id=1, source_target_pairs={{0,28},{1,29},{2,30},{3,31},{4,0},{5,1},{6,2},{7,3},{8,4},{9,5},{1... | collective-permute-start | bytes 221192 | tf_op jit(solution)/shard_map/ppermute | solution.py:366
  19.6 5.5 %collective-permute-start.6 = (bf16[144,256]{1,0:T(8,128)(2,1)}, bf16[144,256]{1,0:T(8,128)(2,1)S(1)}, u32[]{:S(2)}, u32[]{:S(2)}) collective-permute-start(bf16[144,256]{1,0:T(8,128)(2,1)} %get-tuple-element.23), channel_id=1, source_target_pairs={{0,29},{1,28},{2,31},{3,30},{4,1},{5,0},{6,3},{7,2},{8,5},{9,4},{1... | collective-permute-start | bytes 221192 | tf_op jit(solution)/shard_map/ppermute | solution.py:366
  20.1 5.0 %collective-permute-start.7 = (bf16[144,256]{1,0:T(8,128)(2,1)}, bf16[144,256]{1,0:T(8,128)(2,1)S(1)}, u32[]{:S(2)}, u32[]{:S(2)}) collective-permute-start(bf16[144,256]{1,0:T(8,128)(2,1)} %get-tuple-element.24), channel_id=1, source_target_pairs={{0,30},{1,31},{2,0},{3,1},{4,2},{5,3},{6,4},{7,5},{8,6},{9,7},{10,... | collective-permute-start | bytes 221192 | tf_op jit(solution)/shard_map/ppermute | solution.py:366
  21.7 0.9 %copy-start.1 = (f32[6]{0:T(128)S(1)}, f32[6]{0:T(128)}, u32[]{:S(2)}) copy-start(f32[6]{0:T(128)} %weight_ref.1) | copy-start | bytes 76
  21.7 4.2 %collective-permute-start.8 = (bf16[144,256]{1,0:T(8,128)(2,1)}, bf16[144,256]{1,0:T(8,128)(2,1)S(1)}, u32[]{:S(2)}, u32[]{:S(2)}) collective-permute-start(bf16[144,256]{1,0:T(8,128)(2,1)} %get-tuple-element.25), channel_id=1, source_target_pairs={{0,31},{1,30},{2,1},{3,0},{4,3},{5,2},{6,5},{7,4},{8,7},{9,6},{10,... | collective-permute-start | bytes 221192 | tf_op jit(solution)/shard_map/ppermute | solution.py:366
  22.6 0.9 %copy-start = (bf16[144,256]{1,0:T(8,128)(2,1)S(1)}, bf16[144,256]{1,0:T(8,128)(2,1)}, u32[]{:S(2)}) copy-start(bf16[144,256]{1,0:T(8,128)(2,1)} %get-tuple-element.14.refs_0_) | copy-start | bytes 221188

commit v8 on v7

--- a/solution.py
+++ b/solution.py
@@ -37,7 +37,8 @@
     tiles_hbm,
     *rest,
 ):
-    messages = rest[: SPREAD * groups]
+    far = rest[:groups]
+    cross, kept = rest[groups : groups + 2]
     (
         table_ref,
         weight_ref,
@@ -53,7 +54,7 @@
         extra,
         arrival,
         ready,
-    ) = rest[SPREAD * groups :]
+    ) = rest[groups + 2 :]
     visits = band_ref.shape[0]
     tile_count, rows, width = tiles_ref.shape
     per_visit = tile_count // visits
@@ -63,6 +64,7 @@
     slot = slot_rows(row_share)
     owner = lax.axis_index("ra")
     group = lax.axis_index("band")
+    way = 2 * lax.rem(owner, 2) - 1
 
     small = [
         pltpu.make_async_copy(source, target, ready.at[place])
@@ -208,56 +210,76 @@
                 axis=1,
             )
 
-        for bucket in range(SPREAD):
-            for turn in range(groups):
-                part = lax.rem(group + turn, groups)
-                own = sums[bucket, pl.ds(pl.multiple_of(part * row_share, row_share), row_share), :]
-                if slot > row_share:
-                    own = jnp.concatenate(
-                        [own, jnp.zeros((slot - row_share, PW), jnp.float32)], axis=0
-                    )
-                messages[bucket * groups + turn][
-                    pl.ds(pl.multiple_of(visit * slot, slot), slot), :
-                ] = own.astype(jnp.bfloat16)
+        for turn in range(groups):
+            part = lax.rem(group + turn, groups)
+            own = sums[
+                REACH + 2 * way, pl.ds(pl.multiple_of(part * row_share, row_share), row_share), :
+            ]
+            if slot > row_share:
+                own = jnp.concatenate(
+                    [own, jnp.zeros((slot - row_share, PW), jnp.float32)], axis=0
+                )
+            far[turn][pl.ds(pl.multiple_of(visit * slot, slot), slot), :] = own.astype(
+                jnp.bfloat16
+            )
+        held = pl.ds(pl.multiple_of(visit * rows, rows), rows)
+        cross[0, held, :] = sums[REACH - 2 * way].astype(jnp.bfloat16)
+        cross[1, held, :] = sums[REACH - way].astype(jnp.bfloat16)
+        kept[0, held, :] = sums[REACH + way].astype(jnp.bfloat16)
+        kept[1, held, :] = sums[REACH].astype(jnp.bfloat16)
         return unused
 
     lax.fori_loop(0, visits, one_visit, 0)
 
     row = iota((EXTRA, PW), 0)
     lane = iota((1, PW), 1)
-    by_row = jnp.zeros((1, PW), jnp.float32)
-    by_weight = jnp.full((1, PW), -1.0, jnp.float32)
-    for visit in range(visits):
-        band = band_ref[visit].astype(jnp.float32)
-        by_row = jnp.where(lane // slot == visit, band, by_row)
-        by_weight = jnp.where(
-            (lane < 2 * visits) & (lax.rem(lane, visits) == visit), band, by_weight
-        )
-    for bucket in range(SPREAD):
+
+    def spread_bands(visit_of, limit):
+        line = jnp.full((1, PW), -1.0, jnp.float32)
+        for visit in range(visits):
+            line = jnp.where(
+                (lane < limit) & (visit_of == visit), band_ref[visit].astype(jnp.float32), line
+            )
+        return line
+
+    by_slot = spread_bands(lane // slot, visits * slot)
+    by_rows = spread_bands(lane // rows, visits * rows)
+    by_weight = spread_bands(lax.rem(lane, visits), 2 * visits)
+
+    def footer(bucket, by_row):
         held = extra[bucket]
         high = held.astype(jnp.bfloat16).astype(jnp.float32)
         low = jnp.concatenate([held[-visits:], (held - high)[:-visits]], axis=0)
         mixed = jnp.where((row >= visits) & (row < 2 * visits), low, high)
         mixed = jnp.where(row == 2 * visits, by_row, mixed)
-        mixed = jnp.where(row == 2 * visits + 1, by_weight, mixed).astype(jnp.bfloat16)
-        for turn in range(groups):
-            messages[bucket * groups + turn][slot * visits :, :] = mixed
-
-
-def add_messages(count, row_share, messages):
-    slot = slot_rows(row_share)
-    depth = slot * count
+        return jnp.where(row == 2 * visits + 1, by_weight, mixed).astype(jnp.bfloat16)
+
+    for turn in range(groups):
+        far[turn][slot * visits :, :] = footer(REACH + 2 * way, by_slot)
+    cross[0, rows * visits :, :] = footer(REACH - 2 * way, by_rows)
+    cross[1, rows * visits :, :] = footer(REACH - way, by_rows)
+    kept[0, rows * visits :, :] = footer(REACH + way, by_rows)
+    kept[1, rows * visits :, :] = footer(REACH, by_rows)
+
+
+def add_messages(count, span, row_share, parts, messages):
+    depth = span * count
     line = lax.broadcasted_iota(jnp.int32, (row_share, depth), 0)
-    lane = lax.broadcasted_iota(jnp.int32, (row_share, depth), 1)
-    same = (lax.rem(lane, slot) == line).astype(jnp.float32)
+    lane = lax.rem(lax.broadcasted_iota(jnp.int32, (row_share, depth), 1), span)
+    same = [(lane == line + part * row_share).astype(jnp.float32) for part in range(parts)]
     band_line = lax.broadcasted_iota(jnp.int32, (8, EXTRA), 0).astype(jnp.float32)
-    totals = jnp.zeros((BANDS * row_share, PW), jnp.float32)
+    totals = jnp.zeros((parts * BANDS * row_share, PW), jnp.float32)
     weight_totals = jnp.zeros((8, PW), jnp.float32)
     for message in messages:
         extra = message[depth:, :]
         bands = extra[2 * count : 2 * count + 2].astype(jnp.float32)
         pick = jnp.concatenate(
-            [jnp.where(bands[:1, :depth] == float(b), same, 0.0) for b in range(BANDS)], axis=0
+            [
+                jnp.where(bands[:1, :depth] == float(b), same[part], 0.0)
+                for part in range(parts)
+                for b in range(BANDS)
+            ],
+            axis=0,
         ).astype(jnp.bfloat16)
         totals += jnp.dot(pick, message[:depth, :], preferred_element_type=jnp.float32)
         pick = (bands[1:, :EXTRA] == band_line).astype(jnp.bfloat16)
@@ -265,9 +287,52 @@
     return totals, weight_totals
 
 
-def early_kernel(count, row_share, weight_ref, *refs):
+def keep_kernel(count, groups, kept_ref, totals_ref, weights_ref):
+    span = (kept_ref.shape[1] - EXTRA) // count
+    for place in range(2):
+        totals_ref[place], weights_ref[place] = add_messages(
+            count, span, span // groups, groups, (kept_ref.at[place],)
+        )
+
+
+def merge_kernel(count, groups, totals_ref, weights_ref, cross_ref, *refs):
+    near = refs[:groups]
+    home = refs[groups : 2 * groups - 1]
+    own_ref, own_weight_ref, held = refs[2 * groups - 1 :]
+    span = (cross_ref.shape[1] - EXTRA) // count
+    row_share = span // groups
+    depth = BANDS * row_share
+    group = lax.axis_index("band")
+    for place, messages in enumerate((near, home)):
+        totals, weight_totals = add_messages(
+            count, span, row_share, groups, (cross_ref.at[place],)
+        )
+        held[place] = totals + totals_ref[place]
+        weight_totals += weights_ref[place]
+        high = weight_totals.astype(jnp.bfloat16).astype(jnp.float32)
+        footer = jnp.concatenate([high, weight_totals - high], axis=0).astype(jnp.bfloat16)
+        for turn, message in enumerate(messages, groups - len(messages)):
+            part = lax.rem(group + turn, groups)
+            message[:depth, :] = held[
+                place, pl.ds(pl.multiple_of(part * depth, depth), depth), :
+            ].astype(jnp.bfloat16)
+            message[depth:, :] = footer
+    own_ref[...] = held[1, pl.ds(pl.multiple_of(group * depth, depth), depth), :]
+    own_weight_ref[...] = weight_totals
+
+
+def early_kernel(weight_ref, own_ref, own_weight_ref, *refs):
+    messages = refs[:-2]
     totals_ref, rows_ref = refs[-2:]
-    totals_ref[...], rows_ref[:8] = add_messages(count, row_share, refs[:-2])
+    depth = own_ref.shape[0]
+    totals = own_ref[...]
+    weight_totals = own_weight_ref[...]
+    for message in messages:
+        totals += message[:depth, :].astype(jnp.float32)
+        footer = message[depth:, :].astype(jnp.float32)
+        weight_totals += footer[:8] + footer[8:]
+    totals_ref[...] = totals
+    rows_ref[:8] = weight_totals
     line = lax.broadcasted_iota(jnp.int32, (8, PW), 0)
     band_weights = jnp.zeros((8, PW), jnp.float32)
     for b in range(BANDS):
@@ -278,14 +343,12 @@
 def combine_kernel(count, totals_ref, rows_ref, *refs):
     coadd_ref, detection_ref = refs[-2:]
     row_share = coadd_ref.shape[1]
-    totals, weight_totals = add_messages(count, row_share, refs[:-2])
+    totals, weight_totals = add_messages(count, slot_rows(row_share), row_share, 1, refs[:-2])
     weight_totals = jnp.maximum(weight_totals + rows_ref[:8], 1.0)
     detection = jnp.zeros((row_share, PW), jnp.float32)
     for b in range(BANDS):
-        held = pl.ds(b * row_share, row_share)
-        coadd = (totals[b * row_share : (b + 1) * row_share] + totals_ref[held, :]) / (
-            weight_totals[b : b + 1]
-        )
+        held = slice(b * row_share, (b + 1) * row_share)
+        coadd = (totals[held] + totals_ref[held, :]) / weight_totals[b : b + 1]
         coadd_ref[b] = coadd
         detection += rows_ref[8 + b : 9 + b] * coadd
     detection_ref[...] = detection
@@ -311,16 +374,19 @@
     groups = lax.axis_size("band")
     row_share = rows // groups
     slot = slot_rows(row_share)
-    length = visits * slot + EXTRA
+    far_shape = jax.ShapeDtypeStruct((visits * slot + EXTRA, PW), jnp.bfloat16)
+    pair_shape = jax.ShapeDtypeStruct((2, visits * rows + EXTRA, PW), jnp.bfloat16)
+    band_shape = jax.ShapeDtypeStruct((BANDS * row_share + EXTRA, PW), jnp.bfloat16)
+    total_shape = jax.ShapeDtypeStruct((BANDS * row_share, PW), jnp.float32)
     smem = pl.BlockSpec(memory_space=pltpu.SMEM)
 
     vmem = pl.BlockSpec(memory_space=pltpu.VMEM)
     anywhere = pl.BlockSpec(memory_space=pl.ANY)
-    messages = pl.pallas_call(
+    *far, cross, kept = pl.pallas_call(
         functools.partial(match_kernel, patches, groups),
         in_specs=[smem] * 4 + [anywhere] * 5,
-        out_specs=[vmem] * (SPREAD * groups),
-        out_shape=[jax.ShapeDtypeStruct((length, PW), jnp.bfloat16)] * (SPREAD * groups),
+        out_specs=[vmem] * (groups + 2),
+        out_shape=[far_shape] * groups + [pair_shape] * 2,
         scratch_shapes=[
             pltpu.VMEM(coeff_table.shape[::-1], jnp.float32),
             pltpu.VMEM((1, tile_count), jnp.bfloat16),
@@ -351,37 +417,54 @@
         tiles,
     )
 
-    order = [(d, t) for d in range(1, REACH + 1) for t in range(groups)]
-    order += [(0, t) for t in range(1, groups)]
-    early = len(order)
-    order += [(d, t) for d in range(-REACH, 0) for t in range(groups)]
-    arrived = []
-    for distance, turn in order:
+    def send(message, goal, turn):
         route = [
-            (o * groups + g, (o + distance) % patches * groups + (g + turn) % groups)
+            (o * groups + g, goal(o) % patches * groups + (g + turn) % groups)
             for o in range(patches)
             for g in range(groups)
         ]
-        arrived.append(
-            lax.ppermute(messages[(distance + REACH) * groups + turn], ("ra", "band"), route)
-        )
+        return lax.ppermute(message, ("ra", "band"), route)
+
+    def onward(distance):
+        return lambda o: o + distance if o % 2 else o - distance
 
     params = pltpu.CompilerParams(vmem_limit_bytes=40 * 1024 * 1024)
-    first = [messages[REACH * groups]] + arrived[:early]
-    totals = pl.pallas_call(
-        functools.partial(early_kernel, visits, row_share),
-        in_specs=[smem] + [vmem] * len(first),
+    cross = send(cross, onward(-1), 0)
+    far = [send(far[turn], onward(2), turn) for turn in range(groups)]
+    kept = pl.pallas_call(
+        functools.partial(keep_kernel, visits, groups),
+        in_specs=[vmem],
         out_specs=(vmem, vmem),
         out_shape=(
-            jax.ShapeDtypeStruct((BANDS * row_share, PW), jnp.float32),
-            jax.ShapeDtypeStruct((16, PW), jnp.float32),
+            jax.ShapeDtypeStruct((2, BANDS * rows, PW), jnp.float32),
+            jax.ShapeDtypeStruct((2, 8, PW), jnp.float32),
         ),
         compiler_params=params,
+        name="keep",
+    )(kept)
+    *merged, own, own_weight = pl.pallas_call(
+        functools.partial(merge_kernel, visits, groups),
+        in_specs=[vmem] * 3,
+        out_specs=[vmem] * (2 * groups + 1),
+        out_shape=[band_shape] * (2 * groups - 1)
+        + [total_shape, jax.ShapeDtypeStruct((8, PW), jnp.float32)],
+        scratch_shapes=[pltpu.VMEM((2, BANDS * rows, PW), jnp.float32)],
+        compiler_params=params,
+        name="merge",
+    )(*kept, cross)
+    near = [send(merged[turn], onward(1), turn) for turn in range(groups)]
+    home = [send(merged[groups - 1 + turn], onward(0), turn) for turn in range(1, groups)]
+    totals = pl.pallas_call(
+        early_kernel,
+        in_specs=[smem] + [vmem] * (2 * groups + 1),
+        out_specs=(vmem, vmem),
+        out_shape=(total_shape, jax.ShapeDtypeStruct((16, PW), jnp.float32)),
+        compiler_params=params,
         name="combine_early",
-    )(band_weight, *first)
+    )(band_weight, own, own_weight, *near, *home)
     return pl.pallas_call(
         functools.partial(combine_kernel, visits),
-        in_specs=[vmem] * (len(arrived) - early + 2),
+        in_specs=[vmem] * (groups + 2),
         out_specs=(vmem, vmem),
         out_shape=(
             jax.ShapeDtypeStruct((BANDS, row_share, PW), jnp.float32),
@@ -389,7 +472,7 @@
         ),
         compiler_params=params,
         name="combine",
-    )(*totals, *arrived[early:])
+    )(*totals, *far)
 
 
 def solution(mesh):

time: 27.2 us -> 27.3 us (level)
  starting transfers between devices: 14.4 us -> 12.1 us
  waiting for transfers between devices: 2.07 us -> 3.51 us
  local copies, waits for them, and re-layouts: 0.89 us -> 1.62 us
  Pallas kernels: 8.82 us -> 9.16 us
    ppermute x9 -> x6, starting transfers between devices: 14.4 us -> 12.1 us  [send(): return lax.ppermute(message, ('ra', 'band'), route)]
    ppermute x9 -> x6, waiting for transfers between devices: 2.07 us -> 3.51 us  [send(): return lax.ppermute(message, ('ra', 'band'), route)]
    unnamed x4 -> x8, local copies, waits for them, and re-layouts: 0.89 us -> 1.62 us
    pallas_call x1 -> x3, Pallas kernels: 0.87 us -> 1.27 us  [the longest x1 0.59 us: local(): pl.pallas_call(early_kernel, in_specs=[smem] + [vmem] * (2 * groups + 1),...]
  transfers between devices with their start and end apart: 9 -> 6, of which waited for: 3 -> 3; matrix products, arithmetic and copies ran while one was open for 0% -> 0% of each run, Pallas kernels for 3% -> 3%
where the time goes in v8:
time: 27.3 us; the launch traced here: 27 us
  starting transfers between devices  12.1 us (44%)
  Pallas kernels  9.16 us (34%)
  waiting for transfers between devices  3.51 us (13%)
  local copies, waits for them, and re-layouts  1.62 us (6%)
  between operations  0.67 us (2%)
    ppermute x6, starting transfers between devices, send(): return lax.ppermute(message, ('ra', 'band'), route)  12.1 us
    pallas_call x1, Pallas kernels, local(): pl.pallas_call(functools.partial(match_kernel, patches, groups), in_specs...  6.98 us
    ppermute x6, waiting for transfers between devices, send(): return lax.ppermute(message, ('ra', 'band'), route)  3.51 us
    unnamed x8, local copies, waits for them, and re-layouts  1.62 us
    pallas_call x1, Pallas kernels, local(): pl.pallas_call(functools.partial(combine_kernel, visits), in_specs=[vmem]...  0.91 us
    pallas_call x1, Pallas kernels, local(): pl.pallas_call(early_kernel, in_specs=[smem] + [vmem] * (2 * groups + 1),...  0.59 us
  transfers between devices with their start and end apart: 6, of which 3 were waited for; matrix products, arithmetic and copies ran while one was open for 0% of the time, Pallas kernels for 3%

profile of v8, /device:TPU:0, one launch (start us, length us, event | category | flops | bytes accessed | tf_op | source)
XLA Modules:
  0.0 27.0 jit_solution(5566067475104781575)
XLA Ops:
  0.6 7.0 %match_and_sum.1 = (bf16[144,256]{1,0:T(8,128)(2,1)}, bf16[144,256]{1,0:T(8,128)(2,1)}, bf16[2,272,256]{2,1,0:T(8,128)(2,1)}, bf16[2,272,256]{2,1,0:T(8,128)(2,1)}) custom-call(s32[32]{0:T(128)} %patch_ref.1, s32[32]{0:T(128)} %offset_ref.1, s32[32]{0:T(128)} %index_ref.1, s32[4]{0:T(128)} %band_ref.1, f32[21,64]{1,0:T(8,128)} %bitcast.2, ...), custom_call_target="tpu_custom_call" | custom-call | tf_op jit(solution)/shard_map/match_and_sum/pallas_call | solution.py:385
  7.6 0.5 %collective-permute-start = (bf16[2,272,256]{2,1,0:T(8,128)(2,1)}, bf16[2,272,256]{2,1,0:T(8,128)(2,1)S(1)}, u32[]{:S(2)}, u32[]{:S(2)}) collective-permute-start(bf16[2,272,256]{2,1,0:T(8,128)(2,1)} %get-tuple-element.18), channel_id=1, source_target_pairs={{0,2},{1,3},{2,0},{3,1},{4,6},{5,7},{6,4},{7,5},{8,10},{9,11},{10,... | collective-permute-start | bytes 835592 | tf_op jit(solution)/shard_map/ppermute | solution.py:426
  8.1 0.0 copy-start
  8.1 1.0 %copy-done = bf16[2,272,256]{2,1,0:T(8,128)(2,1)S(1)} copy-done((bf16[2,272,256]{2,1,0:T(8,128)(2,1)S(1)}, bf16[2,272,256]{2,1,0:T(8,128)(2,1)}, u32[]{:S(2)}) %copy-start) | copy-done | bytes 278552
  9.1 0.3 keep.1
  9.4 0.2 collective-permute-done.cross_ref
  9.5 0.0 copy-start.3
  9.5 0.0 copy-start.2
  9.5 0.4 %merge.1 = (bf16[208,256]{1,0:T(8,128)(2,1)S(1)}, bf16[208,256]{1,0:T(8,128)(2,1)S(1)}, bf16[208,256]{1,0:T(8,128)(2,1)S(1)}, f32[192,256]{1,0:T(8,128)S(1)}, f32[8,256]{1,0:T(8,128)S(1)}) custom-call(f32[2,384,256]{2,1,0:T(8,128)S(1)} %get-tuple-element.16.totals_ref, f32[2,8,256]{2,1,0:T(8,128)S(1)} %get-tuple-element.17.weights_ref, ...), custom_call_target="tpu_custom_call" | custom-call | tf_op jit(solution)/shard_map/merge/pallas_call | solution.py:445
  10.0 5.7 %collective-permute-start.1 = (bf16[208,256]{1,0:T(8,128)(2,1)S(1)}, bf16[208,256]{1,0:T(8,128)(2,1)S(1)}, u32[]{:S(2)}, u32[]{:S(2)}) collective-permute-start(bf16[208,256]{1,0:T(8,128)(2,1)S(1)} %get-tuple-element.21), channel_id=1, source_target_pairs={{0,30},{1,31},{2,4},{3,5},{4,2},{5,3},{6,8},{7,9},{8,6},{9,7},{10,... | collective-permute-start | bytes 319496 | tf_op jit(solution)/shard_map/ppermute | solution.py:426
  15.7 1.1 %collective-permute-start.2 = (bf16[208,256]{1,0:T(8,128)(2,1)S(1)}, bf16[208,256]{1,0:T(8,128)(2,1)S(1)}, u32[]{:S(2)}, u32[]{:S(2)}) collective-permute-start(bf16[208,256]{1,0:T(8,128)(2,1)S(1)} %get-tuple-element.22), channel_id=1, source_target_pairs={{0,31},{1,30},{2,5},{3,4},{4,3},{5,2},{6,9},{7,8},{8,7},{9,6},{10,... | collective-permute-start | bytes 319496 | tf_op jit(solution)/shard_map/ppermute | solution.py:426
  16.8 0.4 %collective-permute-start.3 = (bf16[208,256]{1,0:T(8,128)(2,1)S(1)}, bf16[208,256]{1,0:T(8,128)(2,1)S(1)}, u32[]{:S(2)}, u32[]{:S(2)}) collective-permute-start(bf16[208,256]{1,0:T(8,128)(2,1)S(1)} %get-tuple-element.23), channel_id=1, source_target_pairs={{0,1},{1,0},{2,3},{3,2},{4,5},{5,4},{6,7},{7,6},{8,9},{9,8},{10,11... | collective-permute-start | bytes 319496 | tf_op jit(solution)/shard_map/ppermute | solution.py:426
  17.2 0.0 copy-done.3
  17.2 1.9 %collective-permute-start.4 = (bf16[144,256]{1,0:T(8,128)(2,1)S(1)}, bf16[144,256]{1,0:T(8,128)(2,1)S(1)}, u32[]{:S(2)}, u32[]{:S(2)}) collective-permute-start(bf16[144,256]{1,0:T(8,128)(2,1)S(1)} %copy-done.3), channel_id=1, source_target_pairs={{0,28},{1,29},{2,6},{3,7},{4,0},{5,1},{6,10},{7,11},{8,4},{9,5},{1... | collective-permute-start | bytes 221192 | tf_op jit(solution)/shard_map/ppermute | solution.py:426
  19.1 0.0 copy-done.2
  19.1 2.4 %collective-permute-start.5 = (bf16[144,256]{1,0:T(8,128)(2,1)S(1)}, bf16[144,256]{1,0:T(8,128)(2,1)S(1)}, u32[]{:S(2)}, u32[]{:S(2)}) collective-permute-start(bf16[144,256]{1,0:T(8,128)(2,1)S(1)} %copy-done.2), channel_id=1, source_target_pairs={{0,29},{1,28},{2,7},{3,6},{4,1},{5,0},{6,11},{7,10},{8,5},{9,4},{1... | collective-permute-start | bytes 221192 | tf_op jit(solution)/shard_map/ppermute | solution.py:426
  21.5 0.0 collective-permute-done.1.refs_0_
  21.5 2.0 %collective-permute-done.2.refs_1_ = bf16[208,256]{1,0:T(8,128)(2,1)S(1)} collective-permute-done((bf16[208,256]{1,0:T(8,128)(2,1)S(1)}, bf16[208,256]{1,0:T(8,128)(2,1)S(1)}, u32[]{:S(2)}, u32[]{:S(2)}) %collective-permute-start.2) | collective-permute-done | bytes 106528 | tf_op jit(solution)/shard_map/ppermute | solution.py:426
  23.5 0.0 collective-permute-done.3.refs_2_
  23.5 0.7 %copy-done.1 = f32[6]{0:T(128)S(1)} copy-done((f32[6]{0:T(128)S(1)}, f32[6]{0:T(128)}, u32[]{:S(2)}) %copy-start.1) | copy-done | bytes 48
  24.2 0.6 %combine_early.1 = (f32[192,256]{1,0:T(8,128)S(1)}, f32[16,256]{1,0:T(8,128)S(1)}) custom-call(f32[6]{0:T(128)S(1)} %copy-done.1, f32[192,256]{1,0:T(8,128)S(1)} %get-tuple-element.19.own_ref, f32[8,256]{1,0:T(8,128)S(1)} %get-tuple-element.20.own_weight_ref, bf16[208,256]{1,0:T(8,128)(2,1)S(1)} %collective-permute-done.1.refs_0_, ...), custom_call_target="tpu_custom_call" | custom-call | tf_op jit(solution)/shard_map/combine_early/pallas_call | solution.py:457
  24.8 0.0 collective-permute-done.4.refs_0_
  24.8 1.4 %collective-permute-done.5.refs_1_ = bf16[144,256]{1,0:T(8,128)(2,1)S(1)} collective-permute-done((bf16[144,256]{1,0:T(8,128)(2,1)S(1)}, bf16[144,256]{1,0:T(8,128)(2,1)S(1)}, u32[]{:S(2)}, u32[]{:S(2)}) %collective-permute-start.5) | collective-permute-done | bytes 73760 | tf_op jit(solution)/shard_map/ppermute | solution.py:426
  26.1 0.9 %combine.1 = (f32[6,32,256]{2,1,0:T(8,128)}, f32[32,256]{1,0:T(8,128)}) custom-call(f32[192,256]{1,0:T(8,128)S(1)} %get-tuple-element.24.totals_ref, f32[16,256]{1,0:T(8,128)S(1)} %get-tuple-element.25.rows_ref, bf16[144,256]{1,0:T(8,128)(2,1)S(1)} %collective-permute-done.4.refs_0_, bf16[144,256]{1,0:T(8,128)(2,1)S(1)} %collective-permute-done.5.refs_1_), custom_call_target="tpu_custom_call" | custom-call | tf_op jit(solution)/shard_map/combine/pallas_call | solution.py:465
  (1 shorter events, 0.0 us)
Async XLA Ops:
  7.6 1.9 %collective-permute-start = (bf16[2,272,256]{2,1,0:T(8,128)(2,1)}, bf16[2,272,256]{2,1,0:T(8,128)(2,1)S(1)}, u32[]{:S(2)}, u32[]{:S(2)}) collective-permute-start(bf16[2,272,256]{2,1,0:T(8,128)(2,1)} %get-tuple-element.18), channel_id=1, source_target_pairs={{0,2},{1,3},{2,0},{3,1},{4,6},{5,7},{6,4},{7,5},{8,10},{9,11},{10,... | collective-permute-start | bytes 835592 | tf_op jit(solution)/shard_map/ppermute | solution.py:426
  8.1 1.0 %copy-start = (bf16[2,272,256]{2,1,0:T(8,128)(2,1)S(1)}, bf16[2,272,256]{2,1,0:T(8,128)(2,1)}, u32[]{:S(2)}) copy-start(bf16[2,272,256]{2,1,0:T(8,128)(2,1)} %get-tuple-element.15.kept_ref) | copy-start | bytes 835588
  9.5 7.7 %copy-start.3 = (bf16[144,256]{1,0:T(8,128)(2,1)S(1)}, bf16[144,256]{1,0:T(8,128)(2,1)}, u32[]{:S(2)}) copy-start(bf16[144,256]{1,0:T(8,128)(2,1)} %get-tuple-element.26) | copy-start | bytes 221188
  9.5 9.6 %copy-start.2 = (bf16[144,256]{1,0:T(8,128)(2,1)S(1)}, bf16[144,256]{1,0:T(8,128)(2,1)}, u32[]{:S(2)}) copy-start(bf16[144,256]{1,0:T(8,128)(2,1)} %get-tuple-element.27) | copy-start | bytes 221188
  10.0 11.6 %collective-permute-start.1 = (bf16[208,256]{1,0:T(8,128)(2,1)S(1)}, bf16[208,256]{1,0:T(8,128)(2,1)S(1)}, u32[]{:S(2)}, u32[]{:S(2)}) collective-permute-start(bf16[208,256]{1,0:T(8,128)(2,1)S(1)} %get-tuple-element.21), channel_id=1, source_target_pairs={{0,30},{1,31},{2,4},{3,5},{4,2},{5,3},{6,8},{7,9},{8,6},{9,7},{10,... | collective-permute-start | bytes 319496 | tf_op jit(solution)/shard_map/ppermute | solution.py:426
  15.7 7.8 %collective-permute-start.2 = (bf16[208,256]{1,0:T(8,128)(2,1)S(1)}, bf16[208,256]{1,0:T(8,128)(2,1)S(1)}, u32[]{:S(2)}, u32[]{:S(2)}) collective-permute-start(bf16[208,256]{1,0:T(8,128)(2,1)S(1)} %get-tuple-element.22), channel_id=1, source_target_pairs={{0,31},{1,30},{2,5},{3,4},{4,3},{5,2},{6,9},{7,8},{8,7},{9,6},{10,... | collective-permute-start | bytes 319496 | tf_op jit(solution)/shard_map/ppermute | solution.py:426
  16.8 6.7 %collective-permute-start.3 = (bf16[208,256]{1,0:T(8,128)(2,1)S(1)}, bf16[208,256]{1,0:T(8,128)(2,1)S(1)}, u32[]{:S(2)}, u32[]{:S(2)}) collective-permute-start(bf16[208,256]{1,0:T(8,128)(2,1)S(1)} %get-tuple-element.23), channel_id=1, source_target_pairs={{0,1},{1,0},{2,3},{3,2},{4,5},{5,4},{6,7},{7,6},{8,9},{9,8},{10,11... | collective-permute-start | bytes 319496 | tf_op jit(solution)/shard_map/ppermute | solution.py:426
  17.2 7.5 %collective-permute-start.4 = (bf16[144,256]{1,0:T(8,128)(2,1)S(1)}, bf16[144,256]{1,0:T(8,128)(2,1)S(1)}, u32[]{:S(2)}, u32[]{:S(2)}) collective-permute-start(bf16[144,256]{1,0:T(8,128)(2,1)S(1)} %copy-done.3), channel_id=1, source_target_pairs={{0,28},{1,29},{2,6},{3,7},{4,0},{5,1},{6,10},{7,11},{8,4},{9,5},{1... | collective-permute-start | bytes 221192 | tf_op jit(solution)/shard_map/ppermute | solution.py:426
  19.1 7.0 %collective-permute-start.5 = (bf16[144,256]{1,0:T(8,128)(2,1)S(1)}, bf16[144,256]{1,0:T(8,128)(2,1)S(1)}, u32[]{:S(2)}, u32[]{:S(2)}) collective-permute-start(bf16[144,256]{1,0:T(8,128)(2,1)S(1)} %copy-done.2), channel_id=1, source_target_pairs={{0,29},{1,28},{2,7},{3,6},{4,1},{5,0},{6,11},{7,10},{8,5},{9,4},{1... | collective-permute-start | bytes 221192 | tf_op jit(solution)/shard_map/ppermute | solution.py:426
  23.5 0.7 %copy-start.1 = (f32[6]{0:T(128)S(1)}, f32[6]{0:T(128)}, u32[]{:S(2)}) copy-start(f32[6]{0:T(128)} %weight_ref.1) | copy-start | bytes 76

commit v9 on v4

--- a/solution.py
+++ b/solution.py
@@ -12,6 +12,7 @@
 REACH = 2
 SPREAD = 2 * REACH + 1
 EXTRA = 16
+DETECT = 10
 BLOCK = 32
 COARSE = 3
 VECTORS = 16
@@ -19,50 +20,43 @@
 LEAD = 6
 
 
-def slot_rows(row_share):
-    return max(row_share, 16)
-
-
 def match_kernel(
     patches,
-    groups,
     patch_ref,
     offset_ref,
     index_ref,
     band_ref,
+    detect_ref,
     table_hbm,
     weight_hbm,
     rowk_hbm,
     colk_hbm,
     tiles_hbm,
-    *rest,
-):
-    messages = rest[: SPREAD * groups]
-    (
-        table_ref,
-        weight_ref,
-        rowk_ref,
-        colk_ref,
-        tiles_ref,
-        kernels,
-        weights,
-        shifted,
-        toeplitz,
-        matches,
-        sums,
-        extra,
-        arrival,
-        ready,
-    ) = rest[SPREAD * groups :]
+    far,
+    cross,
+    kept,
+    table_ref,
+    weight_ref,
+    rowk_ref,
+    colk_ref,
+    tiles_ref,
+    kernels,
+    weights,
+    shifted,
+    toeplitz,
+    matches,
+    sums,
+    extra,
+    arrival,
+    ready,
+    ):
     visits = band_ref.shape[0]
     tile_count, rows, width = tiles_ref.shape
     per_visit = tile_count // visits
     basis, taps = rowk_ref.shape
     half = taps // 2
-    row_share = rows // groups
-    slot = slot_rows(row_share)
     owner = lax.axis_index("ra")
-    group = lax.axis_index("band")
+    way = 2 * lax.rem(owner, 2) - 1
 
     small = [
         pltpu.make_async_copy(source, target, ready.at[place])
@@ -208,56 +202,155 @@
                 axis=1,
             )
 
-        for bucket in range(SPREAD):
-            extra[bucket, pl.ds(2 * visits + visit, 1), :] = jnp.full(
-                (1, PW), band_ref[visit], jnp.int32
-            ).astype(jnp.float32)
-            for turn in range(groups):
-                part = lax.rem(group + turn, groups)
-                own = sums[bucket, pl.ds(pl.multiple_of(part * row_share, row_share), row_share), :]
-                if slot > row_share:
-                    own = jnp.concatenate(
-                        [own, jnp.zeros((slot - row_share, PW), jnp.float32)], axis=0
-                    )
-                messages[bucket * groups + turn][
-                    pl.ds(pl.multiple_of(visit * slot, slot), slot), :
-                ] = own.astype(jnp.bfloat16)
+        held = pl.ds(pl.multiple_of(visit * rows, rows), rows)
+        far[held, :] = sums[REACH + 2 * way].astype(jnp.bfloat16)
+        cross[0, held, :] = sums[REACH - 2 * way].astype(jnp.bfloat16)
+        cross[1, held, :] = sums[REACH - way].astype(jnp.bfloat16)
+        kept[0, held, :] = sums[REACH + way].astype(jnp.bfloat16)
+        kept[1, held, :] = sums[REACH].astype(jnp.bfloat16)
         return unused
 
     lax.fori_loop(0, visits, one_visit, 0)
 
     row = iota((EXTRA, PW), 0)
-    for bucket in range(SPREAD):
+    lane = iota((1, PW), 1)
+
+    def spread_bands(visit_of, limit):
+        line = jnp.full((1, PW), -1.0, jnp.float32)
+        for visit in range(visits):
+            line = jnp.where(
+                (lane < limit) & (visit_of == visit), band_ref[visit].astype(jnp.float32), line
+            )
+        return line
+
+    by_row = spread_bands(lane // rows, visits * rows)
+    by_weight = spread_bands(lax.rem(lane, visits), 2 * visits)
+    detect = jnp.zeros((1, PW), jnp.float32)
+    for b in range(BANDS):
+        detect = jnp.where(lane == b, detect_ref[b], detect)
+
+    def footer(bucket):
         held = extra[bucket]
         high = held.astype(jnp.bfloat16).astype(jnp.float32)
         low = jnp.concatenate([held[-visits:], (held - high)[:-visits]], axis=0)
-        mixed = jnp.where((row >= visits) & (row < 2 * visits), low, high).astype(jnp.bfloat16)
-        for turn in range(groups):
-            messages[bucket * groups + turn][slot * visits :, :] = mixed
-
-
-def combine_kernel(count, weight_ref, *refs):
-    messages = refs[:-2]
+        mixed = jnp.where((row >= visits) & (row < 2 * visits), low, high)
+        mixed = jnp.where(row == 2 * visits, by_row, mixed)
+        mixed = jnp.where(row == 2 * visits + 1, by_weight, mixed)
+        rest = detect
+        for place in range(DETECT, DETECT + 3):
+            piece = rest.astype(jnp.bfloat16).astype(jnp.float32)
+            rest = rest - piece
+            mixed = jnp.where(row == place, piece, mixed)
+        return mixed.astype(jnp.bfloat16)
+
+    far[rows * visits :, :] = footer(REACH + 2 * way)
+    cross[0, rows * visits :, :] = footer(REACH - 2 * way)
+    cross[1, rows * visits :, :] = footer(REACH - way)
+    kept[0, rows * visits :, :] = footer(REACH + way)
+    kept[1, rows * visits :, :] = footer(REACH)
+
+
+def add_message(count, groups, message):
+    depth = message.shape[0] - EXTRA
+    span = depth // count
+    row_share = span // groups
+    line = lax.broadcasted_iota(jnp.int32, (row_share, depth), 0)
+    lane = lax.rem(lax.broadcasted_iota(jnp.int32, (row_share, depth), 1), span)
+    band_line = lax.broadcasted_iota(jnp.int32, (8, EXTRA), 0).astype(jnp.float32)
+    extra = message[depth:, :]
+    bands = extra[2 * count : 2 * count + 2].astype(jnp.float32)
+    pick = jnp.concatenate(
+        [
+            jnp.where(
+                (lane == line + part * row_share) & (bands[:1, :depth] == float(b)), 1.0, 0.0
+            )
+            for part in range(groups)
+            for b in range(BANDS)
+        ],
+        axis=0,
+    ).astype(jnp.bfloat16)
+    totals = jnp.dot(pick, message[:depth, :], preferred_element_type=jnp.float32)
+    pick = (bands[1:, :EXTRA] == band_line).astype(jnp.bfloat16)
+    return totals, jnp.dot(pick, extra, preferred_element_type=jnp.float32)
+
+
+def add_banded(totals, weights, messages):
+    depth = totals.shape[0]
+    for message in messages:
+        totals += message[:depth, :].astype(jnp.float32)
+        footer = message[depth:, :].astype(jnp.float32)
+        weights += footer[:8] + footer[8:]
+    return totals, weights
+
+
+def write_banded(message, totals, weights):
+    depth = totals.shape[0]
+    high = weights.astype(jnp.bfloat16).astype(jnp.float32)
+    message[:depth, :] = totals.astype(jnp.bfloat16)
+    message[depth:, :] = jnp.concatenate([high, weights - high], axis=0).astype(jnp.bfloat16)
+
+
+def part_of(held, turn, groups):
+    depth = held.shape[0] // groups
+    part = lax.rem(lax.axis_index("band") + turn, groups)
+    return held[pl.ds(pl.multiple_of(part * depth, depth), depth), :]
+
+
+def keep_kernel(count, groups, kept_ref, totals_ref, weights_ref, detect_ref):
+    for place in range(2):
+        totals_ref[place], weights_ref[place] = add_message(count, groups, kept_ref.at[place])
+    extra = kept_ref[0, kept_ref.shape[1] - EXTRA :, :].astype(jnp.float32)
+    detect = extra[DETECT : DETECT + 1] + extra[DETECT + 1 : DETECT + 2]
+    detect += extra[DETECT + 2 : DETECT + 3]
+    line = lax.broadcasted_iota(jnp.int32, (8, PW), 0)
+    lane = lax.broadcasted_iota(jnp.int32, (8, PW), 1)
+    chosen = jnp.sum(jnp.where(line == lane, detect, 0.0), axis=1, keepdims=True)
+    detect_ref[...] = jnp.broadcast_to(chosen, (8, PW))
+
+
+def merge_kernel(count, groups, totals_ref, weights_ref, cross_ref, *refs):
+    messages = refs[: groups - 1]
+    near_ref, near_weight_ref, home_ref, home_weight_ref, held = refs[groups - 1 :]
+    totals, weights = add_message(count, groups, cross_ref.at[0])
+    held[...] = totals + totals_ref[0]
+    weights += weights_ref[0]
+    for turn, message in enumerate(messages, 1):
+        write_banded(message, part_of(held, turn, groups), weights)
+    near_ref[...] = part_of(held, 0, groups)
+    near_weight_ref[...] = weights
+    totals, weights = add_message(count, groups, cross_ref.at[1])
+    home_ref[...] = totals + totals_ref[1]
+    home_weight_ref[...] = weights + weights_ref[1]
+
+
+def forward_kernel(
+    count, groups, near_ref, near_weight_ref, home_ref, home_weight_ref, far_ref, *refs
+):
+    arrived = refs[: groups - 1]
+    onward_ref = refs[groups - 1]
+    messages = refs[groups : 2 * groups - 1]
+    own_ref, own_weight_ref, held = refs[2 * groups - 1 :]
+    totals, weights = add_banded(near_ref[...], near_weight_ref[...], arrived)
+    write_banded(onward_ref, totals, weights)
+    totals, weights = add_message(count, groups, far_ref)
+    held[...] = totals + home_ref[...]
+    weights += home_weight_ref[...]
+    for turn, message in enumerate(messages, 1):
+        write_banded(message, part_of(held, turn, groups), weights)
+    own_ref[...] = part_of(held, 0, groups)
+    own_weight_ref[...] = weights
+
+
+def combine_kernel(detect_ref, own_ref, own_weight_ref, *refs):
     coadd_ref, detection_ref = refs[-2:]
     row_share = coadd_ref.shape[1]
-    slot = slot_rows(row_share)
-    totals = [jnp.zeros((row_share, PW), jnp.float32) for _ in range(BANDS)]
-    weight_totals = [jnp.zeros((1, PW), jnp.float32) for _ in range(BANDS)]
-    for message in messages:
-        extra = message[slot * count :, :].astype(jnp.float32)
-        for visit in range(count):
-            band = extra[2 * count + visit : 2 * count + visit + 1]
-            weight = extra[visit : visit + 1] + extra[count + visit : count + visit + 1]
-            part = message[slot * visit : slot * (visit + 1), :].astype(jnp.float32)[:row_share]
-            for b in range(BANDS):
-                here = band == float(b)
-                totals[b] += jnp.where(here, part, 0.0)
-                weight_totals[b] += jnp.where(here, weight, 0.0)
+    totals, weights = add_banded(own_ref[...], own_weight_ref[...], refs[:-2])
+    weights = jnp.maximum(weights, 1.0)
     detection = jnp.zeros((row_share, PW), jnp.float32)
     for b in range(BANDS):
-        coadd = totals[b] / jnp.maximum(weight_totals[b], 1.0)
+        coadd = totals[b * row_share : (b + 1) * row_share] / weights[b : b + 1]
         coadd_ref[b] = coadd
-        detection += weight_ref[b] * coadd
+        detection += detect_ref[b : b + 1] * coadd
     detection_ref[...] = detection
 
 
@@ -280,17 +373,22 @@
     patches = lax.axis_size("ra")
     groups = lax.axis_size("band")
     row_share = rows // groups
-    slot = slot_rows(row_share)
-    length = visits * slot + EXTRA
+    length = visits * rows + EXTRA
+    message_shape = jax.ShapeDtypeStruct((length, PW), jnp.bfloat16)
+    pair_shape = jax.ShapeDtypeStruct((2, length, PW), jnp.bfloat16)
+    band_shape = jax.ShapeDtypeStruct((BANDS * row_share + EXTRA, PW), jnp.bfloat16)
+    part_shape = jax.ShapeDtypeStruct((BANDS * row_share, PW), jnp.float32)
+    whole_shape = jax.ShapeDtypeStruct((BANDS * rows, PW), jnp.float32)
+    weight_shape = jax.ShapeDtypeStruct((8, PW), jnp.float32)
     smem = pl.BlockSpec(memory_space=pltpu.SMEM)
 
     vmem = pl.BlockSpec(memory_space=pltpu.VMEM)
     anywhere = pl.BlockSpec(memory_space=pl.ANY)
-    messages = pl.pallas_call(
-        functools.partial(match_kernel, patches, groups),
-        in_specs=[smem] * 4 + [anywhere] * 5,
-        out_specs=[vmem] * (SPREAD * groups),
-        out_shape=[jax.ShapeDtypeStruct((length, PW), jnp.bfloat16)] * (SPREAD * groups),
+    far, cross, kept = pl.pallas_call(
+        functools.partial(match_kernel, patches),
+        in_specs=[smem] * 5 + [anywhere] * 5,
+        out_specs=[vmem] * 3,
+        out_shape=[message_shape, pair_shape, pair_shape],
         scratch_shapes=[
             pltpu.VMEM(coeff_table.shape[::-1], jnp.float32),
             pltpu.VMEM((1, tile_count), jnp.bfloat16),
@@ -314,6 +412,7 @@
         tile_offset,
         coeff_index,
         visit_band,
+        band_weight,
         coeff_table.T,
         tile_weight.reshape(1, tile_count),
         row_kernels,
@@ -321,31 +420,77 @@
         tiles,
     )
 
-    arrived = []
-    for bucket in range(SPREAD):
-        for turn in range(groups):
-            message = messages[bucket * groups + turn]
-            distance = bucket - REACH
-            if distance != 0 or turn != 0:
-                route = [
-                    (o * groups + g, (o + distance) % patches * groups + (g + turn) % groups)
-                    for o in range(patches)
-                    for g in range(groups)
-                ]
-                message = lax.ppermute(message, ("ra", "band"), route)
-            arrived.append(message)
-
-    return pl.pallas_call(
-        functools.partial(combine_kernel, visits),
-        in_specs=[smem] + [vmem] * len(arrived),
-        out_specs=(vmem, vmem),
-        out_shape=(
+    def send(message, goal, turn):
+        route = [
+            (o * groups + g, goal(o) % patches * groups + (g + turn) % groups)
+            for o in range(patches)
+            for g in range(groups)
+        ]
+        return lax.ppermute(message, ("ra", "band"), route)
+
+    def onward(distance):
+        return lambda o: o + distance if o % 2 else o - distance
+
+    def local_call(kernel, name, out_shape, *operands, **options):
+        return pl.pallas_call(
+            kernel,
+            in_specs=[vmem] * len(operands),
+            out_specs=[vmem] * len(out_shape),
+            out_shape=out_shape,
+            compiler_params=pltpu.CompilerParams(vmem_limit_bytes=40 * 1024 * 1024),
+            name=name,
+            **options,
+        )(*operands)
+
+    held = [pltpu.VMEM(whole_shape.shape, jnp.float32)]
+    cross = send(cross, onward(-1), 0)
+    far = send(far, onward(2), 0)
+    *kept, detect = local_call(
+        functools.partial(keep_kernel, visits, groups),
+        "keep",
+        [
+            jax.ShapeDtypeStruct((2,) + whole_shape.shape, jnp.float32),
+            jax.ShapeDtypeStruct((2,) + weight_shape.shape, jnp.float32),
+            weight_shape,
+        ],
+        kept,
+    )
+    *others, near, near_weight, home, home_weight = local_call(
+        functools.partial(merge_kernel, visits, groups),
+        "merge",
+        [band_shape] * (groups - 1) + [part_shape, weight_shape, whole_shape, weight_shape],
+        *kept,
+        cross,
+        scratch_shapes=held,
+    )
+    others = [send(others[turn - 1], onward(0), turn) for turn in range(1, groups)]
+    near, *others, own, own_weight = local_call(
+        functools.partial(forward_kernel, visits, groups),
+        "forward",
+        [band_shape] * groups + [part_shape, weight_shape],
+        near,
+        near_weight,
+        home,
+        home_weight,
+        far,
+        *others,
+        scratch_shapes=held,
+    )
+    near = send(near, onward(1), 0)
+    others = [send(others[turn - 1], onward(0), turn) for turn in range(1, groups)]
+    return local_call(
+        combine_kernel,
+        "combine",
+        (
             jax.ShapeDtypeStruct((BANDS, row_share, PW), jnp.float32),
             jax.ShapeDtypeStruct((row_share, PW), jnp.float32),
         ),
-        compiler_params=pltpu.CompilerParams(vmem_limit_bytes=40 * 1024 * 1024),
-        name="combine",
-    )(band_weight, *arrived)
+        detect,
+        own,
+        own_weight,
+        near,
+        *others,
+    )
 
 
 def solution(mesh):

time: 33.5 us -> 28.2 us (0.84)
  starting transfers between devices: 13.7 us -> 9.33 us
  Pallas kernels: 9.44 us -> 8.61 us
    ppermute x9 -> x5, starting transfers between devices: 13.7 us -> 9.33 us  [send(): return lax.ppermute(message, ('ra', 'band'), route)]
    pallas_call x2 -> x5, Pallas kernels: 9.44 us -> 8.61 us  [the longest x1 7 us: local(): pl.pallas_call(functools.partial(match_kernel, patches), in_specs=[smem]...]
    ppermute x9 -> x5, waiting for transfers between devices: 8.57 us -> 8.43 us  [send(): return lax.ppermute(message, ('ra', 'band'), route)]
    unnamed x4 -> x2, local copies, waits for them, and re-layouts: 0.89 us -> 0.96 us
  transfers between devices with their start and end apart: 9 -> 5, of which waited for: 4 -> 2; matrix products, arithmetic and copies ran while one was open for 0% -> 0% of each run, Pallas kernels for 0% -> 2%
where the time goes in v9:
time: 28.2 us; the launch traced here: 28 us
  starting transfers between devices  9.33 us (33%)
  Pallas kernels  8.61 us (31%)
  waiting for transfers between devices  8.43 us (30%)
  local copies, waits for them, and re-layouts  0.96 us (3%)
  between operations  0.67 us (2%)
    ppermute x5, starting transfers between devices, send(): return lax.ppermute(message, ('ra', 'band'), route)  9.33 us
    ppermute x5, waiting for transfers between devices, send(): return lax.ppermute(message, ('ra', 'band'), route)  8.43 us
    pallas_call x1, Pallas kernels, local(): pl.pallas_call(functools.partial(match_kernel, patches), in_specs=[smem]...  7 us
    pallas_call x4, Pallas kernels, local_call(): pl.pallas_call(kernel, in_specs=[vmem] * len(operands), out_specs=[vmem]...  1.61 us
    unnamed x2, local copies, waits for them, and re-layouts  0.96 us
  transfers between devices with their start and end apart: 5, of which 2 were waited for; matrix products, arithmetic and copies ran while one was open for 0% of the time, Pallas kernels for 2%

profile of v9, /device:TPU:0, one launch (start us, length us, event | category | flops | bytes accessed | tf_op | source)
XLA Modules:
  0.0 28.0 jit_solution(9731934558708900118)
XLA Ops:
  0.6 7.0 %match_and_sum.1 = (bf16[272,256]{1,0:T(8,128)(2,1)}, bf16[2,272,256]{2,1,0:T(8,128)(2,1)}, bf16[2,272,256]{2,1,0:T(8,128)(2,1)}) custom-call(s32[32]{0:T(128)} %patch_ref.1, s32[32]{0:T(128)} %offset_ref.1, s32[32]{0:T(128)} %index_ref.1, s32[4]{0:T(128)} %band_ref.1, f32[6]{0:T(128)} %detect_ref.1, f32[21,64]{1,0:T(8,128)} %bitcast.2, ...), custom_call_target="tpu_custom_call" | custom-call | tf_op jit(solution)/shard_map/match_and_sum/pallas_call | solution.py:387
  7.6 0.5 %collective-permute-start = (bf16[2,272,256]{2,1,0:T(8,128)(2,1)}, bf16[2,272,256]{2,1,0:T(8,128)(2,1)S(1)}, u32[]{:S(2)}, u32[]{:S(2)}) collective-permute-start(bf16[2,272,256]{2,1,0:T(8,128)(2,1)} %get-tuple-element.21), channel_id=1, source_target_pairs={{0,2},{1,3},{2,0},{3,1},{4,6},{5,7},{6,4},{7,5},{8,10},{9,11},{10,... | collective-permute-start | bytes 835592 | tf_op jit(solution)/shard_map/ppermute | solution.py:429
  8.2 5.6 %collective-permute-start.1 = (bf16[272,256]{1,0:T(8,128)(2,1)}, bf16[272,256]{1,0:T(8,128)(2,1)S(1)}, u32[]{:S(2)}, u32[]{:S(2)}) collective-permute-start(bf16[272,256]{1,0:T(8,128)(2,1)} %get-tuple-element.26), channel_id=1, source_target_pairs={{0,28},{1,29},{2,6},{3,7},{4,0},{5,1},{6,10},{7,11},{8,4},{9,5},{1... | collective-permute-start | bytes 417800 | tf_op jit(solution)/shard_map/ppermute | solution.py:429
  13.7 0.0 copy-start
  13.8 1.0 %copy-done = bf16[2,272,256]{2,1,0:T(8,128)(2,1)S(1)} copy-done((bf16[2,272,256]{2,1,0:T(8,128)(2,1)S(1)}, bf16[2,272,256]{2,1,0:T(8,128)(2,1)}, u32[]{:S(2)}) %copy-start) | copy-done | bytes 278552
  14.7 0.3 keep.1
  15.0 0.0 collective-permute-done.cross_ref
  15.0 0.3 %merge.1 = (bf16[208,256]{1,0:T(8,128)(2,1)S(1)}, f32[192,256]{1,0:T(8,128)S(1)}, f32[8,256]{1,0:T(8,128)S(1)}, f32[384,256]{1,0:T(8,128)S(1)}, f32[8,256]{1,0:T(8,128)S(1)}) custom-call(f32[2,384,256]{2,1,0:T(8,128)S(1)} %get-tuple-element.19.totals_ref, f32[2,8,256]{2,1,0:T(8,128)S(1)} %get-tuple-element.20.weights_ref, ...), custom_call_target="tpu_custom_call" | custom-call | tf_op jit(solution)/shard_map/merge/pallas_call | solution.py:435
  15.3 1.6 %collective-permute-start.2 = (bf16[208,256]{1,0:T(8,128)(2,1)S(1)}, bf16[208,256]{1,0:T(8,128)(2,1)S(1)}, u32[]{:S(2)}, u32[]{:S(2)}) collective-permute-start(bf16[208,256]{1,0:T(8,128)(2,1)S(1)} %get-tuple-element.27), channel_id=1, source_target_pairs={{0,1},{1,0},{2,3},{3,2},{4,5},{5,4},{6,7},{7,6},{8,9},{9,8},{10,11... | collective-permute-start | bytes 319496 | tf_op jit(solution)/shard_map/ppermute | solution.py:429
  16.9 0.0 collective-permute-done.1.far_ref
  16.9 3.2 %collective-permute-done.2.refs_0_ = bf16[208,256]{1,0:T(8,128)(2,1)S(1)} collective-permute-done((bf16[208,256]{1,0:T(8,128)(2,1)S(1)}, bf16[208,256]{1,0:T(8,128)(2,1)S(1)}, u32[]{:S(2)}, u32[]{:S(2)}) %collective-permute-start.2) | collective-permute-done | bytes 106528 | tf_op jit(solution)/shard_map/ppermute | solution.py:429
  20.1 0.3 %forward.1 = (bf16[208,256]{1,0:T(8,128)(2,1)S(1)}, bf16[208,256]{1,0:T(8,128)(2,1)S(1)}, f32[192,256]{1,0:T(8,128)S(1)}, f32[8,256]{1,0:T(8,128)S(1)}) custom-call(f32[192,256]{1,0:T(8,128)S(1)} %get-tuple-element.22.near_ref, f32[8,256]{1,0:T(8,128)S(1)} %get-tuple-element.23.near_weight_ref, f32[384,256]{1,0:T(8,128)S(1)} %get-tuple-element.24.home_ref, ...), custom_call_target="tpu_custom_call" | custom-call | tf_op jit(solution)/shard_map/forward/pallas_call | solution.py:435
  20.4 0.1 collective-permute-start.3
  20.5 1.6 %collective-permute-start.4 = (bf16[208,256]{1,0:T(8,128)(2,1)S(1)}, bf16[208,256]{1,0:T(8,128)(2,1)S(1)}, u32[]{:S(2)}, u32[]{:S(2)}) collective-permute-start(bf16[208,256]{1,0:T(8,128)(2,1)S(1)} %get-tuple-element.31), channel_id=1, source_target_pairs={{0,1},{1,0},{2,3},{3,2},{4,5},{5,4},{6,7},{7,6},{8,9},{9,8},{10,11... | collective-permute-start | bytes 319496 | tf_op jit(solution)/shard_map/ppermute | solution.py:429
  22.0 5.2 %collective-permute-done.3.refs_0_ = bf16[208,256]{1,0:T(8,128)(2,1)S(1)} collective-permute-done((bf16[208,256]{1,0:T(8,128)(2,1)S(1)}, bf16[208,256]{1,0:T(8,128)(2,1)S(1)}, u32[]{:S(2)}, u32[]{:S(2)}) %collective-permute-start.3) | collective-permute-done | bytes 106528 | tf_op jit(solution)/shard_map/ppermute | solution.py:429
  27.3 0.0 collective-permute-done.4.refs_1_
  27.3 0.7 %combine.1 = (f32[6,32,256]{2,1,0:T(8,128)}, f32[32,256]{1,0:T(8,128)}) custom-call(f32[8,256]{1,0:T(8,128)S(1)} %get-tuple-element.18.detect_ref, f32[192,256]{1,0:T(8,128)S(1)} %get-tuple-element.28.own_ref, f32[8,256]{1,0:T(8,128)S(1)} %get-tuple-element.29.own_weight_ref, bf16[208,256]{1,0:T(8,128)(2,1)S(1)} %collective-permute-done.3.refs_0_, ...), custom_call_target="tpu_custom_call" | custom-call | tf_op jit(solution)/shard_map/combine/pallas_call | solution.py:435
Async XLA Ops:
  7.6 7.3 %collective-permute-start = (bf16[2,272,256]{2,1,0:T(8,128)(2,1)}, bf16[2,272,256]{2,1,0:T(8,128)(2,1)S(1)}, u32[]{:S(2)}, u32[]{:S(2)}) collective-permute-start(bf16[2,272,256]{2,1,0:T(8,128)(2,1)} %get-tuple-element.21), channel_id=1, source_target_pairs={{0,2},{1,3},{2,0},{3,1},{4,6},{5,7},{6,4},{7,5},{8,10},{9,11},{10,... | collective-permute-start | bytes 835592 | tf_op jit(solution)/shard_map/ppermute | solution.py:429
  8.2 8.7 %collective-permute-start.1 = (bf16[272,256]{1,0:T(8,128)(2,1)}, bf16[272,256]{1,0:T(8,128)(2,1)S(1)}, u32[]{:S(2)}, u32[]{:S(2)}) collective-permute-start(bf16[272,256]{1,0:T(8,128)(2,1)} %get-tuple-element.26), channel_id=1, source_target_pairs={{0,28},{1,29},{2,6},{3,7},{4,0},{5,1},{6,10},{7,11},{8,4},{9,5},{1... | collective-permute-start | bytes 417800 | tf_op jit(solution)/shard_map/ppermute | solution.py:429
  13.7 1.0 %copy-start = (bf16[2,272,256]{2,1,0:T(8,128)(2,1)S(1)}, bf16[2,272,256]{2,1,0:T(8,128)(2,1)}, u32[]{:S(2)}) copy-start(bf16[2,272,256]{2,1,0:T(8,128)(2,1)} %get-tuple-element.17.kept_ref) | copy-start | bytes 835588
  15.3 4.8 %collective-permute-start.2 = (bf16[208,256]{1,0:T(8,128)(2,1)S(1)}, bf16[208,256]{1,0:T(8,128)(2,1)S(1)}, u32[]{:S(2)}, u32[]{:S(2)}) collective-permute-start(bf16[208,256]{1,0:T(8,128)(2,1)S(1)} %get-tuple-element.27), channel_id=1, source_target_pairs={{0,1},{1,0},{2,3},{3,2},{4,5},{5,4},{6,7},{7,6},{8,9},{9,8},{10,11... | collective-permute-start | bytes 319496 | tf_op jit(solution)/shard_map/ppermute | solution.py:429
  20.4 6.9 %collective-permute-start.3 = (bf16[208,256]{1,0:T(8,128)(2,1)S(1)}, bf16[208,256]{1,0:T(8,128)(2,1)S(1)}, u32[]{:S(2)}, u32[]{:S(2)}) collective-permute-start(bf16[208,256]{1,0:T(8,128)(2,1)S(1)} %get-tuple-element.30), channel_id=1, source_target_pairs={{0,30},{1,31},{2,4},{3,5},{4,2},{5,3},{6,8},{7,9},{8,6},{9,7},{10,... | collective-permute-start | bytes 319496 | tf_op jit(solution)/shard_map/ppermute | solution.py:429
  20.5 6.8 %collective-permute-start.4 = (bf16[208,256]{1,0:T(8,128)(2,1)S(1)}, bf16[208,256]{1,0:T(8,128)(2,1)S(1)}, u32[]{:S(2)}, u32[]{:S(2)}) collective-permute-start(bf16[208,256]{1,0:T(8,128)(2,1)S(1)} %get-tuple-element.31), channel_id=1, source_target_pairs={{0,1},{1,0},{2,3},{3,2},{4,5},{5,4},{6,7},{7,6},{8,9},{9,8},{10,11... | collective-permute-start | bytes 319496 | tf_op jit(solution)/shard_map/ppermute | solution.py:429

commit v10 on v9

--- a/solution.py
+++ b/solution.py
@@ -32,7 +32,6 @@
     rowk_hbm,
     colk_hbm,
     tiles_hbm,
-    far,
     cross,
     kept,
     table_ref,
@@ -49,7 +48,7 @@
     extra,
     arrival,
     ready,
-    ):
+):
     visits = band_ref.shape[0]
     tile_count, rows, width = tiles_ref.shape
     per_visit = tile_count // visits
@@ -203,7 +202,7 @@
             )
 
         held = pl.ds(pl.multiple_of(visit * rows, rows), rows)
-        far[held, :] = sums[REACH + 2 * way].astype(jnp.bfloat16)
+        kept[2, held, :] = sums[REACH + 2 * way].astype(jnp.bfloat16)
         cross[0, held, :] = sums[REACH - 2 * way].astype(jnp.bfloat16)
         cross[1, held, :] = sums[REACH - way].astype(jnp.bfloat16)
         kept[0, held, :] = sums[REACH + way].astype(jnp.bfloat16)
@@ -243,7 +242,7 @@
             mixed = jnp.where(row == place, piece, mixed)
         return mixed.astype(jnp.bfloat16)
 
-    far[rows * visits :, :] = footer(REACH + 2 * way)
+    kept[2, rows * visits :, :] = footer(REACH + 2 * way)
     cross[0, rows * visits :, :] = footer(REACH - 2 * way)
     cross[1, rows * visits :, :] = footer(REACH - way)
     kept[0, rows * visits :, :] = footer(REACH + way)
@@ -296,7 +295,8 @@
     return held[pl.ds(pl.multiple_of(part * depth, depth), depth), :]
 
 
-def keep_kernel(count, groups, kept_ref, totals_ref, weights_ref, detect_ref):
+def keep_kernel(count, groups, kept_ref, totals_ref, weights_ref, detect_ref, far_ref):
+    far_ref[...] = kept_ref[2]
     for place in range(2):
         totals_ref[place], weights_ref[place] = add_message(count, groups, kept_ref.at[place])
     extra = kept_ref[0, kept_ref.shape[1] - EXTRA :, :].astype(jnp.float32)
@@ -308,9 +308,9 @@
     detect_ref[...] = jnp.broadcast_to(chosen, (8, PW))
 
 
-def merge_kernel(count, groups, totals_ref, weights_ref, cross_ref, *refs):
+def near_kernel(count, groups, totals_ref, weights_ref, cross_ref, *refs):
     messages = refs[: groups - 1]
-    near_ref, near_weight_ref, home_ref, home_weight_ref, held = refs[groups - 1 :]
+    near_ref, near_weight_ref, held = refs[groups - 1 :]
     totals, weights = add_message(count, groups, cross_ref.at[0])
     held[...] = totals + totals_ref[0]
     weights += weights_ref[0]
@@ -318,20 +318,39 @@
         write_banded(message, part_of(held, turn, groups), weights)
     near_ref[...] = part_of(held, 0, groups)
     near_weight_ref[...] = weights
+
+
+def merge_kernel(
+    count,
+    groups,
+    after_ref,
+    totals_ref,
+    weights_ref,
+    far_in_ref,
+    cross_ref,
+    home_ref,
+    home_weight_ref,
+    far_ref,
+    rest_ref,
+):
+    far_ref[...] = far_in_ref[: far_ref.shape[0]]
+    rest_ref[...] = far_in_ref[far_ref.shape[0] :]
     totals, weights = add_message(count, groups, cross_ref.at[1])
     home_ref[...] = totals + totals_ref[1]
     home_weight_ref[...] = weights + weights_ref[1]
 
 
-def forward_kernel(
-    count, groups, near_ref, near_weight_ref, home_ref, home_weight_ref, far_ref, *refs
-):
-    arrived = refs[: groups - 1]
-    onward_ref = refs[groups - 1]
-    messages = refs[groups : 2 * groups - 1]
-    own_ref, own_weight_ref, held = refs[2 * groups - 1 :]
-    totals, weights = add_banded(near_ref[...], near_weight_ref[...], arrived)
-    write_banded(onward_ref, totals, weights)
+def forward_kernel(near_ref, near_weight_ref, *refs):
+    totals, weights = add_banded(near_ref[...], near_weight_ref[...], refs[:-2])
+    write_banded(refs[-2], totals, weights)
+    refs[-1][...] = weights
+
+
+def home_kernel(count, groups, after_ref, home_ref, home_weight_ref, top_ref, rest_ref, *refs):
+    messages = refs[: groups - 1]
+    own_ref, own_weight_ref, held, far_ref = refs[groups - 1 :]
+    far_ref[: top_ref.shape[0]] = top_ref[...]
+    far_ref[top_ref.shape[0] :] = rest_ref[...]
     totals, weights = add_message(count, groups, far_ref)
     held[...] = totals + home_ref[...]
     weights += home_weight_ref[...]
@@ -375,7 +394,6 @@
     row_share = rows // groups
     length = visits * rows + EXTRA
     message_shape = jax.ShapeDtypeStruct((length, PW), jnp.bfloat16)
-    pair_shape = jax.ShapeDtypeStruct((2, length, PW), jnp.bfloat16)
     band_shape = jax.ShapeDtypeStruct((BANDS * row_share + EXTRA, PW), jnp.bfloat16)
     part_shape = jax.ShapeDtypeStruct((BANDS * row_share, PW), jnp.float32)
     whole_shape = jax.ShapeDtypeStruct((BANDS * rows, PW), jnp.float32)
@@ -384,11 +402,14 @@
 
     vmem = pl.BlockSpec(memory_space=pltpu.VMEM)
     anywhere = pl.BlockSpec(memory_space=pl.ANY)
-    far, cross, kept = pl.pallas_call(
+    cross, kept = pl.pallas_call(
         functools.partial(match_kernel, patches),
         in_specs=[smem] * 5 + [anywhere] * 5,
-        out_specs=[vmem] * 3,
-        out_shape=[message_shape, pair_shape, pair_shape],
+        out_specs=[vmem] * 2,
+        out_shape=[
+            jax.ShapeDtypeStruct((2,) + message_shape.shape, jnp.bfloat16),
+            jax.ShapeDtypeStruct((3,) + message_shape.shape, jnp.bfloat16),
+        ],
         scratch_shapes=[
             pltpu.VMEM(coeff_table.shape[::-1], jnp.float32),
             pltpu.VMEM((1, tile_count), jnp.bfloat16),
@@ -444,39 +465,61 @@
 
     held = [pltpu.VMEM(whole_shape.shape, jnp.float32)]
     cross = send(cross, onward(-1), 0)
-    far = send(far, onward(2), 0)
-    *kept, detect = local_call(
+    *kept, detect, far = local_call(
         functools.partial(keep_kernel, visits, groups),
         "keep",
         [
             jax.ShapeDtypeStruct((2,) + whole_shape.shape, jnp.float32),
             jax.ShapeDtypeStruct((2,) + weight_shape.shape, jnp.float32),
             weight_shape,
+            message_shape,
         ],
         kept,
     )
-    *others, near, near_weight, home, home_weight = local_call(
-        functools.partial(merge_kernel, visits, groups),
-        "merge",
-        [band_shape] * (groups - 1) + [part_shape, weight_shape, whole_shape, weight_shape],
+    *others, near, near_weight = local_call(
+        functools.partial(near_kernel, visits, groups),
+        "near",
+        [band_shape] * (groups - 1) + [part_shape, weight_shape],
         *kept,
         cross,
         scratch_shapes=held,
     )
     others = [send(others[turn - 1], onward(0), turn) for turn in range(1, groups)]
-    near, *others, own, own_weight = local_call(
-        functools.partial(forward_kernel, visits, groups),
+    home, home_weight, *far = local_call(
+        functools.partial(merge_kernel, visits, groups),
+        "merge",
+        [
+            whole_shape,
+            weight_shape,
+            jax.ShapeDtypeStruct((length // 32 * 16 + EXTRA, PW), jnp.bfloat16),
+            jax.ShapeDtypeStruct((length - length // 32 * 16 - EXTRA, PW), jnp.bfloat16),
+        ],
+        near_weight,
+        *kept,
+        far,
+        cross,
+    )
+    far = [send(piece, onward(2), 0) for piece in far]
+    near, after = local_call(
+        forward_kernel,
         "forward",
-        [band_shape] * groups + [part_shape, weight_shape],
+        [band_shape, weight_shape],
         near,
         near_weight,
+        *others,
+        cost_estimate=pl.CostEstimate(flops=0, bytes_accessed=1 << 26, transcendentals=0),
+    )
+    near = send(near, onward(1), 0)
+    *others, own, own_weight = local_call(
+        functools.partial(home_kernel, visits, groups),
+        "home",
+        [band_shape] * (groups - 1) + [part_shape, weight_shape],
+        after,
         home,
         home_weight,
-        far,
-        *others,
-        scratch_shapes=held,
-    )
-    near = send(near, onward(1), 0)
+        *far,
+        scratch_shapes=held + [pltpu.VMEM(message_shape.shape, jnp.bfloat16)],
+    )
     others = [send(others[turn - 1], onward(0), turn) for turn in range(1, groups)]
     return local_call(
         combine_kernel,

time: 28.2 us -> 27.9 us (0.989)
  waiting for transfers between devices: 8.43 us -> 6.37 us
  starting transfers between devices: 9.33 us -> 10.8 us
    ppermute x5 -> x6, waiting for transfers between devices: 8.43 us -> 6.37 us  [send(): return lax.ppermute(message, ('ra', 'band'), route)]
    ppermute x5 -> x6, starting transfers between devices: 9.33 us -> 10.8 us  [send(): return lax.ppermute(message, ('ra', 'band'), route)]
    pallas_call x4 -> x6, Pallas kernels: 1.61 us -> 1.8 us  [local_call(): pl.pallas_call(kernel, in_specs=[vmem] * len(operands), out_specs=[vmem]...]
  transfers between devices with their start and end apart: 5 -> 6, of which waited for: 2 -> 4; matrix products, arithmetic and copies ran while one was open for 0% -> 0% of each run, Pallas kernels for 2% -> 3%
where the time goes in v10:
time: 27.9 us; the launch traced here: 27.7 us
  starting transfers between devices  10.8 us (39%)
  Pallas kernels  8.83 us (32%)
  waiting for transfers between devices  6.37 us (23%)
  local copies, waits for them, and re-layouts  1 us (4%)
  between operations  0.67 us (2%)
    ppermute x6, starting transfers between devices, send(): return lax.ppermute(message, ('ra', 'band'), route)  10.8 us
    pallas_call x1, Pallas kernels, local(): pl.pallas_call(functools.partial(match_kernel, patches), in_specs=[smem]...  7.04 us
    ppermute x6, waiting for transfers between devices, send(): return lax.ppermute(message, ('ra', 'band'), route)  6.37 us
    pallas_call x6, Pallas kernels, local_call(): pl.pallas_call(kernel, in_specs=[vmem] * len(operands), out_specs=[vmem]...  1.8 us
    unnamed x2, local copies, waits for them, and re-layouts  1 us
  transfers between devices with their start and end apart: 6, of which 4 were waited for; matrix products, arithmetic and copies ran while one was open for 0% of the time, Pallas kernels for 3%

profile of v10, /device:TPU:0, one launch (start us, length us, event | category | flops | bytes accessed | tf_op | source)
XLA Modules:
  0.0 27.7 jit_solution(8078687336752453215)
XLA Ops:
  0.6 7.0 %match_and_sum.1 = (bf16[2,272,256]{2,1,0:T(8,128)(2,1)}, bf16[3,272,256]{2,1,0:T(8,128)(2,1)}) custom-call(s32[32]{0:T(128)} %patch_ref.1, s32[32]{0:T(128)} %offset_ref.1, s32[32]{0:T(128)} %index_ref.1, s32[4]{0:T(128)} %band_ref.1, f32[6]{0:T(128)} %detect_ref.1, f32[21,64]{1,0:T(8,128)} %bitcast.2, bf16[1,32]{1,0:T(2,128)(2,1)} %bitcast.3, ...), custom_call_target="tpu_custom_call" | custom-call | tf_op jit(solution)/shard_map/match_and_sum/pallas_call | solution.py:405
  7.7 0.5 %collective-permute-start = (bf16[2,272,256]{2,1,0:T(8,128)(2,1)}, bf16[2,272,256]{2,1,0:T(8,128)(2,1)S(1)}, u32[]{:S(2)}, u32[]{:S(2)}) collective-permute-start(bf16[2,272,256]{2,1,0:T(8,128)(2,1)} %get-tuple-element.24), channel_id=1, source_target_pairs={{0,2},{1,3},{2,0},{3,1},{4,6},{5,7},{6,4},{7,5},{8,10},{9,11},{10,... | collective-permute-start | bytes 835592 | tf_op jit(solution)/shard_map/ppermute | solution.py:450
  8.2 0.0 copy-start
  8.2 1.0 %copy-done = bf16[3,272,256]{2,1,0:T(8,128)(2,1)S(1)} copy-done((bf16[3,272,256]{2,1,0:T(8,128)(2,1)S(1)}, bf16[3,272,256]{2,1,0:T(8,128)(2,1)}, u32[]{:S(2)}) %copy-start) | copy-done | bytes 417816
  9.2 0.3 keep.1
  9.5 0.1 collective-permute-done.cross_ref
  9.6 0.3 near.1
  9.9 3.0 %collective-permute-start.1 = (bf16[208,256]{1,0:T(8,128)(2,1)S(1)}, bf16[208,256]{1,0:T(8,128)(2,1)S(1)}, u32[]{:S(2)}, u32[]{:S(2)}) collective-permute-start(bf16[208,256]{1,0:T(8,128)(2,1)S(1)} %get-tuple-element.27), channel_id=1, source_target_pairs={{0,1},{1,0},{2,3},{3,2},{4,5},{5,4},{6,7},{7,6},{8,9},{9,8},{10,11... | collective-permute-start | bytes 319496 | tf_op jit(solution)/shard_map/ppermute | solution.py:450
  12.8 0.2 merge.1
  13.0 4.6 %collective-permute-start.2 = (bf16[144,256]{1,0:T(8,128)(2,1)S(1)}, bf16[144,256]{1,0:T(8,128)(2,1)S(1)}, u32[]{:S(2)}, u32[]{:S(2)}) collective-permute-start(bf16[144,256]{1,0:T(8,128)(2,1)S(1)} %get-tuple-element.32), channel_id=1, source_target_pairs={{0,28},{1,29},{2,6},{3,7},{4,0},{5,1},{6,10},{7,11},{8,4},{9,5},{1... | collective-permute-start | bytes 221192 | tf_op jit(solution)/shard_map/ppermute | solution.py:450
  17.6 0.5 %collective-permute-start.3 = (bf16[128,256]{1,0:T(8,128)(2,1)S(1)}, bf16[128,256]{1,0:T(8,128)(2,1)S(1)}, u32[]{:S(2)}, u32[]{:S(2)}) collective-permute-start(bf16[128,256]{1,0:T(8,128)(2,1)S(1)} %get-tuple-element.33), channel_id=1, source_target_pairs={{0,28},{1,29},{2,6},{3,7},{4,0},{5,1},{6,10},{7,11},{8,4},{9,5},{1... | collective-permute-start | bytes 196616 | tf_op jit(solution)/shard_map/ppermute | solution.py:450
  18.2 0.0 collective-permute-done.1.refs_0_
  18.2 1.6 %collective-permute-start.4 = (bf16[208,256]{1,0:T(8,128)(2,1)S(1)}, bf16[208,256]{1,0:T(8,128)(2,1)S(1)}, u32[]{:S(2)}, u32[]{:S(2)}) collective-permute-start(bf16[208,256]{1,0:T(8,128)(2,1)S(1)} %get-tuple-element.36), channel_id=1, source_target_pairs={{0,30},{1,31},{2,4},{3,5},{4,2},{5,3},{6,8},{7,9},{8,6},{9,7},{10,... | collective-permute-start | bytes 319496 | tf_op jit(solution)/shard_map/ppermute | solution.py:450
  19.8 2.0 %collective-permute-done.3.rest_ref = bf16[128,256]{1,0:T(8,128)(2,1)S(1)} collective-permute-done((bf16[128,256]{1,0:T(8,128)(2,1)S(1)}, bf16[128,256]{1,0:T(8,128)(2,1)S(1)}, u32[]{:S(2)}, u32[]{:S(2)}) %collective-permute-start.3) | collective-permute-done | bytes 65568 | tf_op jit(solution)/shard_map/ppermute | solution.py:450
  21.9 0.0 collective-permute-done.2.top_ref
  21.9 0.3 home.1
  22.2 0.6 %collective-permute-start.5 = (bf16[208,256]{1,0:T(8,128)(2,1)S(1)}, bf16[208,256]{1,0:T(8,128)(2,1)S(1)}, u32[]{:S(2)}, u32[]{:S(2)}) collective-permute-start(bf16[208,256]{1,0:T(8,128)(2,1)S(1)} %get-tuple-element.37), channel_id=1, source_target_pairs={{0,1},{1,0},{2,3},{3,2},{4,5},{5,4},{6,7},{7,6},{8,9},{9,8},{10,11... | collective-permute-start | bytes 319496 | tf_op jit(solution)/shard_map/ppermute | solution.py:450
  22.7 2.4 %collective-permute-done.4.refs_0_ = bf16[208,256]{1,0:T(8,128)(2,1)S(1)} collective-permute-done((bf16[208,256]{1,0:T(8,128)(2,1)S(1)}, bf16[208,256]{1,0:T(8,128)(2,1)S(1)}, u32[]{:S(2)}, u32[]{:S(2)}) %collective-permute-start.4) | collective-permute-done | bytes 106528 | tf_op jit(solution)/shard_map/ppermute | solution.py:450
  25.1 1.8 %collective-permute-done.5.refs_1_ = bf16[208,256]{1,0:T(8,128)(2,1)S(1)} collective-permute-done((bf16[208,256]{1,0:T(8,128)(2,1)S(1)}, bf16[208,256]{1,0:T(8,128)(2,1)S(1)}, u32[]{:S(2)}, u32[]{:S(2)}) %collective-permute-start.5) | collective-permute-done | bytes 106528 | tf_op jit(solution)/shard_map/ppermute | solution.py:450
  26.9 0.7 %combine.1 = (f32[6,32,256]{2,1,0:T(8,128)}, f32[32,256]{1,0:T(8,128)}) custom-call(f32[8,256]{1,0:T(8,128)S(1)} %get-tuple-element.21.detect_ref, f32[192,256]{1,0:T(8,128)S(1)} %get-tuple-element.34.own_ref, f32[8,256]{1,0:T(8,128)S(1)} %get-tuple-element.35.own_weight_ref, bf16[208,256]{1,0:T(8,128)(2,1)S(1)} %collective-permute-done.4.refs_0_, ...), custom_call_target="tpu_custom_call" | custom-call | tf_op jit(solution)/shard_map/combine/pallas_call | solution.py:456
  (1 shorter events, 0.0 us)
Async XLA Ops:
  7.7 1.9 %collective-permute-start = (bf16[2,272,256]{2,1,0:T(8,128)(2,1)}, bf16[2,272,256]{2,1,0:T(8,128)(2,1)S(1)}, u32[]{:S(2)}, u32[]{:S(2)}) collective-permute-start(bf16[2,272,256]{2,1,0:T(8,128)(2,1)} %get-tuple-element.24), channel_id=1, source_target_pairs={{0,2},{1,3},{2,0},{3,1},{4,6},{5,7},{6,4},{7,5},{8,10},{9,11},{10,... | collective-permute-start | bytes 835592 | tf_op jit(solution)/shard_map/ppermute | solution.py:450
  8.2 1.0 %copy-start = (bf16[3,272,256]{2,1,0:T(8,128)(2,1)S(1)}, bf16[3,272,256]{2,1,0:T(8,128)(2,1)}, u32[]{:S(2)}) copy-start(bf16[3,272,256]{2,1,0:T(8,128)(2,1)} %get-tuple-element.20.kept_ref) | copy-start | bytes 1253380
  9.9 8.3 %collective-permute-start.1 = (bf16[208,256]{1,0:T(8,128)(2,1)S(1)}, bf16[208,256]{1,0:T(8,128)(2,1)S(1)}, u32[]{:S(2)}, u32[]{:S(2)}) collective-permute-start(bf16[208,256]{1,0:T(8,128)(2,1)S(1)} %get-tuple-element.27), channel_id=1, source_target_pairs={{0,1},{1,0},{2,3},{3,2},{4,5},{5,4},{6,7},{7,6},{8,9},{9,8},{10,11... | collective-permute-start | bytes 319496 | tf_op jit(solution)/shard_map/ppermute | solution.py:450
  13.0 8.8 %collective-permute-start.2 = (bf16[144,256]{1,0:T(8,128)(2,1)S(1)}, bf16[144,256]{1,0:T(8,128)(2,1)S(1)}, u32[]{:S(2)}, u32[]{:S(2)}) collective-permute-start(bf16[144,256]{1,0:T(8,128)(2,1)S(1)} %get-tuple-element.32), channel_id=1, source_target_pairs={{0,28},{1,29},{2,6},{3,7},{4,0},{5,1},{6,10},{7,11},{8,4},{9,5},{1... | collective-permute-start | bytes 221192 | tf_op jit(solution)/shard_map/ppermute | solution.py:450
  17.6 4.3 %collective-permute-start.3 = (bf16[128,256]{1,0:T(8,128)(2,1)S(1)}, bf16[128,256]{1,0:T(8,128)(2,1)S(1)}, u32[]{:S(2)}, u32[]{:S(2)}) collective-permute-start(bf16[128,256]{1,0:T(8,128)(2,1)S(1)} %get-tuple-element.33), channel_id=1, source_target_pairs={{0,28},{1,29},{2,6},{3,7},{4,0},{5,1},{6,10},{7,11},{8,4},{9,5},{1... | collective-permute-start | bytes 196616 | tf_op jit(solution)/shard_map/ppermute | solution.py:450
  18.2 6.9 %collective-permute-start.4 = (bf16[208,256]{1,0:T(8,128)(2,1)S(1)}, bf16[208,256]{1,0:T(8,128)(2,1)S(1)}, u32[]{:S(2)}, u32[]{:S(2)}) collective-permute-start(bf16[208,256]{1,0:T(8,128)(2,1)S(1)} %get-tuple-element.36), channel_id=1, source_target_pairs={{0,30},{1,31},{2,4},{3,5},{4,2},{5,3},{6,8},{7,9},{8,6},{9,7},{10,... | collective-permute-start | bytes 319496 | tf_op jit(solution)/shard_map/ppermute | solution.py:450
  22.2 4.8 %collective-permute-start.5 = (bf16[208,256]{1,0:T(8,128)(2,1)S(1)}, bf16[208,256]{1,0:T(8,128)(2,1)S(1)}, u32[]{:S(2)}, u32[]{:S(2)}) collective-permute-start(bf16[208,256]{1,0:T(8,128)(2,1)S(1)} %get-tuple-element.37), channel_id=1, source_target_pairs={{0,1},{1,0},{2,3},{3,2},{4,5},{5,4},{6,7},{7,6},{8,9},{9,8},{10,11... | collective-permute-start | bytes 319496 | tf_op jit(solution)/shard_map/ppermute | solution.py:450

commit v11 on v7

--- a/solution.py
+++ b/solution.py
@@ -78,12 +78,8 @@
     for copy in small:
         copy.start()
 
-    def fetch(visit):
-        held = pl.ds(visit * per_visit, per_visit)
-        return pltpu.make_async_copy(tiles_hbm.at[held], tiles_ref.at[held], arrival.at[visit])
-
-    for visit in range(visits):
-        fetch(visit).start()
+    fetch = pltpu.make_async_copy(tiles_hbm, tiles_ref, arrival)
+    fetch.start()
 
     def iota(shape, axis):
         return lax.broadcasted_iota(jnp.int32, shape, axis)
@@ -99,16 +95,17 @@
 
     extra[...] = jnp.zeros_like(extra)
     shifted[...] = jnp.zeros_like(shifted)
-    eye = (iota((tile_count, tile_count), 0) == iota((tile_count, tile_count), 1)).astype(
-        jnp.bfloat16
-    )
+    eye = (iota((8 * tile_count, tile_count), 0) // 8 == iota((8 * tile_count, tile_count), 1))
     entry = iota((1, table_ref.shape[1]), 1)
     chosen = jnp.concatenate(
         [(entry == index_ref[j]).astype(jnp.float32) for j in range(tile_count)], axis=0
     )
     for copy in small:
         copy.wait()
-    weights[...] = across(eye, jnp.broadcast_to(weight_ref[...], (width, tile_count)))
+    fetch.wait()
+    weights[...] = across(
+        eye.astype(jnp.bfloat16), jnp.broadcast_to(weight_ref[...], (width, tile_count))
+    ).reshape(weights.shape)
     coeffs = across(chosen, table_ref[...], precision=lax.Precision.HIGHEST)
 
     line = iota((2 * VECTORS, taps), 0)
@@ -134,7 +131,7 @@
             low, row_taps, preferred_element_type=jnp.float32
         )
         total = term if total is None else total + term
-    kernels[...] = total
+    kernels[...] = total.reshape(kernels.shape)
 
     lane = iota((rows, width), 1)
     column = iota((1, width), 1)
@@ -146,64 +143,64 @@
         here = lane[: value.shape[0]] + distance
         return jnp.where((here >= 0) & (here < width), turned, jnp.zeros_like(turned))
 
-    def one_visit(visit, unused):
-        fetch(visit).wait()
+    def build(visit, place, buffer):
+        tile = visit * per_visit + place
+        pixels = tiles_ref[tile]
+        for side in range(2):
+            for fine in range(4):
+                part = moved(pixels, -1 - fine if side else fine)
+                top = fine * FINE_ROWS
+                shifted[buffer, place, side, top + 16 : top + 64, :width] = part[:48]
+                shifted[buffer, place, side, top : top + 48, width:] = part[16:]
+            for coarse in range(COARSE):
+                for pair in range(2):
+                    vector = (side * COARSE + coarse) * 2 + pair
+                    spread = jnp.broadcast_to(
+                        kernels[tile, vector : vector + 1, :], (BLOCK, width)
+                    )
+                    turned = pltpu.roll(spread, 0, 1, stride=1, stride_axis=0)
+                    toeplitz[
+                        buffer,
+                        place,
+                        side,
+                        coarse * BLOCK : (coarse + 1) * BLOCK,
+                        pair * width : (pair + 1) * width,
+                    ] = turned.astype(jnp.bfloat16)
+
+    def multiply(place, buffer):
+        matched = [jnp.zeros((BLOCK, width), jnp.float32) for _ in range(2)]
+        for side in range(2):
+            passed = jnp.dot(
+                toeplitz[buffer, place, side],
+                shifted[buffer, place, side],
+                preferred_element_type=jnp.float32,
+            )
+            for part in range(2):
+                for coarse in range(COARSE):
+                    matched[part] += moved(
+                        passed[
+                            coarse * BLOCK : (coarse + 1) * BLOCK,
+                            part * width : (part + 1) * width,
+                        ],
+                        -4 * coarse if side else 4 * coarse,
+                    )
+        matches[buffer, place] = jnp.concatenate(matched, axis=0)
+
+    def deliver(visit, buffer):
         sums[...] = jnp.zeros_like(sums)
-        first = visit * per_visit
         for place in range(per_visit):
-            tile = first + place
-            pixels = tiles_ref[tile]
-            for side in range(2):
-                for fine in range(4):
-                    part = moved(pixels, -1 - fine if side else fine)
-                    top = fine * FINE_ROWS
-                    shifted[place, side, top + 16 : top + 64, :width] = part[:48]
-                    shifted[place, side, top : top + 48, width:] = part[16:]
-                for coarse in range(COARSE):
-                    for pair in range(2):
-                        vector = pl.ds(
-                            tile * VECTORS + (side * COARSE + coarse) * 2 + pair, 1
-                        )
-                        spread = jnp.broadcast_to(kernels[vector, :], (BLOCK, width))
-                        turned = pltpu.roll(spread, 0, 1, stride=1, stride_axis=0)
-                        toeplitz[
-                            place,
-                            side,
-                            coarse * BLOCK : (coarse + 1) * BLOCK,
-                            pair * width : (pair + 1) * width,
-                        ] = turned.astype(jnp.bfloat16)
-        for place in range(per_visit):
-            matched = [jnp.zeros((BLOCK, width), jnp.float32) for _ in range(2)]
-            for side in range(2):
-                passed = jnp.dot(
-                    toeplitz[place, side],
-                    shifted[place, side],
-                    preferred_element_type=jnp.float32,
-                )
-                for part in range(2):
-                    for coarse in range(COARSE):
-                        matched[part] += moved(
-                            passed[
-                                coarse * BLOCK : (coarse + 1) * BLOCK,
-                                part * width : (part + 1) * width,
-                            ],
-                            -4 * coarse if side else 4 * coarse,
-                        )
-            matches[place] = jnp.concatenate(matched, axis=0)
-        for place in range(per_visit):
-            tile = first + place
+            tile = visit * per_visit + place
             offset = offset_ref[tile]
             bucket = lax.rem(patch_ref[tile] - owner + REACH + patches, patches)
-            weight = weights[pl.ds(tile, 1), :]
-            turned = pltpu.roll(
-                matches[place] * weight, lax.rem(offset, width), 1
-            )
+            weight = weights[tile]
+            value = matches[buffer, place].reshape(rows // 8, 8, width) * weight[None]
+            turned = pltpu.roll(value.reshape(rows, width), lax.rem(offset, width), 1)
             sums[bucket, :, :width] += jnp.where(lane >= offset, turned, 0.0)
             sums[bucket, :, width:] += jnp.where(lane < offset, turned, 0.0)
             extra[bucket, pl.ds(visit, 1), :] += jnp.concatenate(
                 [
-                    jnp.where(column >= offset, weight, 0.0),
-                    jnp.where(column < offset, weight, 0.0),
+                    jnp.where(column >= offset, weight[:1], 0.0),
+                    jnp.where(column < offset, weight[:1], 0.0),
                 ],
                 axis=1,
             )
@@ -219,9 +216,20 @@
                 messages[bucket * groups + turn][
                     pl.ds(pl.multiple_of(visit * slot, slot), slot), :
                 ] = own.astype(jnp.bfloat16)
+
+    def two_visits(step, unused):
+        for buffer in range(2):
+            visit = 2 * step + buffer
+            later = jnp.minimum(visit + 1, visits - 1)
+            for place in range(per_visit):
+                build(later, place, 1 - buffer)
+                multiply(place, buffer)
+            deliver(visit, buffer)
         return unused
 
-    lax.fori_loop(0, visits, one_visit, 0)
+    for place in range(per_visit):
+        build(0, place, 0)
+    lax.fori_loop(0, visits // 2, two_visits, 0)
 
     row = iota((EXTRA, PW), 0)
     lane = iota((1, PW), 1)
@@ -327,14 +335,14 @@
             pltpu.VMEM((basis, taps), jnp.bfloat16),
             pltpu.VMEM((basis, taps), jnp.bfloat16),
             pltpu.VMEM((tile_count, rows, width), jnp.bfloat16),
-            pltpu.VMEM((tile_count * VECTORS, width), jnp.float32),
-            pltpu.VMEM((tile_count, width), jnp.float32),
-            pltpu.VMEM((per_visit, 2, 4 * FINE_ROWS, 2 * width), jnp.bfloat16),
-            pltpu.VMEM((per_visit, 2, COARSE * BLOCK, 2 * width), jnp.bfloat16),
-            pltpu.VMEM((per_visit, rows, width), jnp.float32),
+            pltpu.VMEM((tile_count, VECTORS, width), jnp.float32),
+            pltpu.VMEM((tile_count, 8, width), jnp.float32),
+            pltpu.VMEM((2, per_visit, 2, 4 * FINE_ROWS, 2 * width), jnp.bfloat16),
+            pltpu.VMEM((2, per_visit, 2, COARSE * BLOCK, 2 * width), jnp.bfloat16),
+            pltpu.VMEM((2, per_visit, rows, width), jnp.float32),
             pltpu.VMEM((SPREAD, rows, PW), jnp.float32),
             pltpu.VMEM((SPREAD, EXTRA, PW), jnp.float32),
-            pltpu.SemaphoreType.DMA((visits,)),
+            pltpu.SemaphoreType.DMA,
             pltpu.SemaphoreType.DMA((4,)),
         ],
         compiler_params=pltpu.CompilerParams(vmem_limit_bytes=62 * 1024 * 1024),

time: 27.2 us -> 27.7 us (1.018)
  Pallas kernels: 8.82 us -> 9.34 us
    pallas_call x1, Pallas kernels: 7 us -> 7.52 us  [local(): pl.pallas_call(functools.partial(match_kernel, patches, groups), in_specs...]
where the time goes in v11:
time: 27.7 us; the launch traced here: 27.4 us
  starting transfers between devices  14.4 us (52%)
  Pallas kernels  9.34 us (34%)
  waiting for transfers between devices  2.07 us (7%)
  local copies, waits for them, and re-layouts  0.89 us (3%)
  between operations  0.67 us (2%)
    ppermute x9, starting transfers between devices, local(): lax.ppermute(messages[(distance + REACH) * groups + turn], ('ra', 'band')...  14.4 us
    pallas_call x1, Pallas kernels, local(): pl.pallas_call(functools.partial(match_kernel, patches, groups), in_specs...  7.52 us
    ppermute x9, waiting for transfers between devices, local(): lax.ppermute(messages[(distance + REACH) * groups + turn], ('ra', 'band')...  2.07 us
    pallas_call x1, Pallas kernels, local(): pl.pallas_call(functools.partial(combine_kernel, visits), in_specs=[vmem]...  0.95 us
    unnamed x4, local copies, waits for them, and re-layouts  0.89 us
    pallas_call x1, Pallas kernels, local(): pl.pallas_call(functools.partial(early_kernel, visits, row_share), in_spe...  0.87 us
  transfers between devices with their start and end apart: 9, of which 3 were waited for; matrix products, arithmetic and copies ran while one was open for 0% of the time, Pallas kernels for 3%

profile of v11, /device:TPU:0, one launch (start us, length us, event | category | flops | bytes accessed | tf_op | source)
XLA Modules:
  0.0 27.4 jit_solution(6153849480104709006)
XLA Ops:
  0.6 7.5 %match_and_sum.1 = (bf16[144,256]{1,0:T(8,128)(2,1)}, bf16[144,256]{1,0:T(8,128)(2,1)}, bf16[144,256]{1,0:T(8,128)(2,1)}, bf16[144,256]{1,0:T(8,128)(2,1)}, bf16...) custom-call(s32[32]{0:T(128)} %patch_ref.1, ...), custom_call_target="tpu_custom_call" | custom-call | tf_op jit(solution)/shard_map/match_and_sum/pallas_call | solution.py:327
  8.2 0.5 %collective-permute-start = (bf16[144,256]{1,0:T(8,128)(2,1)}, bf16[144,256]{1,0:T(8,128)(2,1)S(1)}, u32[]{:S(2)}, u32[]{:S(2)}) collective-permute-start(bf16[144,256]{1,0:T(8,128)(2,1)} %get-tuple-element.15), channel_id=1, source_target_pairs={{0,2},{1,3},{2,4},{3,5},{4,6},{5,7},{6,8},{7,9},{8,10},{9,11},{10,... | collective-permute-start | bytes 221192 | tf_op jit(solution)/shard_map/ppermute | solution.py:374
  8.7 3.7 %collective-permute-start.1 = (bf16[144,256]{1,0:T(8,128)(2,1)}, bf16[144,256]{1,0:T(8,128)(2,1)S(1)}, u32[]{:S(2)}, u32[]{:S(2)}) collective-permute-start(bf16[144,256]{1,0:T(8,128)(2,1)} %get-tuple-element.16), channel_id=1, source_target_pairs={{0,3},{1,2},{2,5},{3,4},{4,7},{5,6},{6,9},{7,8},{8,11},{9,10},{10,... | collective-permute-start | bytes 221192 | tf_op jit(solution)/shard_map/ppermute | solution.py:374
  12.4 1.6 %collective-permute-start.2 = (bf16[144,256]{1,0:T(8,128)(2,1)}, bf16[144,256]{1,0:T(8,128)(2,1)S(1)}, u32[]{:S(2)}, u32[]{:S(2)}) collective-permute-start(bf16[144,256]{1,0:T(8,128)(2,1)} %get-tuple-element.17), channel_id=1, source_target_pairs={{0,4},{1,5},{2,6},{3,7},{4,8},{5,9},{6,10},{7,11},{8,12},{9,13},{1... | collective-permute-start | bytes 221192 | tf_op jit(solution)/shard_map/ppermute | solution.py:374
  13.9 1.4 %collective-permute-start.3 = (bf16[144,256]{1,0:T(8,128)(2,1)}, bf16[144,256]{1,0:T(8,128)(2,1)S(1)}, u32[]{:S(2)}, u32[]{:S(2)}) collective-permute-start(bf16[144,256]{1,0:T(8,128)(2,1)} %get-tuple-element.18), channel_id=1, source_target_pairs={{0,5},{1,4},{2,7},{3,6},{4,9},{5,8},{6,11},{7,10},{8,13},{9,12},{1... | collective-permute-start | bytes 221192 | tf_op jit(solution)/shard_map/ppermute | solution.py:374
  15.4 1.5 %collective-permute-start.4 = (bf16[144,256]{1,0:T(8,128)(2,1)}, bf16[144,256]{1,0:T(8,128)(2,1)S(1)}, u32[]{:S(2)}, u32[]{:S(2)}) collective-permute-start(bf16[144,256]{1,0:T(8,128)(2,1)} %get-tuple-element.19), channel_id=1, source_target_pairs={{0,1},{1,0},{2,3},{3,2},{4,5},{5,4},{6,7},{7,6},{8,9},{9,8},{10,11... | collective-permute-start | bytes 221192 | tf_op jit(solution)/shard_map/ppermute | solution.py:374
  16.9 0.0 collective-permute-done.refs_1_
  16.9 3.2 %collective-permute-start.5 = (bf16[144,256]{1,0:T(8,128)(2,1)}, bf16[144,256]{1,0:T(8,128)(2,1)S(1)}, u32[]{:S(2)}, u32[]{:S(2)}) collective-permute-start(bf16[144,256]{1,0:T(8,128)(2,1)} %get-tuple-element.22), channel_id=1, source_target_pairs={{0,28},{1,29},{2,30},{3,31},{4,0},{5,1},{6,2},{7,3},{8,4},{9,5},{1... | collective-permute-start | bytes 221192 | tf_op jit(solution)/shard_map/ppermute | solution.py:374
  20.1 0.0 collective-permute-done.1.refs_2_
  20.1 0.4 %collective-permute-start.6 = (bf16[144,256]{1,0:T(8,128)(2,1)}, bf16[144,256]{1,0:T(8,128)(2,1)S(1)}, u32[]{:S(2)}, u32[]{:S(2)}) collective-permute-start(bf16[144,256]{1,0:T(8,128)(2,1)} %get-tuple-element.23), channel_id=1, source_target_pairs={{0,29},{1,28},{2,31},{3,30},{4,1},{5,0},{6,3},{7,2},{8,5},{9,4},{1... | collective-permute-start | bytes 221192 | tf_op jit(solution)/shard_map/ppermute | solution.py:374
  20.6 0.0 collective-permute-done.2.refs_3_
  20.6 1.1 %collective-permute-start.7 = (bf16[144,256]{1,0:T(8,128)(2,1)}, bf16[144,256]{1,0:T(8,128)(2,1)S(1)}, u32[]{:S(2)}, u32[]{:S(2)}) collective-permute-start(bf16[144,256]{1,0:T(8,128)(2,1)} %get-tuple-element.24), channel_id=1, source_target_pairs={{0,30},{1,31},{2,0},{3,1},{4,2},{5,3},{6,4},{7,5},{8,6},{9,7},{10,... | collective-permute-start | bytes 221192 | tf_op jit(solution)/shard_map/ppermute | solution.py:374
  21.7 0.5 %collective-permute-done.3.refs_4_ = bf16[144,256]{1,0:T(8,128)(2,1)S(1)} collective-permute-done((bf16[144,256]{1,0:T(8,128)(2,1)}, bf16[144,256]{1,0:T(8,128)(2,1)S(1)}, u32[]{:S(2)}, u32[]{:S(2)}) %collective-permute-start.3) | collective-permute-done | bytes 73760 | tf_op jit(solution)/shard_map/ppermute | solution.py:374
  22.2 0.0 copy-start.1
  22.2 0.9 %collective-permute-start.8 = (bf16[144,256]{1,0:T(8,128)(2,1)}, bf16[144,256]{1,0:T(8,128)(2,1)S(1)}, u32[]{:S(2)}, u32[]{:S(2)}) collective-permute-start(bf16[144,256]{1,0:T(8,128)(2,1)} %get-tuple-element.25), channel_id=1, source_target_pairs={{0,31},{1,30},{2,1},{3,0},{4,3},{5,2},{6,5},{7,4},{8,7},{9,6},{10,... | collective-permute-start | bytes 221192 | tf_op jit(solution)/shard_map/ppermute | solution.py:374
  23.1 0.0 collective-permute-done.4.refs_5_
  23.1 0.0 copy-done.1
  23.1 0.9 %copy-done = bf16[144,256]{1,0:T(8,128)(2,1)S(1)} copy-done((bf16[144,256]{1,0:T(8,128)(2,1)S(1)}, bf16[144,256]{1,0:T(8,128)(2,1)}, u32[]{:S(2)}) %copy-start) | copy-done | bytes 73752
  24.0 0.9 %combine_early.1 = (f32[192,256]{1,0:T(8,128)S(1)}, f32[16,256]{1,0:T(8,128)S(1)}) custom-call(f32[6]{0:T(128)S(1)} %copy-done.1, bf16[144,256]{1,0:T(8,128)(2,1)S(1)} %copy-done, bf16[144,256]{1,0:T(8,128)(2,1)S(1)} %collective-permute-done.refs_1_, bf16[144,256]{1,0:T(8,128)(2,1)S(1)} %collective-permute-done.1.refs_2_, ...), custom_call_target="tpu_custom_call" | custom-call | tf_op jit(solution)/shard_map/combine_early/pallas_call | solution.py:379
  24.8 0.0 collective-permute-done.5.refs_0_
  24.9 0.8 %collective-permute-done.6.refs_1_ = bf16[144,256]{1,0:T(8,128)(2,1)S(1)} collective-permute-done((bf16[144,256]{1,0:T(8,128)(2,1)}, bf16[144,256]{1,0:T(8,128)(2,1)S(1)}, u32[]{:S(2)}, u32[]{:S(2)}) %collective-permute-start.6) | collective-permute-done | bytes 73760 | tf_op jit(solution)/shard_map/ppermute | solution.py:374
  25.6 0.0 collective-permute-done.7.refs_2_
  25.6 0.8 %collective-permute-done.8.refs_3_ = bf16[144,256]{1,0:T(8,128)(2,1)S(1)} collective-permute-done((bf16[144,256]{1,0:T(8,128)(2,1)}, bf16[144,256]{1,0:T(8,128)(2,1)S(1)}, u32[]{:S(2)}, u32[]{:S(2)}) %collective-permute-start.8) | collective-permute-done | bytes 73760 | tf_op jit(solution)/shard_map/ppermute | solution.py:374
  26.4 1.0 %combine.1 = (f32[6,32,256]{2,1,0:T(8,128)}, f32[32,256]{1,0:T(8,128)}) custom-call(f32[192,256]{1,0:T(8,128)S(1)} %get-tuple-element.20.totals_ref, f32[16,256]{1,0:T(8,128)S(1)} %get-tuple-element.21.rows_ref, bf16[144,256]{1,0:T(8,128)(2,1)S(1)} %collective-permute-done.5.refs_0_, bf16[144,256]{1,0:T(8,128)(2,1)S(1)} %collective-permute-done.6.refs_1_, ...), custom_call_target="tpu_custom_call" | custom-call | tf_op jit(solution)/shard_map/combine/pallas_call | solution.py:390
  (1 shorter events, 0.0 us)
Async XLA Ops:
  8.2 8.7 %collective-permute-start = (bf16[144,256]{1,0:T(8,128)(2,1)}, bf16[144,256]{1,0:T(8,128)(2,1)S(1)}, u32[]{:S(2)}, u32[]{:S(2)}) collective-permute-start(bf16[144,256]{1,0:T(8,128)(2,1)} %get-tuple-element.15), channel_id=1, source_target_pairs={{0,2},{1,3},{2,4},{3,5},{4,6},{5,7},{6,8},{7,9},{8,10},{9,11},{10,... | collective-permute-start | bytes 221192 | tf_op jit(solution)/shard_map/ppermute | solution.py:374
  8.7 11.5 %collective-permute-start.1 = (bf16[144,256]{1,0:T(8,128)(2,1)}, bf16[144,256]{1,0:T(8,128)(2,1)S(1)}, u32[]{:S(2)}, u32[]{:S(2)}) collective-permute-start(bf16[144,256]{1,0:T(8,128)(2,1)} %get-tuple-element.16), channel_id=1, source_target_pairs={{0,3},{1,2},{2,5},{3,4},{4,7},{5,6},{6,9},{7,8},{8,11},{9,10},{10,... | collective-permute-start | bytes 221192 | tf_op jit(solution)/shard_map/ppermute | solution.py:374
  12.4 8.2 %collective-permute-start.2 = (bf16[144,256]{1,0:T(8,128)(2,1)}, bf16[144,256]{1,0:T(8,128)(2,1)S(1)}, u32[]{:S(2)}, u32[]{:S(2)}) collective-permute-start(bf16[144,256]{1,0:T(8,128)(2,1)} %get-tuple-element.17), channel_id=1, source_target_pairs={{0,4},{1,5},{2,6},{3,7},{4,8},{5,9},{6,10},{7,11},{8,12},{9,13},{1... | collective-permute-start | bytes 221192 | tf_op jit(solution)/shard_map/ppermute | solution.py:374
  13.9 8.3 %collective-permute-start.3 = (bf16[144,256]{1,0:T(8,128)(2,1)}, bf16[144,256]{1,0:T(8,128)(2,1)S(1)}, u32[]{:S(2)}, u32[]{:S(2)}) collective-permute-start(bf16[144,256]{1,0:T(8,128)(2,1)} %get-tuple-element.18), channel_id=1, source_target_pairs={{0,5},{1,4},{2,7},{3,6},{4,9},{5,8},{6,11},{7,10},{8,13},{9,12},{1... | collective-permute-start | bytes 221192 | tf_op jit(solution)/shard_map/ppermute | solution.py:374
  15.4 7.7 %collective-permute-start.4 = (bf16[144,256]{1,0:T(8,128)(2,1)}, bf16[144,256]{1,0:T(8,128)(2,1)S(1)}, u32[]{:S(2)}, u32[]{:S(2)}) collective-permute-start(bf16[144,256]{1,0:T(8,128)(2,1)} %get-tuple-element.19), channel_id=1, source_target_pairs={{0,1},{1,0},{2,3},{3,2},{4,5},{5,4},{6,7},{7,6},{8,9},{9,8},{10,11... | collective-permute-start | bytes 221192 | tf_op jit(solution)/shard_map/ppermute | solution.py:374
  16.9 7.9 %collective-permute-start.5 = (bf16[144,256]{1,0:T(8,128)(2,1)}, bf16[144,256]{1,0:T(8,128)(2,1)S(1)}, u32[]{:S(2)}, u32[]{:S(2)}) collective-permute-start(bf16[144,256]{1,0:T(8,128)(2,1)} %get-tuple-element.22), channel_id=1, source_target_pairs={{0,28},{1,29},{2,30},{3,31},{4,0},{5,1},{6,2},{7,3},{8,4},{9,5},{1... | collective-permute-start | bytes 221192 | tf_op jit(solution)/shard_map/ppermute | solution.py:374
  20.1 5.5 %collective-permute-start.6 = (bf16[144,256]{1,0:T(8,128)(2,1)}, bf16[144,256]{1,0:T(8,128)(2,1)S(1)}, u32[]{:S(2)}, u32[]{:S(2)}) collective-permute-start(bf16[144,256]{1,0:T(8,128)(2,1)} %get-tuple-element.23), channel_id=1, source_target_pairs={{0,29},{1,28},{2,31},{3,30},{4,1},{5,0},{6,3},{7,2},{8,5},{9,4},{1... | collective-permute-start | bytes 221192 | tf_op jit(solution)/shard_map/ppermute | solution.py:374
  20.6 5.0 %collective-permute-start.7 = (bf16[144,256]{1,0:T(8,128)(2,1)}, bf16[144,256]{1,0:T(8,128)(2,1)S(1)}, u32[]{:S(2)}, u32[]{:S(2)}) collective-permute-start(bf16[144,256]{1,0:T(8,128)(2,1)} %get-tuple-element.24), channel_id=1, source_target_pairs={{0,30},{1,31},{2,0},{3,1},{4,2},{5,3},{6,4},{7,5},{8,6},{9,7},{10,... | collective-permute-start | bytes 221192 | tf_op jit(solution)/shard_map/ppermute | solution.py:374
  22.2 0.9 %copy-start.1 = (f32[6]{0:T(128)S(1)}, f32[6]{0:T(128)}, u32[]{:S(2)}) copy-start(f32[6]{0:T(128)} %weight_ref.1) | copy-start | bytes 76
  22.2 4.2 %collective-permute-start.8 = (bf16[144,256]{1,0:T(8,128)(2,1)}, bf16[144,256]{1,0:T(8,128)(2,1)S(1)}, u32[]{:S(2)}, u32[]{:S(2)}) collective-permute-start(bf16[144,256]{1,0:T(8,128)(2,1)} %get-tuple-element.25), channel_id=1, source_target_pairs={{0,31},{1,30},{2,1},{3,0},{4,3},{5,2},{6,5},{7,4},{8,7},{9,6},{10,... | collective-permute-start | bytes 221192 | tf_op jit(solution)/shard_map/ppermute | solution.py:374
  23.1 0.9 %copy-start = (bf16[144,256]{1,0:T(8,128)(2,1)S(1)}, bf16[144,256]{1,0:T(8,128)(2,1)}, u32[]{:S(2)}) copy-start(bf16[144,256]{1,0:T(8,128)(2,1)} %get-tuple-element.14.refs_0_) | copy-start | bytes 221188

commit v12 on v11

--- a/solution.py
+++ b/solution.py
@@ -46,9 +46,12 @@
         tiles_ref,
         kernels,
         weights,
-        shifted,
-        toeplitz,
-        matches,
+        shifted_even,
+        shifted_odd,
+        toeplitz_even,
+        toeplitz_odd,
+        matches_even,
+        matches_odd,
         sums,
         extra,
         arrival,
@@ -94,7 +97,11 @@
         )
 
     extra[...] = jnp.zeros_like(extra)
-    shifted[...] = jnp.zeros_like(shifted)
+    shifted = (shifted_even, shifted_odd)
+    toeplitz = (toeplitz_even, toeplitz_odd)
+    matches = (matches_even, matches_odd)
+    for buffer in range(2):
+        shifted[buffer][...] = jnp.zeros_like(shifted[buffer])
     eye = (iota((8 * tile_count, tile_count), 0) // 8 == iota((8 * tile_count, tile_count), 1))
     entry = iota((1, table_ref.shape[1]), 1)
     chosen = jnp.concatenate(
@@ -150,8 +157,8 @@
             for fine in range(4):
                 part = moved(pixels, -1 - fine if side else fine)
                 top = fine * FINE_ROWS
-                shifted[buffer, place, side, top + 16 : top + 64, :width] = part[:48]
-                shifted[buffer, place, side, top : top + 48, width:] = part[16:]
+                shifted[buffer][place, side, top + 16 : top + 64, :width] = part[:48]
+                shifted[buffer][place, side, top : top + 48, width:] = part[16:]
             for coarse in range(COARSE):
                 for pair in range(2):
                     vector = (side * COARSE + coarse) * 2 + pair
@@ -159,8 +166,7 @@
                         kernels[tile, vector : vector + 1, :], (BLOCK, width)
                     )
                     turned = pltpu.roll(spread, 0, 1, stride=1, stride_axis=0)
-                    toeplitz[
-                        buffer,
+                    toeplitz[buffer][
                         place,
                         side,
                         coarse * BLOCK : (coarse + 1) * BLOCK,
@@ -171,8 +177,8 @@
         matched = [jnp.zeros((BLOCK, width), jnp.float32) for _ in range(2)]
         for side in range(2):
             passed = jnp.dot(
-                toeplitz[buffer, place, side],
-                shifted[buffer, place, side],
+                toeplitz[buffer][place, side],
+                shifted[buffer][place, side],
                 preferred_element_type=jnp.float32,
             )
             for part in range(2):
@@ -184,7 +190,7 @@
                         ],
                         -4 * coarse if side else 4 * coarse,
                     )
-        matches[buffer, place] = jnp.concatenate(matched, axis=0)
+        matches[buffer][place] = jnp.concatenate(matched, axis=0)
 
     def deliver(visit, buffer):
         sums[...] = jnp.zeros_like(sums)
@@ -193,7 +199,7 @@
             offset = offset_ref[tile]
             bucket = lax.rem(patch_ref[tile] - owner + REACH + patches, patches)
             weight = weights[tile]
-            value = matches[buffer, place].reshape(rows // 8, 8, width) * weight[None]
+            value = matches[buffer][place].reshape(rows // 8, 8, width) * weight[None]
             turned = pltpu.roll(value.reshape(rows, width), lax.rem(offset, width), 1)
             sums[bucket, :, :width] += jnp.where(lane >= offset, turned, 0.0)
             sums[bucket, :, width:] += jnp.where(lane < offset, turned, 0.0)
@@ -337,9 +343,11 @@
             pltpu.VMEM((tile_count, rows, width), jnp.bfloat16),
             pltpu.VMEM((tile_count, VECTORS, width), jnp.float32),
             pltpu.VMEM((tile_count, 8, width), jnp.float32),
-            pltpu.VMEM((2, per_visit, 2, 4 * FINE_ROWS, 2 * width), jnp.bfloat16),
-            pltpu.VMEM((2, per_visit, 2, COARSE * BLOCK, 2 * width), jnp.bfloat16),
-            pltpu.VMEM((2, per_visit, rows, width), jnp.float32),
+        ]
+        + [pltpu.VMEM((per_visit, 2, 4 * FINE_ROWS, 2 * width), jnp.bfloat16)] * 2
+        + [pltpu.VMEM((per_visit, 2, COARSE * BLOCK, 2 * width), jnp.bfloat16)] * 2
+        + [pltpu.VMEM((per_visit, rows, width), jnp.float32)] * 2
+        + [
             pltpu.VMEM((SPREAD, rows, PW), jnp.float32),
             pltpu.VMEM((SPREAD, EXTRA, PW), jnp.float32),
             pltpu.SemaphoreType.DMA,

time: 27.7 us -> 27.7 us (level)
  no operation moved by 1% of the time
where the time goes in v12:
time: 27.7 us; the launch traced here: 27.4 us
  starting transfers between devices  14.4 us (52%)
  Pallas kernels  9.35 us (34%)
  waiting for transfers between devices  2.07 us (7%)
  local copies, waits for them, and re-layouts  0.89 us (3%)
  between operations  0.67 us (2%)
    ppermute x9, starting transfers between devices, local(): lax.ppermute(messages[(distance + REACH) * groups + turn], ('ra', 'band')...  14.4 us
    pallas_call x1, Pallas kernels, local(): pl.pallas_call(functools.partial(match_kernel, patches, groups), in_specs...  7.52 us
    ppermute x9, waiting for transfers between devices, local(): lax.ppermute(messages[(distance + REACH) * groups + turn], ('ra', 'band')...  2.07 us
    pallas_call x1, Pallas kernels, local(): pl.pallas_call(functools.partial(combine_kernel, visits), in_specs=[vmem]...  0.96 us
    unnamed x4, local copies, waits for them, and re-layouts  0.89 us
    pallas_call x1, Pallas kernels, local(): pl.pallas_call(functools.partial(early_kernel, visits, row_share), in_spe...  0.87 us
  transfers between devices with their start and end apart: 9, of which 3 were waited for; matrix products, arithmetic and copies ran while one was open for 0% of the time, Pallas kernels for 3%

profile of v12, /device:TPU:0, one launch (start us, length us, event | category | flops | bytes accessed | tf_op | source)
XLA Modules:
  0.0 27.4 jit_solution(6153849480104709006)
XLA Ops:
  0.6 7.5 %match_and_sum.1 = (bf16[144,256]{1,0:T(8,128)(2,1)}, bf16[144,256]{1,0:T(8,128)(2,1)}, bf16[144,256]{1,0:T(8,128)(2,1)}, bf16[144,256]{1,0:T(8,128)(2,1)}, bf16...) custom-call(s32[32]{0:T(128)} %patch_ref.1, ...), custom_call_target="tpu_custom_call" | custom-call | tf_op jit(solution)/shard_map/match_and_sum/pallas_call | solution.py:333
  8.2 0.5 %collective-permute-start = (bf16[144,256]{1,0:T(8,128)(2,1)}, bf16[144,256]{1,0:T(8,128)(2,1)S(1)}, u32[]{:S(2)}, u32[]{:S(2)}) collective-permute-start(bf16[144,256]{1,0:T(8,128)(2,1)} %get-tuple-element.15), channel_id=1, source_target_pairs={{0,2},{1,3},{2,4},{3,5},{4,6},{5,7},{6,8},{7,9},{8,10},{9,11},{10,... | collective-permute-start | bytes 221192 | tf_op jit(solution)/shard_map/ppermute | solution.py:382
  8.7 3.7 %collective-permute-start.1 = (bf16[144,256]{1,0:T(8,128)(2,1)}, bf16[144,256]{1,0:T(8,128)(2,1)S(1)}, u32[]{:S(2)}, u32[]{:S(2)}) collective-permute-start(bf16[144,256]{1,0:T(8,128)(2,1)} %get-tuple-element.16), channel_id=1, source_target_pairs={{0,3},{1,2},{2,5},{3,4},{4,7},{5,6},{6,9},{7,8},{8,11},{9,10},{10,... | collective-permute-start | bytes 221192 | tf_op jit(solution)/shard_map/ppermute | solution.py:382
  12.4 1.5 %collective-permute-start.2 = (bf16[144,256]{1,0:T(8,128)(2,1)}, bf16[144,256]{1,0:T(8,128)(2,1)S(1)}, u32[]{:S(2)}, u32[]{:S(2)}) collective-permute-start(bf16[144,256]{1,0:T(8,128)(2,1)} %get-tuple-element.17), channel_id=1, source_target_pairs={{0,4},{1,5},{2,6},{3,7},{4,8},{5,9},{6,10},{7,11},{8,12},{9,13},{1... | collective-permute-start | bytes 221192 | tf_op jit(solution)/shard_map/ppermute | solution.py:382
  13.9 1.4 %collective-permute-start.3 = (bf16[144,256]{1,0:T(8,128)(2,1)}, bf16[144,256]{1,0:T(8,128)(2,1)S(1)}, u32[]{:S(2)}, u32[]{:S(2)}) collective-permute-start(bf16[144,256]{1,0:T(8,128)(2,1)} %get-tuple-element.18), channel_id=1, source_target_pairs={{0,5},{1,4},{2,7},{3,6},{4,9},{5,8},{6,11},{7,10},{8,13},{9,12},{1... | collective-permute-start | bytes 221192 | tf_op jit(solution)/shard_map/ppermute | solution.py:382
  15.4 1.5 %collective-permute-start.4 = (bf16[144,256]{1,0:T(8,128)(2,1)}, bf16[144,256]{1,0:T(8,128)(2,1)S(1)}, u32[]{:S(2)}, u32[]{:S(2)}) collective-permute-start(bf16[144,256]{1,0:T(8,128)(2,1)} %get-tuple-element.19), channel_id=1, source_target_pairs={{0,1},{1,0},{2,3},{3,2},{4,5},{5,4},{6,7},{7,6},{8,9},{9,8},{10,11... | collective-permute-start | bytes 221192 | tf_op jit(solution)/shard_map/ppermute | solution.py:382
  16.9 0.0 collective-permute-done.refs_1_
  16.9 3.2 %collective-permute-start.5 = (bf16[144,256]{1,0:T(8,128)(2,1)}, bf16[144,256]{1,0:T(8,128)(2,1)S(1)}, u32[]{:S(2)}, u32[]{:S(2)}) collective-permute-start(bf16[144,256]{1,0:T(8,128)(2,1)} %get-tuple-element.22), channel_id=1, source_target_pairs={{0,28},{1,29},{2,30},{3,31},{4,0},{5,1},{6,2},{7,3},{8,4},{9,5},{1... | collective-permute-start | bytes 221192 | tf_op jit(solution)/shard_map/ppermute | solution.py:382
  20.1 0.0 collective-permute-done.1.refs_2_
  20.1 0.4 %collective-permute-start.6 = (bf16[144,256]{1,0:T(8,128)(2,1)}, bf16[144,256]{1,0:T(8,128)(2,1)S(1)}, u32[]{:S(2)}, u32[]{:S(2)}) collective-permute-start(bf16[144,256]{1,0:T(8,128)(2,1)} %get-tuple-element.23), channel_id=1, source_target_pairs={{0,29},{1,28},{2,31},{3,30},{4,1},{5,0},{6,3},{7,2},{8,5},{9,4},{1... | collective-permute-start | bytes 221192 | tf_op jit(solution)/shard_map/ppermute | solution.py:382
  20.6 0.0 collective-permute-done.2.refs_3_
  20.6 1.1 %collective-permute-start.7 = (bf16[144,256]{1,0:T(8,128)(2,1)}, bf16[144,256]{1,0:T(8,128)(2,1)S(1)}, u32[]{:S(2)}, u32[]{:S(2)}) collective-permute-start(bf16[144,256]{1,0:T(8,128)(2,1)} %get-tuple-element.24), channel_id=1, source_target_pairs={{0,30},{1,31},{2,0},{3,1},{4,2},{5,3},{6,4},{7,5},{8,6},{9,7},{10,... | collective-permute-start | bytes 221192 | tf_op jit(solution)/shard_map/ppermute | solution.py:382
  21.7 0.5 %collective-permute-done.3.refs_4_ = bf16[144,256]{1,0:T(8,128)(2,1)S(1)} collective-permute-done((bf16[144,256]{1,0:T(8,128)(2,1)}, bf16[144,256]{1,0:T(8,128)(2,1)S(1)}, u32[]{:S(2)}, u32[]{:S(2)}) %collective-permute-start.3) | collective-permute-done | bytes 73760 | tf_op jit(solution)/shard_map/ppermute | solution.py:382
  22.2 0.0 copy-start.1
  22.2 0.9 %collective-permute-start.8 = (bf16[144,256]{1,0:T(8,128)(2,1)}, bf16[144,256]{1,0:T(8,128)(2,1)S(1)}, u32[]{:S(2)}, u32[]{:S(2)}) collective-permute-start(bf16[144,256]{1,0:T(8,128)(2,1)} %get-tuple-element.25), channel_id=1, source_target_pairs={{0,31},{1,30},{2,1},{3,0},{4,3},{5,2},{6,5},{7,4},{8,7},{9,6},{10,... | collective-permute-start | bytes 221192 | tf_op jit(solution)/shard_map/ppermute | solution.py:382
  23.1 0.0 collective-permute-done.4.refs_5_
  23.1 0.0 copy-done.1
  23.1 0.9 %copy-done = bf16[144,256]{1,0:T(8,128)(2,1)S(1)} copy-done((bf16[144,256]{1,0:T(8,128)(2,1)S(1)}, bf16[144,256]{1,0:T(8,128)(2,1)}, u32[]{:S(2)}) %copy-start) | copy-done | bytes 73752
  24.0 0.9 %combine_early.1 = (f32[192,256]{1,0:T(8,128)S(1)}, f32[16,256]{1,0:T(8,128)S(1)}) custom-call(f32[6]{0:T(128)S(1)} %copy-done.1, bf16[144,256]{1,0:T(8,128)(2,1)S(1)} %copy-done, bf16[144,256]{1,0:T(8,128)(2,1)S(1)} %collective-permute-done.refs_1_, bf16[144,256]{1,0:T(8,128)(2,1)S(1)} %collective-permute-done.1.refs_2_, ...), custom_call_target="tpu_custom_call" | custom-call | tf_op jit(solution)/shard_map/combine_early/pallas_call | solution.py:387
  24.8 0.0 collective-permute-done.5.refs_0_
  24.9 0.8 %collective-permute-done.6.refs_1_ = bf16[144,256]{1,0:T(8,128)(2,1)S(1)} collective-permute-done((bf16[144,256]{1,0:T(8,128)(2,1)}, bf16[144,256]{1,0:T(8,128)(2,1)S(1)}, u32[]{:S(2)}, u32[]{:S(2)}) %collective-permute-start.6) | collective-permute-done | bytes 73760 | tf_op jit(solution)/shard_map/ppermute | solution.py:382
  25.6 0.0 collective-permute-done.7.refs_2_
  25.6 0.8 %collective-permute-done.8.refs_3_ = bf16[144,256]{1,0:T(8,128)(2,1)S(1)} collective-permute-done((bf16[144,256]{1,0:T(8,128)(2,1)}, bf16[144,256]{1,0:T(8,128)(2,1)S(1)}, u32[]{:S(2)}, u32[]{:S(2)}) %collective-permute-start.8) | collective-permute-done | bytes 73760 | tf_op jit(solution)/shard_map/ppermute | solution.py:382
  26.4 1.0 %combine.1 = (f32[6,32,256]{2,1,0:T(8,128)}, f32[32,256]{1,0:T(8,128)}) custom-call(f32[192,256]{1,0:T(8,128)S(1)} %get-tuple-element.20.totals_ref, f32[16,256]{1,0:T(8,128)S(1)} %get-tuple-element.21.rows_ref, bf16[144,256]{1,0:T(8,128)(2,1)S(1)} %collective-permute-done.5.refs_0_, bf16[144,256]{1,0:T(8,128)(2,1)S(1)} %collective-permute-done.6.refs_1_, ...), custom_call_target="tpu_custom_call" | custom-call | tf_op jit(solution)/shard_map/combine/pallas_call | solution.py:398
  (1 shorter events, 0.0 us)
Async XLA Ops:
  8.2 8.7 %collective-permute-start = (bf16[144,256]{1,0:T(8,128)(2,1)}, bf16[144,256]{1,0:T(8,128)(2,1)S(1)}, u32[]{:S(2)}, u32[]{:S(2)}) collective-permute-start(bf16[144,256]{1,0:T(8,128)(2,1)} %get-tuple-element.15), channel_id=1, source_target_pairs={{0,2},{1,3},{2,4},{3,5},{4,6},{5,7},{6,8},{7,9},{8,10},{9,11},{10,... | collective-permute-start | bytes 221192 | tf_op jit(solution)/shard_map/ppermute | solution.py:382
  8.7 11.5 %collective-permute-start.1 = (bf16[144,256]{1,0:T(8,128)(2,1)}, bf16[144,256]{1,0:T(8,128)(2,1)S(1)}, u32[]{:S(2)}, u32[]{:S(2)}) collective-permute-start(bf16[144,256]{1,0:T(8,128)(2,1)} %get-tuple-element.16), channel_id=1, source_target_pairs={{0,3},{1,2},{2,5},{3,4},{4,7},{5,6},{6,9},{7,8},{8,11},{9,10},{10,... | collective-permute-start | bytes 221192 | tf_op jit(solution)/shard_map/ppermute | solution.py:382
  12.4 8.2 %collective-permute-start.2 = (bf16[144,256]{1,0:T(8,128)(2,1)}, bf16[144,256]{1,0:T(8,128)(2,1)S(1)}, u32[]{:S(2)}, u32[]{:S(2)}) collective-permute-start(bf16[144,256]{1,0:T(8,128)(2,1)} %get-tuple-element.17), channel_id=1, source_target_pairs={{0,4},{1,5},{2,6},{3,7},{4,8},{5,9},{6,10},{7,11},{8,12},{9,13},{1... | collective-permute-start | bytes 221192 | tf_op jit(solution)/shard_map/ppermute | solution.py:382
  13.9 8.3 %collective-permute-start.3 = (bf16[144,256]{1,0:T(8,128)(2,1)}, bf16[144,256]{1,0:T(8,128)(2,1)S(1)}, u32[]{:S(2)}, u32[]{:S(2)}) collective-permute-start(bf16[144,256]{1,0:T(8,128)(2,1)} %get-tuple-element.18), channel_id=1, source_target_pairs={{0,5},{1,4},{2,7},{3,6},{4,9},{5,8},{6,11},{7,10},{8,13},{9,12},{1... | collective-permute-start | bytes 221192 | tf_op jit(solution)/shard_map/ppermute | solution.py:382
  15.4 7.7 %collective-permute-start.4 = (bf16[144,256]{1,0:T(8,128)(2,1)}, bf16[144,256]{1,0:T(8,128)(2,1)S(1)}, u32[]{:S(2)}, u32[]{:S(2)}) collective-permute-start(bf16[144,256]{1,0:T(8,128)(2,1)} %get-tuple-element.19), channel_id=1, source_target_pairs={{0,1},{1,0},{2,3},{3,2},{4,5},{5,4},{6,7},{7,6},{8,9},{9,8},{10,11... | collective-permute-start | bytes 221192 | tf_op jit(solution)/shard_map/ppermute | solution.py:382
  16.9 7.9 %collective-permute-start.5 = (bf16[144,256]{1,0:T(8,128)(2,1)}, bf16[144,256]{1,0:T(8,128)(2,1)S(1)}, u32[]{:S(2)}, u32[]{:S(2)}) collective-permute-start(bf16[144,256]{1,0:T(8,128)(2,1)} %get-tuple-element.22), channel_id=1, source_target_pairs={{0,28},{1,29},{2,30},{3,31},{4,0},{5,1},{6,2},{7,3},{8,4},{9,5},{1... | collective-permute-start | bytes 221192 | tf_op jit(solution)/shard_map/ppermute | solution.py:382
  20.1 5.5 %collective-permute-start.6 = (bf16[144,256]{1,0:T(8,128)(2,1)}, bf16[144,256]{1,0:T(8,128)(2,1)S(1)}, u32[]{:S(2)}, u32[]{:S(2)}) collective-permute-start(bf16[144,256]{1,0:T(8,128)(2,1)} %get-tuple-element.23), channel_id=1, source_target_pairs={{0,29},{1,28},{2,31},{3,30},{4,1},{5,0},{6,3},{7,2},{8,5},{9,4},{1... | collective-permute-start | bytes 221192 | tf_op jit(solution)/shard_map/ppermute | solution.py:382
  20.6 5.0 %collective-permute-start.7 = (bf16[144,256]{1,0:T(8,128)(2,1)}, bf16[144,256]{1,0:T(8,128)(2,1)S(1)}, u32[]{:S(2)}, u32[]{:S(2)}) collective-permute-start(bf16[144,256]{1,0:T(8,128)(2,1)} %get-tuple-element.24), channel_id=1, source_target_pairs={{0,30},{1,31},{2,0},{3,1},{4,2},{5,3},{6,4},{7,5},{8,6},{9,7},{10,... | collective-permute-start | bytes 221192 | tf_op jit(solution)/shard_map/ppermute | solution.py:382
  22.2 0.9 %copy-start.1 = (f32[6]{0:T(128)S(1)}, f32[6]{0:T(128)}, u32[]{:S(2)}) copy-start(f32[6]{0:T(128)} %weight_ref.1) | copy-start | bytes 76
  22.2 4.2 %collective-permute-start.8 = (bf16[144,256]{1,0:T(8,128)(2,1)}, bf16[144,256]{1,0:T(8,128)(2,1)S(1)}, u32[]{:S(2)}, u32[]{:S(2)}) collective-permute-start(bf16[144,256]{1,0:T(8,128)(2,1)} %get-tuple-element.25), channel_id=1, source_target_pairs={{0,31},{1,30},{2,1},{3,0},{4,3},{5,2},{6,5},{7,4},{8,7},{9,6},{10,... | collective-permute-start | bytes 221192 | tf_op jit(solution)/shard_map/ppermute | solution.py:382
  23.1 0.9 %copy-start = (bf16[144,256]{1,0:T(8,128)(2,1)S(1)}, bf16[144,256]{1,0:T(8,128)(2,1)}, u32[]{:S(2)}) copy-start(bf16[144,256]{1,0:T(8,128)(2,1)} %get-tuple-element.14.refs_0_) | copy-start | bytes 221188

commit v13 on v7

--- a/solution.py
+++ b/solution.py
@@ -26,10 +26,10 @@
 def match_kernel(
     patches,
     groups,
-    patch_ref,
-    offset_ref,
-    index_ref,
-    band_ref,
+    patch_hbm,
+    offset_hbm,
+    index_hbm,
+    band_hbm,
     table_hbm,
     weight_hbm,
     rowk_hbm,
@@ -39,6 +39,10 @@
 ):
     messages = rest[: SPREAD * groups]
     (
+        patch_ref,
+        offset_ref,
+        index_ref,
+        band_ref,
         table_ref,
         weight_ref,
         rowk_ref,
@@ -68,10 +72,14 @@
         pltpu.make_async_copy(source, target, ready.at[place])
         for place, (source, target) in enumerate(
             (
+                (index_hbm, index_ref),
                 (table_hbm, table_ref),
                 (weight_hbm, weight_ref),
                 (rowk_hbm, rowk_ref),
                 (colk_hbm, colk_ref),
+                (patch_hbm, patch_ref),
+                (offset_hbm, offset_ref),
+                (band_hbm, band_ref),
             )
         )
     ]
@@ -98,18 +106,32 @@
         )
 
     extra[...] = jnp.zeros_like(extra)
-    shifted[...] = jnp.zeros_like(shifted)
+    for place in range(per_visit):
+        for side in range(2):
+            for fine in range(4):
+                top = fine * FINE_ROWS
+                shifted[place, side, top : top + 16, :width] = jnp.zeros(
+                    (16, width), jnp.bfloat16
+                )
+                shifted[place, side, top + 48 : top + 64, width:] = jnp.zeros(
+                    (16, width), jnp.bfloat16
+                )
     eye = (iota((tile_count, tile_count), 0) == iota((tile_count, tile_count), 1)).astype(
         jnp.bfloat16
-    )
-    entry = iota((1, table_ref.shape[1]), 1)
-    chosen = jnp.concatenate(
-        [(entry == index_ref[j]).astype(jnp.float32) for j in range(tile_count)], axis=0
     )
     for copy in small:
         copy.wait()
     weights[...] = across(eye, jnp.broadcast_to(weight_ref[...], (width, tile_count)))
-    coeffs = across(chosen, table_ref[...], precision=lax.Precision.HIGHEST)
+    entry = iota((1, table_ref.shape[1]), 1)
+    chosen = jnp.concatenate(
+        [(entry == index_ref[j]).astype(jnp.float32) for j in range(tile_count)], axis=0
+    ).astype(jnp.bfloat16)
+    rest_of = table_ref[...]
+    coeffs = jnp.zeros((tile_count, basis), jnp.float32)
+    for _ in range(3):
+        piece = rest_of.astype(jnp.bfloat16)
+        rest_of = rest_of - piece.astype(jnp.float32)
+        coeffs += across(chosen, piece)
 
     line = iota((2 * VECTORS, taps), 0)
     column = iota((2 * VECTORS, taps), 1)
@@ -139,6 +161,18 @@
     lane = iota((rows, width), 1)
     column = iota((1, width), 1)
 
+    def edge(distance):
+        here = iota((16, width), 1) + distance
+        return ((here >= 0) & (here < width)).astype(jnp.float32).astype(jnp.bfloat16)
+
+    edges = {distance: edge(distance) for distance in range(-4, 4) if distance != 0}
+
+    def moved_tile(value, distance):
+        if distance == 0:
+            return value
+        turned = pltpu.roll(value, -distance % width, 1).reshape(rows // 16, 16, width)
+        return (turned * edges[distance][None]).reshape(rows, width)
+
     def moved(value, distance):
         if distance == 0:
             return value
@@ -155,7 +189,7 @@
             pixels = tiles_ref[tile]
             for side in range(2):
                 for fine in range(4):
-                    part = moved(pixels, -1 - fine if side else fine)
+                    part = moved_tile(pixels, -1 - fine if side else fine)
                     top = fine * FINE_ROWS
                     shifted[place, side, top + 16 : top + 64, :width] = part[:48]
                     shifted[place, side, top : top + 48, width:] = part[16:]
@@ -318,10 +352,14 @@
     anywhere = pl.BlockSpec(memory_space=pl.ANY)
     messages = pl.pallas_call(
         functools.partial(match_kernel, patches, groups),
-        in_specs=[smem] * 4 + [anywhere] * 5,
+        in_specs=[anywhere] * 9,
         out_specs=[vmem] * (SPREAD * groups),
         out_shape=[jax.ShapeDtypeStruct((length, PW), jnp.bfloat16)] * (SPREAD * groups),
         scratch_shapes=[
+            pltpu.SMEM((tile_count,), jnp.int32),
+            pltpu.SMEM((tile_count,), jnp.int32),
+            pltpu.SMEM((tile_count,), jnp.int32),
+            pltpu.SMEM((visits,), jnp.int32),
             pltpu.VMEM(coeff_table.shape[::-1], jnp.float32),
             pltpu.VMEM((1, tile_count), jnp.bfloat16),
             pltpu.VMEM((basis, taps), jnp.bfloat16),
@@ -335,7 +373,7 @@
             pltpu.VMEM((SPREAD, rows, PW), jnp.float32),
             pltpu.VMEM((SPREAD, EXTRA, PW), jnp.float32),
             pltpu.SemaphoreType.DMA((visits,)),
-            pltpu.SemaphoreType.DMA((4,)),
+            pltpu.SemaphoreType.DMA((8,)),
         ],
         compiler_params=pltpu.CompilerParams(vmem_limit_bytes=62 * 1024 * 1024),
         name="match_and_sum",

time: 27.2 us -> 26.4 us (0.971)
  Pallas kernels: 8.82 us -> 8.05 us
    pallas_call x1, Pallas kernels: 7 us -> 6.23 us  [local(): pl.pallas_call(functools.partial(match_kernel, patches, groups), in_specs...]
where the time goes in v13:
time: 26.4 us; the launch traced here: 26.1 us
  starting transfers between devices  14.4 us (55%)
  Pallas kernels  8.05 us (30%)
  waiting for transfers between devices  2.06 us (8%)
  local copies, waits for them, and re-layouts  0.89 us (3%)
  between operations  0.67 us (3%)
    ppermute x9, starting transfers between devices, local(): lax.ppermute(messages[(distance + REACH) * groups + turn], ('ra', 'band')...  14.4 us
    pallas_call x1, Pallas kernels, local(): pl.pallas_call(functools.partial(match_kernel, patches, groups), in_specs...  6.23 us
    ppermute x9, waiting for transfers between devices, local(): lax.ppermute(messages[(distance + REACH) * groups + turn], ('ra', 'band')...  2.06 us
    pallas_call x1, Pallas kernels, local(): pl.pallas_call(functools.partial(combine_kernel, visits), in_specs=[vmem]...  0.95 us
    unnamed x4, local copies, waits for them, and re-layouts  0.89 us
    pallas_call x1, Pallas kernels, local(): pl.pallas_call(functools.partial(early_kernel, visits, row_share), in_spe...  0.87 us
  transfers between devices with their start and end apart: 9, of which 3 were waited for; matrix products, arithmetic and copies ran while one was open for 0% of the time, Pallas kernels for 3%

profile of v13, /device:TPU:0, one launch (start us, length us, event | category | flops | bytes accessed | tf_op | source)
XLA Modules:
  0.0 26.1 jit_solution(12649280798201284557)
XLA Ops:
  0.6 6.2 %match_and_sum.1 = (bf16[144,256]{1,0:T(8,128)(2,1)}, bf16[144,256]{1,0:T(8,128)(2,1)}, bf16[144,256]{1,0:T(8,128)(2,1)}, bf16[144,256]{1,0:T(8,128)(2,1)}, bf16...) custom-call(s32[32]{0:T(128)} %patch_hbm.1, ...), custom_call_target="tpu_custom_call" | custom-call | tf_op jit(solution)/shard_map/match_and_sum/pallas_call | solution.py:353
  6.9 0.5 %collective-permute-start = (bf16[144,256]{1,0:T(8,128)(2,1)}, bf16[144,256]{1,0:T(8,128)(2,1)S(1)}, u32[]{:S(2)}, u32[]{:S(2)}) collective-permute-start(bf16[144,256]{1,0:T(8,128)(2,1)} %get-tuple-element.15), channel_id=1, source_target_pairs={{0,2},{1,3},{2,4},{3,5},{4,6},{5,7},{6,8},{7,9},{8,10},{9,11},{10,... | collective-permute-start | bytes 221192 | tf_op jit(solution)/shard_map/ppermute | solution.py:404
  7.4 3.7 %collective-permute-start.1 = (bf16[144,256]{1,0:T(8,128)(2,1)}, bf16[144,256]{1,0:T(8,128)(2,1)S(1)}, u32[]{:S(2)}, u32[]{:S(2)}) collective-permute-start(bf16[144,256]{1,0:T(8,128)(2,1)} %get-tuple-element.16), channel_id=1, source_target_pairs={{0,3},{1,2},{2,5},{3,4},{4,7},{5,6},{6,9},{7,8},{8,11},{9,10},{10,... | collective-permute-start | bytes 221192 | tf_op jit(solution)/shard_map/ppermute | solution.py:404
  11.1 1.5 %collective-permute-start.2 = (bf16[144,256]{1,0:T(8,128)(2,1)}, bf16[144,256]{1,0:T(8,128)(2,1)S(1)}, u32[]{:S(2)}, u32[]{:S(2)}) collective-permute-start(bf16[144,256]{1,0:T(8,128)(2,1)} %get-tuple-element.17), channel_id=1, source_target_pairs={{0,4},{1,5},{2,6},{3,7},{4,8},{5,9},{6,10},{7,11},{8,12},{9,13},{1... | collective-permute-start | bytes 221192 | tf_op jit(solution)/shard_map/ppermute | solution.py:404
  12.7 1.4 %collective-permute-start.3 = (bf16[144,256]{1,0:T(8,128)(2,1)}, bf16[144,256]{1,0:T(8,128)(2,1)S(1)}, u32[]{:S(2)}, u32[]{:S(2)}) collective-permute-start(bf16[144,256]{1,0:T(8,128)(2,1)} %get-tuple-element.18), channel_id=1, source_target_pairs={{0,5},{1,4},{2,7},{3,6},{4,9},{5,8},{6,11},{7,10},{8,13},{9,12},{1... | collective-permute-start | bytes 221192 | tf_op jit(solution)/shard_map/ppermute | solution.py:404
  14.1 1.5 %collective-permute-start.4 = (bf16[144,256]{1,0:T(8,128)(2,1)}, bf16[144,256]{1,0:T(8,128)(2,1)S(1)}, u32[]{:S(2)}, u32[]{:S(2)}) collective-permute-start(bf16[144,256]{1,0:T(8,128)(2,1)} %get-tuple-element.19), channel_id=1, source_target_pairs={{0,1},{1,0},{2,3},{3,2},{4,5},{5,4},{6,7},{7,6},{8,9},{9,8},{10,11... | collective-permute-start | bytes 221192 | tf_op jit(solution)/shard_map/ppermute | solution.py:404
  15.6 0.0 collective-permute-done.refs_1_
  15.6 3.2 %collective-permute-start.5 = (bf16[144,256]{1,0:T(8,128)(2,1)}, bf16[144,256]{1,0:T(8,128)(2,1)S(1)}, u32[]{:S(2)}, u32[]{:S(2)}) collective-permute-start(bf16[144,256]{1,0:T(8,128)(2,1)} %get-tuple-element.22), channel_id=1, source_target_pairs={{0,28},{1,29},{2,30},{3,31},{4,0},{5,1},{6,2},{7,3},{8,4},{9,5},{1... | collective-permute-start | bytes 221192 | tf_op jit(solution)/shard_map/ppermute | solution.py:404
  18.8 0.0 collective-permute-done.1.refs_2_
  18.8 0.4 %collective-permute-start.6 = (bf16[144,256]{1,0:T(8,128)(2,1)}, bf16[144,256]{1,0:T(8,128)(2,1)S(1)}, u32[]{:S(2)}, u32[]{:S(2)}) collective-permute-start(bf16[144,256]{1,0:T(8,128)(2,1)} %get-tuple-element.23), channel_id=1, source_target_pairs={{0,29},{1,28},{2,31},{3,30},{4,1},{5,0},{6,3},{7,2},{8,5},{9,4},{1... | collective-permute-start | bytes 221192 | tf_op jit(solution)/shard_map/ppermute | solution.py:404
  19.3 0.0 collective-permute-done.2.refs_3_
  19.3 1.1 %collective-permute-start.7 = (bf16[144,256]{1,0:T(8,128)(2,1)}, bf16[144,256]{1,0:T(8,128)(2,1)S(1)}, u32[]{:S(2)}, u32[]{:S(2)}) collective-permute-start(bf16[144,256]{1,0:T(8,128)(2,1)} %get-tuple-element.24), channel_id=1, source_target_pairs={{0,30},{1,31},{2,0},{3,1},{4,2},{5,3},{6,4},{7,5},{8,6},{9,7},{10,... | collective-permute-start | bytes 221192 | tf_op jit(solution)/shard_map/ppermute | solution.py:404
  20.4 0.5 %collective-permute-done.3.refs_4_ = bf16[144,256]{1,0:T(8,128)(2,1)S(1)} collective-permute-done((bf16[144,256]{1,0:T(8,128)(2,1)}, bf16[144,256]{1,0:T(8,128)(2,1)S(1)}, u32[]{:S(2)}, u32[]{:S(2)}) %collective-permute-start.3) | collective-permute-done | bytes 73760 | tf_op jit(solution)/shard_map/ppermute | solution.py:404
  20.9 0.0 copy-start.1
  20.9 0.9 %collective-permute-start.8 = (bf16[144,256]{1,0:T(8,128)(2,1)}, bf16[144,256]{1,0:T(8,128)(2,1)S(1)}, u32[]{:S(2)}, u32[]{:S(2)}) collective-permute-start(bf16[144,256]{1,0:T(8,128)(2,1)} %get-tuple-element.25), channel_id=1, source_target_pairs={{0,31},{1,30},{2,1},{3,0},{4,3},{5,2},{6,5},{7,4},{8,7},{9,6},{10,... | collective-permute-start | bytes 221192 | tf_op jit(solution)/shard_map/ppermute | solution.py:404
  21.8 0.0 collective-permute-done.4.refs_5_
  21.8 0.0 copy-done.1
  21.8 0.9 %copy-done = bf16[144,256]{1,0:T(8,128)(2,1)S(1)} copy-done((bf16[144,256]{1,0:T(8,128)(2,1)S(1)}, bf16[144,256]{1,0:T(8,128)(2,1)}, u32[]{:S(2)}) %copy-start) | copy-done | bytes 73752
  22.7 0.9 %combine_early.1 = (f32[192,256]{1,0:T(8,128)S(1)}, f32[16,256]{1,0:T(8,128)S(1)}) custom-call(f32[6]{0:T(128)S(1)} %copy-done.1, bf16[144,256]{1,0:T(8,128)(2,1)S(1)} %copy-done, bf16[144,256]{1,0:T(8,128)(2,1)S(1)} %collective-permute-done.refs_1_, bf16[144,256]{1,0:T(8,128)(2,1)S(1)} %collective-permute-done.1.refs_2_, ...), custom_call_target="tpu_custom_call" | custom-call | tf_op jit(solution)/shard_map/combine_early/pallas_call | solution.py:409
  23.6 0.0 collective-permute-done.5.refs_0_
  23.6 0.8 %collective-permute-done.6.refs_1_ = bf16[144,256]{1,0:T(8,128)(2,1)S(1)} collective-permute-done((bf16[144,256]{1,0:T(8,128)(2,1)}, bf16[144,256]{1,0:T(8,128)(2,1)S(1)}, u32[]{:S(2)}, u32[]{:S(2)}) %collective-permute-start.6) | collective-permute-done | bytes 73760 | tf_op jit(solution)/shard_map/ppermute | solution.py:404
  24.3 0.0 collective-permute-done.7.refs_2_
  24.3 0.8 %collective-permute-done.8.refs_3_ = bf16[144,256]{1,0:T(8,128)(2,1)S(1)} collective-permute-done((bf16[144,256]{1,0:T(8,128)(2,1)}, bf16[144,256]{1,0:T(8,128)(2,1)S(1)}, u32[]{:S(2)}, u32[]{:S(2)}) %collective-permute-start.8) | collective-permute-done | bytes 73760 | tf_op jit(solution)/shard_map/ppermute | solution.py:404
  25.1 1.0 %combine.1 = (f32[6,32,256]{2,1,0:T(8,128)}, f32[32,256]{1,0:T(8,128)}) custom-call(f32[192,256]{1,0:T(8,128)S(1)} %get-tuple-element.20.totals_ref, f32[16,256]{1,0:T(8,128)S(1)} %get-tuple-element.21.rows_ref, bf16[144,256]{1,0:T(8,128)(2,1)S(1)} %collective-permute-done.5.refs_0_, bf16[144,256]{1,0:T(8,128)(2,1)S(1)} %collective-permute-done.6.refs_1_, ...), custom_call_target="tpu_custom_call" | custom-call | tf_op jit(solution)/shard_map/combine/pallas_call | solution.py:420
  (1 shorter events, 0.0 us)
Async XLA Ops:
  6.9 8.7 %collective-permute-start = (bf16[144,256]{1,0:T(8,128)(2,1)}, bf16[144,256]{1,0:T(8,128)(2,1)S(1)}, u32[]{:S(2)}, u32[]{:S(2)}) collective-permute-start(bf16[144,256]{1,0:T(8,128)(2,1)} %get-tuple-element.15), channel_id=1, source_target_pairs={{0,2},{1,3},{2,4},{3,5},{4,6},{5,7},{6,8},{7,9},{8,10},{9,11},{10,... | collective-permute-start | bytes 221192 | tf_op jit(solution)/shard_map/ppermute | solution.py:404
  7.4 11.5 %collective-permute-start.1 = (bf16[144,256]{1,0:T(8,128)(2,1)}, bf16[144,256]{1,0:T(8,128)(2,1)S(1)}, u32[]{:S(2)}, u32[]{:S(2)}) collective-permute-start(bf16[144,256]{1,0:T(8,128)(2,1)} %get-tuple-element.16), channel_id=1, source_target_pairs={{0,3},{1,2},{2,5},{3,4},{4,7},{5,6},{6,9},{7,8},{8,11},{9,10},{10,... | collective-permute-start | bytes 221192 | tf_op jit(solution)/shard_map/ppermute | solution.py:404
  11.1 8.2 %collective-permute-start.2 = (bf16[144,256]{1,0:T(8,128)(2,1)}, bf16[144,256]{1,0:T(8,128)(2,1)S(1)}, u32[]{:S(2)}, u32[]{:S(2)}) collective-permute-start(bf16[144,256]{1,0:T(8,128)(2,1)} %get-tuple-element.17), channel_id=1, source_target_pairs={{0,4},{1,5},{2,6},{3,7},{4,8},{5,9},{6,10},{7,11},{8,12},{9,13},{1... | collective-permute-start | bytes 221192 | tf_op jit(solution)/shard_map/ppermute | solution.py:404
  12.7 8.3 %collective-permute-start.3 = (bf16[144,256]{1,0:T(8,128)(2,1)}, bf16[144,256]{1,0:T(8,128)(2,1)S(1)}, u32[]{:S(2)}, u32[]{:S(2)}) collective-permute-start(bf16[144,256]{1,0:T(8,128)(2,1)} %get-tuple-element.18), channel_id=1, source_target_pairs={{0,5},{1,4},{2,7},{3,6},{4,9},{5,8},{6,11},{7,10},{8,13},{9,12},{1... | collective-permute-start | bytes 221192 | tf_op jit(solution)/shard_map/ppermute | solution.py:404
  14.1 7.7 %collective-permute-start.4 = (bf16[144,256]{1,0:T(8,128)(2,1)}, bf16[144,256]{1,0:T(8,128)(2,1)S(1)}, u32[]{:S(2)}, u32[]{:S(2)}) collective-permute-start(bf16[144,256]{1,0:T(8,128)(2,1)} %get-tuple-element.19), channel_id=1, source_target_pairs={{0,1},{1,0},{2,3},{3,2},{4,5},{5,4},{6,7},{7,6},{8,9},{9,8},{10,11... | collective-permute-start | bytes 221192 | tf_op jit(solution)/shard_map/ppermute | solution.py:404
  15.6 7.9 %collective-permute-start.5 = (bf16[144,256]{1,0:T(8,128)(2,1)}, bf16[144,256]{1,0:T(8,128)(2,1)S(1)}, u32[]{:S(2)}, u32[]{:S(2)}) collective-permute-start(bf16[144,256]{1,0:T(8,128)(2,1)} %get-tuple-element.22), channel_id=1, source_target_pairs={{0,28},{1,29},{2,30},{3,31},{4,0},{5,1},{6,2},{7,3},{8,4},{9,5},{1... | collective-permute-start | bytes 221192 | tf_op jit(solution)/shard_map/ppermute | solution.py:404
  18.8 5.5 %collective-permute-start.6 = (bf16[144,256]{1,0:T(8,128)(2,1)}, bf16[144,256]{1,0:T(8,128)(2,1)S(1)}, u32[]{:S(2)}, u32[]{:S(2)}) collective-permute-start(bf16[144,256]{1,0:T(8,128)(2,1)} %get-tuple-element.23), channel_id=1, source_target_pairs={{0,29},{1,28},{2,31},{3,30},{4,1},{5,0},{6,3},{7,2},{8,5},{9,4},{1... | collective-permute-start | bytes 221192 | tf_op jit(solution)/shard_map/ppermute | solution.py:404
  19.3 5.0 %collective-permute-start.7 = (bf16[144,256]{1,0:T(8,128)(2,1)}, bf16[144,256]{1,0:T(8,128)(2,1)S(1)}, u32[]{:S(2)}, u32[]{:S(2)}) collective-permute-start(bf16[144,256]{1,0:T(8,128)(2,1)} %get-tuple-element.24), channel_id=1, source_target_pairs={{0,30},{1,31},{2,0},{3,1},{4,2},{5,3},{6,4},{7,5},{8,6},{9,7},{10,... | collective-permute-start | bytes 221192 | tf_op jit(solution)/shard_map/ppermute | solution.py:404
  20.9 0.9 %copy-start.1 = (f32[6]{0:T(128)S(1)}, f32[6]{0:T(128)}, u32[]{:S(2)}) copy-start(f32[6]{0:T(128)} %weight_ref.1) | copy-start | bytes 76
  20.9 4.2 %collective-permute-start.8 = (bf16[144,256]{1,0:T(8,128)(2,1)}, bf16[144,256]{1,0:T(8,128)(2,1)S(1)}, u32[]{:S(2)}, u32[]{:S(2)}) collective-permute-start(bf16[144,256]{1,0:T(8,128)(2,1)} %get-tuple-element.25), channel_id=1, source_target_pairs={{0,31},{1,30},{2,1},{3,0},{4,3},{5,2},{6,5},{7,4},{8,7},{9,6},{10,... | collective-permute-start | bytes 221192 | tf_op jit(solution)/shard_map/ppermute | solution.py:404
  21.8 0.9 %copy-start = (bf16[144,256]{1,0:T(8,128)(2,1)S(1)}, bf16[144,256]{1,0:T(8,128)(2,1)}, u32[]{:S(2)}) copy-start(bf16[144,256]{1,0:T(8,128)(2,1)} %get-tuple-element.14.refs_0_) | copy-start | bytes 221188

commit v14 on v13

--- a/solution.py
+++ b/solution.py
@@ -390,9 +390,9 @@
     )
 
     order = [(d, t) for d in range(1, REACH + 1) for t in range(groups)]
-    order += [(0, t) for t in range(1, groups)]
     early = len(order)
     order += [(d, t) for d in range(-REACH, 0) for t in range(groups)]
+    order += [(0, t) for t in range(1, groups)]
     arrived = []
     for distance, turn in order:
         route = [

time: 26.4 us -> 27.5 us (1.042)
  waiting for transfers between devices: 2.06 us -> 3.83 us
  starting transfers between devices: 14.4 us -> 13.8 us
    ppermute x9, waiting for transfers between devices: 2.06 us -> 3.83 us  [local(): lax.ppermute(messages[(distance + REACH) * groups + turn], ('ra', 'band')...]
    ppermute x9, starting transfers between devices: 14.4 us -> 13.8 us  [local(): lax.ppermute(messages[(distance + REACH) * groups + turn], ('ra', 'band')...]
  transfers between devices with their start and end apart: 9 -> 9, of which waited for: 3 -> 4; matrix products, arithmetic and copies ran while one was open for 0% -> 0% of each run, Pallas kernels for 3% -> 3%
where the time goes in v14:
time: 27.5 us; the launch traced here: 27.3 us
  starting transfers between devices  13.8 us (50%)
  Pallas kernels  8.07 us (29%)
  waiting for transfers between devices  3.83 us (14%)
  local copies, waits for them, and re-layouts  0.89 us (3%)
  between operations  0.68 us (2%)
    ppermute x9, starting transfers between devices, local(): lax.ppermute(messages[(distance + REACH) * groups + turn], ('ra', 'band')...  13.8 us
    pallas_call x1, Pallas kernels, local(): pl.pallas_call(functools.partial(match_kernel, patches, groups), in_specs...  6.23 us
    ppermute x9, waiting for transfers between devices, local(): lax.ppermute(messages[(distance + REACH) * groups + turn], ('ra', 'band')...  3.83 us
    pallas_call x1, Pallas kernels, local(): pl.pallas_call(functools.partial(combine_kernel, visits), in_specs=[vmem]...  1 us
    unnamed x4, local copies, waits for them, and re-layouts  0.89 us
    pallas_call x1, Pallas kernels, local(): pl.pallas_call(functools.partial(early_kernel, visits, row_share), in_spe...  0.84 us
  transfers between devices with their start and end apart: 9, of which 4 were waited for; matrix products, arithmetic and copies ran while one was open for 0% of the time, Pallas kernels for 3%

profile of v14, /device:TPU:0, one launch (start us, length us, event | category | flops | bytes accessed | tf_op | source)
XLA Modules:
  0.0 27.3 jit_solution(6781126088088054970)
XLA Ops:
  0.6 6.2 %match_and_sum.1 = (bf16[144,256]{1,0:T(8,128)(2,1)}, bf16[144,256]{1,0:T(8,128)(2,1)}, bf16[144,256]{1,0:T(8,128)(2,1)}, bf16[144,256]{1,0:T(8,128)(2,1)}, bf16...) custom-call(s32[32]{0:T(128)} %patch_hbm.1, ...), custom_call_target="tpu_custom_call" | custom-call | tf_op jit(solution)/shard_map/match_and_sum/pallas_call | solution.py:353
  6.9 0.5 %collective-permute-start = (bf16[144,256]{1,0:T(8,128)(2,1)}, bf16[144,256]{1,0:T(8,128)(2,1)S(1)}, u32[]{:S(2)}, u32[]{:S(2)}) collective-permute-start(bf16[144,256]{1,0:T(8,128)(2,1)} %get-tuple-element.15), channel_id=1, source_target_pairs={{0,2},{1,3},{2,4},{3,5},{4,6},{5,7},{6,8},{7,9},{8,10},{9,11},{10,... | collective-permute-start | bytes 221192 | tf_op jit(solution)/shard_map/ppermute | solution.py:404
  7.4 3.7 %collective-permute-start.1 = (bf16[144,256]{1,0:T(8,128)(2,1)}, bf16[144,256]{1,0:T(8,128)(2,1)S(1)}, u32[]{:S(2)}, u32[]{:S(2)}) collective-permute-start(bf16[144,256]{1,0:T(8,128)(2,1)} %get-tuple-element.16), channel_id=1, source_target_pairs={{0,3},{1,2},{2,5},{3,4},{4,7},{5,6},{6,9},{7,8},{8,11},{9,10},{10,... | collective-permute-start | bytes 221192 | tf_op jit(solution)/shard_map/ppermute | solution.py:404
  11.1 1.5 %collective-permute-start.2 = (bf16[144,256]{1,0:T(8,128)(2,1)}, bf16[144,256]{1,0:T(8,128)(2,1)S(1)}, u32[]{:S(2)}, u32[]{:S(2)}) collective-permute-start(bf16[144,256]{1,0:T(8,128)(2,1)} %get-tuple-element.17), channel_id=1, source_target_pairs={{0,4},{1,5},{2,6},{3,7},{4,8},{5,9},{6,10},{7,11},{8,12},{9,13},{1... | collective-permute-start | bytes 221192 | tf_op jit(solution)/shard_map/ppermute | solution.py:404
  12.7 1.4 %collective-permute-start.3 = (bf16[144,256]{1,0:T(8,128)(2,1)}, bf16[144,256]{1,0:T(8,128)(2,1)S(1)}, u32[]{:S(2)}, u32[]{:S(2)}) collective-permute-start(bf16[144,256]{1,0:T(8,128)(2,1)} %get-tuple-element.18), channel_id=1, source_target_pairs={{0,5},{1,4},{2,7},{3,6},{4,9},{5,8},{6,11},{7,10},{8,13},{9,12},{1... | collective-permute-start | bytes 221192 | tf_op jit(solution)/shard_map/ppermute | solution.py:404
  14.1 3.2 %collective-permute-start.4 = (bf16[144,256]{1,0:T(8,128)(2,1)}, bf16[144,256]{1,0:T(8,128)(2,1)S(1)}, u32[]{:S(2)}, u32[]{:S(2)}) collective-permute-start(bf16[144,256]{1,0:T(8,128)(2,1)} %get-tuple-element.21), channel_id=1, source_target_pairs={{0,28},{1,29},{2,30},{3,31},{4,0},{5,1},{6,2},{7,3},{8,4},{9,5},{1... | collective-permute-start | bytes 221192 | tf_op jit(solution)/shard_map/ppermute | solution.py:404
  17.3 0.0 collective-permute-done.refs_1_
  17.3 1.4 %collective-permute-start.5 = (bf16[144,256]{1,0:T(8,128)(2,1)}, bf16[144,256]{1,0:T(8,128)(2,1)S(1)}, u32[]{:S(2)}, u32[]{:S(2)}) collective-permute-start(bf16[144,256]{1,0:T(8,128)(2,1)} %get-tuple-element.22), channel_id=1, source_target_pairs={{0,29},{1,28},{2,31},{3,30},{4,1},{5,0},{6,3},{7,2},{8,5},{9,4},{1... | collective-permute-start | bytes 221192 | tf_op jit(solution)/shard_map/ppermute | solution.py:404
  18.8 0.0 collective-permute-done.1.refs_2_
  18.8 0.0 collective-permute-start.6
  18.8 0.3 %collective-permute-done.2.refs_3_ = bf16[144,256]{1,0:T(8,128)(2,1)S(1)} collective-permute-done((bf16[144,256]{1,0:T(8,128)(2,1)}, bf16[144,256]{1,0:T(8,128)(2,1)S(1)}, u32[]{:S(2)}, u32[]{:S(2)}) %collective-permute-start.2) | collective-permute-done | bytes 73760 | tf_op jit(solution)/shard_map/ppermute | solution.py:404
  19.1 1.1 %collective-permute-start.7 = (bf16[144,256]{1,0:T(8,128)(2,1)}, bf16[144,256]{1,0:T(8,128)(2,1)S(1)}, u32[]{:S(2)}, u32[]{:S(2)}) collective-permute-start(bf16[144,256]{1,0:T(8,128)(2,1)} %get-tuple-element.24), channel_id=1, source_target_pairs={{0,31},{1,30},{2,1},{3,0},{4,3},{5,2},{6,5},{7,4},{8,7},{9,6},{10,... | collective-permute-start | bytes 221192 | tf_op jit(solution)/shard_map/ppermute | solution.py:404
  20.1 0.8 %collective-permute-done.3.refs_4_ = bf16[144,256]{1,0:T(8,128)(2,1)S(1)} collective-permute-done((bf16[144,256]{1,0:T(8,128)(2,1)}, bf16[144,256]{1,0:T(8,128)(2,1)S(1)}, u32[]{:S(2)}, u32[]{:S(2)}) %collective-permute-start.3) | collective-permute-done | bytes 73760 | tf_op jit(solution)/shard_map/ppermute | solution.py:404
  20.9 0.0 copy-start.1
  20.9 0.9 %collective-permute-start.8 = (bf16[144,256]{1,0:T(8,128)(2,1)}, bf16[144,256]{1,0:T(8,128)(2,1)S(1)}, u32[]{:S(2)}, u32[]{:S(2)}) collective-permute-start(bf16[144,256]{1,0:T(8,128)(2,1)} %get-tuple-element.25), channel_id=1, source_target_pairs={{0,1},{1,0},{2,3},{3,2},{4,5},{5,4},{6,7},{7,6},{8,9},{9,8},{10,11... | collective-permute-start | bytes 221192 | tf_op jit(solution)/shard_map/ppermute | solution.py:404
  21.8 0.0 copy-done.1
  21.8 0.9 %copy-done = bf16[144,256]{1,0:T(8,128)(2,1)S(1)} copy-done((bf16[144,256]{1,0:T(8,128)(2,1)S(1)}, bf16[144,256]{1,0:T(8,128)(2,1)}, u32[]{:S(2)}) %copy-start) | copy-done | bytes 73752
  22.7 0.8 %combine_early.1 = (f32[192,256]{1,0:T(8,128)S(1)}, f32[16,256]{1,0:T(8,128)S(1)}) custom-call(f32[6]{0:T(128)S(1)} %copy-done.1, bf16[144,256]{1,0:T(8,128)(2,1)S(1)} %copy-done, bf16[144,256]{1,0:T(8,128)(2,1)S(1)} %collective-permute-done.refs_1_, bf16[144,256]{1,0:T(8,128)(2,1)S(1)} %collective-permute-done.1.refs_2_, ...), custom_call_target="tpu_custom_call" | custom-call | tf_op jit(solution)/shard_map/combine_early/pallas_call | solution.py:409
  23.5 0.0 collective-permute-done.4.refs_0_
  23.5 0.0 collective-permute-done.5.refs_1_
  23.5 0.0 collective-permute-done.6.refs_2_
  23.5 0.4 %collective-permute-done.7.refs_3_ = bf16[144,256]{1,0:T(8,128)(2,1)S(1)} collective-permute-done((bf16[144,256]{1,0:T(8,128)(2,1)}, bf16[144,256]{1,0:T(8,128)(2,1)S(1)}, u32[]{:S(2)}, u32[]{:S(2)}) %collective-permute-start.7) | collective-permute-done | bytes 73760 | tf_op jit(solution)/shard_map/ppermute | solution.py:404
  23.9 2.4 %collective-permute-done.8.refs_4_ = bf16[144,256]{1,0:T(8,128)(2,1)S(1)} collective-permute-done((bf16[144,256]{1,0:T(8,128)(2,1)}, bf16[144,256]{1,0:T(8,128)(2,1)S(1)}, u32[]{:S(2)}, u32[]{:S(2)}) %collective-permute-start.8) | collective-permute-done | bytes 73760 | tf_op jit(solution)/shard_map/ppermute | solution.py:404
  26.3 1.0 %combine.1 = (f32[6,32,256]{2,1,0:T(8,128)}, f32[32,256]{1,0:T(8,128)}) custom-call(f32[192,256]{1,0:T(8,128)S(1)} %get-tuple-element.19.totals_ref, f32[16,256]{1,0:T(8,128)S(1)} %get-tuple-element.20.rows_ref, bf16[144,256]{1,0:T(8,128)(2,1)S(1)} %collective-permute-done.4.refs_0_, bf16[144,256]{1,0:T(8,128)(2,1)S(1)} %collective-permute-done.5.refs_1_, ...), custom_call_target="tpu_custom_call" | custom-call | tf_op jit(solution)/shard_map/combine/pallas_call | solution.py:420
  (1 shorter events, 0.0 us)
Async XLA Ops:
  6.9 10.5 %collective-permute-start = (bf16[144,256]{1,0:T(8,128)(2,1)}, bf16[144,256]{1,0:T(8,128)(2,1)S(1)}, u32[]{:S(2)}, u32[]{:S(2)}) collective-permute-start(bf16[144,256]{1,0:T(8,128)(2,1)} %get-tuple-element.15), channel_id=1, source_target_pairs={{0,2},{1,3},{2,4},{3,5},{4,6},{5,7},{6,8},{7,9},{8,10},{9,11},{10,... | collective-permute-start | bytes 221192 | tf_op jit(solution)/shard_map/ppermute | solution.py:404
  7.4 11.4 %collective-permute-start.1 = (bf16[144,256]{1,0:T(8,128)(2,1)}, bf16[144,256]{1,0:T(8,128)(2,1)S(1)}, u32[]{:S(2)}, u32[]{:S(2)}) collective-permute-start(bf16[144,256]{1,0:T(8,128)(2,1)} %get-tuple-element.16), channel_id=1, source_target_pairs={{0,3},{1,2},{2,5},{3,4},{4,7},{5,6},{6,9},{7,8},{8,11},{9,10},{10,... | collective-permute-start | bytes 221192 | tf_op jit(solution)/shard_map/ppermute | solution.py:404
  11.1 8.0 %collective-permute-start.2 = (bf16[144,256]{1,0:T(8,128)(2,1)}, bf16[144,256]{1,0:T(8,128)(2,1)S(1)}, u32[]{:S(2)}, u32[]{:S(2)}) collective-permute-start(bf16[144,256]{1,0:T(8,128)(2,1)} %get-tuple-element.17), channel_id=1, source_target_pairs={{0,4},{1,5},{2,6},{3,7},{4,8},{5,9},{6,10},{7,11},{8,12},{9,13},{1... | collective-permute-start | bytes 221192 | tf_op jit(solution)/shard_map/ppermute | solution.py:404
  12.7 8.3 %collective-permute-start.3 = (bf16[144,256]{1,0:T(8,128)(2,1)}, bf16[144,256]{1,0:T(8,128)(2,1)S(1)}, u32[]{:S(2)}, u32[]{:S(2)}) collective-permute-start(bf16[144,256]{1,0:T(8,128)(2,1)} %get-tuple-element.18), channel_id=1, source_target_pairs={{0,5},{1,4},{2,7},{3,6},{4,9},{5,8},{6,11},{7,10},{8,13},{9,12},{1... | collective-permute-start | bytes 221192 | tf_op jit(solution)/shard_map/ppermute | solution.py:404
  14.1 9.4 %collective-permute-start.4 = (bf16[144,256]{1,0:T(8,128)(2,1)}, bf16[144,256]{1,0:T(8,128)(2,1)S(1)}, u32[]{:S(2)}, u32[]{:S(2)}) collective-permute-start(bf16[144,256]{1,0:T(8,128)(2,1)} %get-tuple-element.21), channel_id=1, source_target_pairs={{0,28},{1,29},{2,30},{3,31},{4,0},{5,1},{6,2},{7,3},{8,4},{9,5},{1... | collective-permute-start | bytes 221192 | tf_op jit(solution)/shard_map/ppermute | solution.py:404
  17.3 6.2 %collective-permute-start.5 = (bf16[144,256]{1,0:T(8,128)(2,1)}, bf16[144,256]{1,0:T(8,128)(2,1)S(1)}, u32[]{:S(2)}, u32[]{:S(2)}) collective-permute-start(bf16[144,256]{1,0:T(8,128)(2,1)} %get-tuple-element.22), channel_id=1, source_target_pairs={{0,29},{1,28},{2,31},{3,30},{4,1},{5,0},{6,3},{7,2},{8,5},{9,4},{1... | collective-permute-start | bytes 221192 | tf_op jit(solution)/shard_map/ppermute | solution.py:404
  18.8 4.8 %collective-permute-start.6 = (bf16[144,256]{1,0:T(8,128)(2,1)}, bf16[144,256]{1,0:T(8,128)(2,1)S(1)}, u32[]{:S(2)}, u32[]{:S(2)}) collective-permute-start(bf16[144,256]{1,0:T(8,128)(2,1)} %get-tuple-element.23), channel_id=1, source_target_pairs={{0,30},{1,31},{2,0},{3,1},{4,2},{5,3},{6,4},{7,5},{8,6},{9,7},{10,... | collective-permute-start | bytes 221192 | tf_op jit(solution)/shard_map/ppermute | solution.py:404
  19.1 4.9 %collective-permute-start.7 = (bf16[144,256]{1,0:T(8,128)(2,1)}, bf16[144,256]{1,0:T(8,128)(2,1)S(1)}, u32[]{:S(2)}, u32[]{:S(2)}) collective-permute-start(bf16[144,256]{1,0:T(8,128)(2,1)} %get-tuple-element.24), channel_id=1, source_target_pairs={{0,31},{1,30},{2,1},{3,0},{4,3},{5,2},{6,5},{7,4},{8,7},{9,6},{10,... | collective-permute-start | bytes 221192 | tf_op jit(solution)/shard_map/ppermute | solution.py:404
  20.9 0.9 %copy-start.1 = (f32[6]{0:T(128)S(1)}, f32[6]{0:T(128)}, u32[]{:S(2)}) copy-start(f32[6]{0:T(128)} %weight_ref.1) | copy-start | bytes 76
  20.9 5.4 %collective-permute-start.8 = (bf16[144,256]{1,0:T(8,128)(2,1)}, bf16[144,256]{1,0:T(8,128)(2,1)S(1)}, u32[]{:S(2)}, u32[]{:S(2)}) collective-permute-start(bf16[144,256]{1,0:T(8,128)(2,1)} %get-tuple-element.25), channel_id=1, source_target_pairs={{0,1},{1,0},{2,3},{3,2},{4,5},{5,4},{6,7},{7,6},{8,9},{9,8},{10,11... | collective-permute-start | bytes 221192 | tf_op jit(solution)/shard_map/ppermute | solution.py:404
  21.8 0.9 %copy-start = (bf16[144,256]{1,0:T(8,128)(2,1)S(1)}, bf16[144,256]{1,0:T(8,128)(2,1)}, u32[]{:S(2)}) copy-start(bf16[144,256]{1,0:T(8,128)(2,1)} %get-tuple-element.14.refs_0_) | copy-start | bytes 221188

commit v15 on v9

--- a/solution.py
+++ b/solution.py
@@ -22,11 +22,11 @@
 
 def match_kernel(
     patches,
-    patch_ref,
-    offset_ref,
-    index_ref,
-    band_ref,
-    detect_ref,
+    patch_hbm,
+    offset_hbm,
+    index_hbm,
+    band_hbm,
+    detect_hbm,
     table_hbm,
     weight_hbm,
     rowk_hbm,
@@ -35,6 +35,11 @@
     far,
     cross,
     kept,
+    patch_ref,
+    offset_ref,
+    index_ref,
+    band_ref,
+    detect_ref,
     table_ref,
     weight_ref,
     rowk_ref,
@@ -49,7 +54,7 @@
     extra,
     arrival,
     ready,
-    ):
+):
     visits = band_ref.shape[0]
     tile_count, rows, width = tiles_ref.shape
     per_visit = tile_count // visits
@@ -62,10 +67,15 @@
         pltpu.make_async_copy(source, target, ready.at[place])
         for place, (source, target) in enumerate(
             (
+                (index_hbm, index_ref),
                 (table_hbm, table_ref),
                 (weight_hbm, weight_ref),
                 (rowk_hbm, rowk_ref),
                 (colk_hbm, colk_ref),
+                (patch_hbm, patch_ref),
+                (offset_hbm, offset_ref),
+                (band_hbm, band_ref),
+                (detect_hbm, detect_ref),
             )
         )
     ]
@@ -92,18 +102,32 @@
         )
 
     extra[...] = jnp.zeros_like(extra)
-    shifted[...] = jnp.zeros_like(shifted)
+    for place in range(per_visit):
+        for side in range(2):
+            for fine in range(4):
+                top = fine * FINE_ROWS
+                shifted[place, side, top : top + 16, :width] = jnp.zeros(
+                    (16, width), jnp.bfloat16
+                )
+                shifted[place, side, top + 48 : top + 64, width:] = jnp.zeros(
+                    (16, width), jnp.bfloat16
+                )
     eye = (iota((tile_count, tile_count), 0) == iota((tile_count, tile_count), 1)).astype(
         jnp.bfloat16
     )
+    for copy in small:
+        copy.wait()
+    weights[...] = across(eye, jnp.broadcast_to(weight_ref[...], (width, tile_count)))
     entry = iota((1, table_ref.shape[1]), 1)
     chosen = jnp.concatenate(
         [(entry == index_ref[j]).astype(jnp.float32) for j in range(tile_count)], axis=0
-    )
-    for copy in small:
-        copy.wait()
-    weights[...] = across(eye, jnp.broadcast_to(weight_ref[...], (width, tile_count)))
-    coeffs = across(chosen, table_ref[...], precision=lax.Precision.HIGHEST)
+    ).astype(jnp.bfloat16)
+    rest_of = table_ref[...]
+    coeffs = jnp.zeros((tile_count, basis), jnp.float32)
+    for _ in range(3):
+        piece = rest_of.astype(jnp.bfloat16)
+        rest_of = rest_of - piece.astype(jnp.float32)
+        coeffs += across(chosen, piece)
 
     line = iota((2 * VECTORS, taps), 0)
     column = iota((2 * VECTORS, taps), 1)
@@ -133,6 +157,18 @@
     lane = iota((rows, width), 1)
     column = iota((1, width), 1)
 
+    def edge(distance):
+        here = iota((16, width), 1) + distance
+        return ((here >= 0) & (here < width)).astype(jnp.float32).astype(jnp.bfloat16)
+
+    edges = {distance: edge(distance) for distance in range(-4, 4) if distance != 0}
+
+    def moved_tile(value, distance):
+        if distance == 0:
+            return value
+        turned = pltpu.roll(value, -distance % width, 1).reshape(rows // 16, 16, width)
+        return (turned * edges[distance][None]).reshape(rows, width)
+
     def moved(value, distance):
         if distance == 0:
             return value
@@ -149,7 +185,7 @@
             pixels = tiles_ref[tile]
             for side in range(2):
                 for fine in range(4):
-                    part = moved(pixels, -1 - fine if side else fine)
+                    part = moved_tile(pixels, -1 - fine if side else fine)
                     top = fine * FINE_ROWS
                     shifted[place, side, top + 16 : top + 64, :width] = part[:48]
                     shifted[place, side, top : top + 48, width:] = part[16:]
@@ -309,29 +345,21 @@
 
 
 def merge_kernel(count, groups, totals_ref, weights_ref, cross_ref, *refs):
-    messages = refs[: groups - 1]
-    near_ref, near_weight_ref, home_ref, home_weight_ref, held = refs[groups - 1 :]
+    messages = refs[:groups]
+    home_ref, home_weight_ref, held = refs[groups:]
     totals, weights = add_message(count, groups, cross_ref.at[0])
     held[...] = totals + totals_ref[0]
     weights += weights_ref[0]
-    for turn, message in enumerate(messages, 1):
+    for turn, message in enumerate(messages):
         write_banded(message, part_of(held, turn, groups), weights)
-    near_ref[...] = part_of(held, 0, groups)
-    near_weight_ref[...] = weights
     totals, weights = add_message(count, groups, cross_ref.at[1])
     home_ref[...] = totals + totals_ref[1]
     home_weight_ref[...] = weights + weights_ref[1]
 
 
-def forward_kernel(
-    count, groups, near_ref, near_weight_ref, home_ref, home_weight_ref, far_ref, *refs
-):
-    arrived = refs[: groups - 1]
-    onward_ref = refs[groups - 1]
-    messages = refs[groups : 2 * groups - 1]
-    own_ref, own_weight_ref, held = refs[2 * groups - 1 :]
-    totals, weights = add_banded(near_ref[...], near_weight_ref[...], arrived)
-    write_banded(onward_ref, totals, weights)
+def home_kernel(count, groups, home_ref, home_weight_ref, far_ref, *refs):
+    messages = refs[: groups - 1]
+    own_ref, own_weight_ref, held = refs[groups - 1 :]
     totals, weights = add_message(count, groups, far_ref)
     held[...] = totals + home_ref[...]
     weights += home_weight_ref[...]
@@ -341,10 +369,23 @@
     own_weight_ref[...] = weights
 
 
-def combine_kernel(detect_ref, own_ref, own_weight_ref, *refs):
+def early_kernel(*refs):
+    messages = refs[:-2]
+    totals_ref, weights_ref = refs[-2:]
+    depth = totals_ref.shape[0]
+    totals_ref[...], weights_ref[...] = add_banded(
+        jnp.zeros((depth, PW), jnp.float32), jnp.zeros((8, PW), jnp.float32), messages
+    )
+
+
+def combine_kernel(
+    detect_ref, own_ref, own_weight_ref, near_ref, near_weight_ref, *refs
+):
     coadd_ref, detection_ref = refs[-2:]
     row_share = coadd_ref.shape[1]
-    totals, weights = add_banded(own_ref[...], own_weight_ref[...], refs[:-2])
+    totals, weights = add_banded(
+        own_ref[...] + near_ref[...], own_weight_ref[...] + near_weight_ref[...], refs[:-2]
+    )
     weights = jnp.maximum(weights, 1.0)
     detection = jnp.zeros((row_share, PW), jnp.float32)
     for b in range(BANDS):
@@ -380,16 +421,20 @@
     part_shape = jax.ShapeDtypeStruct((BANDS * row_share, PW), jnp.float32)
     whole_shape = jax.ShapeDtypeStruct((BANDS * rows, PW), jnp.float32)
     weight_shape = jax.ShapeDtypeStruct((8, PW), jnp.float32)
-    smem = pl.BlockSpec(memory_space=pltpu.SMEM)
 
     vmem = pl.BlockSpec(memory_space=pltpu.VMEM)
     anywhere = pl.BlockSpec(memory_space=pl.ANY)
     far, cross, kept = pl.pallas_call(
         functools.partial(match_kernel, patches),
-        in_specs=[smem] * 5 + [anywhere] * 5,
+        in_specs=[anywhere] * 10,
         out_specs=[vmem] * 3,
         out_shape=[message_shape, pair_shape, pair_shape],
         scratch_shapes=[
+            pltpu.SMEM((tile_count,), jnp.int32),
+            pltpu.SMEM((tile_count,), jnp.int32),
+            pltpu.SMEM((tile_count,), jnp.int32),
+            pltpu.SMEM((visits,), jnp.int32),
+            pltpu.SMEM((BANDS,), jnp.float32),
             pltpu.VMEM(coeff_table.shape[::-1], jnp.float32),
             pltpu.VMEM((1, tile_count), jnp.bfloat16),
             pltpu.VMEM((basis, taps), jnp.bfloat16),
@@ -403,7 +448,7 @@
             pltpu.VMEM((SPREAD, rows, PW), jnp.float32),
             pltpu.VMEM((SPREAD, EXTRA, PW), jnp.float32),
             pltpu.SemaphoreType.DMA((visits,)),
-            pltpu.SemaphoreType.DMA((4,)),
+            pltpu.SemaphoreType.DMA((9,)),
         ],
         compiler_params=pltpu.CompilerParams(vmem_limit_bytes=62 * 1024 * 1024),
         name="match_and_sum",
@@ -455,29 +500,26 @@
         ],
         kept,
     )
-    *others, near, near_weight, home, home_weight = local_call(
+    *near, home, home_weight = local_call(
         functools.partial(merge_kernel, visits, groups),
         "merge",
-        [band_shape] * (groups - 1) + [part_shape, weight_shape, whole_shape, weight_shape],
+        [band_shape] * groups + [whole_shape, weight_shape],
         *kept,
         cross,
         scratch_shapes=held,
     )
-    others = [send(others[turn - 1], onward(0), turn) for turn in range(1, groups)]
-    near, *others, own, own_weight = local_call(
-        functools.partial(forward_kernel, visits, groups),
-        "forward",
-        [band_shape] * groups + [part_shape, weight_shape],
-        near,
-        near_weight,
+    near = [send(near[turn], onward(1), turn) for turn in range(groups)]
+    *others, own, own_weight = local_call(
+        functools.partial(home_kernel, visits, groups),
+        "home",
+        [band_shape] * (groups - 1) + [part_shape, weight_shape],
         home,
         home_weight,
         far,
-        *others,
         scratch_shapes=held,
     )
-    near = send(near, onward(1), 0)
     others = [send(others[turn - 1], onward(0), turn) for turn in range(1, groups)]
+    near = local_call(early_kernel, "combine_early", [part_shape, weight_shape], *near)
     return local_call(
         combine_kernel,
         "combine",
@@ -488,7 +530,7 @@
         detect,
         own,
         own_weight,
-        near,
+        *near,
         *others,
     )
 

time: 28.2 us -> 26 us (0.922)
  waiting for transfers between devices: 8.43 us -> 4.17 us
  starting transfers between devices: 9.33 us -> 12.1 us
  Pallas kernels: 8.61 us -> 7.87 us
    ppermute x5, waiting for transfers between devices: 8.43 us -> 4.17 us  [send(): return lax.ppermute(message, ('ra', 'band'), route)]
    ppermute x5, starting transfers between devices: 9.33 us -> 12.1 us  [send(): return lax.ppermute(message, ('ra', 'band'), route)]
    pallas_call x1, Pallas kernels: 7 us -> 6.24 us  [local(): pl.pallas_call(functools.partial(match_kernel, patches), in_specs=[anywhe...]
    pallas_call x4 -> x5, Pallas kernels: 1.61 us -> 1.62 us  [local_call(): pl.pallas_call(kernel, in_specs=[vmem] * len(operands), out_specs=[vmem]...]
  transfers between devices with their start and end apart: 5 -> 5, of which waited for: 2 -> 3; matrix products, arithmetic and copies ran while one was open for 0% -> 0% of each run, Pallas kernels for 2% -> 3%
where the time goes in v15:
time: 26 us; the launch traced here: 25.8 us
  starting transfers between devices  12.1 us (47%)
  Pallas kernels  7.87 us (30%)
  waiting for transfers between devices  4.17 us (16%)
  local copies, waits for them, and re-layouts  0.96 us (4%)
  between operations  0.67 us (3%)
    ppermute x5, starting transfers between devices, send(): return lax.ppermute(message, ('ra', 'band'), route)  12.1 us
    pallas_call x1, Pallas kernels, local(): pl.pallas_call(functools.partial(match_kernel, patches), in_specs=[anywhe...  6.24 us
    ppermute x5, waiting for transfers between devices, send(): return lax.ppermute(message, ('ra', 'band'), route)  4.17 us
    pallas_call x5, Pallas kernels, local_call(): pl.pallas_call(kernel, in_specs=[vmem] * len(operands), out_specs=[vmem]...  1.62 us
    unnamed x2, local copies, waits for them, and re-layouts  0.96 us
  transfers between devices with their start and end apart: 5, of which 3 were waited for; matrix products, arithmetic and copies ran while one was open for 0% of the time, Pallas kernels for 3%

profile of v15, /device:TPU:0, one launch (start us, length us, event | category | flops | bytes accessed | tf_op | source)
XLA Modules:
  0.0 25.8 jit_solution(825733714093706183)
XLA Ops:
  0.6 6.2 %match_and_sum.1 = (bf16[272,256]{1,0:T(8,128)(2,1)}, bf16[2,272,256]{2,1,0:T(8,128)(2,1)}, bf16[2,272,256]{2,1,0:T(8,128)(2,1)}) custom-call(s32[32]{0:T(128)} %patch_hbm.1, s32[32]{0:T(128)} %offset_hbm.1, s32[32]{0:T(128)} %index_hbm.1, s32[4]{0:T(128)} %band_hbm.1, f32[6]{0:T(128)} %detect_hbm.1, f32[21,64]{1,0:T(8,128)} %bitcast.2, ...), custom_call_target="tpu_custom_call" | custom-call | tf_op jit(solution)/shard_map/match_and_sum/pallas_call | solution.py:427
  6.9 0.5 %collective-permute-start = (bf16[2,272,256]{2,1,0:T(8,128)(2,1)}, bf16[2,272,256]{2,1,0:T(8,128)(2,1)S(1)}, u32[]{:S(2)}, u32[]{:S(2)}) collective-permute-start(bf16[2,272,256]{2,1,0:T(8,128)(2,1)} %get-tuple-element.21), channel_id=1, source_target_pairs={{0,2},{1,3},{2,0},{3,1},{4,6},{5,7},{6,4},{7,5},{8,10},{9,11},{10,... | collective-permute-start | bytes 835592 | tf_op jit(solution)/shard_map/ppermute | solution.py:474
  7.4 5.6 %collective-permute-start.1 = (bf16[272,256]{1,0:T(8,128)(2,1)}, bf16[272,256]{1,0:T(8,128)(2,1)S(1)}, u32[]{:S(2)}, u32[]{:S(2)}) collective-permute-start(bf16[272,256]{1,0:T(8,128)(2,1)} %get-tuple-element.24), channel_id=1, source_target_pairs={{0,28},{1,29},{2,6},{3,7},{4,0},{5,1},{6,10},{7,11},{8,4},{9,5},{1... | collective-permute-start | bytes 417800 | tf_op jit(solution)/shard_map/ppermute | solution.py:474
  13.0 0.0 copy-start
  13.0 1.0 %copy-done = bf16[2,272,256]{2,1,0:T(8,128)(2,1)S(1)} copy-done((bf16[2,272,256]{2,1,0:T(8,128)(2,1)S(1)}, bf16[2,272,256]{2,1,0:T(8,128)(2,1)}, u32[]{:S(2)}) %copy-start) | copy-done | bytes 278552
  13.9 0.3 %keep.1 = (f32[2,384,256]{2,1,0:T(8,128)S(1)}, f32[2,8,256]{2,1,0:T(8,128)S(1)}, f32[8,256]{1,0:T(8,128)S(1)}) custom-call(bf16[2,272,256]{2,1,0:T(8,128)(2,1)S(1)} %copy-done), custom_call_target="tpu_custom_call" | custom-call | tf_op jit(solution)/shard_map/keep/pallas_call | solution.py:480
  14.2 0.0 collective-permute-done.cross_ref
  14.2 0.3 %merge.1 = (bf16[208,256]{1,0:T(8,128)(2,1)S(1)}, bf16[208,256]{1,0:T(8,128)(2,1)S(1)}, f32[384,256]{1,0:T(8,128)S(1)}, f32[8,256]{1,0:T(8,128)S(1)}) custom-call(f32[2,384,256]{2,1,0:T(8,128)S(1)} %get-tuple-element.19.totals_ref, f32[2,8,256]{2,1,0:T(8,128)S(1)} %get-tuple-element.20.weights_ref, bf16[2,272,256]{2,1,0:T(8,128)(2,1)S(1)} %collective-permute-done.cross_ref), custom_call_target="tpu_custom_call" | custom-call | tf_op jit(solution)/shard_map/merge/pallas_call | solution.py:480
  14.6 0.3 %collective-permute-start.2 = (bf16[208,256]{1,0:T(8,128)(2,1)S(1)}, bf16[208,256]{1,0:T(8,128)(2,1)S(1)}, u32[]{:S(2)}, u32[]{:S(2)}) collective-permute-start(bf16[208,256]{1,0:T(8,128)(2,1)S(1)} %get-tuple-element.27), channel_id=1, source_target_pairs={{0,30},{1,31},{2,4},{3,5},{4,2},{5,3},{6,8},{7,9},{8,6},{9,7},{10,... | collective-permute-start | bytes 319496 | tf_op jit(solution)/shard_map/ppermute | solution.py:474
  14.8 5.2 %collective-permute-start.3 = (bf16[208,256]{1,0:T(8,128)(2,1)S(1)}, bf16[208,256]{1,0:T(8,128)(2,1)S(1)}, u32[]{:S(2)}, u32[]{:S(2)}) collective-permute-start(bf16[208,256]{1,0:T(8,128)(2,1)S(1)} %get-tuple-element.28), channel_id=1, source_target_pairs={{0,31},{1,30},{2,5},{3,4},{4,3},{5,2},{6,9},{7,8},{8,7},{9,6},{10,... | collective-permute-start | bytes 319496 | tf_op jit(solution)/shard_map/ppermute | solution.py:474
  20.0 0.0 collective-permute-done.1.far_ref
  20.0 0.3 %home.1 = (bf16[208,256]{1,0:T(8,128)(2,1)S(1)}, f32[192,256]{1,0:T(8,128)S(1)}, f32[8,256]{1,0:T(8,128)S(1)}) custom-call(f32[384,256]{1,0:T(8,128)S(1)} %get-tuple-element.22.home_ref, f32[8,256]{1,0:T(8,128)S(1)} %get-tuple-element.23.home_weight_ref, bf16[272,256]{1,0:T(8,128)(2,1)S(1)} %collective-permute-done.1.far_ref), custom_call_target="tpu_custom_call" | custom-call | tf_op jit(solution)/shard_map/home/pallas_call | solution.py:480
  20.3 0.6 %collective-permute-start.4 = (bf16[208,256]{1,0:T(8,128)(2,1)S(1)}, bf16[208,256]{1,0:T(8,128)(2,1)S(1)}, u32[]{:S(2)}, u32[]{:S(2)}) collective-permute-start(bf16[208,256]{1,0:T(8,128)(2,1)S(1)} %get-tuple-element.31), channel_id=1, source_target_pairs={{0,1},{1,0},{2,3},{3,2},{4,5},{5,4},{6,7},{7,6},{8,9},{9,8},{10,11... | collective-permute-start | bytes 319496 | tf_op jit(solution)/shard_map/ppermute | solution.py:474
  20.9 0.6 %collective-permute-done.2.refs_0_ = bf16[208,256]{1,0:T(8,128)(2,1)S(1)} collective-permute-done((bf16[208,256]{1,0:T(8,128)(2,1)S(1)}, bf16[208,256]{1,0:T(8,128)(2,1)S(1)}, u32[]{:S(2)}, u32[]{:S(2)}) %collective-permute-start.2) | collective-permute-done | bytes 106528 | tf_op jit(solution)/shard_map/ppermute | solution.py:474
  21.5 2.1 %collective-permute-done.3.refs_1_ = bf16[208,256]{1,0:T(8,128)(2,1)S(1)} collective-permute-done((bf16[208,256]{1,0:T(8,128)(2,1)S(1)}, bf16[208,256]{1,0:T(8,128)(2,1)S(1)}, u32[]{:S(2)}, u32[]{:S(2)}) %collective-permute-start.3) | collective-permute-done | bytes 106528 | tf_op jit(solution)/shard_map/ppermute | solution.py:474
  23.6 1.5 %collective-permute-done.4.refs_0_ = bf16[208,256]{1,0:T(8,128)(2,1)S(1)} collective-permute-done((bf16[208,256]{1,0:T(8,128)(2,1)S(1)}, bf16[208,256]{1,0:T(8,128)(2,1)S(1)}, u32[]{:S(2)}, u32[]{:S(2)}) %collective-permute-start.4) | collective-permute-done | bytes 106528 | tf_op jit(solution)/shard_map/ppermute | solution.py:474
  25.1 0.7 %combine.1 = (f32[6,32,256]{2,1,0:T(8,128)}, f32[32,256]{1,0:T(8,128)}) custom-call(f32[8,256]{1,0:T(8,128)S(1)} %get-tuple-element.18.detect_ref, f32[192,256]{1,0:T(8,128)S(1)} %get-tuple-element.25.own_ref, f32[8,256]{1,0:T(8,128)S(1)} %get-tuple-element.26.own_weight_ref, f32[192,256]{1,0:T(8,128)S(1)} %get-tuple-element.29.near_ref, ...), custom_call_target="tpu_custom_call" | custom-call | tf_op jit(solution)/shard_map/combine/pallas_call | solution.py:480
  (1 shorter events, 0.0 us)
Async XLA Ops:
  6.9 7.3 %collective-permute-start = (bf16[2,272,256]{2,1,0:T(8,128)(2,1)}, bf16[2,272,256]{2,1,0:T(8,128)(2,1)S(1)}, u32[]{:S(2)}, u32[]{:S(2)}) collective-permute-start(bf16[2,272,256]{2,1,0:T(8,128)(2,1)} %get-tuple-element.21), channel_id=1, source_target_pairs={{0,2},{1,3},{2,0},{3,1},{4,6},{5,7},{6,4},{7,5},{8,10},{9,11},{10,... | collective-permute-start | bytes 835592 | tf_op jit(solution)/shard_map/ppermute | solution.py:474
  7.4 12.6 %collective-permute-start.1 = (bf16[272,256]{1,0:T(8,128)(2,1)}, bf16[272,256]{1,0:T(8,128)(2,1)S(1)}, u32[]{:S(2)}, u32[]{:S(2)}) collective-permute-start(bf16[272,256]{1,0:T(8,128)(2,1)} %get-tuple-element.24), channel_id=1, source_target_pairs={{0,28},{1,29},{2,6},{3,7},{4,0},{5,1},{6,10},{7,11},{8,4},{9,5},{1... | collective-permute-start | bytes 417800 | tf_op jit(solution)/shard_map/ppermute | solution.py:474
  13.0 1.0 %copy-start = (bf16[2,272,256]{2,1,0:T(8,128)(2,1)S(1)}, bf16[2,272,256]{2,1,0:T(8,128)(2,1)}, u32[]{:S(2)}) copy-start(bf16[2,272,256]{2,1,0:T(8,128)(2,1)} %get-tuple-element.17.kept_ref) | copy-start | bytes 835588
  14.6 6.9 %collective-permute-start.2 = (bf16[208,256]{1,0:T(8,128)(2,1)S(1)}, bf16[208,256]{1,0:T(8,128)(2,1)S(1)}, u32[]{:S(2)}, u32[]{:S(2)}) collective-permute-start(bf16[208,256]{1,0:T(8,128)(2,1)S(1)} %get-tuple-element.27), channel_id=1, source_target_pairs={{0,30},{1,31},{2,4},{3,5},{4,2},{5,3},{6,8},{7,9},{8,6},{9,7},{10,... | collective-permute-start | bytes 319496 | tf_op jit(solution)/shard_map/ppermute | solution.py:474
  14.8 8.7 %collective-permute-start.3 = (bf16[208,256]{1,0:T(8,128)(2,1)S(1)}, bf16[208,256]{1,0:T(8,128)(2,1)S(1)}, u32[]{:S(2)}, u32[]{:S(2)}) collective-permute-start(bf16[208,256]{1,0:T(8,128)(2,1)S(1)} %get-tuple-element.28), channel_id=1, source_target_pairs={{0,31},{1,30},{2,5},{3,4},{4,3},{5,2},{6,9},{7,8},{8,7},{9,6},{10,... | collective-permute-start | bytes 319496 | tf_op jit(solution)/shard_map/ppermute | solution.py:474
  20.3 4.8 %collective-permute-start.4 = (bf16[208,256]{1,0:T(8,128)(2,1)S(1)}, bf16[208,256]{1,0:T(8,128)(2,1)S(1)}, u32[]{:S(2)}, u32[]{:S(2)}) collective-permute-start(bf16[208,256]{1,0:T(8,128)(2,1)S(1)} %get-tuple-element.31), channel_id=1, source_target_pairs={{0,1},{1,0},{2,3},{3,2},{4,5},{5,4},{6,7},{7,6},{8,9},{9,8},{10,11... | collective-permute-start | bytes 319496 | tf_op jit(solution)/shard_map/ppermute | solution.py:474

commit v16 on v15

--- a/solution.py
+++ b/solution.py
@@ -20,8 +20,13 @@
 LEAD = 6
 
 
+def slot_rows(row_share):
+    return max(row_share, 16)
+
+
 def match_kernel(
     patches,
+    groups,
     patch_hbm,
     offset_hbm,
     index_hbm,
@@ -35,32 +40,39 @@
     far,
     cross,
     kept,
-    patch_ref,
-    offset_ref,
-    index_ref,
-    band_ref,
-    detect_ref,
-    table_ref,
-    weight_ref,
-    rowk_ref,
-    colk_ref,
-    tiles_ref,
-    kernels,
-    weights,
-    shifted,
-    toeplitz,
-    matches,
-    sums,
-    extra,
-    arrival,
-    ready,
+    *rest,
 ):
+    left = rest[:groups]
+    (
+        patch_ref,
+        offset_ref,
+        index_ref,
+        band_ref,
+        detect_ref,
+        table_ref,
+        weight_ref,
+        rowk_ref,
+        colk_ref,
+        tiles_ref,
+        kernels,
+        weights,
+        shifted,
+        toeplitz,
+        matches,
+        sums,
+        extra,
+        arrival,
+        ready,
+    ) = rest[groups:]
     visits = band_ref.shape[0]
     tile_count, rows, width = tiles_ref.shape
     per_visit = tile_count // visits
     basis, taps = rowk_ref.shape
     half = taps // 2
+    row_share = rows // groups
+    slot = slot_rows(row_share)
     owner = lax.axis_index("ra")
+    group = lax.axis_index("band")
     way = 2 * lax.rem(owner, 2) - 1
 
     small = [
@@ -238,6 +250,18 @@
                 axis=1,
             )
 
+        for turn in range(groups):
+            part = lax.rem(group + turn, groups)
+            own = sums[
+                REACH + 2 * way, pl.ds(pl.multiple_of(part * row_share, row_share), row_share), :
+            ]
+            if slot > row_share:
+                own = jnp.concatenate(
+                    [own, jnp.zeros((slot - row_share, PW), jnp.float32)], axis=0
+                )
+            left[turn][pl.ds(pl.multiple_of(visit * slot, slot), slot), :] = own.astype(
+                jnp.bfloat16
+            )
         held = pl.ds(pl.multiple_of(visit * rows, rows), rows)
         far[held, :] = sums[REACH + 2 * way].astype(jnp.bfloat16)
         cross[0, held, :] = sums[REACH - 2 * way].astype(jnp.bfloat16)
@@ -260,12 +284,13 @@
         return line
 
     by_row = spread_bands(lane // rows, visits * rows)
+    by_slot = spread_bands(lane // slot, visits * slot)
     by_weight = spread_bands(lax.rem(lane, visits), 2 * visits)
     detect = jnp.zeros((1, PW), jnp.float32)
     for b in range(BANDS):
         detect = jnp.where(lane == b, detect_ref[b], detect)
 
-    def footer(bucket):
+    def footer(bucket, by_row):
         held = extra[bucket]
         high = held.astype(jnp.bfloat16).astype(jnp.float32)
         low = jnp.concatenate([held[-visits:], (held - high)[:-visits]], axis=0)
@@ -279,17 +304,19 @@
             mixed = jnp.where(row == place, piece, mixed)
         return mixed.astype(jnp.bfloat16)
 
-    far[rows * visits :, :] = footer(REACH + 2 * way)
-    cross[0, rows * visits :, :] = footer(REACH - 2 * way)
-    cross[1, rows * visits :, :] = footer(REACH - way)
-    kept[0, rows * visits :, :] = footer(REACH + way)
-    kept[1, rows * visits :, :] = footer(REACH)
-
-
-def add_message(count, groups, message):
+    for turn in range(groups):
+        left[turn][slot * visits :, :] = footer(REACH + 2 * way, by_slot)
+    far[rows * visits :, :] = footer(REACH + 2 * way, by_row)
+    cross[0, rows * visits :, :] = footer(REACH - 2 * way, by_row)
+    cross[1, rows * visits :, :] = footer(REACH - way, by_row)
+    kept[0, rows * visits :, :] = footer(REACH + way, by_row)
+    kept[1, rows * visits :, :] = footer(REACH, by_row)
+
+
+def add_message(count, groups, message, row_share=None):
     depth = message.shape[0] - EXTRA
     span = depth // count
-    row_share = span // groups
+    row_share = row_share or span // groups
     line = lax.broadcasted_iota(jnp.int32, (row_share, depth), 0)
     lane = lax.rem(lax.broadcasted_iota(jnp.int32, (row_share, depth), 1), span)
     band_line = lax.broadcasted_iota(jnp.int32, (8, EXTRA), 0).astype(jnp.float32)
@@ -379,13 +406,19 @@
 
 
 def combine_kernel(
-    detect_ref, own_ref, own_weight_ref, near_ref, near_weight_ref, *refs
+    count, groups, detect_ref, own_ref, own_weight_ref, near_ref, near_weight_ref, *refs
 ):
     coadd_ref, detection_ref = refs[-2:]
     row_share = coadd_ref.shape[1]
     totals, weights = add_banded(
-        own_ref[...] + near_ref[...], own_weight_ref[...] + near_weight_ref[...], refs[:-2]
-    )
+        own_ref[...] + near_ref[...],
+        own_weight_ref[...] + near_weight_ref[...],
+        refs[: groups - 1],
+    )
+    for message in refs[groups - 1 : -2]:
+        more, more_weights = add_message(count, 1, message, row_share)
+        totals += more
+        weights += more_weights
     weights = jnp.maximum(weights, 1.0)
     detection = jnp.zeros((row_share, PW), jnp.float32)
     for b in range(BANDS):
@@ -416,6 +449,9 @@
     row_share = rows // groups
     length = visits * rows + EXTRA
     message_shape = jax.ShapeDtypeStruct((length, PW), jnp.bfloat16)
+    left_shape = jax.ShapeDtypeStruct(
+        (visits * slot_rows(row_share) + EXTRA, PW), jnp.bfloat16
+    )
     pair_shape = jax.ShapeDtypeStruct((2, length, PW), jnp.bfloat16)
     band_shape = jax.ShapeDtypeStruct((BANDS * row_share + EXTRA, PW), jnp.bfloat16)
     part_shape = jax.ShapeDtypeStruct((BANDS * row_share, PW), jnp.float32)
@@ -424,11 +460,11 @@
 
     vmem = pl.BlockSpec(memory_space=pltpu.VMEM)
     anywhere = pl.BlockSpec(memory_space=pl.ANY)
-    far, cross, kept = pl.pallas_call(
-        functools.partial(match_kernel, patches),
+    far, cross, kept, *left = pl.pallas_call(
+        functools.partial(match_kernel, patches, groups),
         in_specs=[anywhere] * 10,
-        out_specs=[vmem] * 3,
-        out_shape=[message_shape, pair_shape, pair_shape],
+        out_specs=[vmem] * (3 + groups),
+        out_shape=[message_shape, pair_shape, pair_shape] + [left_shape] * groups,
         scratch_shapes=[
             pltpu.SMEM((tile_count,), jnp.int32),
             pltpu.SMEM((tile_count,), jnp.int32),
@@ -465,10 +501,10 @@
         tiles,
     )
 
-    def send(message, goal, turn):
+    def send(message, goal, turn, owners=range(patches)):
         route = [
             (o * groups + g, goal(o) % patches * groups + (g + turn) % groups)
-            for o in range(patches)
+            for o in owners
             for g in range(groups)
         ]
         return lax.ppermute(message, ("ra", "band"), route)
@@ -489,7 +525,8 @@
 
     held = [pltpu.VMEM(whole_shape.shape, jnp.float32)]
     cross = send(cross, onward(-1), 0)
-    far = send(far, onward(2), 0)
+    far = send(far, onward(2), 0, range(1, patches, 2))
+    left = [send(left[turn], onward(2), turn, range(0, patches, 2)) for turn in range(groups)]
     *kept, detect = local_call(
         functools.partial(keep_kernel, visits, groups),
         "keep",
@@ -521,7 +558,7 @@
     others = [send(others[turn - 1], onward(0), turn) for turn in range(1, groups)]
     near = local_call(early_kernel, "combine_early", [part_shape, weight_shape], *near)
     return local_call(
-        combine_kernel,
+        functools.partial(combine_kernel, visits, groups),
         "combine",
         (
             jax.ShapeDtypeStruct((BANDS, row_share, PW), jnp.float32),
@@ -532,6 +569,7 @@
         own_weight,
         *near,
         *others,
+        *left,
     )
 
 

time: 26 us -> 30.6 us (1.18)
  starting transfers between devices: 12.1 us -> 17.7 us
  waiting for transfers between devices: 4.17 us -> 2.81 us
    ppermute x5 -> x7, starting transfers between devices: 12.1 us -> 17.7 us  [send(): return lax.ppermute(message, ('ra', 'band'), route)]
    ppermute x5 -> x7, waiting for transfers between devices: 4.17 us -> 2.81 us  [send(): return lax.ppermute(message, ('ra', 'band'), route)]
    unnamed x2 -> x6, local copies, waits for them, and re-layouts: 0.96 us -> 0.99 us
  transfers between devices with their start and end apart: 5 -> 7, of which waited for: 3 -> 1; matrix products, arithmetic and copies ran while one was open for 0% -> 0% of each run, Pallas kernels for 3% -> 3%
where the time goes in v16:
time: 30.6 us; the launch traced here: 30.3 us
  starting transfers between devices  17.7 us (58%)
  Pallas kernels  8.09 us (26%)
  waiting for transfers between devices  2.81 us (9%)
  local copies, waits for them, and re-layouts  0.99 us (3%)
  between operations  0.74 us (2%)
    ppermute x7, starting transfers between devices, send(): return lax.ppermute(message, ('ra', 'band'), route)  17.7 us
    pallas_call x1, Pallas kernels, local(): pl.pallas_call(functools.partial(match_kernel, patches, groups), in_specs...  6.3 us
    ppermute x7, waiting for transfers between devices, send(): return lax.ppermute(message, ('ra', 'band'), route)  2.81 us
    pallas_call x5, Pallas kernels, local_call(): pl.pallas_call(kernel, in_specs=[vmem] * len(operands), out_specs=[vmem]...  1.79 us
    unnamed x6, local copies, waits for them, and re-layouts  0.99 us
  transfers between devices with their start and end apart: 7, of which 1 were waited for; matrix products, arithmetic and copies ran while one was open for 0% of the time, Pallas kernels for 3%

profile of v16, /device:TPU:0, one launch (start us, length us, event | category | flops | bytes accessed | tf_op | source)
XLA Modules:
  0.0 30.3 jit_solution(15425101202103598361)
XLA Ops:
  0.6 6.3 %match_and_sum.1 = (bf16[272,256]{1,0:T(8,128)(2,1)}, bf16[2,272,256]{2,1,0:T(8,128)(2,1)}, bf16[2,272,256]{2,1,0:T(8,128)(2,1)}, bf16[144,256]{1,0:T(8,128)(2,1)}, bf16[144,256]{1,0:T(8,128)(2,1)}) custom-call(s32[32]{0:T(128)} %patch_hbm.1, s32[32]{0:T(128)} %offset_hbm.1, s32[32]{0:T(128)} %index_hbm.1, s32[4]{0:T(128)} %band_hbm.1, f32[6]{0:T(128)} %detect_hbm.1, ...), custom_call_target="tpu_custom_call" | custom-call | tf_op jit(solution)/shard_map/match_and_sum/pallas_call | solution.py:463
  6.9 0.5 %collective-permute-start = (bf16[2,272,256]{2,1,0:T(8,128)(2,1)}, bf16[2,272,256]{2,1,0:T(8,128)(2,1)S(1)}, u32[]{:S(2)}, u32[]{:S(2)}) collective-permute-start(bf16[2,272,256]{2,1,0:T(8,128)(2,1)} %get-tuple-element.23), channel_id=1, source_target_pairs={{0,2},{1,3},{2,0},{3,1},{4,6},{5,7},{6,4},{7,5},{8,10},{9,11},{10,... | collective-permute-start | bytes 835592 | tf_op jit(solution)/shard_map/ppermute | solution.py:510
  7.5 0.7 %collective-permute-start.1 = (bf16[272,256]{1,0:T(8,128)(2,1)}, bf16[272,256]{1,0:T(8,128)(2,1)S(1)}, u32[]{:S(2)}, u32[]{:S(2)}) collective-permute-start(bf16[272,256]{1,0:T(8,128)(2,1)} %get-tuple-element.26), channel_id=1, source_target_pairs={{2,6},{3,7},{6,10},{7,11},{10,14},{11,15},{14,18},{15,19},{18,22},... | collective-permute-start | bytes 417800 | tf_op jit(solution)/shard_map/ppermute | solution.py:510
  8.1 0.0 copy-start
  8.1 0.9 %copy-done = bf16[2,272,256]{2,1,0:T(8,128)(2,1)S(1)} copy-done((bf16[2,272,256]{2,1,0:T(8,128)(2,1)S(1)}, bf16[2,272,256]{2,1,0:T(8,128)(2,1)}, u32[]{:S(2)}) %copy-start) | copy-done | bytes 278552
  9.1 0.3 keep.1
  9.3 0.0 collective-permute-done.cross_ref
  9.4 0.3 %merge.1 = (bf16[208,256]{1,0:T(8,128)(2,1)S(1)}, bf16[208,256]{1,0:T(8,128)(2,1)S(1)}, f32[384,256]{1,0:T(8,128)S(1)}, f32[8,256]{1,0:T(8,128)S(1)}) custom-call(f32[2,384,256]{2,1,0:T(8,128)S(1)} %get-tuple-element.21.totals_ref, f32[2,8,256]{2,1,0:T(8,128)S(1)} %get-tuple-element.22.weights_ref, bf16[2,272,256]{2,1,0:T(8,128)(2,1)S(1)} %collective-permute-done.cross_ref), custom_call_target="tpu_custom_call" | custom-call | tf_op jit(solution)/shard_map/merge/pallas_call | solution.py:516
  9.7 7.0 %collective-permute-start.2 = (bf16[208,256]{1,0:T(8,128)(2,1)S(1)}, bf16[208,256]{1,0:T(8,128)(2,1)S(1)}, u32[]{:S(2)}, u32[]{:S(2)}) collective-permute-start(bf16[208,256]{1,0:T(8,128)(2,1)S(1)} %get-tuple-element.29), channel_id=1, source_target_pairs={{0,30},{1,31},{2,4},{3,5},{4,2},{5,3},{6,8},{7,9},{8,6},{9,7},{10,... | collective-permute-start | bytes 319496 | tf_op jit(solution)/shard_map/ppermute | solution.py:510
  16.7 1.0 %collective-permute-start.3 = (bf16[208,256]{1,0:T(8,128)(2,1)S(1)}, bf16[208,256]{1,0:T(8,128)(2,1)S(1)}, u32[]{:S(2)}, u32[]{:S(2)}) collective-permute-start(bf16[208,256]{1,0:T(8,128)(2,1)S(1)} %get-tuple-element.30), channel_id=1, source_target_pairs={{0,31},{1,30},{2,5},{3,4},{4,3},{5,2},{6,9},{7,8},{8,7},{9,6},{10,... | collective-permute-start | bytes 319496 | tf_op jit(solution)/shard_map/ppermute | solution.py:510
  17.7 0.0 collective-permute-done.1.far_ref
  17.7 0.0 copy-start.2
  17.7 0.3 home.1
  18.0 0.6 %collective-permute-start.4 = (bf16[208,256]{1,0:T(8,128)(2,1)S(1)}, bf16[208,256]{1,0:T(8,128)(2,1)S(1)}, u32[]{:S(2)}, u32[]{:S(2)}) collective-permute-start(bf16[208,256]{1,0:T(8,128)(2,1)S(1)} %get-tuple-element.33), channel_id=1, source_target_pairs={{0,1},{1,0},{2,3},{3,2},{4,5},{5,4},{6,7},{7,6},{8,9},{9,8},{10,11... | collective-permute-start | bytes 319496 | tf_op jit(solution)/shard_map/ppermute | solution.py:510
  18.5 0.0 copy-done.2
  18.6 3.6 %collective-permute-start.5 = (bf16[144,256]{1,0:T(8,128)(2,1)S(1)}, bf16[144,256]{1,0:T(8,128)(2,1)S(1)}, u32[]{:S(2)}, u32[]{:S(2)}) collective-permute-start(bf16[144,256]{1,0:T(8,128)(2,1)S(1)} %copy-done.2), channel_id=1, source_target_pairs={{0,28},{1,29},{4,0},{5,1},{8,4},{9,5},{12,8},{13,9},{16,12},{17,13... | collective-permute-start | bytes 221192 | tf_op jit(solution)/shard_map/ppermute | solution.py:510
  22.2 0.0 copy-done.1
  22.2 4.3 %collective-permute-start.6 = (bf16[144,256]{1,0:T(8,128)(2,1)S(1)}, bf16[144,256]{1,0:T(8,128)(2,1)S(1)}, u32[]{:S(2)}, u32[]{:S(2)}) collective-permute-start(bf16[144,256]{1,0:T(8,128)(2,1)S(1)} %copy-done.1), channel_id=1, source_target_pairs={{0,29},{1,28},{4,1},{5,0},{8,5},{9,4},{12,9},{13,8},{16,13},{17,12... | collective-permute-start | bytes 221192 | tf_op jit(solution)/shard_map/ppermute | solution.py:510
  26.5 0.0 collective-permute-done.2.refs_0_
  26.5 0.0 collective-permute-done.3.refs_1_
  26.6 0.0 collective-permute-done.5.refs_1_
  26.6 2.8 %collective-permute-done.6.refs_2_ = bf16[144,256]{1,0:T(8,128)(2,1)S(1)} collective-permute-done((bf16[144,256]{1,0:T(8,128)(2,1)S(1)}, bf16[144,256]{1,0:T(8,128)(2,1)S(1)}, u32[]{:S(2)}, u32[]{:S(2)}) %collective-permute-start.6) | collective-permute-done | bytes 73760 | tf_op jit(solution)/shard_map/ppermute | solution.py:510
  29.4 0.0 collective-permute-done.4.refs_0_
  29.4 0.9 %combine.1 = (f32[6,32,256]{2,1,0:T(8,128)}, f32[32,256]{1,0:T(8,128)}) custom-call(f32[8,256]{1,0:T(8,128)S(1)} %get-tuple-element.20.detect_ref, f32[192,256]{1,0:T(8,128)S(1)} %get-tuple-element.27.own_ref, f32[8,256]{1,0:T(8,128)S(1)} %get-tuple-element.28.own_weight_ref, f32[192,256]{1,0:T(8,128)S(1)} %get-tuple-element.31.near_ref, ...), custom_call_target="tpu_custom_call" | custom-call | tf_op jit(solution)/shard_map/combine/pallas_call | solution.py:516
  (2 shorter events, 0.0 us)
Async XLA Ops:
  6.9 2.4 %collective-permute-start = (bf16[2,272,256]{2,1,0:T(8,128)(2,1)}, bf16[2,272,256]{2,1,0:T(8,128)(2,1)S(1)}, u32[]{:S(2)}, u32[]{:S(2)}) collective-permute-start(bf16[2,272,256]{2,1,0:T(8,128)(2,1)} %get-tuple-element.23), channel_id=1, source_target_pairs={{0,2},{1,3},{2,0},{3,1},{4,6},{5,7},{6,4},{7,5},{8,10},{9,11},{10,... | collective-permute-start | bytes 835592 | tf_op jit(solution)/shard_map/ppermute | solution.py:510
  7.5 10.2 %collective-permute-start.1 = (bf16[272,256]{1,0:T(8,128)(2,1)}, bf16[272,256]{1,0:T(8,128)(2,1)S(1)}, u32[]{:S(2)}, u32[]{:S(2)}) collective-permute-start(bf16[272,256]{1,0:T(8,128)(2,1)} %get-tuple-element.26), channel_id=1, source_target_pairs={{2,6},{3,7},{6,10},{7,11},{10,14},{11,15},{14,18},{15,19},{18,22},... | collective-permute-start | bytes 417800 | tf_op jit(solution)/shard_map/ppermute | solution.py:510
  8.1 1.0 %copy-start = (bf16[2,272,256]{2,1,0:T(8,128)(2,1)S(1)}, bf16[2,272,256]{2,1,0:T(8,128)(2,1)}, u32[]{:S(2)}) copy-start(bf16[2,272,256]{2,1,0:T(8,128)(2,1)} %get-tuple-element.19.kept_ref) | copy-start | bytes 835588
  9.7 16.8 %collective-permute-start.2 = (bf16[208,256]{1,0:T(8,128)(2,1)S(1)}, bf16[208,256]{1,0:T(8,128)(2,1)S(1)}, u32[]{:S(2)}, u32[]{:S(2)}) collective-permute-start(bf16[208,256]{1,0:T(8,128)(2,1)S(1)} %get-tuple-element.29), channel_id=1, source_target_pairs={{0,30},{1,31},{2,4},{3,5},{4,2},{5,3},{6,8},{7,9},{8,6},{9,7},{10,... | collective-permute-start | bytes 319496 | tf_op jit(solution)/shard_map/ppermute | solution.py:510
  16.7 9.9 %collective-permute-start.3 = (bf16[208,256]{1,0:T(8,128)(2,1)S(1)}, bf16[208,256]{1,0:T(8,128)(2,1)S(1)}, u32[]{:S(2)}, u32[]{:S(2)}) collective-permute-start(bf16[208,256]{1,0:T(8,128)(2,1)S(1)} %get-tuple-element.30), channel_id=1, source_target_pairs={{0,31},{1,30},{2,5},{3,4},{4,3},{5,2},{6,9},{7,8},{8,7},{9,6},{10,... | collective-permute-start | bytes 319496 | tf_op jit(solution)/shard_map/ppermute | solution.py:510
  17.7 0.9 %copy-start.2 = (bf16[144,256]{1,0:T(8,128)(2,1)S(1)}, bf16[144,256]{1,0:T(8,128)(2,1)}, u32[]{:S(2)}) copy-start(bf16[144,256]{1,0:T(8,128)(2,1)} %get-tuple-element.34) | copy-start | bytes 221188
  17.7 4.5 %copy-start.1 = (bf16[144,256]{1,0:T(8,128)(2,1)S(1)}, bf16[144,256]{1,0:T(8,128)(2,1)}, u32[]{:S(2)}) copy-start(bf16[144,256]{1,0:T(8,128)(2,1)} %get-tuple-element.35) | copy-start | bytes 221188
  18.0 11.4 %collective-permute-start.4 = (bf16[208,256]{1,0:T(8,128)(2,1)S(1)}, bf16[208,256]{1,0:T(8,128)(2,1)S(1)}, u32[]{:S(2)}, u32[]{:S(2)}) collective-permute-start(bf16[208,256]{1,0:T(8,128)(2,1)S(1)} %get-tuple-element.33), channel_id=1, source_target_pairs={{0,1},{1,0},{2,3},{3,2},{4,5},{5,4},{6,7},{7,6},{8,9},{9,8},{10,11... | collective-permute-start | bytes 319496 | tf_op jit(solution)/shard_map/ppermute | solution.py:510
  18.6 8.0 %collective-permute-start.5 = (bf16[144,256]{1,0:T(8,128)(2,1)S(1)}, bf16[144,256]{1,0:T(8,128)(2,1)S(1)}, u32[]{:S(2)}, u32[]{:S(2)}) collective-permute-start(bf16[144,256]{1,0:T(8,128)(2,1)S(1)} %copy-done.2), channel_id=1, source_target_pairs={{0,28},{1,29},{4,0},{5,1},{8,4},{9,5},{12,8},{13,9},{16,12},{17,13... | collective-permute-start | bytes 221192 | tf_op jit(solution)/shard_map/ppermute | solution.py:510
  22.2 7.1 %collective-permute-start.6 = (bf16[144,256]{1,0:T(8,128)(2,1)S(1)}, bf16[144,256]{1,0:T(8,128)(2,1)S(1)}, u32[]{:S(2)}, u32[]{:S(2)}) collective-permute-start(bf16[144,256]{1,0:T(8,128)(2,1)S(1)} %copy-done.1), channel_id=1, source_target_pairs={{0,29},{1,28},{4,1},{5,0},{8,5},{9,4},{12,9},{13,8},{16,13},{17,12... | collective-permute-start | bytes 221192 | tf_op jit(solution)/shard_map/ppermute | solution.py:510

commit v17 on v15

--- a/solution.py
+++ b/solution.py
@@ -115,6 +115,31 @@
     eye = (iota((tile_count, tile_count), 0) == iota((tile_count, tile_count), 1)).astype(
         jnp.bfloat16
     )
+
+    def edge(distance):
+        here = iota((16, width), 1) + distance
+        return ((here >= 0) & (here < width)).astype(jnp.float32).astype(jnp.bfloat16)
+
+    edges = {distance: edge(distance) for distance in range(-4, 4) if distance != 0}
+
+    def moved_tile(value, distance):
+        if distance == 0:
+            return value
+        turned = pltpu.roll(value, -distance % width, 1).reshape(rows // 16, 16, width)
+        return (turned * edges[distance][None]).reshape(rows, width)
+
+    def shift_tiles(visit):
+        for place in range(per_visit):
+            pixels = tiles_ref[visit * per_visit + place]
+            for side in range(2):
+                for fine in range(4):
+                    part = moved_tile(pixels, -1 - fine if side else fine)
+                    top = fine * FINE_ROWS
+                    shifted[place, side, top + 16 : top + 64, :width] = part[:48]
+                    shifted[place, side, top : top + 48, width:] = part[16:]
+
+    fetch(0).wait()
+    shift_tiles(0)
     for copy in small:
         copy.wait()
     weights[...] = across(eye, jnp.broadcast_to(weight_ref[...], (width, tile_count)))
@@ -157,18 +182,6 @@
     lane = iota((rows, width), 1)
     column = iota((1, width), 1)
 
-    def edge(distance):
-        here = iota((16, width), 1) + distance
-        return ((here >= 0) & (here < width)).astype(jnp.float32).astype(jnp.bfloat16)
-
-    edges = {distance: edge(distance) for distance in range(-4, 4) if distance != 0}
-
-    def moved_tile(value, distance):
-        if distance == 0:
-            return value
-        turned = pltpu.roll(value, -distance % width, 1).reshape(rows // 16, 16, width)
-        return (turned * edges[distance][None]).reshape(rows, width)
-
     def moved(value, distance):
         if distance == 0:
             return value
@@ -177,31 +190,28 @@
         return jnp.where((here >= 0) & (here < width), turned, jnp.zeros_like(turned))
 
     def one_visit(visit, unused):
-        fetch(visit).wait()
         sums[...] = jnp.zeros_like(sums)
         first = visit * per_visit
         for place in range(per_visit):
             tile = first + place
-            pixels = tiles_ref[tile]
             for side in range(2):
-                for fine in range(4):
-                    part = moved_tile(pixels, -1 - fine if side else fine)
-                    top = fine * FINE_ROWS
-                    shifted[place, side, top + 16 : top + 64, :width] = part[:48]
-                    shifted[place, side, top : top + 48, width:] = part[16:]
                 for coarse in range(COARSE):
                     for pair in range(2):
                         vector = pl.ds(
                             tile * VECTORS + (side * COARSE + coarse) * 2 + pair, 1
                         )
-                        spread = jnp.broadcast_to(kernels[vector, :], (BLOCK, width))
-                        turned = pltpu.roll(spread, 0, 1, stride=1, stride_axis=0)
-                        toeplitz[
-                            place,
-                            side,
-                            coarse * BLOCK : (coarse + 1) * BLOCK,
-                            pair * width : (pair + 1) * width,
-                        ] = turned.astype(jnp.bfloat16)
+                        spread = jnp.broadcast_to(kernels[vector, :], (16, width))
+                        turned = pltpu.roll(spread, 0, 1, stride=1, stride_axis=0).astype(
+                            jnp.bfloat16
+                        )
+                        for lower in range(BLOCK // 16):
+                            top = coarse * BLOCK + lower * 16
+                            toeplitz[
+                                place,
+                                side,
+                                top : top + 16,
+                                pair * width : (pair + 1) * width,
+                            ] = pltpu.roll(turned, lower * 16, 1) if lower else turned
         for place in range(per_visit):
             matched = [jnp.zeros((BLOCK, width), jnp.float32) for _ in range(2)]
             for side in range(2):
@@ -237,6 +247,12 @@
                 ],
                 axis=1,
             )
+
+
+        @pl.when(visit + 1 < visits)
+        def prepare():
+            fetch(visit + 1).wait()
+            shift_tiles(visit + 1)
 
         held = pl.ds(pl.multiple_of(visit * rows, rows), rows)
         far[held, :] = sums[REACH + 2 * way].astype(jnp.bfloat16)

time: 26 us -> 34.9 us (1.34)
  Pallas kernels: 7.87 us -> 16.8 us
    pallas_call x1, Pallas kernels: 6.24 us -> 15.2 us  [local(): pl.pallas_call(functools.partial(match_kernel, patches), in_specs=[anywhe...]
where the time goes in v17:
time: 34.9 us; the launch traced here: 34.7 us
  Pallas kernels  16.8 us (48%)
  starting transfers between devices  12.2 us (35%)
  waiting for transfers between devices  4.17 us (12%)
  local copies, waits for them, and re-layouts  0.96 us (3%)
  between operations  0.67 us (2%)
    pallas_call x1, Pallas kernels, local(): pl.pallas_call(functools.partial(match_kernel, patches), in_specs=[anywhe...  15.2 us
    ppermute x5, starting transfers between devices, send(): return lax.ppermute(message, ('ra', 'band'), route)  12.2 us
    ppermute x5, waiting for transfers between devices, send(): return lax.ppermute(message, ('ra', 'band'), route)  4.17 us
    pallas_call x5, Pallas kernels, local_call(): pl.pallas_call(kernel, in_specs=[vmem] * len(operands), out_specs=[vmem]...  1.62 us
    unnamed x2, local copies, waits for them, and re-layouts  0.96 us
  transfers between devices with their start and end apart: 5, of which 3 were waited for; matrix products, arithmetic and copies ran while one was open for 0% of the time, Pallas kernels for 3%

profile of v17, /device:TPU:0, one launch (start us, length us, event | category | flops | bytes accessed | tf_op | source)
XLA Modules:
  0.0 34.7 jit_solution(8140286995328388769)
XLA Ops:
  0.6 15.2 %match_and_sum.1 = (bf16[272,256]{1,0:T(8,128)(2,1)}, bf16[2,272,256]{2,1,0:T(8,128)(2,1)}, bf16[2,272,256]{2,1,0:T(8,128)(2,1)}) custom-call(s32[32]{0:T(128)} %patch_hbm.1, s32[32]{0:T(128)} %offset_hbm.1, s32[32]{0:T(128)} %index_hbm.1, s32[4]{0:T(128)} %band_hbm.1, f32[6]{0:T(128)} %detect_hbm.1, f32[21,64]{1,0:T(8,128)} %bitcast.2, ...), custom_call_target="tpu_custom_call" | custom-call | tf_op jit(solution)/shard_map/match_and_sum/pallas_call | solution.py:443
  15.8 0.5 %collective-permute-start = (bf16[2,272,256]{2,1,0:T(8,128)(2,1)}, bf16[2,272,256]{2,1,0:T(8,128)(2,1)S(1)}, u32[]{:S(2)}, u32[]{:S(2)}) collective-permute-start(bf16[2,272,256]{2,1,0:T(8,128)(2,1)} %get-tuple-element.21), channel_id=1, source_target_pairs={{0,2},{1,3},{2,0},{3,1},{4,6},{5,7},{6,4},{7,5},{8,10},{9,11},{10,... | collective-permute-start | bytes 835592 | tf_op jit(solution)/shard_map/ppermute | solution.py:490
  16.3 5.6 %collective-permute-start.1 = (bf16[272,256]{1,0:T(8,128)(2,1)}, bf16[272,256]{1,0:T(8,128)(2,1)S(1)}, u32[]{:S(2)}, u32[]{:S(2)}) collective-permute-start(bf16[272,256]{1,0:T(8,128)(2,1)} %get-tuple-element.24), channel_id=1, source_target_pairs={{0,28},{1,29},{2,6},{3,7},{4,0},{5,1},{6,10},{7,11},{8,4},{9,5},{1... | collective-permute-start | bytes 417800 | tf_op jit(solution)/shard_map/ppermute | solution.py:490
  21.9 0.0 copy-start
  21.9 1.0 %copy-done = bf16[2,272,256]{2,1,0:T(8,128)(2,1)S(1)} copy-done((bf16[2,272,256]{2,1,0:T(8,128)(2,1)S(1)}, bf16[2,272,256]{2,1,0:T(8,128)(2,1)}, u32[]{:S(2)}) %copy-start) | copy-done | bytes 278552
  22.9 0.3 keep.1
  23.2 0.0 collective-permute-done.cross_ref
  23.2 0.3 merge.1
  23.5 0.3 collective-permute-start.2
  23.8 5.2 %collective-permute-start.3 = (bf16[208,256]{1,0:T(8,128)(2,1)S(1)}, bf16[208,256]{1,0:T(8,128)(2,1)S(1)}, u32[]{:S(2)}, u32[]{:S(2)}) collective-permute-start(bf16[208,256]{1,0:T(8,128)(2,1)S(1)} %get-tuple-element.28), channel_id=1, source_target_pairs={{0,31},{1,30},{2,5},{3,4},{4,3},{5,2},{6,9},{7,8},{8,7},{9,6},{10,... | collective-permute-start | bytes 319496 | tf_op jit(solution)/shard_map/ppermute | solution.py:490
  29.0 0.0 collective-permute-done.1.far_ref
  29.0 0.3 home.1
  29.2 0.6 %collective-permute-start.4 = (bf16[208,256]{1,0:T(8,128)(2,1)S(1)}, bf16[208,256]{1,0:T(8,128)(2,1)S(1)}, u32[]{:S(2)}, u32[]{:S(2)}) collective-permute-start(bf16[208,256]{1,0:T(8,128)(2,1)S(1)} %get-tuple-element.31), channel_id=1, source_target_pairs={{0,1},{1,0},{2,3},{3,2},{4,5},{5,4},{6,7},{7,6},{8,9},{9,8},{10,11... | collective-permute-start | bytes 319496 | tf_op jit(solution)/shard_map/ppermute | solution.py:490
  29.8 0.6 %collective-permute-done.2.refs_0_ = bf16[208,256]{1,0:T(8,128)(2,1)S(1)} collective-permute-done((bf16[208,256]{1,0:T(8,128)(2,1)S(1)}, bf16[208,256]{1,0:T(8,128)(2,1)S(1)}, u32[]{:S(2)}, u32[]{:S(2)}) %collective-permute-start.2) | collective-permute-done | bytes 106528 | tf_op jit(solution)/shard_map/ppermute | solution.py:490
  30.4 2.1 %collective-permute-done.3.refs_1_ = bf16[208,256]{1,0:T(8,128)(2,1)S(1)} collective-permute-done((bf16[208,256]{1,0:T(8,128)(2,1)S(1)}, bf16[208,256]{1,0:T(8,128)(2,1)S(1)}, u32[]{:S(2)}, u32[]{:S(2)}) %collective-permute-start.3) | collective-permute-done | bytes 106528 | tf_op jit(solution)/shard_map/ppermute | solution.py:490
  32.5 1.5 %collective-permute-done.4.refs_0_ = bf16[208,256]{1,0:T(8,128)(2,1)S(1)} collective-permute-done((bf16[208,256]{1,0:T(8,128)(2,1)S(1)}, bf16[208,256]{1,0:T(8,128)(2,1)S(1)}, u32[]{:S(2)}, u32[]{:S(2)}) %collective-permute-start.4) | collective-permute-done | bytes 106528 | tf_op jit(solution)/shard_map/ppermute | solution.py:490
  34.0 0.7 %combine.1 = (f32[6,32,256]{2,1,0:T(8,128)}, f32[32,256]{1,0:T(8,128)}) custom-call(f32[8,256]{1,0:T(8,128)S(1)} %get-tuple-element.18.detect_ref, f32[192,256]{1,0:T(8,128)S(1)} %get-tuple-element.25.own_ref, f32[8,256]{1,0:T(8,128)S(1)} %get-tuple-element.26.own_weight_ref, f32[192,256]{1,0:T(8,128)S(1)} %get-tuple-element.29.near_ref, ...), custom_call_target="tpu_custom_call" | custom-call | tf_op jit(solution)/shard_map/combine/pallas_call | solution.py:496
  (1 shorter events, 0.0 us)
Async XLA Ops:
  15.8 7.3 %collective-permute-start = (bf16[2,272,256]{2,1,0:T(8,128)(2,1)}, bf16[2,272,256]{2,1,0:T(8,128)(2,1)S(1)}, u32[]{:S(2)}, u32[]{:S(2)}) collective-permute-start(bf16[2,272,256]{2,1,0:T(8,128)(2,1)} %get-tuple-element.21), channel_id=1, source_target_pairs={{0,2},{1,3},{2,0},{3,1},{4,6},{5,7},{6,4},{7,5},{8,10},{9,11},{10,... | collective-permute-start | bytes 835592 | tf_op jit(solution)/shard_map/ppermute | solution.py:490
  16.3 12.6 %collective-permute-start.1 = (bf16[272,256]{1,0:T(8,128)(2,1)}, bf16[272,256]{1,0:T(8,128)(2,1)S(1)}, u32[]{:S(2)}, u32[]{:S(2)}) collective-permute-start(bf16[272,256]{1,0:T(8,128)(2,1)} %get-tuple-element.24), channel_id=1, source_target_pairs={{0,28},{1,29},{2,6},{3,7},{4,0},{5,1},{6,10},{7,11},{8,4},{9,5},{1... | collective-permute-start | bytes 417800 | tf_op jit(solution)/shard_map/ppermute | solution.py:490
  21.9 1.0 %copy-start = (bf16[2,272,256]{2,1,0:T(8,128)(2,1)S(1)}, bf16[2,272,256]{2,1,0:T(8,128)(2,1)}, u32[]{:S(2)}) copy-start(bf16[2,272,256]{2,1,0:T(8,128)(2,1)} %get-tuple-element.17.kept_ref) | copy-start | bytes 835588
  23.5 6.9 %collective-permute-start.2 = (bf16[208,256]{1,0:T(8,128)(2,1)S(1)}, bf16[208,256]{1,0:T(8,128)(2,1)S(1)}, u32[]{:S(2)}, u32[]{:S(2)}) collective-permute-start(bf16[208,256]{1,0:T(8,128)(2,1)S(1)} %get-tuple-element.27), channel_id=1, source_target_pairs={{0,30},{1,31},{2,4},{3,5},{4,2},{5,3},{6,8},{7,9},{8,6},{9,7},{10,... | collective-permute-start | bytes 319496 | tf_op jit(solution)/shard_map/ppermute | solution.py:490
  23.8 8.7 %collective-permute-start.3 = (bf16[208,256]{1,0:T(8,128)(2,1)S(1)}, bf16[208,256]{1,0:T(8,128)(2,1)S(1)}, u32[]{:S(2)}, u32[]{:S(2)}) collective-permute-start(bf16[208,256]{1,0:T(8,128)(2,1)S(1)} %get-tuple-element.28), channel_id=1, source_target_pairs={{0,31},{1,30},{2,5},{3,4},{4,3},{5,2},{6,9},{7,8},{8,7},{9,6},{10,... | collective-permute-start | bytes 319496 | tf_op jit(solution)/shard_map/ppermute | solution.py:490
  29.2 4.8 %collective-permute-start.4 = (bf16[208,256]{1,0:T(8,128)(2,1)S(1)}, bf16[208,256]{1,0:T(8,128)(2,1)S(1)}, u32[]{:S(2)}, u32[]{:S(2)}) collective-permute-start(bf16[208,256]{1,0:T(8,128)(2,1)S(1)} %get-tuple-element.31), channel_id=1, source_target_pairs={{0,1},{1,0},{2,3},{3,2},{4,5},{5,4},{6,7},{7,6},{8,9},{9,8},{10,11... | collective-permute-start | bytes 319496 | tf_op jit(solution)/shard_map/ppermute | solution.py:490

commit v18 on v15

--- a/solution.py
+++ b/solution.py
@@ -157,18 +157,6 @@
     lane = iota((rows, width), 1)
     column = iota((1, width), 1)
 
-    def edge(distance):
-        here = iota((16, width), 1) + distance
-        return ((here >= 0) & (here < width)).astype(jnp.float32).astype(jnp.bfloat16)
-
-    edges = {distance: edge(distance) for distance in range(-4, 4) if distance != 0}
-
-    def moved_tile(value, distance):
-        if distance == 0:
-            return value
-        turned = pltpu.roll(value, -distance % width, 1).reshape(rows // 16, 16, width)
-        return (turned * edges[distance][None]).reshape(rows, width)
-
     def moved(value, distance):
         if distance == 0:
             return value
@@ -182,10 +170,10 @@
         first = visit * per_visit
         for place in range(per_visit):
             tile = first + place
-            pixels = tiles_ref[tile]
+            pixels = tiles_ref[tile].astype(jnp.float32)
             for side in range(2):
                 for fine in range(4):
-                    part = moved_tile(pixels, -1 - fine if side else fine)
+                    part = moved(pixels, -1 - fine if side else fine).astype(jnp.bfloat16)
                     top = fine * FINE_ROWS
                     shifted[place, side, top + 16 : top + 64, :width] = part[:48]
                     shifted[place, side, top : top + 48, width:] = part[16:]

time: 26 us -> 26 us (level)
  no operation moved by 1% of the time
where the time goes in v18:
time: 26 us; the launch traced here: 25.9 us
  starting transfers between devices  12.2 us (47%)
  Pallas kernels  7.91 us (30%)
  waiting for transfers between devices  4.17 us (16%)
  local copies, waits for them, and re-layouts  0.96 us (4%)
  between operations  0.67 us (3%)
    ppermute x5, starting transfers between devices, send(): return lax.ppermute(message, ('ra', 'band'), route)  12.2 us
    pallas_call x1, Pallas kernels, local(): pl.pallas_call(functools.partial(match_kernel, patches), in_specs=[anywhe...  6.3 us
    ppermute x5, waiting for transfers between devices, send(): return lax.ppermute(message, ('ra', 'band'), route)  4.17 us
    pallas_call x5, Pallas kernels, local_call(): pl.pallas_call(kernel, in_specs=[vmem] * len(operands), out_specs=[vmem]...  1.61 us
    unnamed x2, local copies, waits for them, and re-layouts  0.96 us
  transfers between devices with their start and end apart: 5, of which 3 were waited for; matrix products, arithmetic and copies ran while one was open for 0% of the time, Pallas kernels for 3%

profile of v18, /device:TPU:0, one launch (start us, length us, event | category | flops | bytes accessed | tf_op | source)
XLA Modules:
  0.0 25.9 jit_solution(14446428485432223955)
XLA Ops:
  0.6 6.3 %match_and_sum.1 = (bf16[272,256]{1,0:T(8,128)(2,1)}, bf16[2,272,256]{2,1,0:T(8,128)(2,1)}, bf16[2,272,256]{2,1,0:T(8,128)(2,1)}) custom-call(s32[32]{0:T(128)} %patch_hbm.1, s32[32]{0:T(128)} %offset_hbm.1, s32[32]{0:T(128)} %index_hbm.1, s32[4]{0:T(128)} %band_hbm.1, f32[6]{0:T(128)} %detect_hbm.1, f32[21,64]{1,0:T(8,128)} %bitcast.2, ...), custom_call_target="tpu_custom_call" | custom-call | tf_op jit(solution)/shard_map/match_and_sum/pallas_call | solution.py:415
  6.9 0.5 %collective-permute-start = (bf16[2,272,256]{2,1,0:T(8,128)(2,1)}, bf16[2,272,256]{2,1,0:T(8,128)(2,1)S(1)}, u32[]{:S(2)}, u32[]{:S(2)}) collective-permute-start(bf16[2,272,256]{2,1,0:T(8,128)(2,1)} %get-tuple-element.21), channel_id=1, source_target_pairs={{0,2},{1,3},{2,0},{3,1},{4,6},{5,7},{6,4},{7,5},{8,10},{9,11},{10,... | collective-permute-start | bytes 835592 | tf_op jit(solution)/shard_map/ppermute | solution.py:462
  7.5 5.6 %collective-permute-start.1 = (bf16[272,256]{1,0:T(8,128)(2,1)}, bf16[272,256]{1,0:T(8,128)(2,1)S(1)}, u32[]{:S(2)}, u32[]{:S(2)}) collective-permute-start(bf16[272,256]{1,0:T(8,128)(2,1)} %get-tuple-element.24), channel_id=1, source_target_pairs={{0,28},{1,29},{2,6},{3,7},{4,0},{5,1},{6,10},{7,11},{8,4},{9,5},{1... | collective-permute-start | bytes 417800 | tf_op jit(solution)/shard_map/ppermute | solution.py:462
  13.1 0.0 copy-start
  13.1 1.0 %copy-done = bf16[2,272,256]{2,1,0:T(8,128)(2,1)S(1)} copy-done((bf16[2,272,256]{2,1,0:T(8,128)(2,1)S(1)}, bf16[2,272,256]{2,1,0:T(8,128)(2,1)}, u32[]{:S(2)}) %copy-start) | copy-done | bytes 278552
  14.0 0.3 keep.1
  14.3 0.0 collective-permute-done.cross_ref
  14.3 0.3 %merge.1 = (bf16[208,256]{1,0:T(8,128)(2,1)S(1)}, bf16[208,256]{1,0:T(8,128)(2,1)S(1)}, f32[384,256]{1,0:T(8,128)S(1)}, f32[8,256]{1,0:T(8,128)S(1)}) custom-call(f32[2,384,256]{2,1,0:T(8,128)S(1)} %get-tuple-element.19.totals_ref, f32[2,8,256]{2,1,0:T(8,128)S(1)} %get-tuple-element.20.weights_ref, bf16[2,272,256]{2,1,0:T(8,128)(2,1)S(1)} %collective-permute-done.cross_ref), custom_call_target="tpu_custom_call" | custom-call | tf_op jit(solution)/shard_map/merge/pallas_call | solution.py:468
  14.6 0.3 %collective-permute-start.2 = (bf16[208,256]{1,0:T(8,128)(2,1)S(1)}, bf16[208,256]{1,0:T(8,128)(2,1)S(1)}, u32[]{:S(2)}, u32[]{:S(2)}) collective-permute-start(bf16[208,256]{1,0:T(8,128)(2,1)S(1)} %get-tuple-element.27), channel_id=1, source_target_pairs={{0,30},{1,31},{2,4},{3,5},{4,2},{5,3},{6,8},{7,9},{8,6},{9,7},{10,... | collective-permute-start | bytes 319496 | tf_op jit(solution)/shard_map/ppermute | solution.py:462
  14.9 5.2 %collective-permute-start.3 = (bf16[208,256]{1,0:T(8,128)(2,1)S(1)}, bf16[208,256]{1,0:T(8,128)(2,1)S(1)}, u32[]{:S(2)}, u32[]{:S(2)}) collective-permute-start(bf16[208,256]{1,0:T(8,128)(2,1)S(1)} %get-tuple-element.28), channel_id=1, source_target_pairs={{0,31},{1,30},{2,5},{3,4},{4,3},{5,2},{6,9},{7,8},{8,7},{9,6},{10,... | collective-permute-start | bytes 319496 | tf_op jit(solution)/shard_map/ppermute | solution.py:462
  20.1 0.0 collective-permute-done.1.far_ref
  20.1 0.3 %home.1 = (bf16[208,256]{1,0:T(8,128)(2,1)S(1)}, f32[192,256]{1,0:T(8,128)S(1)}, f32[8,256]{1,0:T(8,128)S(1)}) custom-call(f32[384,256]{1,0:T(8,128)S(1)} %get-tuple-element.22.home_ref, f32[8,256]{1,0:T(8,128)S(1)} %get-tuple-element.23.home_weight_ref, bf16[272,256]{1,0:T(8,128)(2,1)S(1)} %collective-permute-done.1.far_ref), custom_call_target="tpu_custom_call" | custom-call | tf_op jit(solution)/shard_map/home/pallas_call | solution.py:468
  20.4 0.6 %collective-permute-start.4 = (bf16[208,256]{1,0:T(8,128)(2,1)S(1)}, bf16[208,256]{1,0:T(8,128)(2,1)S(1)}, u32[]{:S(2)}, u32[]{:S(2)}) collective-permute-start(bf16[208,256]{1,0:T(8,128)(2,1)S(1)} %get-tuple-element.31), channel_id=1, source_target_pairs={{0,1},{1,0},{2,3},{3,2},{4,5},{5,4},{6,7},{7,6},{8,9},{9,8},{10,11... | collective-permute-start | bytes 319496 | tf_op jit(solution)/shard_map/ppermute | solution.py:462
  20.9 0.6 %collective-permute-done.2.refs_0_ = bf16[208,256]{1,0:T(8,128)(2,1)S(1)} collective-permute-done((bf16[208,256]{1,0:T(8,128)(2,1)S(1)}, bf16[208,256]{1,0:T(8,128)(2,1)S(1)}, u32[]{:S(2)}, u32[]{:S(2)}) %collective-permute-start.2) | collective-permute-done | bytes 106528 | tf_op jit(solution)/shard_map/ppermute | solution.py:462
  21.5 2.1 %collective-permute-done.3.refs_1_ = bf16[208,256]{1,0:T(8,128)(2,1)S(1)} collective-permute-done((bf16[208,256]{1,0:T(8,128)(2,1)S(1)}, bf16[208,256]{1,0:T(8,128)(2,1)S(1)}, u32[]{:S(2)}, u32[]{:S(2)}) %collective-permute-start.3) | collective-permute-done | bytes 106528 | tf_op jit(solution)/shard_map/ppermute | solution.py:462
  23.6 1.5 %collective-permute-done.4.refs_0_ = bf16[208,256]{1,0:T(8,128)(2,1)S(1)} collective-permute-done((bf16[208,256]{1,0:T(8,128)(2,1)S(1)}, bf16[208,256]{1,0:T(8,128)(2,1)S(1)}, u32[]{:S(2)}, u32[]{:S(2)}) %collective-permute-start.4) | collective-permute-done | bytes 106528 | tf_op jit(solution)/shard_map/ppermute | solution.py:462
  25.1 0.7 %combine.1 = (f32[6,32,256]{2,1,0:T(8,128)}, f32[32,256]{1,0:T(8,128)}) custom-call(f32[8,256]{1,0:T(8,128)S(1)} %get-tuple-element.18.detect_ref, f32[192,256]{1,0:T(8,128)S(1)} %get-tuple-element.25.own_ref, f32[8,256]{1,0:T(8,128)S(1)} %get-tuple-element.26.own_weight_ref, f32[192,256]{1,0:T(8,128)S(1)} %get-tuple-element.29.near_ref, ...), custom_call_target="tpu_custom_call" | custom-call | tf_op jit(solution)/shard_map/combine/pallas_call | solution.py:468
  (1 shorter events, 0.0 us)
Async XLA Ops:
  6.9 7.3 %collective-permute-start = (bf16[2,272,256]{2,1,0:T(8,128)(2,1)}, bf16[2,272,256]{2,1,0:T(8,128)(2,1)S(1)}, u32[]{:S(2)}, u32[]{:S(2)}) collective-permute-start(bf16[2,272,256]{2,1,0:T(8,128)(2,1)} %get-tuple-element.21), channel_id=1, source_target_pairs={{0,2},{1,3},{2,0},{3,1},{4,6},{5,7},{6,4},{7,5},{8,10},{9,11},{10,... | collective-permute-start | bytes 835592 | tf_op jit(solution)/shard_map/ppermute | solution.py:462
  7.5 12.6 %collective-permute-start.1 = (bf16[272,256]{1,0:T(8,128)(2,1)}, bf16[272,256]{1,0:T(8,128)(2,1)S(1)}, u32[]{:S(2)}, u32[]{:S(2)}) collective-permute-start(bf16[272,256]{1,0:T(8,128)(2,1)} %get-tuple-element.24), channel_id=1, source_target_pairs={{0,28},{1,29},{2,6},{3,7},{4,0},{5,1},{6,10},{7,11},{8,4},{9,5},{1... | collective-permute-start | bytes 417800 | tf_op jit(solution)/shard_map/ppermute | solution.py:462
  13.1 1.0 %copy-start = (bf16[2,272,256]{2,1,0:T(8,128)(2,1)S(1)}, bf16[2,272,256]{2,1,0:T(8,128)(2,1)}, u32[]{:S(2)}) copy-start(bf16[2,272,256]{2,1,0:T(8,128)(2,1)} %get-tuple-element.17.kept_ref) | copy-start | bytes 835588
  14.6 6.9 %collective-permute-start.2 = (bf16[208,256]{1,0:T(8,128)(2,1)S(1)}, bf16[208,256]{1,0:T(8,128)(2,1)S(1)}, u32[]{:S(2)}, u32[]{:S(2)}) collective-permute-start(bf16[208,256]{1,0:T(8,128)(2,1)S(1)} %get-tuple-element.27), channel_id=1, source_target_pairs={{0,30},{1,31},{2,4},{3,5},{4,2},{5,3},{6,8},{7,9},{8,6},{9,7},{10,... | collective-permute-start | bytes 319496 | tf_op jit(solution)/shard_map/ppermute | solution.py:462
  14.9 8.7 %collective-permute-start.3 = (bf16[208,256]{1,0:T(8,128)(2,1)S(1)}, bf16[208,256]{1,0:T(8,128)(2,1)S(1)}, u32[]{:S(2)}, u32[]{:S(2)}) collective-permute-start(bf16[208,256]{1,0:T(8,128)(2,1)S(1)} %get-tuple-element.28), channel_id=1, source_target_pairs={{0,31},{1,30},{2,5},{3,4},{4,3},{5,2},{6,9},{7,8},{8,7},{9,6},{10,... | collective-permute-start | bytes 319496 | tf_op jit(solution)/shard_map/ppermute | solution.py:462
  20.4 4.8 %collective-permute-start.4 = (bf16[208,256]{1,0:T(8,128)(2,1)S(1)}, bf16[208,256]{1,0:T(8,128)(2,1)S(1)}, u32[]{:S(2)}, u32[]{:S(2)}) collective-permute-start(bf16[208,256]{1,0:T(8,128)(2,1)S(1)} %get-tuple-element.31), channel_id=1, source_target_pairs={{0,1},{1,0},{2,3},{3,2},{4,5},{5,4},{6,7},{7,6},{8,9},{9,8},{10,11... | collective-permute-start | bytes 319496 | tf_op jit(solution)/shard_map/ppermute | solution.py:462

commit v19 on v15

--- a/solution.py
+++ b/solution.py
@@ -194,8 +194,12 @@
                         vector = pl.ds(
                             tile * VECTORS + (side * COARSE + coarse) * 2 + pair, 1
                         )
-                        spread = jnp.broadcast_to(kernels[vector, :], (BLOCK, width))
+                        spread = jnp.broadcast_to(kernels[vector, :], (8, width))
                         turned = pltpu.roll(spread, 0, 1, stride=1, stride_axis=0)
+                        turned = jnp.concatenate(
+                            [turned] + [pltpu.roll(turned, top, 1) for top in range(8, BLOCK, 8)],
+                            axis=0,
+                        )
                         toeplitz[
                             place,
                             side,

time: 26 us -> 36.9 us (1.42)
  Pallas kernels: 7.87 us -> 18.8 us
    pallas_call x1, Pallas kernels: 6.24 us -> 17.1 us  [local(): pl.pallas_call(functools.partial(match_kernel, patches), in_specs=[anywhe...]
  transfers between devices with their start and end apart: 5 -> 5, of which waited for: 3 -> 3; matrix products, arithmetic and copies ran while one was open for 0% -> 0% of each run, Pallas kernels for 3% -> 2%
where the time goes in v19:
time: 36.9 us; the launch traced here: 36.7 us
  Pallas kernels  18.8 us (51%)
  starting transfers between devices  12.1 us (33%)
  waiting for transfers between devices  4.17 us (11%)
  local copies, waits for them, and re-layouts  0.96 us (3%)
  between operations  0.67 us (2%)
    pallas_call x1, Pallas kernels, local(): pl.pallas_call(functools.partial(match_kernel, patches), in_specs=[anywhe...  17.1 us
    ppermute x5, starting transfers between devices, send(): return lax.ppermute(message, ('ra', 'band'), route)  12.1 us
    ppermute x5, waiting for transfers between devices, send(): return lax.ppermute(message, ('ra', 'band'), route)  4.17 us
    pallas_call x5, Pallas kernels, local_call(): pl.pallas_call(kernel, in_specs=[vmem] * len(operands), out_specs=[vmem]...  1.62 us
    unnamed x2, local copies, waits for them, and re-layouts  0.96 us
  transfers between devices with their start and end apart: 5, of which 3 were waited for; matrix products, arithmetic and copies ran while one was open for 0% of the time, Pallas kernels for 2%

profile of v19, /device:TPU:0, one launch (start us, length us, event | category | flops | bytes accessed | tf_op | source)
XLA Modules:
  0.0 36.7 jit_solution(17145976575375300306)
XLA Ops:
  0.6 17.1 %match_and_sum.1 = (bf16[272,256]{1,0:T(8,128)(2,1)}, bf16[2,272,256]{2,1,0:T(8,128)(2,1)}, bf16[2,272,256]{2,1,0:T(8,128)(2,1)}) custom-call(s32[32]{0:T(128)} %patch_hbm.1, s32[32]{0:T(128)} %offset_hbm.1, s32[32]{0:T(128)} %index_hbm.1, s32[4]{0:T(128)} %band_hbm.1, f32[6]{0:T(128)} %detect_hbm.1, f32[21,64]{1,0:T(8,128)} %bitcast.2, ...), custom_call_target="tpu_custom_call" | custom-call | tf_op jit(solution)/shard_map/match_and_sum/pallas_call | solution.py:431
  17.8 0.5 %collective-permute-start = (bf16[2,272,256]{2,1,0:T(8,128)(2,1)}, bf16[2,272,256]{2,1,0:T(8,128)(2,1)S(1)}, u32[]{:S(2)}, u32[]{:S(2)}) collective-permute-start(bf16[2,272,256]{2,1,0:T(8,128)(2,1)} %get-tuple-element.21), channel_id=1, source_target_pairs={{0,2},{1,3},{2,0},{3,1},{4,6},{5,7},{6,4},{7,5},{8,10},{9,11},{10,... | collective-permute-start | bytes 835592 | tf_op jit(solution)/shard_map/ppermute | solution.py:478
  18.3 5.6 %collective-permute-start.1 = (bf16[272,256]{1,0:T(8,128)(2,1)}, bf16[272,256]{1,0:T(8,128)(2,1)S(1)}, u32[]{:S(2)}, u32[]{:S(2)}) collective-permute-start(bf16[272,256]{1,0:T(8,128)(2,1)} %get-tuple-element.24), channel_id=1, source_target_pairs={{0,28},{1,29},{2,6},{3,7},{4,0},{5,1},{6,10},{7,11},{8,4},{9,5},{1... | collective-permute-start | bytes 417800 | tf_op jit(solution)/shard_map/ppermute | solution.py:478
  23.9 0.0 copy-start
  23.9 1.0 %copy-done = bf16[2,272,256]{2,1,0:T(8,128)(2,1)S(1)} copy-done((bf16[2,272,256]{2,1,0:T(8,128)(2,1)S(1)}, bf16[2,272,256]{2,1,0:T(8,128)(2,1)}, u32[]{:S(2)}) %copy-start) | copy-done | bytes 278552
  24.8 0.3 keep.1
  25.1 0.0 collective-permute-done.cross_ref
  25.1 0.3 merge.1
  25.4 0.3 collective-permute-start.2
  25.7 5.2 %collective-permute-start.3 = (bf16[208,256]{1,0:T(8,128)(2,1)S(1)}, bf16[208,256]{1,0:T(8,128)(2,1)S(1)}, u32[]{:S(2)}, u32[]{:S(2)}) collective-permute-start(bf16[208,256]{1,0:T(8,128)(2,1)S(1)} %get-tuple-element.28), channel_id=1, source_target_pairs={{0,31},{1,30},{2,5},{3,4},{4,3},{5,2},{6,9},{7,8},{8,7},{9,6},{10,... | collective-permute-start | bytes 319496 | tf_op jit(solution)/shard_map/ppermute | solution.py:478
  30.9 0.0 collective-permute-done.1.far_ref
  30.9 0.3 home.1
  31.2 0.6 %collective-permute-start.4 = (bf16[208,256]{1,0:T(8,128)(2,1)S(1)}, bf16[208,256]{1,0:T(8,128)(2,1)S(1)}, u32[]{:S(2)}, u32[]{:S(2)}) collective-permute-start(bf16[208,256]{1,0:T(8,128)(2,1)S(1)} %get-tuple-element.31), channel_id=1, source_target_pairs={{0,1},{1,0},{2,3},{3,2},{4,5},{5,4},{6,7},{7,6},{8,9},{9,8},{10,11... | collective-permute-start | bytes 319496 | tf_op jit(solution)/shard_map/ppermute | solution.py:478
  31.8 0.6 %collective-permute-done.2.refs_0_ = bf16[208,256]{1,0:T(8,128)(2,1)S(1)} collective-permute-done((bf16[208,256]{1,0:T(8,128)(2,1)S(1)}, bf16[208,256]{1,0:T(8,128)(2,1)S(1)}, u32[]{:S(2)}, u32[]{:S(2)}) %collective-permute-start.2) | collective-permute-done | bytes 106528 | tf_op jit(solution)/shard_map/ppermute | solution.py:478
  32.3 2.1 %collective-permute-done.3.refs_1_ = bf16[208,256]{1,0:T(8,128)(2,1)S(1)} collective-permute-done((bf16[208,256]{1,0:T(8,128)(2,1)S(1)}, bf16[208,256]{1,0:T(8,128)(2,1)S(1)}, u32[]{:S(2)}, u32[]{:S(2)}) %collective-permute-start.3) | collective-permute-done | bytes 106528 | tf_op jit(solution)/shard_map/ppermute | solution.py:478
  34.5 1.5 %collective-permute-done.4.refs_0_ = bf16[208,256]{1,0:T(8,128)(2,1)S(1)} collective-permute-done((bf16[208,256]{1,0:T(8,128)(2,1)S(1)}, bf16[208,256]{1,0:T(8,128)(2,1)S(1)}, u32[]{:S(2)}, u32[]{:S(2)}) %collective-permute-start.4) | collective-permute-done | bytes 106528 | tf_op jit(solution)/shard_map/ppermute | solution.py:478
  36.0 0.7 %combine.1 = (f32[6,32,256]{2,1,0:T(8,128)}, f32[32,256]{1,0:T(8,128)}) custom-call(f32[8,256]{1,0:T(8,128)S(1)} %get-tuple-element.18.detect_ref, f32[192,256]{1,0:T(8,128)S(1)} %get-tuple-element.25.own_ref, f32[8,256]{1,0:T(8,128)S(1)} %get-tuple-element.26.own_weight_ref, f32[192,256]{1,0:T(8,128)S(1)} %get-tuple-element.29.near_ref, ...), custom_call_target="tpu_custom_call" | custom-call | tf_op jit(solution)/shard_map/combine/pallas_call | solution.py:484
  (1 shorter events, 0.0 us)
Async XLA Ops:
  17.8 7.3 %collective-permute-start = (bf16[2,272,256]{2,1,0:T(8,128)(2,1)}, bf16[2,272,256]{2,1,0:T(8,128)(2,1)S(1)}, u32[]{:S(2)}, u32[]{:S(2)}) collective-permute-start(bf16[2,272,256]{2,1,0:T(8,128)(2,1)} %get-tuple-element.21), channel_id=1, source_target_pairs={{0,2},{1,3},{2,0},{3,1},{4,6},{5,7},{6,4},{7,5},{8,10},{9,11},{10,... | collective-permute-start | bytes 835592 | tf_op jit(solution)/shard_map/ppermute | solution.py:478
  18.3 12.6 %collective-permute-start.1 = (bf16[272,256]{1,0:T(8,128)(2,1)}, bf16[272,256]{1,0:T(8,128)(2,1)S(1)}, u32[]{:S(2)}, u32[]{:S(2)}) collective-permute-start(bf16[272,256]{1,0:T(8,128)(2,1)} %get-tuple-element.24), channel_id=1, source_target_pairs={{0,28},{1,29},{2,6},{3,7},{4,0},{5,1},{6,10},{7,11},{8,4},{9,5},{1... | collective-permute-start | bytes 417800 | tf_op jit(solution)/shard_map/ppermute | solution.py:478
  23.9 1.0 %copy-start = (bf16[2,272,256]{2,1,0:T(8,128)(2,1)S(1)}, bf16[2,272,256]{2,1,0:T(8,128)(2,1)}, u32[]{:S(2)}) copy-start(bf16[2,272,256]{2,1,0:T(8,128)(2,1)} %get-tuple-element.17.kept_ref) | copy-start | bytes 835588
  25.4 6.9 %collective-permute-start.2 = (bf16[208,256]{1,0:T(8,128)(2,1)S(1)}, bf16[208,256]{1,0:T(8,128)(2,1)S(1)}, u32[]{:S(2)}, u32[]{:S(2)}) collective-permute-start(bf16[208,256]{1,0:T(8,128)(2,1)S(1)} %get-tuple-element.27), channel_id=1, source_target_pairs={{0,30},{1,31},{2,4},{3,5},{4,2},{5,3},{6,8},{7,9},{8,6},{9,7},{10,... | collective-permute-start | bytes 319496 | tf_op jit(solution)/shard_map/ppermute | solution.py:478
  25.7 8.7 %collective-permute-start.3 = (bf16[208,256]{1,0:T(8,128)(2,1)S(1)}, bf16[208,256]{1,0:T(8,128)(2,1)S(1)}, u32[]{:S(2)}, u32[]{:S(2)}) collective-permute-start(bf16[208,256]{1,0:T(8,128)(2,1)S(1)} %get-tuple-element.28), channel_id=1, source_target_pairs={{0,31},{1,30},{2,5},{3,4},{4,3},{5,2},{6,9},{7,8},{8,7},{9,6},{10,... | collective-permute-start | bytes 319496 | tf_op jit(solution)/shard_map/ppermute | solution.py:478
  31.2 4.8 %collective-permute-start.4 = (bf16[208,256]{1,0:T(8,128)(2,1)S(1)}, bf16[208,256]{1,0:T(8,128)(2,1)S(1)}, u32[]{:S(2)}, u32[]{:S(2)}) collective-permute-start(bf16[208,256]{1,0:T(8,128)(2,1)S(1)} %get-tuple-element.31), channel_id=1, source_target_pairs={{0,1},{1,0},{2,3},{3,2},{4,5},{5,4},{6,7},{7,6},{8,9},{9,8},{10,11... | collective-permute-start | bytes 319496 | tf_op jit(solution)/shard_map/ppermute | solution.py:478

commit v20 on v15

--- a/solution.py
+++ b/solution.py
@@ -222,12 +222,15 @@
             matches[place] = jnp.concatenate(matched, axis=0)
         for place in range(per_visit):
             tile = first + place
+            matches[place] = pltpu.roll(
+                matches[place] * weights[pl.ds(tile, 1), :], lax.rem(offset_ref[tile], width), 1
+            )
+        for place in range(per_visit):
+            tile = first + place
             offset = offset_ref[tile]
             bucket = lax.rem(patch_ref[tile] - owner + REACH + patches, patches)
             weight = weights[pl.ds(tile, 1), :]
-            turned = pltpu.roll(
-                matches[place] * weight, lax.rem(offset, width), 1
-            )
+            turned = matches[place]
             sums[bucket, :, :width] += jnp.where(lane >= offset, turned, 0.0)
             sums[bucket, :, width:] += jnp.where(lane < offset, turned, 0.0)
             extra[bucket, pl.ds(visit, 1), :] += jnp.concatenate(

time: 26 us -> 26 us (level)
  no operation moved by 1% of the time
where the time goes in v20:
time: 26 us; the launch traced here: 25.8 us
  starting transfers between devices  12.2 us (47%)
  Pallas kernels  7.86 us (30%)
  waiting for transfers between devices  4.17 us (16%)
  local copies, waits for them, and re-layouts  0.96 us (4%)
  between operations  0.67 us (3%)
    ppermute x5, starting transfers between devices, send(): return lax.ppermute(message, ('ra', 'band'), route)  12.2 us
    pallas_call x1, Pallas kernels, local(): pl.pallas_call(functools.partial(match_kernel, patches), in_specs=[anywhe...  6.24 us
    ppermute x5, waiting for transfers between devices, send(): return lax.ppermute(message, ('ra', 'band'), route)  4.17 us
    pallas_call x5, Pallas kernels, local_call(): pl.pallas_call(kernel, in_specs=[vmem] * len(operands), out_specs=[vmem]...  1.62 us
    unnamed x2, local copies, waits for them, and re-layouts  0.96 us
  transfers between devices with their start and end apart: 5, of which 3 were waited for; matrix products, arithmetic and copies ran while one was open for 0% of the time, Pallas kernels for 3%

profile of v20, /device:TPU:0, one launch (start us, length us, event | category | flops | bytes accessed | tf_op | source)
XLA Modules:
  0.0 25.8 jit_solution(13499292830344810987)
XLA Ops:
  0.6 6.2 %match_and_sum.1 = (bf16[272,256]{1,0:T(8,128)(2,1)}, bf16[2,272,256]{2,1,0:T(8,128)(2,1)}, bf16[2,272,256]{2,1,0:T(8,128)(2,1)}) custom-call(s32[32]{0:T(128)} %patch_hbm.1, s32[32]{0:T(128)} %offset_hbm.1, s32[32]{0:T(128)} %index_hbm.1, s32[4]{0:T(128)} %band_hbm.1, f32[6]{0:T(128)} %detect_hbm.1, f32[21,64]{1,0:T(8,128)} %bitcast.2, ...), custom_call_target="tpu_custom_call" | custom-call | tf_op jit(solution)/shard_map/match_and_sum/pallas_call | solution.py:430
  6.9 0.5 %collective-permute-start = (bf16[2,272,256]{2,1,0:T(8,128)(2,1)}, bf16[2,272,256]{2,1,0:T(8,128)(2,1)S(1)}, u32[]{:S(2)}, u32[]{:S(2)}) collective-permute-start(bf16[2,272,256]{2,1,0:T(8,128)(2,1)} %get-tuple-element.21), channel_id=1, source_target_pairs={{0,2},{1,3},{2,0},{3,1},{4,6},{5,7},{6,4},{7,5},{8,10},{9,11},{10,... | collective-permute-start | bytes 835592 | tf_op jit(solution)/shard_map/ppermute | solution.py:477
  7.4 5.6 %collective-permute-start.1 = (bf16[272,256]{1,0:T(8,128)(2,1)}, bf16[272,256]{1,0:T(8,128)(2,1)S(1)}, u32[]{:S(2)}, u32[]{:S(2)}) collective-permute-start(bf16[272,256]{1,0:T(8,128)(2,1)} %get-tuple-element.24), channel_id=1, source_target_pairs={{0,28},{1,29},{2,6},{3,7},{4,0},{5,1},{6,10},{7,11},{8,4},{9,5},{1... | collective-permute-start | bytes 417800 | tf_op jit(solution)/shard_map/ppermute | solution.py:477
  13.0 0.0 copy-start
  13.0 1.0 %copy-done = bf16[2,272,256]{2,1,0:T(8,128)(2,1)S(1)} copy-done((bf16[2,272,256]{2,1,0:T(8,128)(2,1)S(1)}, bf16[2,272,256]{2,1,0:T(8,128)(2,1)}, u32[]{:S(2)}) %copy-start) | copy-done | bytes 278552
  13.9 0.3 %keep.1 = (f32[2,384,256]{2,1,0:T(8,128)S(1)}, f32[2,8,256]{2,1,0:T(8,128)S(1)}, f32[8,256]{1,0:T(8,128)S(1)}) custom-call(bf16[2,272,256]{2,1,0:T(8,128)(2,1)S(1)} %copy-done), custom_call_target="tpu_custom_call" | custom-call | tf_op jit(solution)/shard_map/keep/pallas_call | solution.py:483
  14.2 0.0 collective-permute-done.cross_ref
  14.2 0.3 %merge.1 = (bf16[208,256]{1,0:T(8,128)(2,1)S(1)}, bf16[208,256]{1,0:T(8,128)(2,1)S(1)}, f32[384,256]{1,0:T(8,128)S(1)}, f32[8,256]{1,0:T(8,128)S(1)}) custom-call(f32[2,384,256]{2,1,0:T(8,128)S(1)} %get-tuple-element.19.totals_ref, f32[2,8,256]{2,1,0:T(8,128)S(1)} %get-tuple-element.20.weights_ref, bf16[2,272,256]{2,1,0:T(8,128)(2,1)S(1)} %collective-permute-done.cross_ref), custom_call_target="tpu_custom_call" | custom-call | tf_op jit(solution)/shard_map/merge/pallas_call | solution.py:483
  14.6 0.3 %collective-permute-start.2 = (bf16[208,256]{1,0:T(8,128)(2,1)S(1)}, bf16[208,256]{1,0:T(8,128)(2,1)S(1)}, u32[]{:S(2)}, u32[]{:S(2)}) collective-permute-start(bf16[208,256]{1,0:T(8,128)(2,1)S(1)} %get-tuple-element.27), channel_id=1, source_target_pairs={{0,30},{1,31},{2,4},{3,5},{4,2},{5,3},{6,8},{7,9},{8,6},{9,7},{10,... | collective-permute-start | bytes 319496 | tf_op jit(solution)/shard_map/ppermute | solution.py:477
  14.8 5.2 %collective-permute-start.3 = (bf16[208,256]{1,0:T(8,128)(2,1)S(1)}, bf16[208,256]{1,0:T(8,128)(2,1)S(1)}, u32[]{:S(2)}, u32[]{:S(2)}) collective-permute-start(bf16[208,256]{1,0:T(8,128)(2,1)S(1)} %get-tuple-element.28), channel_id=1, source_target_pairs={{0,31},{1,30},{2,5},{3,4},{4,3},{5,2},{6,9},{7,8},{8,7},{9,6},{10,... | collective-permute-start | bytes 319496 | tf_op jit(solution)/shard_map/ppermute | solution.py:477
  20.0 0.0 collective-permute-done.1.far_ref
  20.0 0.3 %home.1 = (bf16[208,256]{1,0:T(8,128)(2,1)S(1)}, f32[192,256]{1,0:T(8,128)S(1)}, f32[8,256]{1,0:T(8,128)S(1)}) custom-call(f32[384,256]{1,0:T(8,128)S(1)} %get-tuple-element.22.home_ref, f32[8,256]{1,0:T(8,128)S(1)} %get-tuple-element.23.home_weight_ref, bf16[272,256]{1,0:T(8,128)(2,1)S(1)} %collective-permute-done.1.far_ref), custom_call_target="tpu_custom_call" | custom-call | tf_op jit(solution)/shard_map/home/pallas_call | solution.py:483
  20.3 0.6 %collective-permute-start.4 = (bf16[208,256]{1,0:T(8,128)(2,1)S(1)}, bf16[208,256]{1,0:T(8,128)(2,1)S(1)}, u32[]{:S(2)}, u32[]{:S(2)}) collective-permute-start(bf16[208,256]{1,0:T(8,128)(2,1)S(1)} %get-tuple-element.31), channel_id=1, source_target_pairs={{0,1},{1,0},{2,3},{3,2},{4,5},{5,4},{6,7},{7,6},{8,9},{9,8},{10,11... | collective-permute-start | bytes 319496 | tf_op jit(solution)/shard_map/ppermute | solution.py:477
  20.9 0.6 %collective-permute-done.2.refs_0_ = bf16[208,256]{1,0:T(8,128)(2,1)S(1)} collective-permute-done((bf16[208,256]{1,0:T(8,128)(2,1)S(1)}, bf16[208,256]{1,0:T(8,128)(2,1)S(1)}, u32[]{:S(2)}, u32[]{:S(2)}) %collective-permute-start.2) | collective-permute-done | bytes 106528 | tf_op jit(solution)/shard_map/ppermute | solution.py:477
  21.5 2.1 %collective-permute-done.3.refs_1_ = bf16[208,256]{1,0:T(8,128)(2,1)S(1)} collective-permute-done((bf16[208,256]{1,0:T(8,128)(2,1)S(1)}, bf16[208,256]{1,0:T(8,128)(2,1)S(1)}, u32[]{:S(2)}, u32[]{:S(2)}) %collective-permute-start.3) | collective-permute-done | bytes 106528 | tf_op jit(solution)/shard_map/ppermute | solution.py:477
  23.6 1.5 %collective-permute-done.4.refs_0_ = bf16[208,256]{1,0:T(8,128)(2,1)S(1)} collective-permute-done((bf16[208,256]{1,0:T(8,128)(2,1)S(1)}, bf16[208,256]{1,0:T(8,128)(2,1)S(1)}, u32[]{:S(2)}, u32[]{:S(2)}) %collective-permute-start.4) | collective-permute-done | bytes 106528 | tf_op jit(solution)/shard_map/ppermute | solution.py:477
  25.1 0.7 %combine.1 = (f32[6,32,256]{2,1,0:T(8,128)}, f32[32,256]{1,0:T(8,128)}) custom-call(f32[8,256]{1,0:T(8,128)S(1)} %get-tuple-element.18.detect_ref, f32[192,256]{1,0:T(8,128)S(1)} %get-tuple-element.25.own_ref, f32[8,256]{1,0:T(8,128)S(1)} %get-tuple-element.26.own_weight_ref, f32[192,256]{1,0:T(8,128)S(1)} %get-tuple-element.29.near_ref, ...), custom_call_target="tpu_custom_call" | custom-call | tf_op jit(solution)/shard_map/combine/pallas_call | solution.py:483
  (1 shorter events, 0.0 us)
Async XLA Ops:
  6.9 7.3 %collective-permute-start = (bf16[2,272,256]{2,1,0:T(8,128)(2,1)}, bf16[2,272,256]{2,1,0:T(8,128)(2,1)S(1)}, u32[]{:S(2)}, u32[]{:S(2)}) collective-permute-start(bf16[2,272,256]{2,1,0:T(8,128)(2,1)} %get-tuple-element.21), channel_id=1, source_target_pairs={{0,2},{1,3},{2,0},{3,1},{4,6},{5,7},{6,4},{7,5},{8,10},{9,11},{10,... | collective-permute-start | bytes 835592 | tf_op jit(solution)/shard_map/ppermute | solution.py:477
  7.4 12.6 %collective-permute-start.1 = (bf16[272,256]{1,0:T(8,128)(2,1)}, bf16[272,256]{1,0:T(8,128)(2,1)S(1)}, u32[]{:S(2)}, u32[]{:S(2)}) collective-permute-start(bf16[272,256]{1,0:T(8,128)(2,1)} %get-tuple-element.24), channel_id=1, source_target_pairs={{0,28},{1,29},{2,6},{3,7},{4,0},{5,1},{6,10},{7,11},{8,4},{9,5},{1... | collective-permute-start | bytes 417800 | tf_op jit(solution)/shard_map/ppermute | solution.py:477
  13.0 1.0 %copy-start = (bf16[2,272,256]{2,1,0:T(8,128)(2,1)S(1)}, bf16[2,272,256]{2,1,0:T(8,128)(2,1)}, u32[]{:S(2)}) copy-start(bf16[2,272,256]{2,1,0:T(8,128)(2,1)} %get-tuple-element.17.kept_ref) | copy-start | bytes 835588
  14.6 6.9 %collective-permute-start.2 = (bf16[208,256]{1,0:T(8,128)(2,1)S(1)}, bf16[208,256]{1,0:T(8,128)(2,1)S(1)}, u32[]{:S(2)}, u32[]{:S(2)}) collective-permute-start(bf16[208,256]{1,0:T(8,128)(2,1)S(1)} %get-tuple-element.27), channel_id=1, source_target_pairs={{0,30},{1,31},{2,4},{3,5},{4,2},{5,3},{6,8},{7,9},{8,6},{9,7},{10,... | collective-permute-start | bytes 319496 | tf_op jit(solution)/shard_map/ppermute | solution.py:477
  14.8 8.7 %collective-permute-start.3 = (bf16[208,256]{1,0:T(8,128)(2,1)S(1)}, bf16[208,256]{1,0:T(8,128)(2,1)S(1)}, u32[]{:S(2)}, u32[]{:S(2)}) collective-permute-start(bf16[208,256]{1,0:T(8,128)(2,1)S(1)} %get-tuple-element.28), channel_id=1, source_target_pairs={{0,31},{1,30},{2,5},{3,4},{4,3},{5,2},{6,9},{7,8},{8,7},{9,6},{10,... | collective-permute-start | bytes 319496 | tf_op jit(solution)/shard_map/ppermute | solution.py:477
  20.3 4.8 %collective-permute-start.4 = (bf16[208,256]{1,0:T(8,128)(2,1)S(1)}, bf16[208,256]{1,0:T(8,128)(2,1)S(1)}, u32[]{:S(2)}, u32[]{:S(2)}) collective-permute-start(bf16[208,256]{1,0:T(8,128)(2,1)S(1)} %get-tuple-element.31), channel_id=1, source_target_pairs={{0,1},{1,0},{2,3},{3,2},{4,5},{5,4},{6,7},{7,6},{8,9},{9,8},{10,11... | collective-permute-start | bytes 319496 | tf_op jit(solution)/shard_map/ppermute | solution.py:477

commit v21 on v20

--- a/solution.py
+++ b/solution.py
@@ -189,6 +189,9 @@
                     top = fine * FINE_ROWS
                     shifted[place, side, top + 16 : top + 64, :width] = part[:48]
                     shifted[place, side, top : top + 48, width:] = part[16:]
+        for place in range(per_visit):
+            tile = first + place
+            for side in range(2):
                 for coarse in range(COARSE):
                     for pair in range(2):
                         vector = pl.ds(

time: 26 us -> 26.1 us (level)
  no operation moved by 1% of the time
where the time goes in v21:
time: 26.1 us; the launch traced here: 25.9 us
  starting transfers between devices  12.2 us (47%)
  Pallas kernels  7.96 us (30%)
  waiting for transfers between devices  4.17 us (16%)
  local copies, waits for them, and re-layouts  0.96 us (4%)
  between operations  0.67 us (3%)
    ppermute x5, starting transfers between devices, send(): return lax.ppermute(message, ('ra', 'band'), route)  12.2 us
    pallas_call x1, Pallas kernels, local(): pl.pallas_call(functools.partial(match_kernel, patches), in_specs=[anywhe...  6.34 us
    ppermute x5, waiting for transfers between devices, send(): return lax.ppermute(message, ('ra', 'band'), route)  4.17 us
    pallas_call x5, Pallas kernels, local_call(): pl.pallas_call(kernel, in_specs=[vmem] * len(operands), out_specs=[vmem]...  1.62 us
    unnamed x2, local copies, waits for them, and re-layouts  0.96 us
  transfers between devices with their start and end apart: 5, of which 3 were waited for; matrix products, arithmetic and copies ran while one was open for 0% of the time, Pallas kernels for 3%

profile of v21, /device:TPU:0, one launch (start us, length us, event | category | flops | bytes accessed | tf_op | source)
XLA Modules:
  0.0 25.9 jit_solution(13140945980819342242)
XLA Ops:
  0.6 6.3 %match_and_sum.1 = (bf16[272,256]{1,0:T(8,128)(2,1)}, bf16[2,272,256]{2,1,0:T(8,128)(2,1)}, bf16[2,272,256]{2,1,0:T(8,128)(2,1)}) custom-call(s32[32]{0:T(128)} %patch_hbm.1, s32[32]{0:T(128)} %offset_hbm.1, s32[32]{0:T(128)} %index_hbm.1, s32[4]{0:T(128)} %band_hbm.1, f32[6]{0:T(128)} %detect_hbm.1, f32[21,64]{1,0:T(8,128)} %bitcast.2, ...), custom_call_target="tpu_custom_call" | custom-call | tf_op jit(solution)/shard_map/match_and_sum/pallas_call | solution.py:433
  7.0 0.5 %collective-permute-start = (bf16[2,272,256]{2,1,0:T(8,128)(2,1)}, bf16[2,272,256]{2,1,0:T(8,128)(2,1)S(1)}, u32[]{:S(2)}, u32[]{:S(2)}) collective-permute-start(bf16[2,272,256]{2,1,0:T(8,128)(2,1)} %get-tuple-element.21), channel_id=1, source_target_pairs={{0,2},{1,3},{2,0},{3,1},{4,6},{5,7},{6,4},{7,5},{8,10},{9,11},{10,... | collective-permute-start | bytes 835592 | tf_op jit(solution)/shard_map/ppermute | solution.py:480
  7.5 5.6 %collective-permute-start.1 = (bf16[272,256]{1,0:T(8,128)(2,1)}, bf16[272,256]{1,0:T(8,128)(2,1)S(1)}, u32[]{:S(2)}, u32[]{:S(2)}) collective-permute-start(bf16[272,256]{1,0:T(8,128)(2,1)} %get-tuple-element.24), channel_id=1, source_target_pairs={{0,28},{1,29},{2,6},{3,7},{4,0},{5,1},{6,10},{7,11},{8,4},{9,5},{1... | collective-permute-start | bytes 417800 | tf_op jit(solution)/shard_map/ppermute | solution.py:480
  13.1 0.0 copy-start
  13.1 1.0 %copy-done = bf16[2,272,256]{2,1,0:T(8,128)(2,1)S(1)} copy-done((bf16[2,272,256]{2,1,0:T(8,128)(2,1)S(1)}, bf16[2,272,256]{2,1,0:T(8,128)(2,1)}, u32[]{:S(2)}) %copy-start) | copy-done | bytes 278552
  14.1 0.3 %keep.1 = (f32[2,384,256]{2,1,0:T(8,128)S(1)}, f32[2,8,256]{2,1,0:T(8,128)S(1)}, f32[8,256]{1,0:T(8,128)S(1)}) custom-call(bf16[2,272,256]{2,1,0:T(8,128)(2,1)S(1)} %copy-done), custom_call_target="tpu_custom_call" | custom-call | tf_op jit(solution)/shard_map/keep/pallas_call | solution.py:486
  14.3 0.0 collective-permute-done.cross_ref
  14.3 0.3 %merge.1 = (bf16[208,256]{1,0:T(8,128)(2,1)S(1)}, bf16[208,256]{1,0:T(8,128)(2,1)S(1)}, f32[384,256]{1,0:T(8,128)S(1)}, f32[8,256]{1,0:T(8,128)S(1)}) custom-call(f32[2,384,256]{2,1,0:T(8,128)S(1)} %get-tuple-element.19.totals_ref, f32[2,8,256]{2,1,0:T(8,128)S(1)} %get-tuple-element.20.weights_ref, bf16[2,272,256]{2,1,0:T(8,128)(2,1)S(1)} %collective-permute-done.cross_ref), custom_call_target="tpu_custom_call" | custom-call | tf_op jit(solution)/shard_map/merge/pallas_call | solution.py:486
  14.7 0.3 %collective-permute-start.2 = (bf16[208,256]{1,0:T(8,128)(2,1)S(1)}, bf16[208,256]{1,0:T(8,128)(2,1)S(1)}, u32[]{:S(2)}, u32[]{:S(2)}) collective-permute-start(bf16[208,256]{1,0:T(8,128)(2,1)S(1)} %get-tuple-element.27), channel_id=1, source_target_pairs={{0,30},{1,31},{2,4},{3,5},{4,2},{5,3},{6,8},{7,9},{8,6},{9,7},{10,... | collective-permute-start | bytes 319496 | tf_op jit(solution)/shard_map/ppermute | solution.py:480
  14.9 5.2 %collective-permute-start.3 = (bf16[208,256]{1,0:T(8,128)(2,1)S(1)}, bf16[208,256]{1,0:T(8,128)(2,1)S(1)}, u32[]{:S(2)}, u32[]{:S(2)}) collective-permute-start(bf16[208,256]{1,0:T(8,128)(2,1)S(1)} %get-tuple-element.28), channel_id=1, source_target_pairs={{0,31},{1,30},{2,5},{3,4},{4,3},{5,2},{6,9},{7,8},{8,7},{9,6},{10,... | collective-permute-start | bytes 319496 | tf_op jit(solution)/shard_map/ppermute | solution.py:480
  20.1 0.0 collective-permute-done.1.far_ref
  20.1 0.3 %home.1 = (bf16[208,256]{1,0:T(8,128)(2,1)S(1)}, f32[192,256]{1,0:T(8,128)S(1)}, f32[8,256]{1,0:T(8,128)S(1)}) custom-call(f32[384,256]{1,0:T(8,128)S(1)} %get-tuple-element.22.home_ref, f32[8,256]{1,0:T(8,128)S(1)} %get-tuple-element.23.home_weight_ref, bf16[272,256]{1,0:T(8,128)(2,1)S(1)} %collective-permute-done.1.far_ref), custom_call_target="tpu_custom_call" | custom-call | tf_op jit(solution)/shard_map/home/pallas_call | solution.py:486
  20.4 0.6 %collective-permute-start.4 = (bf16[208,256]{1,0:T(8,128)(2,1)S(1)}, bf16[208,256]{1,0:T(8,128)(2,1)S(1)}, u32[]{:S(2)}, u32[]{:S(2)}) collective-permute-start(bf16[208,256]{1,0:T(8,128)(2,1)S(1)} %get-tuple-element.31), channel_id=1, source_target_pairs={{0,1},{1,0},{2,3},{3,2},{4,5},{5,4},{6,7},{7,6},{8,9},{9,8},{10,11... | collective-permute-start | bytes 319496 | tf_op jit(solution)/shard_map/ppermute | solution.py:480
  21.0 0.6 %collective-permute-done.2.refs_0_ = bf16[208,256]{1,0:T(8,128)(2,1)S(1)} collective-permute-done((bf16[208,256]{1,0:T(8,128)(2,1)S(1)}, bf16[208,256]{1,0:T(8,128)(2,1)S(1)}, u32[]{:S(2)}, u32[]{:S(2)}) %collective-permute-start.2) | collective-permute-done | bytes 106528 | tf_op jit(solution)/shard_map/ppermute | solution.py:480
  21.6 2.1 %collective-permute-done.3.refs_1_ = bf16[208,256]{1,0:T(8,128)(2,1)S(1)} collective-permute-done((bf16[208,256]{1,0:T(8,128)(2,1)S(1)}, bf16[208,256]{1,0:T(8,128)(2,1)S(1)}, u32[]{:S(2)}, u32[]{:S(2)}) %collective-permute-start.3) | collective-permute-done | bytes 106528 | tf_op jit(solution)/shard_map/ppermute | solution.py:480
  23.7 1.5 %collective-permute-done.4.refs_0_ = bf16[208,256]{1,0:T(8,128)(2,1)S(1)} collective-permute-done((bf16[208,256]{1,0:T(8,128)(2,1)S(1)}, bf16[208,256]{1,0:T(8,128)(2,1)S(1)}, u32[]{:S(2)}, u32[]{:S(2)}) %collective-permute-start.4) | collective-permute-done | bytes 106528 | tf_op jit(solution)/shard_map/ppermute | solution.py:480
  25.2 0.7 %combine.1 = (f32[6,32,256]{2,1,0:T(8,128)}, f32[32,256]{1,0:T(8,128)}) custom-call(f32[8,256]{1,0:T(8,128)S(1)} %get-tuple-element.18.detect_ref, f32[192,256]{1,0:T(8,128)S(1)} %get-tuple-element.25.own_ref, f32[8,256]{1,0:T(8,128)S(1)} %get-tuple-element.26.own_weight_ref, f32[192,256]{1,0:T(8,128)S(1)} %get-tuple-element.29.near_ref, ...), custom_call_target="tpu_custom_call" | custom-call | tf_op jit(solution)/shard_map/combine/pallas_call | solution.py:486
  (1 shorter events, 0.0 us)
Async XLA Ops:
  7.0 7.3 %collective-permute-start = (bf16[2,272,256]{2,1,0:T(8,128)(2,1)}, bf16[2,272,256]{2,1,0:T(8,128)(2,1)S(1)}, u32[]{:S(2)}, u32[]{:S(2)}) collective-permute-start(bf16[2,272,256]{2,1,0:T(8,128)(2,1)} %get-tuple-element.21), channel_id=1, source_target_pairs={{0,2},{1,3},{2,0},{3,1},{4,6},{5,7},{6,4},{7,5},{8,10},{9,11},{10,... | collective-permute-start | bytes 835592 | tf_op jit(solution)/shard_map/ppermute | solution.py:480
  7.5 12.6 %collective-permute-start.1 = (bf16[272,256]{1,0:T(8,128)(2,1)}, bf16[272,256]{1,0:T(8,128)(2,1)S(1)}, u32[]{:S(2)}, u32[]{:S(2)}) collective-permute-start(bf16[272,256]{1,0:T(8,128)(2,1)} %get-tuple-element.24), channel_id=1, source_target_pairs={{0,28},{1,29},{2,6},{3,7},{4,0},{5,1},{6,10},{7,11},{8,4},{9,5},{1... | collective-permute-start | bytes 417800 | tf_op jit(solution)/shard_map/ppermute | solution.py:480
  13.1 1.0 %copy-start = (bf16[2,272,256]{2,1,0:T(8,128)(2,1)S(1)}, bf16[2,272,256]{2,1,0:T(8,128)(2,1)}, u32[]{:S(2)}) copy-start(bf16[2,272,256]{2,1,0:T(8,128)(2,1)} %get-tuple-element.17.kept_ref) | copy-start | bytes 835588
  14.7 6.9 %collective-permute-start.2 = (bf16[208,256]{1,0:T(8,128)(2,1)S(1)}, bf16[208,256]{1,0:T(8,128)(2,1)S(1)}, u32[]{:S(2)}, u32[]{:S(2)}) collective-permute-start(bf16[208,256]{1,0:T(8,128)(2,1)S(1)} %get-tuple-element.27), channel_id=1, source_target_pairs={{0,30},{1,31},{2,4},{3,5},{4,2},{5,3},{6,8},{7,9},{8,6},{9,7},{10,... | collective-permute-start | bytes 319496 | tf_op jit(solution)/shard_map/ppermute | solution.py:480
  14.9 8.7 %collective-permute-start.3 = (bf16[208,256]{1,0:T(8,128)(2,1)S(1)}, bf16[208,256]{1,0:T(8,128)(2,1)S(1)}, u32[]{:S(2)}, u32[]{:S(2)}) collective-permute-start(bf16[208,256]{1,0:T(8,128)(2,1)S(1)} %get-tuple-element.28), channel_id=1, source_target_pairs={{0,31},{1,30},{2,5},{3,4},{4,3},{5,2},{6,9},{7,8},{8,7},{9,6},{10,... | collective-permute-start | bytes 319496 | tf_op jit(solution)/shard_map/ppermute | solution.py:480
  20.4 4.8 %collective-permute-start.4 = (bf16[208,256]{1,0:T(8,128)(2,1)S(1)}, bf16[208,256]{1,0:T(8,128)(2,1)S(1)}, u32[]{:S(2)}, u32[]{:S(2)}) collective-permute-start(bf16[208,256]{1,0:T(8,128)(2,1)S(1)} %get-tuple-element.31), channel_id=1, source_target_pairs={{0,1},{1,0},{2,3},{3,2},{4,5},{5,4},{6,7},{7,6},{8,9},{9,8},{10,11... | collective-permute-start | bytes 319496 | tf_op jit(solution)/shard_map/ppermute | solution.py:480

commit v22 on v21

--- a/solution.py
+++ b/solution.py
@@ -364,8 +364,12 @@
 
 
 def home_kernel(count, groups, home_ref, home_weight_ref, far_ref, *refs):
-    messages = refs[: groups - 1]
-    own_ref, own_weight_ref, held = refs[groups - 1 :]
+    passing = refs[: groups - 1]
+    messages = refs[groups - 1 : 2 * (groups - 1)]
+    passed = refs[2 * (groups - 1) : 3 * (groups - 1)]
+    own_ref, own_weight_ref, held = refs[3 * (groups - 1) :]
+    for source, target in zip(passing, passed):
+        target[...] = source[...]
     totals, weights = add_message(count, groups, far_ref)
     held[...] = totals + home_ref[...]
     weights += home_weight_ref[...]
@@ -382,6 +386,10 @@
     totals_ref[...], weights_ref[...] = add_banded(
         jnp.zeros((depth, PW), jnp.float32), jnp.zeros((8, PW), jnp.float32), messages
     )
+
+
+def later_kernel(near_ref, near_weight_ref, *refs):
+    refs[-2][...], refs[-1][...] = add_banded(near_ref[...], near_weight_ref[...], refs[:-2])
 
 
 def combine_kernel(
@@ -514,18 +522,24 @@
         cross,
         scratch_shapes=held,
     )
-    near = [send(near[turn], onward(1), turn) for turn in range(groups)]
+    first = send(near[0], onward(1), 0)
     *others, own, own_weight = local_call(
         functools.partial(home_kernel, visits, groups),
         "home",
-        [band_shape] * (groups - 1) + [part_shape, weight_shape],
+        [band_shape] * (2 * groups - 2) + [part_shape, weight_shape],
         home,
         home_weight,
         far,
+        *near[1:],
         scratch_shapes=held,
     )
+    others, near = others[: groups - 1], others[groups - 1 :]
     others = [send(others[turn - 1], onward(0), turn) for turn in range(1, groups)]
-    near = local_call(early_kernel, "combine_early", [part_shape, weight_shape], *near)
+    near = [send(near[turn - 1], onward(1), turn) for turn in range(1, groups)]
+    early = local_call(early_kernel, "combine_early", [part_shape, weight_shape], first)
+    early = local_call(
+        later_kernel, "combine_later", [part_shape, weight_shape], *early, *others
+    )
     return local_call(
         combine_kernel,
         "combine",
@@ -536,8 +550,8 @@
         detect,
         own,
         own_weight,
+        *early,
         *near,
-        *others,
     )
 
 

time: 26.1 us -> 26.5 us (1.015)
  waiting for transfers between devices: 4.17 us -> 5.91 us
  starting transfers between devices: 12.2 us -> 10.8 us
    ppermute x5, waiting for transfers between devices: 4.17 us -> 5.91 us  [send(): return lax.ppermute(message, ('ra', 'band'), route)]
    ppermute x5, starting transfers between devices: 12.2 us -> 10.8 us  [send(): return lax.ppermute(message, ('ra', 'band'), route)]
    pallas_call x5 -> x6, Pallas kernels: 1.62 us -> 1.64 us  [local_call(): pl.pallas_call(kernel, in_specs=[vmem] * len(operands), out_specs=[vmem]...]
where the time goes in v22:
time: 26.5 us; the launch traced here: 26.3 us
  starting transfers between devices  10.8 us (41%)
  Pallas kernels  7.98 us (30%)
  waiting for transfers between devices  5.91 us (22%)
  local copies, waits for them, and re-layouts  0.96 us (4%)
  between operations  0.68 us (3%)
    ppermute x5, starting transfers between devices, send(): return lax.ppermute(message, ('ra', 'band'), route)  10.8 us
    pallas_call x1, Pallas kernels, local(): pl.pallas_call(functools.partial(match_kernel, patches), in_specs=[anywhe...  6.35 us
    ppermute x5, waiting for transfers between devices, send(): return lax.ppermute(message, ('ra', 'band'), route)  5.91 us
    pallas_call x6, Pallas kernels, local_call(): pl.pallas_call(kernel, in_specs=[vmem] * len(operands), out_specs=[vmem]...  1.64 us
    unnamed x2, local copies, waits for them, and re-layouts  0.96 us
  transfers between devices with their start and end apart: 5, of which 3 were waited for; matrix products, arithmetic and copies ran while one was open for 0% of the time, Pallas kernels for 3%

profile of v22, /device:TPU:0, one launch (start us, length us, event | category | flops | bytes accessed | tf_op | source)
XLA Modules:
  0.0 26.3 jit_solution(12274625051859241604)
XLA Ops:
  0.6 6.3 %match_and_sum.1 = (bf16[272,256]{1,0:T(8,128)(2,1)}, bf16[2,272,256]{2,1,0:T(8,128)(2,1)}, bf16[2,272,256]{2,1,0:T(8,128)(2,1)}) custom-call(s32[32]{0:T(128)} %patch_hbm.1, s32[32]{0:T(128)} %offset_hbm.1, s32[32]{0:T(128)} %index_hbm.1, s32[4]{0:T(128)} %band_hbm.1, f32[6]{0:T(128)} %detect_hbm.1, f32[21,64]{1,0:T(8,128)} %bitcast.2, ...), custom_call_target="tpu_custom_call" | custom-call | tf_op jit(solution)/shard_map/match_and_sum/pallas_call | solution.py:441
  7.0 0.5 %collective-permute-start = (bf16[2,272,256]{2,1,0:T(8,128)(2,1)}, bf16[2,272,256]{2,1,0:T(8,128)(2,1)S(1)}, u32[]{:S(2)}, u32[]{:S(2)}) collective-permute-start(bf16[2,272,256]{2,1,0:T(8,128)(2,1)} %get-tuple-element.24), channel_id=1, source_target_pairs={{0,2},{1,3},{2,0},{3,1},{4,6},{5,7},{6,4},{7,5},{8,10},{9,11},{10,... | collective-permute-start | bytes 835592 | tf_op jit(solution)/shard_map/ppermute | solution.py:488
  7.5 5.6 %collective-permute-start.1 = (bf16[272,256]{1,0:T(8,128)(2,1)}, bf16[272,256]{1,0:T(8,128)(2,1)S(1)}, u32[]{:S(2)}, u32[]{:S(2)}) collective-permute-start(bf16[272,256]{1,0:T(8,128)(2,1)} %get-tuple-element.27), channel_id=1, source_target_pairs={{0,28},{1,29},{2,6},{3,7},{4,0},{5,1},{6,10},{7,11},{8,4},{9,5},{1... | collective-permute-start | bytes 417800 | tf_op jit(solution)/shard_map/ppermute | solution.py:488
  13.1 0.0 copy-start
  13.1 1.0 %copy-done = bf16[2,272,256]{2,1,0:T(8,128)(2,1)S(1)} copy-done((bf16[2,272,256]{2,1,0:T(8,128)(2,1)S(1)}, bf16[2,272,256]{2,1,0:T(8,128)(2,1)}, u32[]{:S(2)}) %copy-start) | copy-done | bytes 278552
  14.1 0.3 keep.1
  14.3 0.0 collective-permute-done.cross_ref
  14.3 0.3 %merge.1 = (bf16[208,256]{1,0:T(8,128)(2,1)S(1)}, bf16[208,256]{1,0:T(8,128)(2,1)S(1)}, f32[384,256]{1,0:T(8,128)S(1)}, f32[8,256]{1,0:T(8,128)S(1)}) custom-call(f32[2,384,256]{2,1,0:T(8,128)S(1)} %get-tuple-element.22.totals_ref, f32[2,8,256]{2,1,0:T(8,128)S(1)} %get-tuple-element.23.weights_ref, bf16[2,272,256]{2,1,0:T(8,128)(2,1)S(1)} %collective-permute-done.cross_ref), custom_call_target="tpu_custom_call" | custom-call | tf_op jit(solution)/shard_map/merge/pallas_call | solution.py:494
  14.7 0.3 %collective-permute-start.2 = (bf16[208,256]{1,0:T(8,128)(2,1)S(1)}, bf16[208,256]{1,0:T(8,128)(2,1)S(1)}, u32[]{:S(2)}, u32[]{:S(2)}) collective-permute-start(bf16[208,256]{1,0:T(8,128)(2,1)S(1)} %get-tuple-element.31), channel_id=1, source_target_pairs={{0,30},{1,31},{2,4},{3,5},{4,2},{5,3},{6,8},{7,9},{8,6},{9,7},{10,... | collective-permute-start | bytes 319496 | tf_op jit(solution)/shard_map/ppermute | solution.py:488
  14.9 1.1 %collective-permute-done.1.far_ref = bf16[272,256]{1,0:T(8,128)(2,1)S(1)} collective-permute-done((bf16[272,256]{1,0:T(8,128)(2,1)}, bf16[272,256]{1,0:T(8,128)(2,1)S(1)}, u32[]{:S(2)}, u32[]{:S(2)}) %collective-permute-start.1) | collective-permute-done | bytes 139296 | tf_op jit(solution)/shard_map/ppermute | solution.py:488
  16.0 0.3 %home.1 = (bf16[208,256]{1,0:T(8,128)(2,1)S(1)}, bf16[208,256]{1,0:T(8,128)(2,1)S(1)}, f32[192,256]{1,0:T(8,128)S(1)}, f32[8,256]{1,0:T(8,128)S(1)}) custom-call(f32[384,256]{1,0:T(8,128)S(1)} %get-tuple-element.25.home_ref, f32[8,256]{1,0:T(8,128)S(1)} %get-tuple-element.26.home_weight_ref, bf16[272,256]{1,0:T(8,128)(2,1)S(1)} %collective-permute-done.1.far_ref, ...), custom_call_target="tpu_custom_call" | custom-call | tf_op jit(solution)/shard_map/home/pallas_call | solution.py:494
  16.3 1.6 %collective-permute-start.3 = (bf16[208,256]{1,0:T(8,128)(2,1)S(1)}, bf16[208,256]{1,0:T(8,128)(2,1)S(1)}, u32[]{:S(2)}, u32[]{:S(2)}) collective-permute-start(bf16[208,256]{1,0:T(8,128)(2,1)S(1)} %get-tuple-element.34), channel_id=1, source_target_pairs={{0,1},{1,0},{2,3},{3,2},{4,5},{5,4},{6,7},{7,6},{8,9},{9,8},{10,11... | collective-permute-start | bytes 319496 | tf_op jit(solution)/shard_map/ppermute | solution.py:488
  17.9 2.8 %collective-permute-start.4 = (bf16[208,256]{1,0:T(8,128)(2,1)S(1)}, bf16[208,256]{1,0:T(8,128)(2,1)S(1)}, u32[]{:S(2)}, u32[]{:S(2)}) collective-permute-start(bf16[208,256]{1,0:T(8,128)(2,1)S(1)} %get-tuple-element.37), channel_id=1, source_target_pairs={{0,31},{1,30},{2,5},{3,4},{4,3},{5,2},{6,9},{7,8},{8,7},{9,6},{10,... | collective-permute-start | bytes 319496 | tf_op jit(solution)/shard_map/ppermute | solution.py:488
  20.7 0.9 %collective-permute-done.2.refs_0_ = bf16[208,256]{1,0:T(8,128)(2,1)S(1)} collective-permute-done((bf16[208,256]{1,0:T(8,128)(2,1)S(1)}, bf16[208,256]{1,0:T(8,128)(2,1)S(1)}, u32[]{:S(2)}, u32[]{:S(2)}) %collective-permute-start.2) | collective-permute-done | bytes 106528 | tf_op jit(solution)/shard_map/ppermute | solution.py:488
  21.7 0.0 collective-permute-done.3.refs_0_
  21.7 3.9 %collective-permute-done.4.refs_0_ = bf16[208,256]{1,0:T(8,128)(2,1)S(1)} collective-permute-done((bf16[208,256]{1,0:T(8,128)(2,1)S(1)}, bf16[208,256]{1,0:T(8,128)(2,1)S(1)}, u32[]{:S(2)}, u32[]{:S(2)}) %collective-permute-start.4) | collective-permute-done | bytes 106528 | tf_op jit(solution)/shard_map/ppermute | solution.py:488
  25.6 0.7 %combine.1 = (f32[6,32,256]{2,1,0:T(8,128)}, f32[32,256]{1,0:T(8,128)}) custom-call(f32[8,256]{1,0:T(8,128)S(1)} %get-tuple-element.21.detect_ref, f32[192,256]{1,0:T(8,128)S(1)} %get-tuple-element.29.own_ref, f32[8,256]{1,0:T(8,128)S(1)} %get-tuple-element.30.own_weight_ref, f32[192,256]{1,0:T(8,128)S(1)} %get-tuple-element.35.near_ref, ...), custom_call_target="tpu_custom_call" | custom-call | tf_op jit(solution)/shard_map/combine/pallas_call | solution.py:494
  (2 shorter events, 0.0 us)
Async XLA Ops:
  7.0 7.3 %collective-permute-start = (bf16[2,272,256]{2,1,0:T(8,128)(2,1)}, bf16[2,272,256]{2,1,0:T(8,128)(2,1)S(1)}, u32[]{:S(2)}, u32[]{:S(2)}) collective-permute-start(bf16[2,272,256]{2,1,0:T(8,128)(2,1)} %get-tuple-element.24), channel_id=1, source_target_pairs={{0,2},{1,3},{2,0},{3,1},{4,6},{5,7},{6,4},{7,5},{8,10},{9,11},{10,... | collective-permute-start | bytes 835592 | tf_op jit(solution)/shard_map/ppermute | solution.py:488
  7.5 8.5 %collective-permute-start.1 = (bf16[272,256]{1,0:T(8,128)(2,1)}, bf16[272,256]{1,0:T(8,128)(2,1)S(1)}, u32[]{:S(2)}, u32[]{:S(2)}) collective-permute-start(bf16[272,256]{1,0:T(8,128)(2,1)} %get-tuple-element.27), channel_id=1, source_target_pairs={{0,28},{1,29},{2,6},{3,7},{4,0},{5,1},{6,10},{7,11},{8,4},{9,5},{1... | collective-permute-start | bytes 417800 | tf_op jit(solution)/shard_map/ppermute | solution.py:488
  13.1 1.0 %copy-start = (bf16[2,272,256]{2,1,0:T(8,128)(2,1)S(1)}, bf16[2,272,256]{2,1,0:T(8,128)(2,1)}, u32[]{:S(2)}) copy-start(bf16[2,272,256]{2,1,0:T(8,128)(2,1)} %get-tuple-element.20.kept_ref) | copy-start | bytes 835588
  14.7 7.0 %collective-permute-start.2 = (bf16[208,256]{1,0:T(8,128)(2,1)S(1)}, bf16[208,256]{1,0:T(8,128)(2,1)S(1)}, u32[]{:S(2)}, u32[]{:S(2)}) collective-permute-start(bf16[208,256]{1,0:T(8,128)(2,1)S(1)} %get-tuple-element.31), channel_id=1, source_target_pairs={{0,30},{1,31},{2,4},{3,5},{4,2},{5,3},{6,8},{7,9},{8,6},{9,7},{10,... | collective-permute-start | bytes 319496 | tf_op jit(solution)/shard_map/ppermute | solution.py:488
  16.3 5.4 %collective-permute-start.3 = (bf16[208,256]{1,0:T(8,128)(2,1)S(1)}, bf16[208,256]{1,0:T(8,128)(2,1)S(1)}, u32[]{:S(2)}, u32[]{:S(2)}) collective-permute-start(bf16[208,256]{1,0:T(8,128)(2,1)S(1)} %get-tuple-element.34), channel_id=1, source_target_pairs={{0,1},{1,0},{2,3},{3,2},{4,5},{5,4},{6,7},{7,6},{8,9},{9,8},{10,11... | collective-permute-start | bytes 319496 | tf_op jit(solution)/shard_map/ppermute | solution.py:488
  17.9 7.7 %collective-permute-start.4 = (bf16[208,256]{1,0:T(8,128)(2,1)S(1)}, bf16[208,256]{1,0:T(8,128)(2,1)S(1)}, u32[]{:S(2)}, u32[]{:S(2)}) collective-permute-start(bf16[208,256]{1,0:T(8,128)(2,1)S(1)} %get-tuple-element.37), channel_id=1, source_target_pairs={{0,31},{1,30},{2,5},{3,4},{4,3},{5,2},{6,9},{7,8},{8,7},{9,6},{10,... | collective-permute-start | bytes 319496 | tf_op jit(solution)/shard_map/ppermute | solution.py:488

commit v23 on v21

--- a/solution.py
+++ b/solution.py
@@ -176,7 +176,7 @@
         here = lane[: value.shape[0]] + distance
         return jnp.where((here >= 0) & (here < width), turned, jnp.zeros_like(turned))
 
-    def one_visit(visit, unused):
+    def one_visit(visit):
         fetch(visit).wait()
         sums[...] = jnp.zeros_like(sums)
         first = visit * per_visit
@@ -250,9 +250,9 @@
         cross[1, held, :] = sums[REACH - way].astype(jnp.bfloat16)
         kept[0, held, :] = sums[REACH + way].astype(jnp.bfloat16)
         kept[1, held, :] = sums[REACH].astype(jnp.bfloat16)
-        return unused
-
-    lax.fori_loop(0, visits, one_visit, 0)
+
+    for visit in range(visits):
+        one_visit(visit)
 
     row = iota((EXTRA, PW), 0)
     lane = iota((1, PW), 1)

time: 26.1 us -> 26 us (level)
  no operation moved by 1% of the time
where the time goes in v23:
time: 26 us; the launch traced here: 25.8 us
  starting transfers between devices  12.1 us (47%)
  Pallas kernels  7.88 us (30%)
  waiting for transfers between devices  4.17 us (16%)
  local copies, waits for them, and re-layouts  0.96 us (4%)
  between operations  0.67 us (3%)
    ppermute x5, starting transfers between devices, send(): return lax.ppermute(message, ('ra', 'band'), route)  12.1 us
    pallas_call x1, Pallas kernels, local(): pl.pallas_call(functools.partial(match_kernel, patches), in_specs=[anywhe...  6.26 us
    ppermute x5, waiting for transfers between devices, send(): return lax.ppermute(message, ('ra', 'band'), route)  4.17 us
    pallas_call x5, Pallas kernels, local_call(): pl.pallas_call(kernel, in_specs=[vmem] * len(operands), out_specs=[vmem]...  1.62 us
    unnamed x2, local copies, waits for them, and re-layouts  0.96 us
  transfers between devices with their start and end apart: 5, of which 3 were waited for; matrix products, arithmetic and copies ran while one was open for 0% of the time, Pallas kernels for 3%

profile of v23, /device:TPU:0, one launch (start us, length us, event | category | flops | bytes accessed | tf_op | source)
XLA Modules:
  0.0 25.8 jit_solution(11821333835231682372)
XLA Ops:
  0.6 6.3 %match_and_sum.1 = (bf16[272,256]{1,0:T(8,128)(2,1)}, bf16[2,272,256]{2,1,0:T(8,128)(2,1)}, bf16[2,272,256]{2,1,0:T(8,128)(2,1)}) custom-call(s32[32]{0:T(128)} %patch_hbm.1, s32[32]{0:T(128)} %offset_hbm.1, s32[32]{0:T(128)} %index_hbm.1, s32[4]{0:T(128)} %band_hbm.1, f32[6]{0:T(128)} %detect_hbm.1, f32[21,64]{1,0:T(8,128)} %bitcast.2, ...), custom_call_target="tpu_custom_call" | custom-call | tf_op jit(solution)/shard_map/match_and_sum/pallas_call | solution.py:433
  6.9 0.5 %collective-permute-start = (bf16[2,272,256]{2,1,0:T(8,128)(2,1)}, bf16[2,272,256]{2,1,0:T(8,128)(2,1)S(1)}, u32[]{:S(2)}, u32[]{:S(2)}) collective-permute-start(bf16[2,272,256]{2,1,0:T(8,128)(2,1)} %get-tuple-element.21), channel_id=1, source_target_pairs={{0,2},{1,3},{2,0},{3,1},{4,6},{5,7},{6,4},{7,5},{8,10},{9,11},{10,... | collective-permute-start | bytes 835592 | tf_op jit(solution)/shard_map/ppermute | solution.py:480
  7.4 5.6 %collective-permute-start.1 = (bf16[272,256]{1,0:T(8,128)(2,1)}, bf16[272,256]{1,0:T(8,128)(2,1)S(1)}, u32[]{:S(2)}, u32[]{:S(2)}) collective-permute-start(bf16[272,256]{1,0:T(8,128)(2,1)} %get-tuple-element.24), channel_id=1, source_target_pairs={{0,28},{1,29},{2,6},{3,7},{4,0},{5,1},{6,10},{7,11},{8,4},{9,5},{1... | collective-permute-start | bytes 417800 | tf_op jit(solution)/shard_map/ppermute | solution.py:480
  13.0 0.0 copy-start
  13.0 1.0 %copy-done = bf16[2,272,256]{2,1,0:T(8,128)(2,1)S(1)} copy-done((bf16[2,272,256]{2,1,0:T(8,128)(2,1)S(1)}, bf16[2,272,256]{2,1,0:T(8,128)(2,1)}, u32[]{:S(2)}) %copy-start) | copy-done | bytes 278552
  14.0 0.3 %keep.1 = (f32[2,384,256]{2,1,0:T(8,128)S(1)}, f32[2,8,256]{2,1,0:T(8,128)S(1)}, f32[8,256]{1,0:T(8,128)S(1)}) custom-call(bf16[2,272,256]{2,1,0:T(8,128)(2,1)S(1)} %copy-done), custom_call_target="tpu_custom_call" | custom-call | tf_op jit(solution)/shard_map/keep/pallas_call | solution.py:486
  14.2 0.0 collective-permute-done.cross_ref
  14.2 0.3 %merge.1 = (bf16[208,256]{1,0:T(8,128)(2,1)S(1)}, bf16[208,256]{1,0:T(8,128)(2,1)S(1)}, f32[384,256]{1,0:T(8,128)S(1)}, f32[8,256]{1,0:T(8,128)S(1)}) custom-call(f32[2,384,256]{2,1,0:T(8,128)S(1)} %get-tuple-element.19.totals_ref, f32[2,8,256]{2,1,0:T(8,128)S(1)} %get-tuple-element.20.weights_ref, bf16[2,272,256]{2,1,0:T(8,128)(2,1)S(1)} %collective-permute-done.cross_ref), custom_call_target="tpu_custom_call" | custom-call | tf_op jit(solution)/shard_map/merge/pallas_call | solution.py:486
  14.6 0.3 %collective-permute-start.2 = (bf16[208,256]{1,0:T(8,128)(2,1)S(1)}, bf16[208,256]{1,0:T(8,128)(2,1)S(1)}, u32[]{:S(2)}, u32[]{:S(2)}) collective-permute-start(bf16[208,256]{1,0:T(8,128)(2,1)S(1)} %get-tuple-element.27), channel_id=1, source_target_pairs={{0,30},{1,31},{2,4},{3,5},{4,2},{5,3},{6,8},{7,9},{8,6},{9,7},{10,... | collective-permute-start | bytes 319496 | tf_op jit(solution)/shard_map/ppermute | solution.py:480
  14.9 5.2 %collective-permute-start.3 = (bf16[208,256]{1,0:T(8,128)(2,1)S(1)}, bf16[208,256]{1,0:T(8,128)(2,1)S(1)}, u32[]{:S(2)}, u32[]{:S(2)}) collective-permute-start(bf16[208,256]{1,0:T(8,128)(2,1)S(1)} %get-tuple-element.28), channel_id=1, source_target_pairs={{0,31},{1,30},{2,5},{3,4},{4,3},{5,2},{6,9},{7,8},{8,7},{9,6},{10,... | collective-permute-start | bytes 319496 | tf_op jit(solution)/shard_map/ppermute | solution.py:480
  20.0 0.0 collective-permute-done.1.far_ref
  20.0 0.3 %home.1 = (bf16[208,256]{1,0:T(8,128)(2,1)S(1)}, f32[192,256]{1,0:T(8,128)S(1)}, f32[8,256]{1,0:T(8,128)S(1)}) custom-call(f32[384,256]{1,0:T(8,128)S(1)} %get-tuple-element.22.home_ref, f32[8,256]{1,0:T(8,128)S(1)} %get-tuple-element.23.home_weight_ref, bf16[272,256]{1,0:T(8,128)(2,1)S(1)} %collective-permute-done.1.far_ref), custom_call_target="tpu_custom_call" | custom-call | tf_op jit(solution)/shard_map/home/pallas_call | solution.py:486
  20.3 0.6 %collective-permute-start.4 = (bf16[208,256]{1,0:T(8,128)(2,1)S(1)}, bf16[208,256]{1,0:T(8,128)(2,1)S(1)}, u32[]{:S(2)}, u32[]{:S(2)}) collective-permute-start(bf16[208,256]{1,0:T(8,128)(2,1)S(1)} %get-tuple-element.31), channel_id=1, source_target_pairs={{0,1},{1,0},{2,3},{3,2},{4,5},{5,4},{6,7},{7,6},{8,9},{9,8},{10,11... | collective-permute-start | bytes 319496 | tf_op jit(solution)/shard_map/ppermute | solution.py:480
  20.9 0.6 %collective-permute-done.2.refs_0_ = bf16[208,256]{1,0:T(8,128)(2,1)S(1)} collective-permute-done((bf16[208,256]{1,0:T(8,128)(2,1)S(1)}, bf16[208,256]{1,0:T(8,128)(2,1)S(1)}, u32[]{:S(2)}, u32[]{:S(2)}) %collective-permute-start.2) | collective-permute-done | bytes 106528 | tf_op jit(solution)/shard_map/ppermute | solution.py:480
  21.5 2.1 %collective-permute-done.3.refs_1_ = bf16[208,256]{1,0:T(8,128)(2,1)S(1)} collective-permute-done((bf16[208,256]{1,0:T(8,128)(2,1)S(1)}, bf16[208,256]{1,0:T(8,128)(2,1)S(1)}, u32[]{:S(2)}, u32[]{:S(2)}) %collective-permute-start.3) | collective-permute-done | bytes 106528 | tf_op jit(solution)/shard_map/ppermute | solution.py:480
  23.6 1.5 %collective-permute-done.4.refs_0_ = bf16[208,256]{1,0:T(8,128)(2,1)S(1)} collective-permute-done((bf16[208,256]{1,0:T(8,128)(2,1)S(1)}, bf16[208,256]{1,0:T(8,128)(2,1)S(1)}, u32[]{:S(2)}, u32[]{:S(2)}) %collective-permute-start.4) | collective-permute-done | bytes 106528 | tf_op jit(solution)/shard_map/ppermute | solution.py:480
  25.1 0.7 %combine.1 = (f32[6,32,256]{2,1,0:T(8,128)}, f32[32,256]{1,0:T(8,128)}) custom-call(f32[8,256]{1,0:T(8,128)S(1)} %get-tuple-element.18.detect_ref, f32[192,256]{1,0:T(8,128)S(1)} %get-tuple-element.25.own_ref, f32[8,256]{1,0:T(8,128)S(1)} %get-tuple-element.26.own_weight_ref, f32[192,256]{1,0:T(8,128)S(1)} %get-tuple-element.29.near_ref, ...), custom_call_target="tpu_custom_call" | custom-call | tf_op jit(solution)/shard_map/combine/pallas_call | solution.py:486
  (1 shorter events, 0.0 us)
Async XLA Ops:
  6.9 7.3 %collective-permute-start = (bf16[2,272,256]{2,1,0:T(8,128)(2,1)}, bf16[2,272,256]{2,1,0:T(8,128)(2,1)S(1)}, u32[]{:S(2)}, u32[]{:S(2)}) collective-permute-start(bf16[2,272,256]{2,1,0:T(8,128)(2,1)} %get-tuple-element.21), channel_id=1, source_target_pairs={{0,2},{1,3},{2,0},{3,1},{4,6},{5,7},{6,4},{7,5},{8,10},{9,11},{10,... | collective-permute-start | bytes 835592 | tf_op jit(solution)/shard_map/ppermute | solution.py:480
  7.4 12.6 %collective-permute-start.1 = (bf16[272,256]{1,0:T(8,128)(2,1)}, bf16[272,256]{1,0:T(8,128)(2,1)S(1)}, u32[]{:S(2)}, u32[]{:S(2)}) collective-permute-start(bf16[272,256]{1,0:T(8,128)(2,1)} %get-tuple-element.24), channel_id=1, source_target_pairs={{0,28},{1,29},{2,6},{3,7},{4,0},{5,1},{6,10},{7,11},{8,4},{9,5},{1... | collective-permute-start | bytes 417800 | tf_op jit(solution)/shard_map/ppermute | solution.py:480
  13.0 1.0 %copy-start = (bf16[2,272,256]{2,1,0:T(8,128)(2,1)S(1)}, bf16[2,272,256]{2,1,0:T(8,128)(2,1)}, u32[]{:S(2)}) copy-start(bf16[2,272,256]{2,1,0:T(8,128)(2,1)} %get-tuple-element.17.kept_ref) | copy-start | bytes 835588
  14.6 6.9 %collective-permute-start.2 = (bf16[208,256]{1,0:T(8,128)(2,1)S(1)}, bf16[208,256]{1,0:T(8,128)(2,1)S(1)}, u32[]{:S(2)}, u32[]{:S(2)}) collective-permute-start(bf16[208,256]{1,0:T(8,128)(2,1)S(1)} %get-tuple-element.27), channel_id=1, source_target_pairs={{0,30},{1,31},{2,4},{3,5},{4,2},{5,3},{6,8},{7,9},{8,6},{9,7},{10,... | collective-permute-start | bytes 319496 | tf_op jit(solution)/shard_map/ppermute | solution.py:480
  14.9 8.7 %collective-permute-start.3 = (bf16[208,256]{1,0:T(8,128)(2,1)S(1)}, bf16[208,256]{1,0:T(8,128)(2,1)S(1)}, u32[]{:S(2)}, u32[]{:S(2)}) collective-permute-start(bf16[208,256]{1,0:T(8,128)(2,1)S(1)} %get-tuple-element.28), channel_id=1, source_target_pairs={{0,31},{1,30},{2,5},{3,4},{4,3},{5,2},{6,9},{7,8},{8,7},{9,6},{10,... | collective-permute-start | bytes 319496 | tf_op jit(solution)/shard_map/ppermute | solution.py:480
  20.3 4.8 %collective-permute-start.4 = (bf16[208,256]{1,0:T(8,128)(2,1)S(1)}, bf16[208,256]{1,0:T(8,128)(2,1)S(1)}, u32[]{:S(2)}, u32[]{:S(2)}) collective-permute-start(bf16[208,256]{1,0:T(8,128)(2,1)S(1)} %get-tuple-element.31), channel_id=1, source_target_pairs={{0,1},{1,0},{2,3},{3,2},{4,5},{5,4},{6,7},{7,6},{8,9},{9,8},{10,11... | collective-permute-start | bytes 319496 | tf_op jit(solution)/shard_map/ppermute | solution.py:480

commit v24 on v21

--- a/solution.py
+++ b/solution.py
@@ -32,6 +32,9 @@
     rowk_hbm,
     colk_hbm,
     tiles_hbm,
+    far_hbm,
+    cross_hbm,
+    kept_hbm,
     far,
     cross,
     kept,
@@ -54,6 +57,7 @@
     extra,
     arrival,
     ready,
+    leaving,
 ):
     visits = band_ref.shape[0]
     tile_count, rows, width = tiles_ref.shape
@@ -175,6 +179,13 @@
         turned = pltpu.roll(value, -distance % width, 1)
         here = lane[: value.shape[0]] + distance
         return jnp.where((here >= 0) & (here < width), turned, jnp.zeros_like(turned))
+
+    def deliver(part, held):
+        return [
+            pltpu.make_async_copy(far.at[held], far_hbm.at[held], leaving.at[part, 0]),
+            pltpu.make_async_copy(cross.at[:, held], cross_hbm.at[:, held], leaving.at[part, 1]),
+            pltpu.make_async_copy(kept.at[:, held], kept_hbm.at[:, held], leaving.at[part, 2]),
+        ]
 
     def one_visit(visit, unused):
         fetch(visit).wait()
@@ -250,6 +261,8 @@
         cross[1, held, :] = sums[REACH - way].astype(jnp.bfloat16)
         kept[0, held, :] = sums[REACH + way].astype(jnp.bfloat16)
         kept[1, held, :] = sums[REACH].astype(jnp.bfloat16)
+        for copy in deliver(visit, held):
+            copy.start()
         return unused
 
     lax.fori_loop(0, visits, one_visit, 0)
@@ -290,6 +303,13 @@
     cross[1, rows * visits :, :] = footer(REACH - way)
     kept[0, rows * visits :, :] = footer(REACH + way)
     kept[1, rows * visits :, :] = footer(REACH)
+    for copy in deliver(visits, pl.ds(rows * visits, EXTRA)):
+        copy.start()
+    for visit in range(visits):
+        for copy in deliver(visit, pl.ds(rows * visit, rows)):
+            copy.wait()
+    for copy in deliver(visits, pl.ds(rows * visits, EXTRA)):
+        copy.wait()
 
 
 def add_message(count, groups, message):
@@ -433,9 +453,12 @@
     far, cross, kept = pl.pallas_call(
         functools.partial(match_kernel, patches),
         in_specs=[anywhere] * 10,
-        out_specs=[vmem] * 3,
+        out_specs=[anywhere] * 3,
         out_shape=[message_shape, pair_shape, pair_shape],
         scratch_shapes=[
+            pltpu.VMEM(message_shape.shape, jnp.bfloat16),
+            pltpu.VMEM(pair_shape.shape, jnp.bfloat16),
+            pltpu.VMEM(pair_shape.shape, jnp.bfloat16),
             pltpu.SMEM((tile_count,), jnp.int32),
             pltpu.SMEM((tile_count,), jnp.int32),
             pltpu.SMEM((tile_count,), jnp.int32),
@@ -455,6 +478,7 @@
             pltpu.VMEM((SPREAD, EXTRA, PW), jnp.float32),
             pltpu.SemaphoreType.DMA((visits,)),
             pltpu.SemaphoreType.DMA((9,)),
+            pltpu.SemaphoreType.DMA((visits + 1, 3)),
         ],
         compiler_params=pltpu.CompilerParams(vmem_limit_bytes=62 * 1024 * 1024),
         name="match_and_sum",

time: 26.1 us -> 26.1 us (level)
  no operation moved by 1% of the time
where the time goes in v24:
time: 26.1 us; the launch traced here: 25.9 us
  starting transfers between devices  12.1 us (46%)
  Pallas kernels  7.95 us (30%)
  waiting for transfers between devices  4.17 us (16%)
  local copies, waits for them, and re-layouts  0.96 us (4%)
  between operations  0.67 us (3%)
    ppermute x5, starting transfers between devices, send(): return lax.ppermute(message, ('ra', 'band'), route)  12.1 us
    pallas_call x1, Pallas kernels, local(): pl.pallas_call(functools.partial(match_kernel, patches), in_specs=[anywhe...  6.33 us
    ppermute x5, waiting for transfers between devices, send(): return lax.ppermute(message, ('ra', 'band'), route)  4.17 us
    pallas_call x5, Pallas kernels, local_call(): pl.pallas_call(kernel, in_specs=[vmem] * len(operands), out_specs=[vmem]...  1.62 us
    unnamed x2, local copies, waits for them, and re-layouts  0.96 us
  transfers between devices with their start and end apart: 5, of which 3 were waited for; matrix products, arithmetic and copies ran while one was open for 0% of the time, Pallas kernels for 3%

profile of v24, /device:TPU:0, one launch (start us, length us, event | category | flops | bytes accessed | tf_op | source)
XLA Modules:
  0.0 25.9 jit_solution(5518435766646559704)
XLA Ops:
  0.6 6.3 %match_and_sum.1 = (bf16[272,256]{1,0:T(8,128)(2,1)}, bf16[2,272,256]{2,1,0:T(8,128)(2,1)}, bf16[2,272,256]{2,1,0:T(8,128)(2,1)}) custom-call(s32[32]{0:T(128)} %patch_hbm.1, s32[32]{0:T(128)} %offset_hbm.1, s32[32]{0:T(128)} %index_hbm.1, s32[4]{0:T(128)} %band_hbm.1, f32[6]{0:T(128)} %detect_hbm.1, f32[21,64]{1,0:T(8,128)} %bitcast.2, ...), custom_call_target="tpu_custom_call" | custom-call | tf_op jit(solution)/shard_map/match_and_sum/pallas_call | solution.py:453
  7.0 0.5 %collective-permute-start = (bf16[2,272,256]{2,1,0:T(8,128)(2,1)}, bf16[2,272,256]{2,1,0:T(8,128)(2,1)S(1)}, u32[]{:S(2)}, u32[]{:S(2)}) collective-permute-start(bf16[2,272,256]{2,1,0:T(8,128)(2,1)} %get-tuple-element.21), channel_id=1, source_target_pairs={{0,2},{1,3},{2,0},{3,1},{4,6},{5,7},{6,4},{7,5},{8,10},{9,11},{10,... | collective-permute-start | bytes 835592 | tf_op jit(solution)/shard_map/ppermute | solution.py:504
  7.5 5.6 %collective-permute-start.1 = (bf16[272,256]{1,0:T(8,128)(2,1)}, bf16[272,256]{1,0:T(8,128)(2,1)S(1)}, u32[]{:S(2)}, u32[]{:S(2)}) collective-permute-start(bf16[272,256]{1,0:T(8,128)(2,1)} %get-tuple-element.24), channel_id=1, source_target_pairs={{0,28},{1,29},{2,6},{3,7},{4,0},{5,1},{6,10},{7,11},{8,4},{9,5},{1... | collective-permute-start | bytes 417800 | tf_op jit(solution)/shard_map/ppermute | solution.py:504
  13.1 0.0 copy-start
  13.1 1.0 %copy-done = bf16[2,272,256]{2,1,0:T(8,128)(2,1)S(1)} copy-done((bf16[2,272,256]{2,1,0:T(8,128)(2,1)S(1)}, bf16[2,272,256]{2,1,0:T(8,128)(2,1)}, u32[]{:S(2)}) %copy-start) | copy-done | bytes 278552
  14.0 0.3 %keep.1 = (f32[2,384,256]{2,1,0:T(8,128)S(1)}, f32[2,8,256]{2,1,0:T(8,128)S(1)}, f32[8,256]{1,0:T(8,128)S(1)}) custom-call(bf16[2,272,256]{2,1,0:T(8,128)(2,1)S(1)} %copy-done), custom_call_target="tpu_custom_call" | custom-call | tf_op jit(solution)/shard_map/keep/pallas_call | solution.py:510
  14.3 0.0 collective-permute-done.cross_ref
  14.3 0.3 %merge.1 = (bf16[208,256]{1,0:T(8,128)(2,1)S(1)}, bf16[208,256]{1,0:T(8,128)(2,1)S(1)}, f32[384,256]{1,0:T(8,128)S(1)}, f32[8,256]{1,0:T(8,128)S(1)}) custom-call(f32[2,384,256]{2,1,0:T(8,128)S(1)} %get-tuple-element.19.totals_ref, f32[2,8,256]{2,1,0:T(8,128)S(1)} %get-tuple-element.20.weights_ref, bf16[2,272,256]{2,1,0:T(8,128)(2,1)S(1)} %collective-permute-done.cross_ref), custom_call_target="tpu_custom_call" | custom-call | tf_op jit(solution)/shard_map/merge/pallas_call | solution.py:510
  14.6 0.3 %collective-permute-start.2 = (bf16[208,256]{1,0:T(8,128)(2,1)S(1)}, bf16[208,256]{1,0:T(8,128)(2,1)S(1)}, u32[]{:S(2)}, u32[]{:S(2)}) collective-permute-start(bf16[208,256]{1,0:T(8,128)(2,1)S(1)} %get-tuple-element.27), channel_id=1, source_target_pairs={{0,30},{1,31},{2,4},{3,5},{4,2},{5,3},{6,8},{7,9},{8,6},{9,7},{10,... | collective-permute-start | bytes 319496 | tf_op jit(solution)/shard_map/ppermute | solution.py:504
  14.9 5.2 %collective-permute-start.3 = (bf16[208,256]{1,0:T(8,128)(2,1)S(1)}, bf16[208,256]{1,0:T(8,128)(2,1)S(1)}, u32[]{:S(2)}, u32[]{:S(2)}) collective-permute-start(bf16[208,256]{1,0:T(8,128)(2,1)S(1)} %get-tuple-element.28), channel_id=1, source_target_pairs={{0,31},{1,30},{2,5},{3,4},{4,3},{5,2},{6,9},{7,8},{8,7},{9,6},{10,... | collective-permute-start | bytes 319496 | tf_op jit(solution)/shard_map/ppermute | solution.py:504
  20.1 0.0 collective-permute-done.1.far_ref
  20.1 0.3 %home.1 = (bf16[208,256]{1,0:T(8,128)(2,1)S(1)}, f32[192,256]{1,0:T(8,128)S(1)}, f32[8,256]{1,0:T(8,128)S(1)}) custom-call(f32[384,256]{1,0:T(8,128)S(1)} %get-tuple-element.22.home_ref, f32[8,256]{1,0:T(8,128)S(1)} %get-tuple-element.23.home_weight_ref, bf16[272,256]{1,0:T(8,128)(2,1)S(1)} %collective-permute-done.1.far_ref), custom_call_target="tpu_custom_call" | custom-call | tf_op jit(solution)/shard_map/home/pallas_call | solution.py:510
  20.4 0.6 %collective-permute-start.4 = (bf16[208,256]{1,0:T(8,128)(2,1)S(1)}, bf16[208,256]{1,0:T(8,128)(2,1)S(1)}, u32[]{:S(2)}, u32[]{:S(2)}) collective-permute-start(bf16[208,256]{1,0:T(8,128)(2,1)S(1)} %get-tuple-element.31), channel_id=1, source_target_pairs={{0,1},{1,0},{2,3},{3,2},{4,5},{5,4},{6,7},{7,6},{8,9},{9,8},{10,11... | collective-permute-start | bytes 319496 | tf_op jit(solution)/shard_map/ppermute | solution.py:504
  21.0 0.6 %collective-permute-done.2.refs_0_ = bf16[208,256]{1,0:T(8,128)(2,1)S(1)} collective-permute-done((bf16[208,256]{1,0:T(8,128)(2,1)S(1)}, bf16[208,256]{1,0:T(8,128)(2,1)S(1)}, u32[]{:S(2)}, u32[]{:S(2)}) %collective-permute-start.2) | collective-permute-done | bytes 106528 | tf_op jit(solution)/shard_map/ppermute | solution.py:504
  21.5 2.1 %collective-permute-done.3.refs_1_ = bf16[208,256]{1,0:T(8,128)(2,1)S(1)} collective-permute-done((bf16[208,256]{1,0:T(8,128)(2,1)S(1)}, bf16[208,256]{1,0:T(8,128)(2,1)S(1)}, u32[]{:S(2)}, u32[]{:S(2)}) %collective-permute-start.3) | collective-permute-done | bytes 106528 | tf_op jit(solution)/shard_map/ppermute | solution.py:504
  23.7 1.5 %collective-permute-done.4.refs_0_ = bf16[208,256]{1,0:T(8,128)(2,1)S(1)} collective-permute-done((bf16[208,256]{1,0:T(8,128)(2,1)S(1)}, bf16[208,256]{1,0:T(8,128)(2,1)S(1)}, u32[]{:S(2)}, u32[]{:S(2)}) %collective-permute-start.4) | collective-permute-done | bytes 106528 | tf_op jit(solution)/shard_map/ppermute | solution.py:504
  25.2 0.7 %combine.1 = (f32[6,32,256]{2,1,0:T(8,128)}, f32[32,256]{1,0:T(8,128)}) custom-call(f32[8,256]{1,0:T(8,128)S(1)} %get-tuple-element.18.detect_ref, f32[192,256]{1,0:T(8,128)S(1)} %get-tuple-element.25.own_ref, f32[8,256]{1,0:T(8,128)S(1)} %get-tuple-element.26.own_weight_ref, f32[192,256]{1,0:T(8,128)S(1)} %get-tuple-element.29.near_ref, ...), custom_call_target="tpu_custom_call" | custom-call | tf_op jit(solution)/shard_map/combine/pallas_call | solution.py:510
  (1 shorter events, 0.0 us)
Async XLA Ops:
  7.0 7.3 %collective-permute-start = (bf16[2,272,256]{2,1,0:T(8,128)(2,1)}, bf16[2,272,256]{2,1,0:T(8,128)(2,1)S(1)}, u32[]{:S(2)}, u32[]{:S(2)}) collective-permute-start(bf16[2,272,256]{2,1,0:T(8,128)(2,1)} %get-tuple-element.21), channel_id=1, source_target_pairs={{0,2},{1,3},{2,0},{3,1},{4,6},{5,7},{6,4},{7,5},{8,10},{9,11},{10,... | collective-permute-start | bytes 835592 | tf_op jit(solution)/shard_map/ppermute | solution.py:504
  7.5 12.6 %collective-permute-start.1 = (bf16[272,256]{1,0:T(8,128)(2,1)}, bf16[272,256]{1,0:T(8,128)(2,1)S(1)}, u32[]{:S(2)}, u32[]{:S(2)}) collective-permute-start(bf16[272,256]{1,0:T(8,128)(2,1)} %get-tuple-element.24), channel_id=1, source_target_pairs={{0,28},{1,29},{2,6},{3,7},{4,0},{5,1},{6,10},{7,11},{8,4},{9,5},{1... | collective-permute-start | bytes 417800 | tf_op jit(solution)/shard_map/ppermute | solution.py:504
  13.1 1.0 %copy-start = (bf16[2,272,256]{2,1,0:T(8,128)(2,1)S(1)}, bf16[2,272,256]{2,1,0:T(8,128)(2,1)}, u32[]{:S(2)}) copy-start(bf16[2,272,256]{2,1,0:T(8,128)(2,1)} %get-tuple-element.17.kept_ref) | copy-start | bytes 835588
  14.6 6.9 %collective-permute-start.2 = (bf16[208,256]{1,0:T(8,128)(2,1)S(1)}, bf16[208,256]{1,0:T(8,128)(2,1)S(1)}, u32[]{:S(2)}, u32[]{:S(2)}) collective-permute-start(bf16[208,256]{1,0:T(8,128)(2,1)S(1)} %get-tuple-element.27), channel_id=1, source_target_pairs={{0,30},{1,31},{2,4},{3,5},{4,2},{5,3},{6,8},{7,9},{8,6},{9,7},{10,... | collective-permute-start | bytes 319496 | tf_op jit(solution)/shard_map/ppermute | solution.py:504
  14.9 8.7 %collective-permute-start.3 = (bf16[208,256]{1,0:T(8,128)(2,1)S(1)}, bf16[208,256]{1,0:T(8,128)(2,1)S(1)}, u32[]{:S(2)}, u32[]{:S(2)}) collective-permute-start(bf16[208,256]{1,0:T(8,128)(2,1)S(1)} %get-tuple-element.28), channel_id=1, source_target_pairs={{0,31},{1,30},{2,5},{3,4},{4,3},{5,2},{6,9},{7,8},{8,7},{9,6},{10,... | collective-permute-start | bytes 319496 | tf_op jit(solution)/shard_map/ppermute | solution.py:504
  20.4 4.8 %collective-permute-start.4 = (bf16[208,256]{1,0:T(8,128)(2,1)S(1)}, bf16[208,256]{1,0:T(8,128)(2,1)S(1)}, u32[]{:S(2)}, u32[]{:S(2)}) collective-permute-start(bf16[208,256]{1,0:T(8,128)(2,1)S(1)} %get-tuple-element.31), channel_id=1, source_target_pairs={{0,1},{1,0},{2,3},{3,2},{4,5},{5,4},{6,7},{7,6},{8,9},{9,8},{10,11... | collective-permute-start | bytes 319496 | tf_op jit(solution)/shard_map/ppermute | solution.py:504

commit v25 on v21

--- a/solution.py
+++ b/solution.py
@@ -32,7 +32,6 @@
     rowk_hbm,
     colk_hbm,
     tiles_hbm,
-    far,
     cross,
     kept,
     patch_ref,
@@ -245,7 +244,7 @@
             )
 
         held = pl.ds(pl.multiple_of(visit * rows, rows), rows)
-        far[held, :] = sums[REACH + 2 * way].astype(jnp.bfloat16)
+        kept[2, held, :] = sums[REACH + 2 * way].astype(jnp.bfloat16)
         cross[0, held, :] = sums[REACH - 2 * way].astype(jnp.bfloat16)
         cross[1, held, :] = sums[REACH - way].astype(jnp.bfloat16)
         kept[0, held, :] = sums[REACH + way].astype(jnp.bfloat16)
@@ -285,7 +284,7 @@
             mixed = jnp.where(row == place, piece, mixed)
         return mixed.astype(jnp.bfloat16)
 
-    far[rows * visits :, :] = footer(REACH + 2 * way)
+    kept[2, rows * visits :, :] = footer(REACH + 2 * way)
     cross[0, rows * visits :, :] = footer(REACH - 2 * way)
     cross[1, rows * visits :, :] = footer(REACH - way)
     kept[0, rows * visits :, :] = footer(REACH + way)
@@ -338,7 +337,8 @@
     return held[pl.ds(pl.multiple_of(part * depth, depth), depth), :]
 
 
-def keep_kernel(count, groups, kept_ref, totals_ref, weights_ref, detect_ref):
+def keep_kernel(count, groups, kept_ref, totals_ref, weights_ref, detect_ref, far_ref):
+    far_ref[...] = kept_ref[2]
     for place in range(2):
         totals_ref[place], weights_ref[place] = add_message(count, groups, kept_ref.at[place])
     extra = kept_ref[0, kept_ref.shape[1] - EXTRA :, :].astype(jnp.float32)
@@ -350,22 +350,42 @@
     detect_ref[...] = jnp.broadcast_to(chosen, (8, PW))
 
 
-def merge_kernel(count, groups, totals_ref, weights_ref, cross_ref, *refs):
+def near_kernel(count, groups, totals_ref, weights_ref, cross_ref, *refs):
     messages = refs[:groups]
-    home_ref, home_weight_ref, held = refs[groups:]
+    after_ref, held = refs[groups:]
     totals, weights = add_message(count, groups, cross_ref.at[0])
     held[...] = totals + totals_ref[0]
     weights += weights_ref[0]
     for turn, message in enumerate(messages):
         write_banded(message, part_of(held, turn, groups), weights)
+    after_ref[...] = weights
+
+
+def merge_kernel(
+    count,
+    groups,
+    after_ref,
+    totals_ref,
+    weights_ref,
+    far_in_ref,
+    cross_ref,
+    home_ref,
+    home_weight_ref,
+    far_ref,
+    rest_ref,
+):
+    far_ref[...] = far_in_ref[: far_ref.shape[0]]
+    rest_ref[...] = far_in_ref[far_ref.shape[0] :]
     totals, weights = add_message(count, groups, cross_ref.at[1])
     home_ref[...] = totals + totals_ref[1]
     home_weight_ref[...] = weights + weights_ref[1]
 
 
-def home_kernel(count, groups, home_ref, home_weight_ref, far_ref, *refs):
+def home_kernel(count, groups, after_ref, home_ref, home_weight_ref, top_ref, rest_ref, *refs):
     messages = refs[: groups - 1]
-    own_ref, own_weight_ref, held = refs[groups - 1 :]
+    own_ref, own_weight_ref, held, far_ref = refs[groups - 1 :]
+    far_ref[: top_ref.shape[0]] = top_ref[...]
+    far_ref[top_ref.shape[0] :] = rest_ref[...]
     totals, weights = add_message(count, groups, far_ref)
     held[...] = totals + home_ref[...]
     weights += home_weight_ref[...]
@@ -430,11 +450,11 @@
 
     vmem = pl.BlockSpec(memory_space=pltpu.VMEM)
     anywhere = pl.BlockSpec(memory_space=pl.ANY)
-    far, cross, kept = pl.pallas_call(
+    cross, kept = pl.pallas_call(
         functools.partial(match_kernel, patches),
         in_specs=[anywhere] * 10,
-        out_specs=[vmem] * 3,
-        out_shape=[message_shape, pair_shape, pair_shape],
+        out_specs=[vmem] * 2,
+        out_shape=[pair_shape, jax.ShapeDtypeStruct((3, length, PW), jnp.bfloat16)],
         scratch_shapes=[
             pltpu.SMEM((tile_count,), jnp.int32),
             pltpu.SMEM((tile_count,), jnp.int32),
@@ -495,37 +515,54 @@
 
     held = [pltpu.VMEM(whole_shape.shape, jnp.float32)]
     cross = send(cross, onward(-1), 0)
-    far = send(far, onward(2), 0)
-    *kept, detect = local_call(
+    *kept, detect, far = local_call(
         functools.partial(keep_kernel, visits, groups),
         "keep",
         [
             jax.ShapeDtypeStruct((2,) + whole_shape.shape, jnp.float32),
             jax.ShapeDtypeStruct((2,) + weight_shape.shape, jnp.float32),
             weight_shape,
+            message_shape,
         ],
         kept,
     )
-    *near, home, home_weight = local_call(
-        functools.partial(merge_kernel, visits, groups),
-        "merge",
-        [band_shape] * groups + [whole_shape, weight_shape],
+    *near, after = local_call(
+        functools.partial(near_kernel, visits, groups),
+        "near",
+        [band_shape] * groups + [weight_shape],
         *kept,
         cross,
         scratch_shapes=held,
     )
+    home, home_weight, *far = local_call(
+        functools.partial(merge_kernel, visits, groups),
+        "merge",
+        [
+            whole_shape,
+            weight_shape,
+            jax.ShapeDtypeStruct((length // 32 * 16 + EXTRA, PW), jnp.bfloat16),
+            jax.ShapeDtypeStruct((length - length // 32 * 16 - EXTRA, PW), jnp.bfloat16),
+        ],
+        after,
+        *kept,
+        far,
+        cross,
+    )
+    far = [send(piece, onward(2), 0) for piece in far]
     near = [send(near[turn], onward(1), turn) for turn in range(groups)]
+    last = near[1:]
+    near = local_call(early_kernel, "combine_early", [part_shape, weight_shape], near[0])
     *others, own, own_weight = local_call(
         functools.partial(home_kernel, visits, groups),
         "home",
         [band_shape] * (groups - 1) + [part_shape, weight_shape],
+        near[1],
         home,
         home_weight,
-        far,
-        scratch_shapes=held,
+        *far,
+        scratch_shapes=held + [pltpu.VMEM(message_shape.shape, jnp.bfloat16)],
     )
     others = [send(others[turn - 1], onward(0), turn) for turn in range(1, groups)]
-    near = local_call(early_kernel, "combine_early", [part_shape, weight_shape], *near)
     return local_call(
         combine_kernel,
         "combine",
@@ -538,6 +575,7 @@
         own_weight,
         *near,
         *others,
+        *last,
     )
 
 

time: 26.1 us -> 27.4 us (1.050)
  waiting for transfers between devices: 4.17 us -> 5.91 us
  starting transfers between devices: 12.2 us -> 11.5 us
    ppermute x5 -> x6, waiting for transfers between devices: 4.17 us -> 5.91 us  [send(): return lax.ppermute(message, ('ra', 'band'), route)]
    ppermute x5 -> x6, starting transfers between devices: 12.2 us -> 11.5 us  [send(): return lax.ppermute(message, ('ra', 'band'), route)]
    pallas_call x5 -> x6, Pallas kernels: 1.62 us -> 1.8 us  [local_call(): pl.pallas_call(kernel, in_specs=[vmem] * len(operands), out_specs=[vmem]...]
  transfers between devices with their start and end apart: 5 -> 6, of which waited for: 3 -> 4; matrix products, arithmetic and copies ran while one was open for 0% -> 0% of each run, Pallas kernels for 3% -> 3%
where the time goes in v25:
time: 27.4 us; the launch traced here: 27.2 us
  starting transfers between devices  11.5 us (42%)
  Pallas kernels  8.16 us (30%)
  waiting for transfers between devices  5.91 us (22%)
  local copies, waits for them, and re-layouts  1 us (4%)
  between operations  0.67 us (2%)
    ppermute x6, starting transfers between devices, send(): return lax.ppermute(message, ('ra', 'band'), route)  11.5 us
    pallas_call x1, Pallas kernels, local(): pl.pallas_call(functools.partial(match_kernel, patches), in_specs=[anywhe...  6.36 us
    ppermute x6, waiting for transfers between devices, send(): return lax.ppermute(message, ('ra', 'band'), route)  5.91 us
    pallas_call x6, Pallas kernels, local_call(): pl.pallas_call(kernel, in_specs=[vmem] * len(operands), out_specs=[vmem]...  1.8 us
    unnamed x2, local copies, waits for them, and re-layouts  1 us
  transfers between devices with their start and end apart: 6, of which 4 were waited for; matrix products, arithmetic and copies ran while one was open for 0% of the time, Pallas kernels for 3%

profile of v25, /device:TPU:0, one launch (start us, length us, event | category | flops | bytes accessed | tf_op | source)
XLA Modules:
  0.0 27.2 jit_solution(10317052015776560156)
XLA Ops:
  0.6 6.4 %match_and_sum.1 = (bf16[2,272,256]{2,1,0:T(8,128)(2,1)}, bf16[3,272,256]{2,1,0:T(8,128)(2,1)}) custom-call(s32[32]{0:T(128)} %patch_hbm.1, s32[32]{0:T(128)} %offset_hbm.1, s32[32]{0:T(128)} %index_hbm.1, s32[4]{0:T(128)} %band_hbm.1, f32[6]{0:T(128)} %detect_hbm.1, f32[21,64]{1,0:T(8,128)} %bitcast.2, bf16[1,32]{1,0:T(2,128)(2,1)} %bitcast.3, ...), custom_call_target="tpu_custom_call" | custom-call | tf_op jit(solution)/shard_map/match_and_sum/pallas_call | solution.py:453
  7.0 0.5 %collective-permute-start = (bf16[2,272,256]{2,1,0:T(8,128)(2,1)}, bf16[2,272,256]{2,1,0:T(8,128)(2,1)S(1)}, u32[]{:S(2)}, u32[]{:S(2)}) collective-permute-start(bf16[2,272,256]{2,1,0:T(8,128)(2,1)} %get-tuple-element.24), channel_id=1, source_target_pairs={{0,2},{1,3},{2,0},{3,1},{4,6},{5,7},{6,4},{7,5},{8,10},{9,11},{10,... | collective-permute-start | bytes 835592 | tf_op jit(solution)/shard_map/ppermute | solution.py:500
  7.5 0.0 copy-start
  7.5 1.0 %copy-done = bf16[3,272,256]{2,1,0:T(8,128)(2,1)S(1)} copy-done((bf16[3,272,256]{2,1,0:T(8,128)(2,1)S(1)}, bf16[3,272,256]{2,1,0:T(8,128)(2,1)}, u32[]{:S(2)}) %copy-start) | copy-done | bytes 417816
  8.5 0.3 keep.1
  8.8 0.1 collective-permute-done.cross_ref
  8.9 0.3 %near.1 = (bf16[208,256]{1,0:T(8,128)(2,1)S(1)}, bf16[208,256]{1,0:T(8,128)(2,1)S(1)}, f32[8,256]{1,0:T(8,128)S(1)}) custom-call(f32[2,384,256]{2,1,0:T(8,128)S(1)} %get-tuple-element.22.totals_ref, f32[2,8,256]{2,1,0:T(8,128)S(1)} %get-tuple-element.23.weights_ref, bf16[2,272,256]{2,1,0:T(8,128)(2,1)S(1)} %collective-permute-done.cross_ref), custom_call_target="tpu_custom_call" | custom-call | tf_op jit(solution)/shard_map/near/pallas_call | solution.py:506
  9.2 5.7 %collective-permute-start.1 = (bf16[208,256]{1,0:T(8,128)(2,1)S(1)}, bf16[208,256]{1,0:T(8,128)(2,1)S(1)}, u32[]{:S(2)}, u32[]{:S(2)}) collective-permute-start(bf16[208,256]{1,0:T(8,128)(2,1)S(1)} %get-tuple-element.25), channel_id=1, source_target_pairs={{0,30},{1,31},{2,4},{3,5},{4,2},{5,3},{6,8},{7,9},{8,6},{9,7},{10,... | collective-permute-start | bytes 319496 | tf_op jit(solution)/shard_map/ppermute | solution.py:500
  14.9 0.2 merge.1
  15.1 0.6 %collective-permute-start.2 = (bf16[144,256]{1,0:T(8,128)(2,1)S(1)}, bf16[144,256]{1,0:T(8,128)(2,1)S(1)}, u32[]{:S(2)}, u32[]{:S(2)}) collective-permute-start(bf16[144,256]{1,0:T(8,128)(2,1)S(1)} %get-tuple-element.31), channel_id=1, source_target_pairs={{0,28},{1,29},{2,6},{3,7},{4,0},{5,1},{6,10},{7,11},{8,4},{9,5},{1... | collective-permute-start | bytes 221192 | tf_op jit(solution)/shard_map/ppermute | solution.py:500
  15.7 1.4 %collective-permute-start.3 = (bf16[128,256]{1,0:T(8,128)(2,1)S(1)}, bf16[128,256]{1,0:T(8,128)(2,1)S(1)}, u32[]{:S(2)}, u32[]{:S(2)}) collective-permute-start(bf16[128,256]{1,0:T(8,128)(2,1)S(1)} %get-tuple-element.32), channel_id=1, source_target_pairs={{0,28},{1,29},{2,6},{3,7},{4,0},{5,1},{6,10},{7,11},{8,4},{9,5},{1... | collective-permute-start | bytes 196616 | tf_op jit(solution)/shard_map/ppermute | solution.py:500
  17.1 1.7 %collective-permute-start.5 = (bf16[208,256]{1,0:T(8,128)(2,1)S(1)}, bf16[208,256]{1,0:T(8,128)(2,1)S(1)}, u32[]{:S(2)}, u32[]{:S(2)}) collective-permute-start(bf16[208,256]{1,0:T(8,128)(2,1)S(1)} %get-tuple-element.37), channel_id=1, source_target_pairs={{0,31},{1,30},{2,5},{3,4},{4,3},{5,2},{6,9},{7,8},{8,7},{9,6},{10,... | collective-permute-start | bytes 319496 | tf_op jit(solution)/shard_map/ppermute | solution.py:500
  18.8 0.0 collective-permute-done.1.refs_0_
  18.8 2.1 %collective-permute-done.3.rest_ref = bf16[128,256]{1,0:T(8,128)(2,1)S(1)} collective-permute-done((bf16[128,256]{1,0:T(8,128)(2,1)S(1)}, bf16[128,256]{1,0:T(8,128)(2,1)S(1)}, u32[]{:S(2)}, u32[]{:S(2)}) %collective-permute-start.3) | collective-permute-done | bytes 65568 | tf_op jit(solution)/shard_map/ppermute | solution.py:500
  20.9 0.0 collective-permute-done.2.top_ref
  20.9 0.3 %home.1 = (bf16[208,256]{1,0:T(8,128)(2,1)S(1)}, f32[192,256]{1,0:T(8,128)S(1)}, f32[8,256]{1,0:T(8,128)S(1)}) custom-call(f32[8,256]{1,0:T(8,128)S(1)} %get-tuple-element.26.after_ref.near_weight_ref, f32[384,256]{1,0:T(8,128)S(1)} %get-tuple-element.29.home_ref, f32[8,256]{1,0:T(8,128)S(1)} %get-tuple-element.30.home_weight_ref, ...), custom_call_target="tpu_custom_call" | custom-call | tf_op jit(solution)/shard_map/home/pallas_call | solution.py:506
  21.2 1.6 %collective-permute-start.4 = (bf16[208,256]{1,0:T(8,128)(2,1)S(1)}, bf16[208,256]{1,0:T(8,128)(2,1)S(1)}, u32[]{:S(2)}, u32[]{:S(2)}) collective-permute-start(bf16[208,256]{1,0:T(8,128)(2,1)S(1)} %get-tuple-element.36), channel_id=1, source_target_pairs={{0,1},{1,0},{2,3},{3,2},{4,5},{5,4},{6,7},{7,6},{8,9},{9,8},{10,11... | collective-permute-start | bytes 319496 | tf_op jit(solution)/shard_map/ppermute | solution.py:500
  22.8 2.1 %collective-permute-done.5.refs_1_ = bf16[208,256]{1,0:T(8,128)(2,1)S(1)} collective-permute-done((bf16[208,256]{1,0:T(8,128)(2,1)S(1)}, bf16[208,256]{1,0:T(8,128)(2,1)S(1)}, u32[]{:S(2)}, u32[]{:S(2)}) %collective-permute-start.5) | collective-permute-done | bytes 106528 | tf_op jit(solution)/shard_map/ppermute | solution.py:500
  24.9 1.5 %collective-permute-done.4.refs_0_ = bf16[208,256]{1,0:T(8,128)(2,1)S(1)} collective-permute-done((bf16[208,256]{1,0:T(8,128)(2,1)S(1)}, bf16[208,256]{1,0:T(8,128)(2,1)S(1)}, u32[]{:S(2)}, u32[]{:S(2)}) %collective-permute-start.4) | collective-permute-done | bytes 106528 | tf_op jit(solution)/shard_map/ppermute | solution.py:500
  26.5 0.7 %combine.1 = (f32[6,32,256]{2,1,0:T(8,128)}, f32[32,256]{1,0:T(8,128)}) custom-call(f32[8,256]{1,0:T(8,128)S(1)} %get-tuple-element.21.detect_ref, f32[192,256]{1,0:T(8,128)S(1)} %get-tuple-element.33.own_ref, f32[8,256]{1,0:T(8,128)S(1)} %get-tuple-element.34.own_weight_ref, f32[192,256]{1,0:T(8,128)S(1)} %get-tuple-element.35.near_ref, ...), custom_call_target="tpu_custom_call" | custom-call | tf_op jit(solution)/shard_map/combine/pallas_call | solution.py:506
  (1 shorter events, 0.0 us)
Async XLA Ops:
  7.0 1.9 %collective-permute-start = (bf16[2,272,256]{2,1,0:T(8,128)(2,1)}, bf16[2,272,256]{2,1,0:T(8,128)(2,1)S(1)}, u32[]{:S(2)}, u32[]{:S(2)}) collective-permute-start(bf16[2,272,256]{2,1,0:T(8,128)(2,1)} %get-tuple-element.24), channel_id=1, source_target_pairs={{0,2},{1,3},{2,0},{3,1},{4,6},{5,7},{6,4},{7,5},{8,10},{9,11},{10,... | collective-permute-start | bytes 835592 | tf_op jit(solution)/shard_map/ppermute | solution.py:500
  7.5 1.0 %copy-start = (bf16[3,272,256]{2,1,0:T(8,128)(2,1)S(1)}, bf16[3,272,256]{2,1,0:T(8,128)(2,1)}, u32[]{:S(2)}) copy-start(bf16[3,272,256]{2,1,0:T(8,128)(2,1)} %get-tuple-element.20.kept_ref) | copy-start | bytes 1253380
  9.2 9.6 %collective-permute-start.1 = (bf16[208,256]{1,0:T(8,128)(2,1)S(1)}, bf16[208,256]{1,0:T(8,128)(2,1)S(1)}, u32[]{:S(2)}, u32[]{:S(2)}) collective-permute-start(bf16[208,256]{1,0:T(8,128)(2,1)S(1)} %get-tuple-element.25), channel_id=1, source_target_pairs={{0,30},{1,31},{2,4},{3,5},{4,2},{5,3},{6,8},{7,9},{8,6},{9,7},{10,... | collective-permute-start | bytes 319496 | tf_op jit(solution)/shard_map/ppermute | solution.py:500
  15.1 5.8 %collective-permute-start.2 = (bf16[144,256]{1,0:T(8,128)(2,1)S(1)}, bf16[144,256]{1,0:T(8,128)(2,1)S(1)}, u32[]{:S(2)}, u32[]{:S(2)}) collective-permute-start(bf16[144,256]{1,0:T(8,128)(2,1)S(1)} %get-tuple-element.31), channel_id=1, source_target_pairs={{0,28},{1,29},{2,6},{3,7},{4,0},{5,1},{6,10},{7,11},{8,4},{9,5},{1... | collective-permute-start | bytes 221192 | tf_op jit(solution)/shard_map/ppermute | solution.py:500
  15.7 5.2 %collective-permute-start.3 = (bf16[128,256]{1,0:T(8,128)(2,1)S(1)}, bf16[128,256]{1,0:T(8,128)(2,1)S(1)}, u32[]{:S(2)}, u32[]{:S(2)}) collective-permute-start(bf16[128,256]{1,0:T(8,128)(2,1)S(1)} %get-tuple-element.32), channel_id=1, source_target_pairs={{0,28},{1,29},{2,6},{3,7},{4,0},{5,1},{6,10},{7,11},{8,4},{9,5},{1... | collective-permute-start | bytes 196616 | tf_op jit(solution)/shard_map/ppermute | solution.py:500
  17.1 7.8 %collective-permute-start.5 = (bf16[208,256]{1,0:T(8,128)(2,1)S(1)}, bf16[208,256]{1,0:T(8,128)(2,1)S(1)}, u32[]{:S(2)}, u32[]{:S(2)}) collective-permute-start(bf16[208,256]{1,0:T(8,128)(2,1)S(1)} %get-tuple-element.37), channel_id=1, source_target_pairs={{0,31},{1,30},{2,5},{3,4},{4,3},{5,2},{6,9},{7,8},{8,7},{9,6},{10,... | collective-permute-start | bytes 319496 | tf_op jit(solution)/shard_map/ppermute | solution.py:500
  21.2 5.2 %collective-permute-start.4 = (bf16[208,256]{1,0:T(8,128)(2,1)S(1)}, bf16[208,256]{1,0:T(8,128)(2,1)S(1)}, u32[]{:S(2)}, u32[]{:S(2)}) collective-permute-start(bf16[208,256]{1,0:T(8,128)(2,1)S(1)} %get-tuple-element.36), channel_id=1, source_target_pairs={{0,1},{1,0},{2,3},{3,2},{4,5},{5,4},{6,7},{7,6},{8,9},{9,8},{10,11... | collective-permute-start | bytes 319496 | tf_op jit(solution)/shard_map/ppermute | solution.py:500

commit v26 on v21

--- a/solution.py
+++ b/solution.py
@@ -514,7 +514,7 @@
         cross,
         scratch_shapes=held,
     )
-    near = [send(near[turn], onward(1), turn) for turn in range(groups)]
+    near = [send(near[turn], onward(1), turn) for turn in reversed(range(groups))]
     *others, own, own_weight = local_call(
         functools.partial(home_kernel, visits, groups),
         "home",

time: 26.1 us -> 26.1 us (level)
  no operation moved by 1% of the time
where the time goes in v26:
time: 26.1 us; the launch traced here: 25.9 us
  starting transfers between devices  12.1 us (46%)
  Pallas kernels  7.96 us (30%)
  waiting for transfers between devices  4.18 us (16%)
  local copies, waits for them, and re-layouts  0.96 us (4%)
  between operations  0.67 us (3%)
    ppermute x5, starting transfers between devices, send(): return lax.ppermute(message, ('ra', 'band'), route)  12.1 us
    pallas_call x1, Pallas kernels, local(): pl.pallas_call(functools.partial(match_kernel, patches), in_specs=[anywhe...  6.34 us
    ppermute x5, waiting for transfers between devices, send(): return lax.ppermute(message, ('ra', 'band'), route)  4.18 us
    pallas_call x5, Pallas kernels, local_call(): pl.pallas_call(kernel, in_specs=[vmem] * len(operands), out_specs=[vmem]...  1.62 us
    unnamed x2, local copies, waits for them, and re-layouts  0.96 us
  transfers between devices with their start and end apart: 5, of which 3 were waited for; matrix products, arithmetic and copies ran while one was open for 0% of the time, Pallas kernels for 3%

profile of v26, /device:TPU:0, one launch (start us, length us, event | category | flops | bytes accessed | tf_op | source)
XLA Modules:
  0.0 25.9 jit_solution(16040852188733952421)
XLA Ops:
  0.6 6.3 %match_and_sum.1 = (bf16[272,256]{1,0:T(8,128)(2,1)}, bf16[2,272,256]{2,1,0:T(8,128)(2,1)}, bf16[2,272,256]{2,1,0:T(8,128)(2,1)}) custom-call(s32[32]{0:T(128)} %patch_hbm.1, s32[32]{0:T(128)} %offset_hbm.1, s32[32]{0:T(128)} %index_hbm.1, s32[4]{0:T(128)} %band_hbm.1, f32[6]{0:T(128)} %detect_hbm.1, f32[21,64]{1,0:T(8,128)} %bitcast.2, ...), custom_call_target="tpu_custom_call" | custom-call | tf_op jit(solution)/shard_map/match_and_sum/pallas_call | solution.py:433
  7.0 0.5 %collective-permute-start = (bf16[2,272,256]{2,1,0:T(8,128)(2,1)}, bf16[2,272,256]{2,1,0:T(8,128)(2,1)S(1)}, u32[]{:S(2)}, u32[]{:S(2)}) collective-permute-start(bf16[2,272,256]{2,1,0:T(8,128)(2,1)} %get-tuple-element.21), channel_id=1, source_target_pairs={{0,2},{1,3},{2,0},{3,1},{4,6},{5,7},{6,4},{7,5},{8,10},{9,11},{10,... | collective-permute-start | bytes 835592 | tf_op jit(solution)/shard_map/ppermute | solution.py:480
  7.5 5.6 %collective-permute-start.1 = (bf16[272,256]{1,0:T(8,128)(2,1)}, bf16[272,256]{1,0:T(8,128)(2,1)S(1)}, u32[]{:S(2)}, u32[]{:S(2)}) collective-permute-start(bf16[272,256]{1,0:T(8,128)(2,1)} %get-tuple-element.24), channel_id=1, source_target_pairs={{0,28},{1,29},{2,6},{3,7},{4,0},{5,1},{6,10},{7,11},{8,4},{9,5},{1... | collective-permute-start | bytes 417800 | tf_op jit(solution)/shard_map/ppermute | solution.py:480
  13.1 0.0 copy-start
  13.1 1.0 %copy-done = bf16[2,272,256]{2,1,0:T(8,128)(2,1)S(1)} copy-done((bf16[2,272,256]{2,1,0:T(8,128)(2,1)S(1)}, bf16[2,272,256]{2,1,0:T(8,128)(2,1)}, u32[]{:S(2)}) %copy-start) | copy-done | bytes 278552
  14.0 0.3 %keep.1 = (f32[2,384,256]{2,1,0:T(8,128)S(1)}, f32[2,8,256]{2,1,0:T(8,128)S(1)}, f32[8,256]{1,0:T(8,128)S(1)}) custom-call(bf16[2,272,256]{2,1,0:T(8,128)(2,1)S(1)} %copy-done), custom_call_target="tpu_custom_call" | custom-call | tf_op jit(solution)/shard_map/keep/pallas_call | solution.py:486
  14.3 0.0 collective-permute-done.cross_ref
  14.3 0.3 %merge.1 = (bf16[208,256]{1,0:T(8,128)(2,1)S(1)}, bf16[208,256]{1,0:T(8,128)(2,1)S(1)}, f32[384,256]{1,0:T(8,128)S(1)}, f32[8,256]{1,0:T(8,128)S(1)}) custom-call(f32[2,384,256]{2,1,0:T(8,128)S(1)} %get-tuple-element.19.totals_ref, f32[2,8,256]{2,1,0:T(8,128)S(1)} %get-tuple-element.20.weights_ref, bf16[2,272,256]{2,1,0:T(8,128)(2,1)S(1)} %collective-permute-done.cross_ref), custom_call_target="tpu_custom_call" | custom-call | tf_op jit(solution)/shard_map/merge/pallas_call | solution.py:486
  14.7 1.2 %collective-permute-start.2 = (bf16[208,256]{1,0:T(8,128)(2,1)S(1)}, bf16[208,256]{1,0:T(8,128)(2,1)S(1)}, u32[]{:S(2)}, u32[]{:S(2)}) collective-permute-start(bf16[208,256]{1,0:T(8,128)(2,1)S(1)} %get-tuple-element.27), channel_id=1, source_target_pairs={{0,31},{1,30},{2,5},{3,4},{4,3},{5,2},{6,9},{7,8},{8,7},{9,6},{10,... | collective-permute-start | bytes 319496 | tf_op jit(solution)/shard_map/ppermute | solution.py:480
  15.9 4.2 %collective-permute-start.3 = (bf16[208,256]{1,0:T(8,128)(2,1)S(1)}, bf16[208,256]{1,0:T(8,128)(2,1)S(1)}, u32[]{:S(2)}, u32[]{:S(2)}) collective-permute-start(bf16[208,256]{1,0:T(8,128)(2,1)S(1)} %get-tuple-element.28), channel_id=1, source_target_pairs={{0,30},{1,31},{2,4},{3,5},{4,2},{5,3},{6,8},{7,9},{8,6},{9,7},{10,... | collective-permute-start | bytes 319496 | tf_op jit(solution)/shard_map/ppermute | solution.py:480
  20.1 0.0 collective-permute-done.1.far_ref
  20.1 0.3 %home.1 = (bf16[208,256]{1,0:T(8,128)(2,1)S(1)}, f32[192,256]{1,0:T(8,128)S(1)}, f32[8,256]{1,0:T(8,128)S(1)}) custom-call(f32[384,256]{1,0:T(8,128)S(1)} %get-tuple-element.22.home_ref, f32[8,256]{1,0:T(8,128)S(1)} %get-tuple-element.23.home_weight_ref, bf16[272,256]{1,0:T(8,128)(2,1)S(1)} %collective-permute-done.1.far_ref), custom_call_target="tpu_custom_call" | custom-call | tf_op jit(solution)/shard_map/home/pallas_call | solution.py:486
  20.4 0.6 %collective-permute-start.4 = (bf16[208,256]{1,0:T(8,128)(2,1)S(1)}, bf16[208,256]{1,0:T(8,128)(2,1)S(1)}, u32[]{:S(2)}, u32[]{:S(2)}) collective-permute-start(bf16[208,256]{1,0:T(8,128)(2,1)S(1)} %get-tuple-element.31), channel_id=1, source_target_pairs={{0,1},{1,0},{2,3},{3,2},{4,5},{5,4},{6,7},{7,6},{8,9},{9,8},{10,11... | collective-permute-start | bytes 319496 | tf_op jit(solution)/shard_map/ppermute | solution.py:480
  21.0 1.5 %collective-permute-done.2.refs_0_ = bf16[208,256]{1,0:T(8,128)(2,1)S(1)} collective-permute-done((bf16[208,256]{1,0:T(8,128)(2,1)S(1)}, bf16[208,256]{1,0:T(8,128)(2,1)S(1)}, u32[]{:S(2)}, u32[]{:S(2)}) %collective-permute-start.2) | collective-permute-done | bytes 106528 | tf_op jit(solution)/shard_map/ppermute | solution.py:480
  22.4 1.2 %collective-permute-done.3.refs_1_ = bf16[208,256]{1,0:T(8,128)(2,1)S(1)} collective-permute-done((bf16[208,256]{1,0:T(8,128)(2,1)S(1)}, bf16[208,256]{1,0:T(8,128)(2,1)S(1)}, u32[]{:S(2)}, u32[]{:S(2)}) %collective-permute-start.3) | collective-permute-done | bytes 106528 | tf_op jit(solution)/shard_map/ppermute | solution.py:480
  23.7 1.5 %collective-permute-done.4.refs_0_ = bf16[208,256]{1,0:T(8,128)(2,1)S(1)} collective-permute-done((bf16[208,256]{1,0:T(8,128)(2,1)S(1)}, bf16[208,256]{1,0:T(8,128)(2,1)S(1)}, u32[]{:S(2)}, u32[]{:S(2)}) %collective-permute-start.4) | collective-permute-done | bytes 106528 | tf_op jit(solution)/shard_map/ppermute | solution.py:480
  25.2 0.7 %combine.1 = (f32[6,32,256]{2,1,0:T(8,128)}, f32[32,256]{1,0:T(8,128)}) custom-call(f32[8,256]{1,0:T(8,128)S(1)} %get-tuple-element.18.detect_ref, f32[192,256]{1,0:T(8,128)S(1)} %get-tuple-element.25.own_ref, f32[8,256]{1,0:T(8,128)S(1)} %get-tuple-element.26.own_weight_ref, f32[192,256]{1,0:T(8,128)S(1)} %get-tuple-element.29.near_ref, ...), custom_call_target="tpu_custom_call" | custom-call | tf_op jit(solution)/shard_map/combine/pallas_call | solution.py:486
  (1 shorter events, 0.0 us)
Async XLA Ops:
  7.0 7.3 %collective-permute-start = (bf16[2,272,256]{2,1,0:T(8,128)(2,1)}, bf16[2,272,256]{2,1,0:T(8,128)(2,1)S(1)}, u32[]{:S(2)}, u32[]{:S(2)}) collective-permute-start(bf16[2,272,256]{2,1,0:T(8,128)(2,1)} %get-tuple-element.21), channel_id=1, source_target_pairs={{0,2},{1,3},{2,0},{3,1},{4,6},{5,7},{6,4},{7,5},{8,10},{9,11},{10,... | collective-permute-start | bytes 835592 | tf_op jit(solution)/shard_map/ppermute | solution.py:480
  7.5 12.6 %collective-permute-start.1 = (bf16[272,256]{1,0:T(8,128)(2,1)}, bf16[272,256]{1,0:T(8,128)(2,1)S(1)}, u32[]{:S(2)}, u32[]{:S(2)}) collective-permute-start(bf16[272,256]{1,0:T(8,128)(2,1)} %get-tuple-element.24), channel_id=1, source_target_pairs={{0,28},{1,29},{2,6},{3,7},{4,0},{5,1},{6,10},{7,11},{8,4},{9,5},{1... | collective-permute-start | bytes 417800 | tf_op jit(solution)/shard_map/ppermute | solution.py:480
  13.1 1.0 %copy-start = (bf16[2,272,256]{2,1,0:T(8,128)(2,1)S(1)}, bf16[2,272,256]{2,1,0:T(8,128)(2,1)}, u32[]{:S(2)}) copy-start(bf16[2,272,256]{2,1,0:T(8,128)(2,1)} %get-tuple-element.17.kept_ref) | copy-start | bytes 835588
  14.7 7.8 %collective-permute-start.2 = (bf16[208,256]{1,0:T(8,128)(2,1)S(1)}, bf16[208,256]{1,0:T(8,128)(2,1)S(1)}, u32[]{:S(2)}, u32[]{:S(2)}) collective-permute-start(bf16[208,256]{1,0:T(8,128)(2,1)S(1)} %get-tuple-element.27), channel_id=1, source_target_pairs={{0,31},{1,30},{2,5},{3,4},{4,3},{5,2},{6,9},{7,8},{8,7},{9,6},{10,... | collective-permute-start | bytes 319496 | tf_op jit(solution)/shard_map/ppermute | solution.py:480
  15.9 7.8 %collective-permute-start.3 = (bf16[208,256]{1,0:T(8,128)(2,1)S(1)}, bf16[208,256]{1,0:T(8,128)(2,1)S(1)}, u32[]{:S(2)}, u32[]{:S(2)}) collective-permute-start(bf16[208,256]{1,0:T(8,128)(2,1)S(1)} %get-tuple-element.28), channel_id=1, source_target_pairs={{0,30},{1,31},{2,4},{3,5},{4,2},{5,3},{6,8},{7,9},{8,6},{9,7},{10,... | collective-permute-start | bytes 319496 | tf_op jit(solution)/shard_map/ppermute | solution.py:480
  20.4 4.8 %collective-permute-start.4 = (bf16[208,256]{1,0:T(8,128)(2,1)S(1)}, bf16[208,256]{1,0:T(8,128)(2,1)S(1)}, u32[]{:S(2)}, u32[]{:S(2)}) collective-permute-start(bf16[208,256]{1,0:T(8,128)(2,1)S(1)} %get-tuple-element.31), channel_id=1, source_target_pairs={{0,1},{1,0},{2,3},{3,2},{4,5},{5,4},{6,7},{7,6},{8,9},{9,8},{10,11... | collective-permute-start | bytes 319496 | tf_op jit(solution)/shard_map/ppermute | solution.py:480

commit v27 on v21

--- a/solution.py
+++ b/solution.py
@@ -147,10 +147,7 @@
         part = col_taps[side * VECTORS : (side + 1) * VECTORS]
         mix = jnp.concatenate([part * coeffs[j : j + 1] for j in range(tile_count)], axis=0)
         high = mix.astype(jnp.bfloat16)
-        low = (mix - high.astype(jnp.float32)).astype(jnp.bfloat16)
-        term = jnp.dot(high, row_taps, preferred_element_type=jnp.float32) + jnp.dot(
-            low, row_taps, preferred_element_type=jnp.float32
-        )
+        term = jnp.dot(high, row_taps, preferred_element_type=jnp.float32)
         total = term if total is None else total + term
     kernels[...] = total
 

time: 26.1 us -> 25.8 us (0.989)
  Pallas kernels: 7.96 us -> 7.66 us
    pallas_call x1, Pallas kernels: 6.34 us -> 6.04 us  [local(): pl.pallas_call(functools.partial(match_kernel, patches), in_specs=[anywhe...]
where the time goes in v27:
time: 25.8 us; the launch traced here: 25.6 us
  starting transfers between devices  12.1 us (47%)
  Pallas kernels  7.66 us (30%)
  waiting for transfers between devices  4.18 us (16%)
  local copies, waits for them, and re-layouts  0.96 us (4%)
  between operations  0.67 us (3%)
    ppermute x5, starting transfers between devices, send(): return lax.ppermute(message, ('ra', 'band'), route)  12.1 us
    pallas_call x1, Pallas kernels, local(): pl.pallas_call(functools.partial(match_kernel, patches), in_specs=[anywhe...  6.04 us
    ppermute x5, waiting for transfers between devices, send(): return lax.ppermute(message, ('ra', 'band'), route)  4.18 us
    pallas_call x5, Pallas kernels, local_call(): pl.pallas_call(kernel, in_specs=[vmem] * len(operands), out_specs=[vmem]...  1.62 us
    unnamed x2, local copies, waits for them, and re-layouts  0.96 us
  transfers between devices with their start and end apart: 5, of which 3 were waited for; matrix products, arithmetic and copies ran while one was open for 0% of the time, Pallas kernels for 3%

profile of v27, /device:TPU:0, one launch (start us, length us, event | category | flops | bytes accessed | tf_op | source)
XLA Modules:
  0.0 25.6 jit_solution(6142893316029820923)
XLA Ops:
  0.6 6.0 %match_and_sum.1 = (bf16[272,256]{1,0:T(8,128)(2,1)}, bf16[2,272,256]{2,1,0:T(8,128)(2,1)}, bf16[2,272,256]{2,1,0:T(8,128)(2,1)}) custom-call(s32[32]{0:T(128)} %patch_hbm.1, s32[32]{0:T(128)} %offset_hbm.1, s32[32]{0:T(128)} %index_hbm.1, s32[4]{0:T(128)} %band_hbm.1, f32[6]{0:T(128)} %detect_hbm.1, f32[21,64]{1,0:T(8,128)} %bitcast.2, ...), custom_call_target="tpu_custom_call" | custom-call | tf_op jit(solution)/shard_map/match_and_sum/pallas_call | solution.py:430
  6.7 0.5 %collective-permute-start = (bf16[2,272,256]{2,1,0:T(8,128)(2,1)}, bf16[2,272,256]{2,1,0:T(8,128)(2,1)S(1)}, u32[]{:S(2)}, u32[]{:S(2)}) collective-permute-start(bf16[2,272,256]{2,1,0:T(8,128)(2,1)} %get-tuple-element.21), channel_id=1, source_target_pairs={{0,2},{1,3},{2,0},{3,1},{4,6},{5,7},{6,4},{7,5},{8,10},{9,11},{10,... | collective-permute-start | bytes 835592 | tf_op jit(solution)/shard_map/ppermute | solution.py:477
  7.2 5.6 %collective-permute-start.1 = (bf16[272,256]{1,0:T(8,128)(2,1)}, bf16[272,256]{1,0:T(8,128)(2,1)S(1)}, u32[]{:S(2)}, u32[]{:S(2)}) collective-permute-start(bf16[272,256]{1,0:T(8,128)(2,1)} %get-tuple-element.24), channel_id=1, source_target_pairs={{0,28},{1,29},{2,6},{3,7},{4,0},{5,1},{6,10},{7,11},{8,4},{9,5},{1... | collective-permute-start | bytes 417800 | tf_op jit(solution)/shard_map/ppermute | solution.py:477
  12.8 0.0 copy-start
  12.8 1.0 %copy-done = bf16[2,272,256]{2,1,0:T(8,128)(2,1)S(1)} copy-done((bf16[2,272,256]{2,1,0:T(8,128)(2,1)S(1)}, bf16[2,272,256]{2,1,0:T(8,128)(2,1)}, u32[]{:S(2)}) %copy-start) | copy-done | bytes 278552
  13.7 0.3 %keep.1 = (f32[2,384,256]{2,1,0:T(8,128)S(1)}, f32[2,8,256]{2,1,0:T(8,128)S(1)}, f32[8,256]{1,0:T(8,128)S(1)}) custom-call(bf16[2,272,256]{2,1,0:T(8,128)(2,1)S(1)} %copy-done), custom_call_target="tpu_custom_call" | custom-call | tf_op jit(solution)/shard_map/keep/pallas_call | solution.py:483
  14.0 0.0 collective-permute-done.cross_ref
  14.0 0.3 %merge.1 = (bf16[208,256]{1,0:T(8,128)(2,1)S(1)}, bf16[208,256]{1,0:T(8,128)(2,1)S(1)}, f32[384,256]{1,0:T(8,128)S(1)}, f32[8,256]{1,0:T(8,128)S(1)}) custom-call(f32[2,384,256]{2,1,0:T(8,128)S(1)} %get-tuple-element.19.totals_ref, f32[2,8,256]{2,1,0:T(8,128)S(1)} %get-tuple-element.20.weights_ref, bf16[2,272,256]{2,1,0:T(8,128)(2,1)S(1)} %collective-permute-done.cross_ref), custom_call_target="tpu_custom_call" | custom-call | tf_op jit(solution)/shard_map/merge/pallas_call | solution.py:483
  14.4 0.3 %collective-permute-start.2 = (bf16[208,256]{1,0:T(8,128)(2,1)S(1)}, bf16[208,256]{1,0:T(8,128)(2,1)S(1)}, u32[]{:S(2)}, u32[]{:S(2)}) collective-permute-start(bf16[208,256]{1,0:T(8,128)(2,1)S(1)} %get-tuple-element.27), channel_id=1, source_target_pairs={{0,30},{1,31},{2,4},{3,5},{4,2},{5,3},{6,8},{7,9},{8,6},{9,7},{10,... | collective-permute-start | bytes 319496 | tf_op jit(solution)/shard_map/ppermute | solution.py:477
  14.6 5.2 %collective-permute-start.3 = (bf16[208,256]{1,0:T(8,128)(2,1)S(1)}, bf16[208,256]{1,0:T(8,128)(2,1)S(1)}, u32[]{:S(2)}, u32[]{:S(2)}) collective-permute-start(bf16[208,256]{1,0:T(8,128)(2,1)S(1)} %get-tuple-element.28), channel_id=1, source_target_pairs={{0,31},{1,30},{2,5},{3,4},{4,3},{5,2},{6,9},{7,8},{8,7},{9,6},{10,... | collective-permute-start | bytes 319496 | tf_op jit(solution)/shard_map/ppermute | solution.py:477
  19.8 0.0 collective-permute-done.1.far_ref
  19.8 0.3 %home.1 = (bf16[208,256]{1,0:T(8,128)(2,1)S(1)}, f32[192,256]{1,0:T(8,128)S(1)}, f32[8,256]{1,0:T(8,128)S(1)}) custom-call(f32[384,256]{1,0:T(8,128)S(1)} %get-tuple-element.22.home_ref, f32[8,256]{1,0:T(8,128)S(1)} %get-tuple-element.23.home_weight_ref, bf16[272,256]{1,0:T(8,128)(2,1)S(1)} %collective-permute-done.1.far_ref), custom_call_target="tpu_custom_call" | custom-call | tf_op jit(solution)/shard_map/home/pallas_call | solution.py:483
  20.1 0.6 %collective-permute-start.4 = (bf16[208,256]{1,0:T(8,128)(2,1)S(1)}, bf16[208,256]{1,0:T(8,128)(2,1)S(1)}, u32[]{:S(2)}, u32[]{:S(2)}) collective-permute-start(bf16[208,256]{1,0:T(8,128)(2,1)S(1)} %get-tuple-element.31), channel_id=1, source_target_pairs={{0,1},{1,0},{2,3},{3,2},{4,5},{5,4},{6,7},{7,6},{8,9},{9,8},{10,11... | collective-permute-start | bytes 319496 | tf_op jit(solution)/shard_map/ppermute | solution.py:477
  20.7 0.6 %collective-permute-done.2.refs_0_ = bf16[208,256]{1,0:T(8,128)(2,1)S(1)} collective-permute-done((bf16[208,256]{1,0:T(8,128)(2,1)S(1)}, bf16[208,256]{1,0:T(8,128)(2,1)S(1)}, u32[]{:S(2)}, u32[]{:S(2)}) %collective-permute-start.2) | collective-permute-done | bytes 106528 | tf_op jit(solution)/shard_map/ppermute | solution.py:477
  21.2 2.1 %collective-permute-done.3.refs_1_ = bf16[208,256]{1,0:T(8,128)(2,1)S(1)} collective-permute-done((bf16[208,256]{1,0:T(8,128)(2,1)S(1)}, bf16[208,256]{1,0:T(8,128)(2,1)S(1)}, u32[]{:S(2)}, u32[]{:S(2)}) %collective-permute-start.3) | collective-permute-done | bytes 106528 | tf_op jit(solution)/shard_map/ppermute | solution.py:477
  23.4 1.5 %collective-permute-done.4.refs_0_ = bf16[208,256]{1,0:T(8,128)(2,1)S(1)} collective-permute-done((bf16[208,256]{1,0:T(8,128)(2,1)S(1)}, bf16[208,256]{1,0:T(8,128)(2,1)S(1)}, u32[]{:S(2)}, u32[]{:S(2)}) %collective-permute-start.4) | collective-permute-done | bytes 106528 | tf_op jit(solution)/shard_map/ppermute | solution.py:477
  24.9 0.7 %combine.1 = (f32[6,32,256]{2,1,0:T(8,128)}, f32[32,256]{1,0:T(8,128)}) custom-call(f32[8,256]{1,0:T(8,128)S(1)} %get-tuple-element.18.detect_ref, f32[192,256]{1,0:T(8,128)S(1)} %get-tuple-element.25.own_ref, f32[8,256]{1,0:T(8,128)S(1)} %get-tuple-element.26.own_weight_ref, f32[192,256]{1,0:T(8,128)S(1)} %get-tuple-element.29.near_ref, ...), custom_call_target="tpu_custom_call" | custom-call | tf_op jit(solution)/shard_map/combine/pallas_call | solution.py:483
  (1 shorter events, 0.0 us)
Async XLA Ops:
  6.7 7.3 %collective-permute-start = (bf16[2,272,256]{2,1,0:T(8,128)(2,1)}, bf16[2,272,256]{2,1,0:T(8,128)(2,1)S(1)}, u32[]{:S(2)}, u32[]{:S(2)}) collective-permute-start(bf16[2,272,256]{2,1,0:T(8,128)(2,1)} %get-tuple-element.21), channel_id=1, source_target_pairs={{0,2},{1,3},{2,0},{3,1},{4,6},{5,7},{6,4},{7,5},{8,10},{9,11},{10,... | collective-permute-start | bytes 835592 | tf_op jit(solution)/shard_map/ppermute | solution.py:477
  7.2 12.6 %collective-permute-start.1 = (bf16[272,256]{1,0:T(8,128)(2,1)}, bf16[272,256]{1,0:T(8,128)(2,1)S(1)}, u32[]{:S(2)}, u32[]{:S(2)}) collective-permute-start(bf16[272,256]{1,0:T(8,128)(2,1)} %get-tuple-element.24), channel_id=1, source_target_pairs={{0,28},{1,29},{2,6},{3,7},{4,0},{5,1},{6,10},{7,11},{8,4},{9,5},{1... | collective-permute-start | bytes 417800 | tf_op jit(solution)/shard_map/ppermute | solution.py:477
  12.8 1.0 %copy-start = (bf16[2,272,256]{2,1,0:T(8,128)(2,1)S(1)}, bf16[2,272,256]{2,1,0:T(8,128)(2,1)}, u32[]{:S(2)}) copy-start(bf16[2,272,256]{2,1,0:T(8,128)(2,1)} %get-tuple-element.17.kept_ref) | copy-start | bytes 835588
  14.4 6.9 %collective-permute-start.2 = (bf16[208,256]{1,0:T(8,128)(2,1)S(1)}, bf16[208,256]{1,0:T(8,128)(2,1)S(1)}, u32[]{:S(2)}, u32[]{:S(2)}) collective-permute-start(bf16[208,256]{1,0:T(8,128)(2,1)S(1)} %get-tuple-element.27), channel_id=1, source_target_pairs={{0,30},{1,31},{2,4},{3,5},{4,2},{5,3},{6,8},{7,9},{8,6},{9,7},{10,... | collective-permute-start | bytes 319496 | tf_op jit(solution)/shard_map/ppermute | solution.py:477
  14.6 8.7 %collective-permute-start.3 = (bf16[208,256]{1,0:T(8,128)(2,1)S(1)}, bf16[208,256]{1,0:T(8,128)(2,1)S(1)}, u32[]{:S(2)}, u32[]{:S(2)}) collective-permute-start(bf16[208,256]{1,0:T(8,128)(2,1)S(1)} %get-tuple-element.28), channel_id=1, source_target_pairs={{0,31},{1,30},{2,5},{3,4},{4,3},{5,2},{6,9},{7,8},{8,7},{9,6},{10,... | collective-permute-start | bytes 319496 | tf_op jit(solution)/shard_map/ppermute | solution.py:477
  20.1 4.8 %collective-permute-start.4 = (bf16[208,256]{1,0:T(8,128)(2,1)S(1)}, bf16[208,256]{1,0:T(8,128)(2,1)S(1)}, u32[]{:S(2)}, u32[]{:S(2)}) collective-permute-start(bf16[208,256]{1,0:T(8,128)(2,1)S(1)} %get-tuple-element.31), channel_id=1, source_target_pairs={{0,1},{1,0},{2,3},{3,2},{4,5},{5,4},{6,7},{7,6},{8,9},{9,8},{10,11... | collective-permute-start | bytes 319496 | tf_op jit(solution)/shard_map/ppermute | solution.py:477
